TPU v7x, 32 devices: a whole 2x2x4 slice. The times are simulated.
32 devices in a mesh: seq: 8 (over z, y), row: 4 (over x, core).
Axes of the slice: x: 2, y: 2, z: 4, core: 2. Of those that a mesh axis runs over, the one named last changes fastest.
Arguments:
- tokens: bfloat16 [32, 2048, 512], P('row', 'seq'), may hold values from -6 to 6
- valid_count: int32 [32], P('row'), may hold values from 1024 to 2048, as said below
- norm_gain: bfloat16 [512], replicated, may hold values from 0.099609375 to 1.8984375
- value_weight: bfloat16 [512, 1024], replicated, may hold values from -0.25 to 0.25
- ema_forget: float32 [512, 16], replicated, may hold values from 5e-07 to 0.03
- ema_beta: float32 [512, 16], replicated, may hold values from -4 to 4
- ema_eta: float32 [512, 16], replicated, may hold values from -1.5 to 1.5
- ema_omega: float32 [512], replicated, may hold values from -4 to 4
- base_weight: bfloat16 [512, 2176], replicated, may hold values from -0.25 to 0.25
- qk_gain: bfloat16 [2, 128], replicated, may hold values from -8 to 8
- qk_bias: bfloat16 [2, 128], replicated, may hold values from -6 to 6
- output_weight: bfloat16 [1024, 512], replicated, may hold values from -0.5 to 0.5
- ffn_gain: bfloat16 [512], replicated, may hold values from 0.099609375 to 1.8984375
- ffn_in: bfloat16 [512, 1024], replicated, may hold values from -0.25 to 0.25
- ffn_out: bfloat16 [1024, 512], replicated, may hold values from -0.1875 to 0.1875
- cotangent: bfloat16 [32, 2048, 512], P('row', 'seq'), may hold values from -6 to 6
Outputs:
- block_out: bfloat16 [32, 2048, 512], P('row', 'seq')
- grad_tokens: bfloat16 [32, 2048, 512], P('row', 'seq')
- grad_norm_gain: float32 [512], replicated
- grad_value_weight: float32 [512, 1024], replicated
- grad_ema_forget: float32 [512, 16], replicated
- grad_ema_beta: float32 [512, 16], replicated
- grad_ema_eta: float32 [512, 16], replicated
- grad_ema_omega: float32 [512], replicated
- grad_base_weight: float32 [512, 2176], replicated
- grad_qk_gain: float32 [2, 128], replicated
- grad_qk_bias: float32 [2, 128], replicated
- grad_output_weight: float32 [1024, 512], replicated
- grad_ffn_gain: float32 [512], replicated
- grad_ffn_in: float32 [512, 1024], replicated
- grad_ffn_out: float32 [1024, 512], replicated
Inputs may be any that keep to these rules, and one draw needn't show every extreme that they name: `valid_count`: each row's count of valid positions; positions at or past it are padding.
All inputs are finite; a program needn't handle non-finite values.
Results may differ from a plain program's by a relative error of at most 0.03.
Values sent between devices are 32-bit elements; how exact they have to be, the bound alone decides.
No kernel may reach another device: no remote copies, remote signals or barrier semaphores. Data moves between devices by JAX's collectives and lax.ppermute only.
A program may use at most 320 MiB of HBM per device.

v0:
```python
import jax
import jax.numpy as jnp
from jax import lax
from jax.sharding import PartitionSpec as P

GROUP = 128


epsilon = 1e-05
very_low = -1e30
careful = lax.Precision.HIGH


def carried_in(value, axis, join, neutral, backward):
    count, mine = (lax.axis_size(axis), lax.axis_index(axis))
    pieces = jax.tree.map(lambda part: lax.all_gather(part, axis), value)
    if backward:
        pieces = jax.tree.map(lambda part: part[::-1], pieces)
        mine = count - 1 - mine
    so_far = jax.tree.map(
        lambda part, zero: jnp.full_like(part, 0) + jnp.asarray(zero, part.dtype), value, neutral
    )

    def turn(position, so_far):
        longer = join(so_far, jax.tree.map(lambda part: part[position], pieces))
        return jax.tree.map(lambda new, old: jnp.where(position < mine, new, old), longer, so_far)

    return lax.fori_loop(0, count - 1, turn, so_far)


def layer_norm(inputs, scales):
    centered = inputs - jnp.mean(inputs, axis=-1, keepdims=True)
    spread = jnp.mean(centered * centered, axis=-1, keepdims=True)
    return centered * lax.rsqrt(spread + epsilon) * scales


def plain_dot(first_op, second_op):
    return jnp.dot(first_op, second_op, preferred_element_type=jnp.float32)


def outer_dot(first_op, second_op):
    return lax.dot_general(
        first_op, second_op, (((0,), (0,)), ((), ())), preferred_element_type=jnp.float32
    )


def inner_dot(first_op, second_op):
    return lax.dot_general(
        first_op, second_op, (((1,), (1,)), ((), ())), preferred_element_type=jnp.float32
    )


def batch_dot(first_op, second_op):
    return lax.dot_general(
        first_op,
        second_op,
        (((2,), (1,)), ((0,), (0,))),
        precision=careful,
        preferred_element_type=jnp.float32,
    )


def decay_terms(ema_forget, ema_beta):
    log_retain = jnp.log(1.0 - ema_forget)
    inflow = ema_beta * jnp.sqrt(ema_forget * (2.0 - ema_forget))
    return (log_retain, inflow)


def end_states(block_inputs, ema_forget, ema_beta):
    row_count, blocks, length, feature_count = block_inputs.shape
    log_retain, inflow = decay_terms(ema_forget, ema_beta)
    places = jnp.arange(length, dtype=jnp.float32)
    to_end = inflow[:, None, :] * jnp.exp(
        (length - 1.0 - places)[None, :, None] * log_retain[:, None, :]
    )
    by_feature = block_inputs.transpose(3, 0, 1, 2).reshape(
        feature_count, row_count * blocks, length
    )
    block_end = batch_dot(by_feature, to_end)
    block_end = block_end.reshape(feature_count, row_count, blocks, -1).transpose(1, 2, 0, 3)
    counts = jnp.arange(blocks, dtype=jnp.float32)
    carried = jnp.exp(((blocks - 1.0 - counts) * length)[:, None, None] * log_retain[None])
    device_end = jnp.sum(block_end * carried[None], axis=1)
    span_decay = jnp.exp(blocks * length * log_retain)
    return (block_end, span_decay, device_end)


def ema_output(block_inputs, ema_forget, ema_beta, ema_eta, block_end, incoming):
    row_count, blocks, length, feature_count = block_inputs.shape
    log_retain, inflow = decay_terms(ema_forget, ema_beta)
    places = jnp.arange(length, dtype=jnp.float32)
    growth = (ema_eta * inflow)[:, None, :] * jnp.exp(
        places[None, :, None] * log_retain[:, None, :]
    )
    shrink = jnp.exp(-places[None, :, None] * log_retain[:, None, :])
    lower_tri = (places[:, None] >= places[None, :]).astype(jnp.float32)
    kernel = (
        lax.dot_general(
            growth,
            shrink,
            (((2,), (2,)), ((0,), (0,))),
            precision=careful,
            preferred_element_type=jnp.float32,
        )
        * lower_tri[None]
    )
    by_feature = block_inputs.transpose(3, 2, 0, 1).reshape(
        feature_count, length, row_count * blocks
    )
    local_part = batch_dot(kernel, by_feature)
    local_part = local_part.reshape(feature_count, length, row_count, blocks).transpose(2, 3, 1, 0)
    step_decay = jnp.exp(length * log_retain)
    before = []
    running = incoming
    for block_index in range(blocks):
        before.append(running)
        running = step_decay * running + block_end[:, block_index]
    entering = jnp.stack(before, axis=1)
    readout = ema_eta[:, None, :] * jnp.exp((places + 1.0)[None, :, None] * log_retain[:, None, :])
    entering_feature = entering.transpose(2, 3, 0, 1).reshape(feature_count, -1, row_count * blocks)
    carried = batch_dot(readout, entering_feature)
    carried = carried.reshape(feature_count, length, row_count, blocks).transpose(2, 3, 1, 0)
    return (local_part + carried).reshape(row_count, blocks * length, feature_count)


def forward_combine(earlier_part, later_part):
    return (earlier_part[0] * later_part[0], later_part[0][None] * earlier_part[1] + later_part[1])


def mix_piece(ema_flat, normed, ema_omega):
    return jax.nn.silu(ema_flat + ema_omega * normed)


def query_piece(shared_pre, gains, biases):
    shared_act = jax.nn.silu(shared_pre)
    return (shared_act * gains[0] + biases[0], shared_act * gains[1] + biases[1])


def merge_piece(candidate_pre, projected, update_pre, flat_in):
    return flat_in + jax.nn.sigmoid(update_pre) * (jax.nn.silu(candidate_pre + projected) - flat_in)


def per_device(
    tokens,
    valid_count,
    norm_gain,
    value_weight,
    ema_forget,
    ema_beta,
    ema_eta,
    ema_omega,
    base_weight,
    qk_gain,
    qk_bias,
    output_weight,
    ffn_gain,
    ffn_in,
    ffn_out,
    cotangent,
):
    row_count, seq_len, model_width = tokens.shape
    block_total = seq_len // GROUP
    query_width = qk_gain.shape[1]
    value_width = value_weight.shape[1]
    token_count = row_count * seq_len
    block_count = row_count * block_total
    score_scale = query_width ** (-0.5)
    device = lax.axis_index("seq")
    places = device * seq_len + jnp.arange(seq_len, dtype=jnp.int32)
    valid_mask = (places[None, :] < valid_count[:, None]).astype(jnp.float32)
    flat_in = tokens.astype(jnp.float32).reshape(token_count, model_width)
    normed, norm_back = jax.vjp(layer_norm, flat_in, norm_gain.astype(jnp.float32))
    normed_low = normed.astype(jnp.bfloat16)
    value_pre = plain_dot(normed_low, value_weight)
    value_act, value_back = jax.vjp(jax.nn.silu, value_pre)
    value_low = value_act.astype(jnp.bfloat16)
    ema_in = (normed.reshape(row_count, seq_len, model_width) * valid_mask[:, :, None]).reshape(
        row_count, block_total, GROUP, model_width
    )
    (block_end, span_decay, device_end), end_back = jax.vjp(
        end_states, ema_in, ema_forget, ema_beta
    )
    incoming = carried_in(
        (span_decay, device_end),
        "seq",
        forward_combine,
        (jnp.ones_like(span_decay), jnp.zeros_like(device_end)),
        False,
    )[1]
    ema_out, ema_back = jax.vjp(
        ema_output, ema_in, ema_forget, ema_beta, ema_eta, block_end, incoming
    )
    ema_flat = ema_out.reshape(token_count, model_width)
    mixed, mix_back = jax.vjp(mix_piece, ema_flat, normed, ema_omega)
    mixed_low = mixed.astype(jnp.bfloat16)
    base_proj = plain_dot(mixed_low, base_weight)
    shared_pre = base_proj[:, :query_width]
    reset_pre = base_proj[:, query_width : query_width + value_width]
    update_pre = base_proj[:, query_width + value_width : query_width + value_width + model_width]
    candidate_pre = base_proj[:, query_width + value_width + model_width :]
    (query_vec, key_vec), query_back = jax.vjp(
        query_piece, shared_pre, qk_gain.astype(jnp.float32), qk_bias.astype(jnp.float32)
    )
    query_low = query_vec.astype(jnp.bfloat16).reshape(block_count, GROUP, query_width)
    key_low = key_vec.astype(jnp.bfloat16).reshape(block_count, GROUP, query_width)
    value_blocks = value_low.reshape(block_count, GROUP, value_width)
    positions = jnp.arange(GROUP, dtype=jnp.int32)
    causal = positions[:, None] >= positions[None, :]
    diagonal = positions[:, None] == positions[None, :]
    block_valid = valid_mask.reshape(block_count, GROUP)
    allowed = causal[None] & ((block_valid[:, None, :] > 0.5) | diagonal[None])
    scores = (
        jnp.einsum("ntz,nsz->nts", query_low, key_low, preferred_element_type=jnp.float32)
        * score_scale
    )
    masked = jnp.where(allowed, scores, very_low)
    row_top = jnp.max(masked, axis=-1, keepdims=True)
    log_total = row_top + jnp.log(jnp.sum(jnp.exp(masked - row_top), axis=-1, keepdims=True))
    probs_low = jnp.where(allowed, jnp.exp(masked - log_total), 0.0).astype(jnp.bfloat16)
    attended = jnp.einsum(
        "nts,nsv->ntv", probs_low, value_blocks, preferred_element_type=jnp.float32
    ).reshape(token_count, value_width)
    reset_act, reset_back = jax.vjp(jax.nn.silu, reset_pre)
    product_low = (attended * reset_act).astype(jnp.bfloat16)
    projected = plain_dot(product_low, output_weight)
    after_mix, merge_back = jax.vjp(merge_piece, candidate_pre, projected, update_pre, flat_in)
    ffn_normed, ffn_norm_back = jax.vjp(layer_norm, after_mix, ffn_gain.astype(jnp.float32))
    ffn_low = ffn_normed.astype(jnp.bfloat16)
    inner_pre = plain_dot(ffn_low, ffn_in)
    inner_act, act_back = jax.vjp(jax.nn.silu, inner_pre)
    act_low = inner_act.astype(jnp.bfloat16)
    ffn_res = plain_dot(act_low, ffn_out)
    block_out = (after_mix + ffn_res).astype(jnp.bfloat16).reshape(row_count, seq_len, model_width)
    grad_out = cotangent.astype(jnp.float32).reshape(token_count, model_width)
    grad_res_low = cotangent.reshape(token_count, model_width)
    grad_ffn_out = outer_dot(act_low, grad_res_low)
    grad_act = inner_dot(grad_res_low, ffn_out)
    grad_inner_low = act_back(grad_act)[0].astype(jnp.bfloat16)
    grad_ffn_in = outer_dot(ffn_low, grad_inner_low)
    grad_ffn_normed = inner_dot(grad_inner_low, ffn_in)
    grad_mix_add, grad_ffn_gain = ffn_norm_back(grad_ffn_normed)
    grad_after = grad_out + grad_mix_add
    grad_candidate, grad_projected, grad_update, grad_residual = merge_back(grad_after)
    grad_proj_low = grad_projected.astype(jnp.bfloat16)
    grad_output_weight = outer_dot(product_low, grad_proj_low)
    grad_product = inner_dot(grad_proj_low, output_weight)
    grad_attended = (
        (grad_product * reset_act).astype(jnp.bfloat16).reshape(block_count, GROUP, value_width)
    )
    grad_reset = reset_back(grad_product * attended)[0]
    again_scores = (
        jnp.einsum("ntz,nsz->nts", query_low, key_low, preferred_element_type=jnp.float32)
        * score_scale
    )
    soft_probs = jnp.where(
        allowed, jnp.exp(jnp.where(allowed, again_scores, very_low) - log_total), 0.0
    )
    soft_low = soft_probs.astype(jnp.bfloat16)
    grad_probs = jnp.einsum(
        "ntv,nsv->nts", grad_attended, value_blocks, preferred_element_type=jnp.float32
    )
    grad_value = jnp.einsum(
        "nts,ntv->nsv", soft_low, grad_attended, preferred_element_type=jnp.float32
    ).reshape(token_count, value_width)
    grad_scores = soft_probs * (
        grad_probs - jnp.sum(grad_probs * soft_probs, axis=-1, keepdims=True)
    )
    grad_raw_low = (grad_scores * score_scale).astype(jnp.bfloat16)
    grad_query = jnp.einsum(
        "nts,nsz->ntz", grad_raw_low, key_low, preferred_element_type=jnp.float32
    ).reshape(token_count, query_width)
    grad_key = jnp.einsum(
        "nts,ntz->nsz", grad_raw_low, query_low, preferred_element_type=jnp.float32
    ).reshape(token_count, query_width)
    grad_shared, grad_qk_gain, grad_qk_bias = query_back((grad_query, grad_key))
    grad_base_low = jnp.concatenate(
        [grad_shared, grad_reset, grad_update, grad_candidate], axis=1
    ).astype(jnp.bfloat16)
    grad_base_weight = outer_dot(mixed_low, grad_base_low)
    grad_mixed = inner_dot(grad_base_low, base_weight)
    grad_ema_flat, grad_normed_mix, grad_omega = mix_back(grad_mixed)
    grad_ema_in, grad_forget_out, grad_beta_out, grad_eta, grad_block_end, grad_incoming = ema_back(
        grad_ema_flat.reshape(row_count, seq_len, model_width)
    )
    later_grad = carried_in(
        (span_decay, grad_incoming),
        "seq",
        forward_combine,
        (jnp.ones_like(span_decay), jnp.zeros_like(grad_incoming)),
        True,
    )[1]
    grad_span = jnp.sum(later_grad * incoming, axis=0)
    grad_ema_end, grad_forget_end, grad_beta_end = end_back((grad_block_end, grad_span, later_grad))
    grad_forget = grad_forget_out + grad_forget_end
    grad_beta = grad_beta_out + grad_beta_end
    grad_ema_total = (grad_ema_in + grad_ema_end).reshape(
        row_count, seq_len, model_width
    ) * valid_mask[:, :, None]
    grad_vpre_low = value_back(grad_value)[0].astype(jnp.bfloat16)
    grad_value_weight = outer_dot(normed_low, grad_vpre_low)
    grad_normed = (
        grad_normed_mix
        + grad_ema_total.reshape(token_count, model_width)
        + inner_dot(grad_vpre_low, value_weight)
    )
    grad_flat, grad_norm_gain = norm_back(grad_normed)
    grad_tokens = (
        (grad_flat + grad_residual).astype(jnp.bfloat16).reshape(row_count, seq_len, model_width)
    )
    summed = tuple(
        lax.psum(
            (
                grad_norm_gain,
                grad_value_weight,
                grad_forget,
                grad_beta,
                grad_eta,
                grad_omega,
                grad_base_weight,
                grad_qk_gain,
                grad_qk_bias,
                grad_output_weight,
                grad_ffn_gain,
                grad_ffn_in,
                grad_ffn_out,
            ),
            ("seq", "row"),
        )
    )
    return (block_out, grad_tokens) + summed


def solution(mesh):
    return jax.shard_map(
        per_device,
        mesh=mesh,
        in_specs=(
            P("row", "seq", None),
            P("row"),
            P(),
            P(),
            P(),
            P(),
            P(),
            P(),
            P(),
            P(),
            P(),
            P(),
            P(),
            P(),
            P(),
            P("row", "seq", None),
        ),
        out_specs=(
            P("row", "seq", None),
            P("row", "seq", None),
            P(),
            P(),
            P(),
            P(),
            P(),
            P(),
            P(),
            P(),
            P(),
            P(),
            P(),
            P(),
            P(),
        ),
        check_vma=False,
    )
```

profile of v0, /device:TPU:0, one launch (start us, length us, event | category | flops | bytes accessed | tf_op | source)
XLA Modules:
  0.0 967.5 jit_solution(3928549899918437645)
XLA Ops:
  8.6 1.9 convert_reduce_fusion
  10.6 2.4 fusion.50
  14.5 3.7 fusion.52
  18.3 7.3 copy.149
  25.6 7.6 fusion.57
  33.2 5.1 copy.151
  39.9 33.1 %all-gather = f32[4096,16]{0,1:T(8,128)S(1)} all-gather(f32[512,16]{0,1:T(8,128)S(1)} %copy-done.77), channel_id=2, replica_groups=mesh['seq'=8,'row'=4] {'seq'}, dimensions={0}, use_global_device_ids=true | all-gather | bytes 294912 | tf_op jit(solution)/shard_map/all_gather | solution.py:16
  84.9 1.8 rev.6
  86.7 7.3 copy.147
  99.3 34.1 %fusion.64 = f32[512,128,128]{2,1,0:T(8,128)} fusion(f32[128]{0:T(128)} %iota_negate_fusion, f32[512,16]{1,0:T(8,128)S(1)} %copy.146, f32[512,16]{1,0:T(8,128)S(1)} %copy.145), kind=kOutput, calls=%fused_computation.113 | convolution fusion | flops 808452096 | bytes 33620480 | tf_op jit(solution)/shard_map/jvp()/dot_general | solution.py:98
  133.4 31.4 %fusion.9 = f32[512,128,16]{1,2,0:T(8,128)} fusion(f32[512,128,16]{1,2,0:T(8,128)S(1)} %bitcast.254, f32[512,128,128]{2,1,0:T(8,128)} %fusion.64, f32[128,128]{1,0:T(8,128)S(1)} %fusion.124), kind=kOutput, calls=%fused_computation.13 | convolution fusion | flops 813694976 | bytes 42008576 | tf_op jit(solution)/shard_map/jvp()/dot_general | solution.py:54
  164.8 13.6 %while.28 = (s32[]{:T(128)}, f32[8,512,16]{1,2,0:T(8,128)S(1)}, s32[]{:T(128)}, f32[8,512,16]{1,2,0:T(8,128)}, f32[8,8,512,16]{2,3,1,0:T(8,128)}, /*index=5*/s32[]{:T(128)}, s32[]{:T(128)}) while((s32[]{:T(128)}, f32[8,512,16]{1,2,0:T(8,128)S(1)}, s32[]{:T(128)}, f32[8,512,16]{1,2,0:T(8,128)}, f32[8,8,512,16]{2,3,1,0:T(8,128)}, ...), condition=%wide.region_4.5_spmd.clone, body=%wide.region_3.4_spmd.clone.sunk | while | flops 262148 | bytes 884849 | solution.py:28
  179.3 4.4 copy.153
  183.8 7.7 fusion.68
  191.5 7.3 copy.154
  198.8 5.2 bitcast_add_fusion.3
  204.1 5.1 fusion.156
  211.2 5.3 multiply_convert_fusion.2
  216.5 1.5 copy-done.12
  220.0 5.4 fusion.24
  225.4 16.8 %fusion.146 = (f32[2048]{0:T(1024)S(1)}, f32[2048,512]{1,0:T(8,128)S(1)}, f32[2048,512]{1,0:T(8,128)}) fusion(f32[2048,2176]{1,0:T(8,128)} %copy-done.12, bf16[8,256,512]{2,1,0:T(8,128)(2,1)S(1)} %copy-done.2, bf16[2048,1024]{1,0:T(8,128)(2,1)S(1)} %fusion.24, bf16[1024,512]{1,0:T(8,128)(2,1)S(1)} %copy-done.119), kind=kOutput, calls=%fused_computation.248 | convolution fusion | flops 2161113088 | bytes 24125440 | tf_op jit(solution)/shard_map/dot_general | solution.py:38
  244.2 6.3 multiply_convert_fusion.1
  250.5 8.2 fusion.17
  258.7 5.5 multiply_reduce_fusion
  264.3 3.3 fusion.145
  267.6 8.8 fusion.30
  277.7 3.7 fusion.161
  281.4 9.9 %multiply_convert_fusion = (bf16[2048,1024]{1,0:T(8,128)(2,1)S(1)}, bf16[2048,1024]{1,0:T(8,128)(2,1)}) fusion(f32[2048,2176]{1,0:T(8,128)} %copy-done.12, f32[16,128,1024]{2,1,0:T(8,128)S(1)} %fusion.122, bf16[2048,512]{1,0:T(8,128)(2,1)} %copy-done.24, bf16[1024,512]{1,0:T(8,128)(2,1)S(1)} %copy-done.120), kind=kOutput, calls=%fused_computation.37 | convolution fusion | flops 2176843776 | bytes 28311552 | tf_op jit(solution)/shard_map/dot_general | solution.py:48
  291.3 2.0 copy-done.15
  293.3 2.2 fusion.157
  295.5 4.2 fusion.153
  299.7 4.3 fusion.150
  304.1 7.2 fusion.120
  311.3 2.0 fusion.106
  313.3 9.1 fusion.32
  322.4 7.3 copy.157
  329.8 21.5 %fusion.7 = f32[512,128,16]{1,2,0:T(8,128)} fusion(f32[512,128,16]{1,2,0:T(8,128)} %bitcast.249, f32[512,128,128]{2,1,0:T(8,128)} %fusion.64, f32[128,128]{1,0:T(8,128)S(1)} %copy-done.30), kind=kOutput, calls=%fused_computation.11 | convolution fusion | flops 813694976 | bytes 42008576 | tf_op jit(solution)/shard_map/transpose(jvp())/dot_general | solution.py:54
  351.3 9.6 fusion.60
  361.0 3.0 copy.159
  365.4 31.8 %fusion.159 = f32[512,128,128]{2,1,0:T(8,128)} fusion(f32[512,128,16]{1,2,0:T(8,128)} %bitcast.250, f32[512,128,16]{1,2,0:T(8,128)} %bitcast.253), kind=kOutput, calls=%fused_computation.256 | convolution fusion | flops 805306368 | bytes 41943040 | tf_op jit(solution)/shard_map/transpose(jvp())/dot_general | solution.py:54
  397.2 7.7 fusion.23
  404.9 3.7 fusion.158
  408.6 7.3 copy.158
  416.0 18.1 %multiply_reduce_fusion.5 = f32[512,16]{1,0:T(8,128)S(1)} fusion(f32[128]{0:T(128)S(1)} %copy-done.95, f32[512,16]{1,0:T(8,128)S(1)} %copy-done.11, f32[512,16]{1,0:T(8,128)S(1)} %copy-done.36, f32[512,128,128]{2,1,0:T(8,128)} %fusion.159, f32[128,128]{1,0:T(8,128)S(1)} %copy-done.30), kind=kOutput, calls=%fused_computation.92 | convolution fusion | flops 819978240 | bytes 33718784 | tf_op jit(solution)/shard_map/transpose(jvp())/dot_general | solution.py:98
  435.5 7.4 fusion.143
  442.9 7.8 fusion.90
  450.7 31.5 %fusion.5 = f32[512,128,16]{1,2,0:T(8,128)} fusion(f32[512,128,128]{2,1,0:T(8,128)} %fusion.159, f32[128,128]{1,0:T(8,128)S(1)} %copy-done.30, f32[128]{0:T(128)S(1)} %copy-done.95, f32[512,16]{1,0:T(8,128)S(1)} %copy-done.11), kind=kOutput, calls=%fused_computation.9 | convolution fusion | flops 814743552 | bytes 37847552 | tf_op jit(solution)/shard_map/transpose(jvp())/dot_general | solution.py:98
  482.2 3.3 rev.7
  485.6 13.6 %while.29 = (s32[]{:T(128)}, f32[8,512,16]{1,2,0:T(8,128)S(1)}, s32[]{:T(128)}, f32[8,512,16]{1,2,0:T(8,128)}, f32[8,8,512,16]{2,3,1,0:T(8,128)}, /*index=5*/s32[]{:T(128)}, s32[]{:T(128)}) while((s32[]{:T(128)}, f32[8,512,16]{1,2,0:T(8,128)S(1)}, s32[]{:T(128)}, f32[8,512,16]{1,2,0:T(8,128)}, f32[8,8,512,16]{2,3,1,0:T(8,128)}, ...), condition=%wide.region_13.14_spmd.clone, body=%wide.region_12.13_spmd.clone.sunk | while | flops 262148 | bytes 884849 | solution.py:28
  500.0 3.8 copy.170
  503.8 7.9 fusion.160
  511.7 7.6 fusion.55
  520.0 7.2 copy.164
  527.3 6.9 bitcast_add_fusion.2
  535.5 6.5 fusion.53
  544.2 17.7 %multiply_reduce_fusion.1 = (f32[512,16]{1,0:T(8,128)}, f32[512,16]{1,0:T(8,128)}, f32[512,16]{1,0:T(8,128)}, f32[512,16]{1,0:T(8,128)}, f32[512,16]{1,0:T(8,128)}, /*index=5*/f32[512,16]{1,0:T(8,128)S(1)}) fusion(f32[128]{0:T(128)S(1)} %copy-done.107, f32[512,16]{1,0:T(8,128)S(1)} %copy-done.11, f32[512,16]{1,0:T(8,128)S(1)} %copy-done.40, ...), kind=kOutput, calls=%fused_computation.88 | convolution fusion | flops 122634240 | bytes 13435904 | tf_op jit(solution)/shard_map/transpose(jvp())/dot_general | solution.py:54
  567.4 5.3 fusion.49
  573.6 6.5 fusion.162
  581.4 7.3 add_convert_fusion.1
  588.7 5.9 add_convert_fusion
  594.6 103.5 %all-reduce.10.cloned.1.call-done = (f32[512]{0:T(512)}, f32[512,16]{0,1:T(8,128)}, f32[512,16]{0,1:T(8,128)}, f32[512,16]{0,1:T(8,128)}, f32[512]{0:T(512)}, /*...) async-done(((f32[512]{0:T(512)}, f32[512,16]{0,1:T(8,128)}, f32[512,16]{0,1:T(8,128)}, f32[512,16]{0,1:T(8,128)}, f32[512]{0:T(512)}, /*index=5*/f32[2,128]{1,0:T(2,128)}, ...) | async-done | bytes 106512 | tf_op jit(solution)/shard_map/psum | solution.py:311
  698.1 245.4 %all-reduce.12.cloned.1.call-done = (f32[512,1024]{1,0:T(8,128)}, f32[512,2176]{1,0:T(8,128)}, f32[1024,512]{1,0:T(8,128)}, f32[512,1024]{1,0:T(8,128)}, f32[1024,512]{1,0:T(8,128)}) async-done(((f32[512,1024]{1,0:T(8,128)}, f32[512,2176]{1,0:T(8,128)}, f32[1024,512]{1,0:T(8,128)}, f32[512,1024]{1,0:T(8,128)}, f32[1024,512]{1,0:T(8,128)}), (f32[512,1024]{1,0:T(8,128)}, f32[512,2176]{1,0:T(8,128)}, ...) | async-done | bytes 12845072 | tf_op jit(solution)/shard_map/psum | solution.py:311
  944.7 3.2 copy.212
  950.3 4.8 copy.217
  (363 shorter events, 81.6 us)
Async XLA Ops:
  7.2 196.8 %copy-start = (bf16[512,2176]{1,0:T(8,128)(2,1)S(1)}, bf16[512,2176]{1,0:T(8,128)(2,1)}, u32[]{:S(2)}) copy-start(bf16[512,2176]{1,0:T(8,128)(2,1)} %param.28) | copy-start | bytes 6684676
  7.2 157.5 %all-gather.7.cloned.1.call-start = ((), (), s32[]{:S(2)}) async-start(), calls=%async_computation.1 | async-start | bytes 2359296 | tf_op jit(solution)/shard_map/all_gather | solution.py:16
  7.3 10.9 %copy-start.108 = (f32[2]{0:T(128)}, f32[2]{0:T(128)S(1)}, u32[]{:S(2)}) copy-start(f32[2]{0:T(128)S(1)} %subtract_multiply_fusion.10) | copy-start | bytes 28
  7.9 17.7 %copy-start.105 = (f32[128]{0:T(128)}, f32[128]{0:T(128)S(1)}, u32[]{:S(2)}) copy-start(f32[128]{0:T(128)S(1)} %get-tuple-element.400) | copy-start | bytes 1540
  7.9 10.4 %copy-start.102 = (s32[256]{0:T(256)}, s32[256]{0:T(256)S(1)}, u32[]{:S(2)}) copy-start(s32[256]{0:T(256)S(1)} %iota_add_fusion) | copy-start | bytes 3076
  8.6 9.7 copy-start.86
  13.7 11.9 %copy-start.64 = (f32[512,16]{0,1:T(8,128)}, f32[512,16]{0,1:T(8,128)S(1)}, u32[]{:S(2)}) copy-start(f32[512,16]{0,1:T(8,128)S(1)} %get-tuple-element.373) | copy-start | bytes 98308
  13.8 169.9 %copy-start.10 = (f32[512,16]{1,0:T(8,128)}, f32[512,16]{1,0:T(8,128)S(1)}, u32[]{:S(2)}) copy-start(f32[512,16]{1,0:T(8,128)S(1)} %copy.146) | copy-start | bytes 98308
  14.3 24.0 %copy-start.53 = (f32[2,512,16]{1,2,0:T(8,128)}, f32[2,512,16]{1,2,0:T(8,128)S(1)}, u32[]{:S(2)}) copy-start(f32[2,512,16]{1,2,0:T(8,128)S(1)} %multiply_exponential_fusion.6) | copy-start | bytes 196612
  14.4 11.1 %copy-start.37 = (f32[512,16]{1,0:T(8,128)}, f32[512,16]{1,0:T(8,128)S(1)}, u32[]{:S(2)}) copy-start(f32[512,16]{1,0:T(8,128)S(1)} %copy.150) | copy-start | bytes 98308
  33.2 40.5 %copy-start.62 = (f32[512,16]{0,1:T(8,128)S(1)}, f32[512,16]{0,1:T(8,128)}, u32[]{:S(2)}) copy-start(f32[512,16]{0,1:T(8,128)} %param.26) | copy-start | bytes 98308
  38.3 140.0 %copy-start.27 = (f32[512,8,2,16]{0,3,1,2:T(8,128)}, f32[512,8,2,16]{0,3,1,2:T(8,128)S(1)}, u32[]{:S(2)}) copy-start(f32[512,8,2,16]{0,3,1,2:T(8,128)S(1)} %copy.151) | copy-start | bytes 1572868
  39.2 443.0 %all-gather.5.cloned.1.call-start = ((), (), s32[]{:S(2)}) async-start(), calls=%async_computation | async-start | bytes 2359296 | tf_op jit(solution)/shard_map/all_gather | solution.py:16
  84.9 14.4 %copy-start.35 = (f32[512,16]{1,0:T(8,128)}, f32[512,16]{1,0:T(8,128)S(1)}, u32[]{:S(2)}) copy-start(f32[512,16]{1,0:T(8,128)S(1)} %copy.145) | copy-start | bytes 98308
  94.6 38.8 %copy-start.29 = (f32[128,128]{1,0:T(8,128)}, f32[128,128]{1,0:T(8,128)S(1)}, u32[]{:S(2)}) copy-start(f32[128,128]{1,0:T(8,128)S(1)} %fusion.124) | copy-start | bytes 196612
  99.3 34.1 %copy-start.6 = (f32[512,128,8,2]{1,3,2,0:T(2,128)S(1)}, f32[512,128,8,2]{1,3,2,0:T(2,128)}, u32[]{:S(2)}) copy-start(f32[512,128,8,2]{1,3,2,0:T(2,128)} %copy.147) | copy-start | bytes 12582916
  178.3 13.2 %copy-start.16 = (f32[8,512,16]{1,2,0:T(8,128)}, f32[8,512,16]{1,2,0:T(8,128)S(1)}, u32[]{:S(2)}) copy-start(f32[8,512,16]{1,2,0:T(8,128)S(1)} %get-tuple-element.203) | copy-start | bytes 786436
  209.2 8.8 copy-start.12
  209.7 8.6 copy-start.55
  209.7 8.8 copy-start.56
  242.2 16.5 %copy-start.18 = (f32[2048,512]{1,0:T(8,128)}, f32[2048,512]{1,0:T(8,128)S(1)}, u32[]{:S(2)}) copy-start(f32[2048,512]{1,0:T(8,128)S(1)} %get-tuple-element.351) | copy-start | bytes 12582916
  242.2 22.0 %copy-start.84 = (f32[2048]{0:T(1024)}, f32[2048]{0:T(1024)S(1)}, u32[]{:S(2)}) copy-start(f32[2048]{0:T(1024)S(1)} %broadcast_multiply_fusion) | copy-start | bytes 24580
  244.2 20.0 %copy-start.92 = (f32[2048]{0:T(1024)}, f32[2048]{0:T(1024)S(1)}, u32[]{:S(2)}) copy-start(f32[2048]{0:T(1024)S(1)} %fusion.134) | copy-start | bytes 24580
  267.5 8.9 copy-start.8
  267.6 8.8 copy-start.80
  304.1 9.2 copy-start.25
  304.1 9.2 copy-start.33
  304.1 9.2 copy-start.45
  313.3 9.1 copy-start.57
  329.7 21.6 %copy-start.4 = (f32[512,128,8,2]{1,3,2,0:T(2,128)S(1)}, f32[512,128,8,2]{1,3,2,0:T(2,128)}, u32[]{:S(2)}) copy-start(f32[512,128,8,2]{1,3,2,0:T(2,128)} %copy.157) | copy-start | bytes 12582916
  329.7 21.6 %copy-start.11 = (f32[512,16]{1,0:T(8,128)S(1)}, f32[512,16]{1,0:T(8,128)}, u32[]{:S(2)}) copy-start(f32[512,16]{1,0:T(8,128)} %copy-done.10) | copy-start | bytes 98308
  329.7 21.6 %copy-start.40 = (f32[512,16]{1,0:T(8,128)S(1)}, f32[512,16]{1,0:T(8,128)}, u32[]{:S(2)}) copy-start(f32[512,16]{1,0:T(8,128)} %copy.148) | copy-start | bytes 98308
  329.7 21.6 %copy-start.107 = (f32[128]{0:T(128)S(1)}, f32[128]{0:T(128)}, u32[]{:S(2)}) copy-start(f32[128]{0:T(128)} %get-tuple-element.401) | copy-start | bytes 1540
  397.2 7.7 copy-start.44
  415.9 18.3 %copy-start.116 = (f32[128]{0:T(128)S(1)}, f32[128]{0:T(128)}, u32[]{:S(2)}) copy-start(f32[128]{0:T(128)} %get-tuple-element.394) | copy-start | bytes 1540
  415.9 18.3 %copy-start.117 = (f32[128]{0:T(128)S(1)}, f32[128]{0:T(128)}, u32[]{:S(2)}) copy-start(f32[128]{0:T(128)} %get-tuple-element.392) | copy-start | bytes 1540
  415.9 19.5 %copy-start.85 = (f32[2048]{0:T(1024)S(1)}, f32[2048]{0:T(1024)}, u32[]{:S(2)}) copy-start(f32[2048]{0:T(1024)} %copy-done.84) | copy-start | bytes 24580
  415.9 19.5 %copy-start.93 = (f32[2048]{0:T(1024)S(1)}, f32[2048]{0:T(1024)}, u32[]{:S(2)}) copy-start(f32[2048]{0:T(1024)} %copy-done.92) | copy-start | bytes 24580
  415.9 19.5 %copy-start.98 = (f32[512]{0:T(512)S(1)}, f32[512]{0:T(512)}, u32[]{:S(2)}) copy-start(f32[512]{0:T(512)} %convert_element_type.106) | copy-start | bytes 6148
  416.0 282.2 %all-reduce.10.cloned.1.call-start = ((), (), s32[]{:S(2)}) async-start(), calls=%async_computation.2 | async-start | bytes 212992 | tf_op jit(solution)/shard_map/psum | solution.py:311
  435.4 7.5 copy-start.26
  435.4 7.5 copy-start.42
  482.2 17.0 %copy-start.17 = (f32[8,512,16]{1,2,0:T(8,128)S(1)}, f32[8,512,16]{1,2,0:T(8,128)}, u32[]{:S(2)}) copy-start(f32[8,512,16]{1,2,0:T(8,128)} %copy-done.16) | copy-start | bytes 786436
  482.2 17.6 %copy-start.28 = (f32[512,8,2,16]{0,3,1,2:T(8,128)S(1)}, f32[512,8,2,16]{0,3,1,2:T(8,128)}, u32[]{:S(2)}) copy-start(f32[512,8,2,16]{0,3,1,2:T(8,128)} %copy-done.27) | copy-start | bytes 1572868
  482.2 17.6 %copy-start.52 = (f32[8,1,512,16]{2,3,0,1:T(8,128)S(1)}, f32[8,1,512,16]{2,3,0,1:T(8,128)}, u32[]{:S(2)}) copy-start(f32[8,1,512,16]{2,3,0,1:T(8,128)} %slice_bitcast_fusion.2) | copy-start | bytes 786436
  482.2 17.6 %copy-start.54 = (f32[2,512,16]{1,2,0:T(8,128)S(1)}, f32[2,512,16]{1,2,0:T(8,128)}, u32[]{:S(2)}) copy-start(f32[2,512,16]{1,2,0:T(8,128)} %copy-done.53) | copy-start | bytes 196612
  503.8 7.9 copy-start.7
  503.8 7.9 copy-start.38
  503.8 7.9 copy-start.106
  511.6 7.7 copy-start.60
  511.7 7.6 copy-start.109
  527.2 8.0 copy-start.32
  527.2 8.0 copy-start.69
  527.2 8.0 copy-start.88
  527.2 8.0 copy-start.96
  527.3 8.0 copy-start.104
  527.3 8.2 copy-start.122
  535.5 8.6 copy-start.34
  544.2 23.1 %copy-start.71 = (f32[2048]{0:T(1024)S(1)}, f32[2048]{0:T(1024)}, u32[]{:S(2)}) copy-start(f32[2048]{0:T(1024)} %rsqrt.24) | copy-start | bytes 24580
  573.4 370.1 %all-reduce.12.cloned.1.call-start = ((), (), s32[]{:S(2)}) async-start(), calls=%async_computation.3 | async-start | bytes 25690112 | tf_op jit(solution)/shard_map/psum | solution.py:311
  698.1 249.7 %copy-start.91 = (f32[512,16]{0,1:T(8,128)S(1)}, f32[512,16]{0,1:T(8,128)}, u32[]{:S(2)}) copy-start(f32[512,16]{0,1:T(8,128)} %get-tuple-element.510) | copy-start | bytes 98308
  698.1 250.4 %copy-start.90 = (f32[512,16]{0,1:T(8,128)S(1)}, f32[512,16]{0,1:T(8,128)}, u32[]{:S(2)}) copy-start(f32[512,16]{0,1:T(8,128)} %get-tuple-element.511) | copy-start | bytes 98308
  698.1 251.0 %copy-start.89 = (f32[512,16]{0,1:T(8,128)S(1)}, f32[512,16]{0,1:T(8,128)}, u32[]{:S(2)}) copy-start(f32[512,16]{0,1:T(8,128)} %get-tuple-element.512) | copy-start | bytes 98308
  698.1 251.6 %copy-start.113 = (f32[512]{0:T(512)S(1)}, f32[512]{0:T(512)}, u32[]{:S(2)}) copy-start(f32[512]{0:T(512)} %get-tuple-element.513) | copy-start | bytes 6148
  (65 other events, 346.6 us)
Sparse Core Ops, SparseCore 0:
  39.3 52.4 all-gather.6
  416.0 50.3 all-gather.4
  573.5 124.5 all-reduce.9
  705.0 238.4 all-reduce.11
where the time goes:
time: 975 us; the launch traced here: 968 us
  matrix products  356 us (37%)
  waiting for transfers between devices  349 us (36%)
  local copies, waits for them, and re-layouts  122 us (13%)
  other arithmetic  91.6 us (9%)
  blocking collectives  33.1 us (3%)
  between operations  15.2 us (2%)
    psum x2, waiting for transfers between devices, per_device(): lax.psum((grad_norm_gain, grad_value_weight, grad_forget, grad_beta, grad...  349 us
    dot_general x9, matrix products, batch_dot(): lax.dot_general(first_op, second_op, (((2,), (1,)), ((0,), (0,))), precis...  143 us
    dot_general x3, matrix products, ema_output(): lax.dot_general(growth, shrink, (((2,), (2,)), ((0,), (0,))), precision=c...  83.7 us
    dot_general x5, matrix products, plain_dot(): return jnp.dot(first_op, second_op, preferred_element_type=jnp.float32)  40.7 us
    dot_general x5, matrix products, inner_dot(): lax.dot_general(first_op, second_op, (((1,), (1,)), ((), ())), preferred_...  39.1 us
    unnamed x269, local copies, waits for them, and re-layouts  33.7 us
    all_gather x1, blocking collectives, carried_in(): pieces = jax.tree.map(lambda part: lax.all_gather(part, axis), value)  33.1 us
    dot_general x5, matrix products, outer_dot(): lax.dot_general(first_op, second_op, (((0,), (0,)), ((), ())), preferred_...  29.1 us
  transfers between devices with their start and end apart: 4, of which 2 were waited for; matrix products, arithmetic and copies ran while one was open for 18% of the time, Pallas kernels for 0%

commit v1 on v0

--- a/solution.py
+++ b/solution.py
@@ -1,31 +1,447 @@
+import functools
+
 import jax
 import jax.numpy as jnp
 from jax import lax
+from jax.experimental import pallas as pl
+from jax.experimental.pallas import tpu as pltpu
 from jax.sharding import PartitionSpec as P
 
 GROUP = 128
-
+STEPS = 32
+LAG = 8
+LANES = 128
 
 epsilon = 1e-05
 very_low = -1e30
-careful = lax.Precision.HIGH
-
-
-def carried_in(value, axis, join, neutral, backward):
-    count, mine = (lax.axis_size(axis), lax.axis_index(axis))
-    pieces = jax.tree.map(lambda part: lax.all_gather(part, axis), value)
+scan_params = pltpu.CompilerParams(vmem_limit_bytes=48 * 2**20)
+
+
+def lane_slices(width):
+    return [slice(low, low + LANES) for low in range(0, width, LANES)]
+
+
+def spread_rows(ref, index, lanes, rows):
+    return jnp.broadcast_to(ref[index : index + 1, lanes], (rows, LANES))
+
+
+def add_all(parts):
+    while len(parts) > 1:
+        parts = [
+            parts[at] + parts[at + 1] if at + 1 < len(parts) else parts[at]
+            for at in range(0, len(parts), 2)
+        ]
+    return parts[0]
+
+
+def enter_body(count_ref, tokens_ref, gain_ref, retain_ref, low_ref, turned_ref, end_ref, state):
+    step = pl.program_id(0)
+    rows, steps, width = tokens_ref.shape
+    states = retain_ref.shape[0]
+
+    @pl.when(step == 0)
+    def _():
+        state[...] = jnp.zeros_like(state)
+
+    values = tokens_ref[...].astype(jnp.float32)
+    centered = values - jnp.mean(values, axis=-1, keepdims=True)
+    spread = jnp.mean(centered * centered, axis=-1, keepdims=True)
+    normed = centered * lax.rsqrt(spread + epsilon) * gain_ref[...]
+    low_ref[...] = normed.astype(jnp.bfloat16)
+    places = step * steps + lax.broadcasted_iota(jnp.int32, (steps, 1), 0)
+    kept = jnp.stack([jnp.where(places < count_ref[row], normed[row], 0.0) for row in range(rows)])
+    for lanes in lane_slices(width):
+        for unit in range(steps // LAG):
+            part = slice(unit * LAG, (unit + 1) * LAG)
+            turned_ref[part, :, lanes] = jnp.swapaxes(kept[:, part, lanes], 0, 1)
+    for lanes in lane_slices(width):
+        retain = [spread_rows(retain_ref, j, lanes, rows) for j in range(states)]
+
+        def unit_step(unit, hidden):
+            for within in range(LAG):
+                entry = turned_ref[unit * LAG + within, :, lanes]
+                hidden = [retain[j] * hidden[j] + entry for j in range(states)]
+            return hidden
+
+        hidden = lax.fori_loop(
+            0, steps // LAG, unit_step, [state[j, :, lanes] for j in range(states)]
+        )
+        for j in range(states):
+            state[j, :, lanes] = hidden[j]
+
+    @pl.when(step == pl.num_programs(0) - 1)
+    def _():
+        end_ref[...] = state[...]
+
+
+def whole_spec(shape):
+    return pl.BlockSpec(shape, lambda step: (0,) * len(shape))
+
+
+def enter_call(counts, tokens, gain, retain):
+    rows, length, width = tokens.shape
+    states = retain.shape[0]
+    natural = pl.BlockSpec((rows, STEPS, width), lambda step: (0, step, 0))
+    return pl.pallas_call(
+        enter_body,
+        grid=(length // STEPS,),
+        in_specs=[
+            pl.BlockSpec(memory_space=pltpu.SMEM),
+            natural,
+            whole_spec((1, width)),
+            whole_spec((states, width)),
+        ],
+        out_specs=(
+            natural,
+            pl.BlockSpec((STEPS, rows, width), lambda step: (step, 0, 0)),
+            whole_spec((states, rows, width)),
+        ),
+        out_shape=(
+            jax.ShapeDtypeStruct(tokens.shape, jnp.bfloat16),
+            jax.ShapeDtypeStruct((length, rows, width), jnp.float32),
+            jax.ShapeDtypeStruct((states, rows, width), jnp.float32),
+        ),
+        scratch_shapes=[pltpu.VMEM((states, rows, width), jnp.float32)],
+        compiler_params=scan_params,
+        name="enter",
+    )(counts, tokens, gain, retain)
+
+
+def average_body(turned_ref, retain_ref, mix_ref, start_ref, out_ref, end_ref, state):
+    step = pl.program_id(0)
+    steps, rows, width = turned_ref.shape
+    states = retain_ref.shape[0]
+
+    @pl.when(step == 0)
+    def _():
+        state[...] = start_ref[...]
+
+    for lanes in lane_slices(width):
+        retain = [spread_rows(retain_ref, j, lanes, rows) for j in range(states)]
+        mix = [spread_rows(mix_ref, j, lanes, rows) for j in range(states)]
+
+        def unit_step(unit, hidden):
+            sums = []
+            for within in range(LAG):
+                entry = turned_ref[unit * LAG + within, :, lanes]
+                hidden = [retain[j] * hidden[j] + entry for j in range(states)]
+                sums.append(add_all([mix[j] * hidden[j] for j in range(states)]))
+            out_ref[:, pl.ds(unit * LAG, LAG), lanes] = jnp.swapaxes(jnp.stack(sums), 0, 1)
+            return hidden
+
+        hidden = lax.fori_loop(
+            0, steps // LAG, unit_step, [state[j, :, lanes] for j in range(states)]
+        )
+        for j in range(states):
+            state[j, :, lanes] = hidden[j]
+
+    @pl.when(step == pl.num_programs(0) - 1)
+    def _():
+        end_ref[...] = state[...]
+
+
+def average_call(turned, retain, mix, start):
+    length, rows, width = turned.shape
+    states = retain.shape[0]
+    held = (states, rows, width)
+    return pl.pallas_call(
+        average_body,
+        grid=(length // STEPS,),
+        in_specs=[
+            pl.BlockSpec((STEPS, rows, width), lambda step: (step, 0, 0)),
+            whole_spec((states, width)),
+            whole_spec((states, width)),
+            whole_spec(held),
+        ],
+        out_specs=(
+            pl.BlockSpec((rows, STEPS, width), lambda step: (0, step, 0)),
+            whole_spec(held),
+        ),
+        out_shape=(
+            jax.ShapeDtypeStruct((rows, length, width), jnp.float32),
+            jax.ShapeDtypeStruct(held, jnp.float32),
+        ),
+        scratch_shapes=[pltpu.VMEM(held, jnp.float32)],
+        compiler_params=scan_params,
+        name="average",
+    )(turned, retain, mix, start)
+
+
+def return_body(grad_ref, retain_ref, turned_ref, end_ref, state):
+    step = pl.program_id(0)
+    rows, steps, width = grad_ref.shape
+    states = retain_ref.shape[0]
+
+    @pl.when(step == 0)
+    def _():
+        state[...] = jnp.zeros_like(state)
+
+    for lanes in lane_slices(width):
+        retain = [spread_rows(retain_ref, j, lanes, rows) for j in range(states)]
+
+        def unit_step(unit, hidden):
+            part = pl.ds((steps // LAG - 1 - unit) * LAG, LAG)
+            turned = jnp.swapaxes(grad_ref[:, part, lanes], 0, 1)
+            turned_ref[part, :, lanes] = turned
+            for within in reversed(range(LAG)):
+                hidden = [retain[j] * hidden[j] + turned[within] for j in range(states)]
+            return hidden
+
+        hidden = lax.fori_loop(
+            0, steps // LAG, unit_step, [state[j, :, lanes] for j in range(states)]
+        )
+        for j in range(states):
+            state[j, :, lanes] = hidden[j]
+
+    @pl.when(step == pl.num_programs(0) - 1)
+    def _():
+        end_ref[...] = state[...]
+
+
+def return_call(grad, retain):
+    rows, length, width = grad.shape
+    states = retain.shape[0]
+    last = length // STEPS - 1
+    return pl.pallas_call(
+        return_body,
+        grid=(length // STEPS,),
+        in_specs=[
+            pl.BlockSpec((rows, STEPS, width), lambda step: (0, last - step, 0)),
+            whole_spec((states, width)),
+        ],
+        out_specs=(
+            pl.BlockSpec((STEPS, rows, width), lambda step: (last - step, 0, 0)),
+            whole_spec((states, rows, width)),
+        ),
+        out_shape=(
+            jax.ShapeDtypeStruct((length, rows, width), jnp.float32),
+            jax.ShapeDtypeStruct((states, rows, width), jnp.float32),
+        ),
+        scratch_shapes=[pltpu.VMEM((states, rows, width), jnp.float32)],
+        compiler_params=scan_params,
+        name="back_enter",
+    )(grad, retain)
+
+
+def adjoint_body(
+    grad_ref,
+    turned_ref,
+    retain_ref,
+    inverse_ref,
+    unit_ref,
+    mix_ref,
+    later_ref,
+    end_ref,
+    out_ref,
+    cross_ref,
+    border_ref,
+    lag_ref,
+    adjoint,
+    state,
+    kept,
+):
+    step = pl.program_id(0)
+    steps, rows, width = grad_ref.shape
+    states = retain_ref.shape[0]
+    half = states // 2
+    units = steps // LAG
+
+    @pl.when(step == 0)
+    def _():
+        adjoint[...] = later_ref[...]
+        state[...] = end_ref[...]
+        cross_ref[...] = jnp.zeros_like(cross_ref)
+        border_ref[...] = jnp.zeros_like(border_ref)
+        lag_ref[...] = jnp.zeros_like(lag_ref)
+
+    for lanes in lane_slices(width):
+        for first in range(0, states, half):
+            chosen = range(first, first + half)
+            retain = [spread_rows(retain_ref, j, lanes, rows) for j in chosen]
+            inverse = [spread_rows(inverse_ref, j, lanes, rows) for j in chosen]
+            mix = [spread_rows(mix_ref, j, lanes, rows) for j in chosen]
+
+            def unit_step(unit, carried):
+                after, hidden, cross = carried
+                unit = units - 1 - unit
+                later = after
+                sums = []
+                for within in reversed(range(LAG)):
+                    place = unit * LAG + within
+                    entry = turned_ref[place, :, lanes]
+                    grad = grad_ref[place, :, lanes]
+                    after = [retain[m] * after[m] + grad for m in range(half)]
+                    total = add_all([mix[m] * after[m] for m in range(half)])
+                    if first == 0:
+                        kept[place] = total
+                    else:
+                        sums.append(total + kept[place])
+                    hidden = [(hidden[m] - entry) * inverse[m] for m in range(half)]
+                    cross = [cross[m] + after[m] * hidden[m] for m in range(half)]
+                for m, j in enumerate(chosen):
+                    unit_decay = spread_rows(unit_ref, j, lanes, rows)
+                    border_ref[j, :, lanes] += hidden[m] * (after[m] - unit_decay * later[m])
+                if first > 0:
+                    out_ref[:, pl.ds(unit * LAG, LAG), lanes] = jnp.swapaxes(
+                        jnp.stack(sums[::-1]), 0, 1
+                    )
+                return after, hidden, cross
+
+            after, hidden, cross = lax.fori_loop(
+                0,
+                units,
+                unit_step,
+                tuple(
+                    [ref[j, :, lanes] for j in chosen] for ref in (adjoint, state, cross_ref)
+                ),
+            )
+            for m, j in enumerate(chosen):
+                adjoint[j, :, lanes] = after[m]
+                state[j, :, lanes] = hidden[m]
+                cross_ref[j, :, lanes] = cross[m]
+
+        def lag_step(unit, lags):
+            entries = [turned_ref[unit * LAG + at, :, lanes] for at in range(LAG)]
+            grads = [grad_ref[unit * LAG + at, :, lanes] for at in range(LAG)]
+            return [
+                lags[lag] + add_all([grads[at] * entries[at - lag] for at in range(lag, LAG)])
+                for lag in range(LAG)
+            ]
+
+        lags = lax.fori_loop(0, units, lag_step, [lag_ref[at, :, lanes] for at in range(LAG)])
+        for at in range(LAG):
+            lag_ref[at, :, lanes] = lags[at]
+
+
+def adjoint_call(grad, turned, retain, inverse, unit_decay, mix, later, end):
+    length, rows, width = grad.shape
+    states = retain.shape[0]
+    held = (states, rows, width)
+    last = length // STEPS - 1
+    turned_spec = pl.BlockSpec((STEPS, rows, width), lambda step: (last - step, 0, 0))
+    param_spec = whole_spec((states, width))
+    return pl.pallas_call(
+        adjoint_body,
+        grid=(length // STEPS,),
+        in_specs=[turned_spec] * 2 + [param_spec] * 4 + [whole_spec(held)] * 2,
+        out_specs=(
+            pl.BlockSpec((rows, STEPS, width), lambda step: (0, last - step, 0)),
+            whole_spec(held),
+            whole_spec(held),
+            whole_spec((LAG, rows, width)),
+        ),
+        out_shape=(
+            jax.ShapeDtypeStruct((rows, length, width), jnp.float32),
+            jax.ShapeDtypeStruct(held, jnp.float32),
+            jax.ShapeDtypeStruct(held, jnp.float32),
+            jax.ShapeDtypeStruct((LAG, rows, width), jnp.float32),
+        ),
+        scratch_shapes=[
+            pltpu.VMEM(held, jnp.float32),
+            pltpu.VMEM(held, jnp.float32),
+            pltpu.VMEM((STEPS, rows, LANES), jnp.float32),
+        ],
+        compiler_params=scan_params,
+        name="adjoint",
+    )(grad, turned, retain, inverse, unit_decay, mix, later, end)
+
+
+def carried_in(local, decay, axis, backward):
+    count, mine = lax.axis_size(axis), lax.axis_index(axis)
     if backward:
-        pieces = jax.tree.map(lambda part: part[::-1], pieces)
         mine = count - 1 - mine
-    so_far = jax.tree.map(
-        lambda part, zero: jnp.full_like(part, 0) + jnp.asarray(zero, part.dtype), value, neutral
-    )
-
-    def turn(position, so_far):
-        longer = join(so_far, jax.tree.map(lambda part: part[position], pieces))
-        return jax.tree.map(lambda new, old: jnp.where(position < mine, new, old), longer, so_far)
-
-    return lax.fori_loop(0, count - 1, turn, so_far)
+
+    def moved(value, hop):
+        if backward:
+            pairs = [(at, at - hop) for at in range(hop, count)]
+        else:
+            pairs = [(at, at + hop) for at in range(count - hop)]
+        return lax.ppermute(value, axis, pairs)
+
+    total = moved(local, 1)
+    hop = 1
+    while hop < count - 1:
+        total = total + decay * moved(total, hop)
+        decay = decay * decay
+        hop *= 2
+    return total
+
+
+mesh_axes = ("seq", "row")
+
+
+def device_total():
+    return lax.axis_size("seq") * lax.axis_size("row")
+
+
+def device_place():
+    return lax.axis_index("seq") * lax.axis_size("row") + lax.axis_index("row")
+
+
+def swapped(value, bit):
+    return lax.ppermute(value, mesh_axes, [(at, at ^ bit) for at in range(device_total())])
+
+
+def half_summed(value, bit):
+    half = value.shape[0] // 2
+    mine = (device_place() // bit) % 2
+    sent = lax.dynamic_slice_in_dim(value, (1 - mine) * half, half, 0)
+    kept = lax.dynamic_slice_in_dim(value, mine * half, half, 0)
+    return kept + swapped(sent, bit)
+
+
+def both_halves(value, bit):
+    mine = (device_place() // bit) % 2 == 1
+    other = swapped(value, bit)
+    return jnp.concatenate([jnp.where(mine, other, value), jnp.where(mine, value, other)], axis=0)
+
+
+def link_orders():
+    total = device_total()
+    bits = [1 << at for at in range(total.bit_length() - 1)]
+    if (lax.axis_size("seq"), lax.axis_size("row")) == (8, 4):
+        core, x, y, z_low, z_high = bits
+        return (
+            (core, x, y, z_low, z_high),
+            (core, y, z_low, z_high, x),
+            (core, z_low, z_high, x, y),
+        )
+    third = len(bits) // 3
+    return tuple(bits[turn * third :] + bits[: turn * third] for turn in range(3))
+
+
+def summed_everywhere(values, choices):
+    orders = link_orders()
+    for at in range(len(orders[0])):
+        values = [half_summed(value, orders[pick][at]) for value, pick in zip(values, choices)]
+    for at in reversed(range(len(orders[0]))):
+        values = [both_halves(value, orders[pick][at]) for value, pick in zip(values, choices)]
+    return values
+
+
+def small_sum(value):
+    bits = [1 << at for at in range(device_total().bit_length() - 1)]
+    first = len(bits) % 2
+    groups = [bits[:first]] if first else []
+    groups += [bits[at : at + 2] for at in range(first, len(bits), 2)]
+    for group in groups:
+        partners = [group[0]] if len(group) == 1 else [group[0], group[1], group[0] + group[1]]
+        arrived = [swapped(value, partner) for partner in partners]
+        if len(arrived) == 1:
+            value = value + arrived[0]
+        else:
+            value = (value + arrived[0]) + (arrived[1] + arrived[2])
+    return value
+
+
+def power_of(value, exponent):
+    result = None
+    while exponent:
+        if exponent & 1:
+            result = value if result is None else result * value
+        value = value * value
+        exponent >>= 1
+    return result
 
 
 def layer_norm(inputs, scales):
@@ -48,83 +464,6 @@
     return lax.dot_general(
         first_op, second_op, (((1,), (1,)), ((), ())), preferred_element_type=jnp.float32
     )
-
-
-def batch_dot(first_op, second_op):
-    return lax.dot_general(
-        first_op,
-        second_op,
-        (((2,), (1,)), ((0,), (0,))),
-        precision=careful,
-        preferred_element_type=jnp.float32,
-    )
-
-
-def decay_terms(ema_forget, ema_beta):
-    log_retain = jnp.log(1.0 - ema_forget)
-    inflow = ema_beta * jnp.sqrt(ema_forget * (2.0 - ema_forget))
-    return (log_retain, inflow)
-
-
-def end_states(block_inputs, ema_forget, ema_beta):
-    row_count, blocks, length, feature_count = block_inputs.shape
-    log_retain, inflow = decay_terms(ema_forget, ema_beta)
-    places = jnp.arange(length, dtype=jnp.float32)
-    to_end = inflow[:, None, :] * jnp.exp(
-        (length - 1.0 - places)[None, :, None] * log_retain[:, None, :]
-    )
-    by_feature = block_inputs.transpose(3, 0, 1, 2).reshape(
-        feature_count, row_count * blocks, length
-    )
-    block_end = batch_dot(by_feature, to_end)
-    block_end = block_end.reshape(feature_count, row_count, blocks, -1).transpose(1, 2, 0, 3)
-    counts = jnp.arange(blocks, dtype=jnp.float32)
-    carried = jnp.exp(((blocks - 1.0 - counts) * length)[:, None, None] * log_retain[None])
-    device_end = jnp.sum(block_end * carried[None], axis=1)
-    span_decay = jnp.exp(blocks * length * log_retain)
-    return (block_end, span_decay, device_end)
-
-
-def ema_output(block_inputs, ema_forget, ema_beta, ema_eta, block_end, incoming):
-    row_count, blocks, length, feature_count = block_inputs.shape
-    log_retain, inflow = decay_terms(ema_forget, ema_beta)
-    places = jnp.arange(length, dtype=jnp.float32)
-    growth = (ema_eta * inflow)[:, None, :] * jnp.exp(
-        places[None, :, None] * log_retain[:, None, :]
-    )
-    shrink = jnp.exp(-places[None, :, None] * log_retain[:, None, :])
-    lower_tri = (places[:, None] >= places[None, :]).astype(jnp.float32)
-    kernel = (
-        lax.dot_general(
-            growth,
-            shrink,
-            (((2,), (2,)), ((0,), (0,))),
-            precision=careful,
-            preferred_element_type=jnp.float32,
-        )
-        * lower_tri[None]
-    )
-    by_feature = block_inputs.transpose(3, 2, 0, 1).reshape(
-        feature_count, length, row_count * blocks
-    )
-    local_part = batch_dot(kernel, by_feature)
-    local_part = local_part.reshape(feature_count, length, row_count, blocks).transpose(2, 3, 1, 0)
-    step_decay = jnp.exp(length * log_retain)
-    before = []
-    running = incoming
-    for block_index in range(blocks):
-        before.append(running)
-        running = step_decay * running + block_end[:, block_index]
-    entering = jnp.stack(before, axis=1)
-    readout = ema_eta[:, None, :] * jnp.exp((places + 1.0)[None, :, None] * log_retain[:, None, :])
-    entering_feature = entering.transpose(2, 3, 0, 1).reshape(feature_count, -1, row_count * blocks)
-    carried = batch_dot(readout, entering_feature)
-    carried = carried.reshape(feature_count, length, row_count, blocks).transpose(2, 3, 1, 0)
-    return (local_part + carried).reshape(row_count, blocks * length, feature_count)
-
-
-def forward_combine(earlier_part, later_part):
-    return (earlier_part[0] * later_part[0], later_part[0][None] * earlier_part[1] + later_part[1])
 
 
 def mix_piece(ema_flat, normed, ema_omega):
@@ -174,22 +513,18 @@
     value_pre = plain_dot(normed_low, value_weight)
     value_act, value_back = jax.vjp(jax.nn.silu, value_pre)
     value_low = value_act.astype(jnp.bfloat16)
-    ema_in = (normed.reshape(row_count, seq_len, model_width) * valid_mask[:, :, None]).reshape(
-        row_count, block_total, GROUP, model_width
-    )
-    (block_end, span_decay, device_end), end_back = jax.vjp(
-        end_states, ema_in, ema_forget, ema_beta
-    )
-    incoming = carried_in(
-        (span_decay, device_end),
-        "seq",
-        forward_combine,
-        (jnp.ones_like(span_decay), jnp.zeros_like(device_end)),
-        False,
-    )[1]
-    ema_out, ema_back = jax.vjp(
-        ema_output, ema_in, ema_forget, ema_beta, ema_eta, block_end, incoming
-    )
+    forget, beta, eta = ema_forget.T, ema_beta.T, ema_eta.T
+    retain = 1.0 - forget
+    gate = jnp.sqrt(forget * (2.0 - forget))
+    inflow = beta * gate
+    mix = eta * inflow
+    span_decay = power_of(retain, seq_len)[:, None, :]
+    counts = valid_count - device * seq_len
+    _, turned, device_end = enter_call(
+        counts, tokens, norm_gain.astype(jnp.float32)[None], retain
+    )
+    incoming = carried_in(device_end, span_decay, "seq", False)
+    ema_out, state_end = average_call(turned, retain, mix, incoming)
     ema_flat = ema_out.reshape(token_count, model_width)
     mixed, mix_back = jax.vjp(mix_piece, ema_flat, normed, ema_omega)
     mixed_low = mixed.astype(jnp.bfloat16)
@@ -279,23 +614,28 @@
     grad_base_weight = outer_dot(mixed_low, grad_base_low)
     grad_mixed = inner_dot(grad_base_low, base_weight)
     grad_ema_flat, grad_normed_mix, grad_omega = mix_back(grad_mixed)
-    grad_ema_in, grad_forget_out, grad_beta_out, grad_eta, grad_block_end, grad_incoming = ema_back(
-        grad_ema_flat.reshape(row_count, seq_len, model_width)
-    )
-    later_grad = carried_in(
-        (span_decay, grad_incoming),
-        "seq",
-        forward_combine,
-        (jnp.ones_like(span_decay), jnp.zeros_like(grad_incoming)),
-        True,
-    )[1]
-    grad_span = jnp.sum(later_grad * incoming, axis=0)
-    grad_ema_end, grad_forget_end, grad_beta_end = end_back((grad_block_end, grad_span, later_grad))
-    grad_forget = grad_forget_out + grad_forget_end
-    grad_beta = grad_beta_out + grad_beta_end
-    grad_ema_total = (grad_ema_in + grad_ema_end).reshape(
-        row_count, seq_len, model_width
-    ) * valid_mask[:, :, None]
+    grad_turned, device_start = return_call(
+        grad_ema_flat.reshape(row_count, seq_len, model_width), retain
+    )
+    later = carried_in(device_start, span_decay, "seq", True)
+    grad_ema_total, cross, border, lags = adjoint_call(
+        grad_turned,
+        turned,
+        retain,
+        1.0 / retain,
+        power_of(retain, LAG),
+        mix,
+        later,
+        state_end,
+    )
+    cross = jnp.sum(cross, axis=1)
+    lags = jnp.sum(lags, axis=1)
+    paired = retain * jnp.sum(border, axis=1)
+    decay = jnp.ones_like(retain)
+    for lag in range(LAG):
+        paired = paired + decay * lags[lag]
+        decay = decay * retain
+    grad_ema_total = grad_ema_total * valid_mask[:, :, None]
     grad_vpre_low = value_back(grad_value)[0].astype(jnp.bfloat16)
     grad_value_weight = outer_dot(normed_low, grad_vpre_low)
     grad_normed = (
@@ -307,27 +647,65 @@
     grad_tokens = (
         (grad_flat + grad_residual).astype(jnp.bfloat16).reshape(row_count, seq_len, model_width)
     )
-    summed = tuple(
-        lax.psum(
-            (
-                grad_norm_gain,
-                grad_value_weight,
-                grad_forget,
-                grad_beta,
-                grad_eta,
-                grad_omega,
-                grad_base_weight,
-                grad_qk_gain,
-                grad_qk_bias,
-                grad_output_weight,
-                grad_ffn_gain,
-                grad_ffn_in,
-                grad_ffn_out,
-            ),
-            ("seq", "row"),
-        )
-    )
-    return (block_out, grad_tokens) + summed
+    width = model_width
+    small = jnp.concatenate(
+        [
+            paired,
+            cross,
+            grad_norm_gain[None],
+            grad_omega[None],
+            grad_ffn_gain[None],
+            jnp.concatenate([grad_qk_gain, grad_qk_bias], axis=0).reshape(-1, width),
+        ],
+        axis=0,
+    )
+    states = retain.shape[0]
+    padding = -small.shape[0] % 8
+    small = small_sum(jnp.pad(small, ((0, padding), (0, 0))))
+    paired, cross = small[:states], small[states : 2 * states]
+    grad_norm_gain, grad_omega, grad_ffn_gain = (small[2 * states + at] for at in range(3))
+    grad_query_key = small[2 * states + 3 : small.shape[0] - padding].reshape(4, query_width)
+    grad_qk_gain, grad_qk_bias = grad_query_key[:2], grad_query_key[2:]
+    grad_eta = (inflow * paired).T
+    grad_beta = (eta * paired * gate).T
+    grad_forget = (eta * paired * beta * (1.0 - forget) / gate - mix * cross).T
+    middle = grad_base_weight.shape[0] // 2
+    (
+        grad_ffn_out,
+        grad_ffn_in,
+        grad_output_weight,
+        base_top,
+        base_bottom,
+        grad_value_weight,
+    ) = summed_everywhere(
+        [
+            grad_ffn_out,
+            grad_ffn_in,
+            grad_output_weight,
+            grad_base_weight[:middle],
+            grad_base_weight[middle:],
+            grad_value_weight,
+        ],
+        (0, 1, 0, 0, 1, 2),
+    )
+    grad_base_weight = jnp.concatenate([base_top, base_bottom], axis=0)
+    return (
+        block_out,
+        grad_tokens,
+        grad_norm_gain,
+        grad_value_weight,
+        grad_forget,
+        grad_beta,
+        grad_eta,
+        grad_omega,
+        grad_base_weight,
+        grad_qk_gain,
+        grad_qk_bias,
+        grad_output_weight,
+        grad_ffn_gain,
+        grad_ffn_in,
+        grad_ffn_out,
+    )
 
 
 def solution(mesh):

time: 975 us -> 480 us (0.49)
  waiting for transfers between devices: 349 us -> 96.2 us
  matrix products: 356 us -> 114 us
  starting transfers between devices: 0.38 us -> 103 us
  local copies, waits for them, and re-layouts: 122 us -> 23.2 us
  Pallas kernels: 0 us -> 57.4 us
  blocking collectives: 33.1 us -> 0 us
  other arithmetic: 91.6 us -> 78 us
  between operations: 15.2 us -> 3.47 us
    psum x2 -> x0, waiting for transfers between devices: 349 us -> none  [per_device(): lax.psum((grad_norm_gain, grad_value_weight, grad_forget, grad_beta, grad...]
    dot_general x12 -> x0, matrix products: 227 us -> none  [the longest x9 143 us: batch_dot(): lax.dot_general(first_op, second_op, (((2,), (1,)), ((0,), (0,))), precis...]
    ppermute x0 -> x75, starting transfers between devices: none -> 103 us  [the longest x67 77.1 us: swapped(): lax.ppermute(value, mesh_axes, [(at, at ^ bit) for at in range(device_tot...]
    ppermute x0 -> x75, waiting for transfers between devices: none -> 96.2 us  [the longest x67 57.5 us: swapped(): lax.ppermute(value, mesh_axes, [(at, at ^ bit) for at in range(device_tot...]
    pallas_call x0 -> x4, Pallas kernels: none -> 57.4 us  [the longest x1 27.1 us: adjoint_call(): pl.pallas_call(adjoint_body, grid=(length // STEPS,), in_specs=[turned_sp...]
    all_gather x1 -> x0, blocking collectives: 33.1 us -> none  [carried_in(): pieces = jax.tree.map(lambda part: lax.all_gather(part, axis), value)]
    transpose x5 -> x0, local copies, waits for them, and re-layouts: 26.3 us -> none  [the longest x1 7.32 us: ema_output(): local_part.reshape(feature_count, length, row_count, blocks)]
    unnamed x269 -> x156, local copies, waits for them, and re-layouts: 33.7 us -> 8.05 us
  transfers between devices with their start and end apart: 4 -> 75, of which waited for: 2 -> 28; matrix products, arithmetic and copies ran while one was open for 18% -> 12% of each run, Pallas kernels for 0% -> 7%
where the time goes in v1:
time: 480 us; the launch traced here: 476 us
  matrix products  114 us (24%)
  starting transfers between devices  103 us (21%)
  waiting for transfers between devices  96.2 us (20%)
  other arithmetic  78 us (16%)
  Pallas kernels  57.4 us (12%)
  local copies, waits for them, and re-layouts  23.2 us (5%)
    ppermute x67, starting transfers between devices, swapped(): lax.ppermute(value, mesh_axes, [(at, at ^ bit) for at in range(device_tot...  77.1 us
    ppermute x67, waiting for transfers between devices, swapped(): lax.ppermute(value, mesh_axes, [(at, at ^ bit) for at in range(device_tot...  57.5 us
    ppermute x8, waiting for transfers between devices, moved(): return lax.ppermute(value, axis, pairs)  38.7 us
    dot_general x5, matrix products, inner_dot(): lax.dot_general(first_op, second_op, (((1,), (1,)), ((), ())), preferred_...  38.6 us
    dot_general x5, matrix products, plain_dot(): return jnp.dot(first_op, second_op, preferred_element_type=jnp.float32)  32.4 us
    pallas_call x1, Pallas kernels, adjoint_call(): pl.pallas_call(adjoint_body, grid=(length // STEPS,), in_specs=[turned_sp...  27.1 us
    ppermute x8, starting transfers between devices, moved(): return lax.ppermute(value, axis, pairs)  26.3 us
    dot_general x5, matrix products, outer_dot(): lax.dot_general(first_op, second_op, (((0,), (0,)), ((), ())), preferred_...  26.3 us
  transfers between devices with their start and end apart: 75, of which 28 were waited for; matrix products, arithmetic and copies ran while one was open for 12% of the time, Pallas kernels for 7%

profile of v1, /device:TPU:0, one launch (start us, length us, event | category | flops | bytes accessed | tf_op | source)
XLA Modules:
  0.0 476.1 jit_solution(1770228248699649296)
XLA Ops:
  4.6 9.5 %enter.1 = (bf16[8,256,512]{2,1,0:T(8,128)(2,1)}, f32[256,8,512]{2,1,0:T(8,128)}, f32[16,8,512]{2,1,0:T(8,128)S(1)}) custom-call(s32[8]{0:T(128)S(1)} %broadcast_subtract_fusion.count_ref, bf16[8,256,512]{2,1,0:T(8,128)(2,1)S(1)} %copy-done.1, f32[1,512]{1,0:T(1,128)S(1)} %bitcast.226, f32[16,512]{1,0:T(8,128)S(1)} %get-tuple-element.132.retain_ref), custom_call_target="tpu_custom_call" | custom-call | tf_op jit(solution)/shard_map/enter/pallas_call | solution.py:85
  14.1 4.9 %collective-permute-start = (f32[16,8,512]{2,1,0:T(8,128)S(1)}, f32[16,8,512]{2,1,0:T(8,128)S(1)}, u32[]{:S(2)}, u32[]{:S(2)}) collective-permute-start(f32[16,8,512]{2,1,0:T(8,128)S(1)} %get-tuple-element.26), channel_id=1, source_target_pairs={{0,4},{4,8},{8,12},{12,16},{16,20},{20,24},{24,28},{1,5},{5,9},{9,... | collective-permute-start | bytes 786440 | tf_op jit(solution)/shard_map/ppermute | solution.py:359
  22.1 2.5 collective-permute-done
  24.6 4.4 collective-permute-start.1
  29.9 3.7 collective-permute-done.1
  33.7 6.3 %collective-permute-start.2 = (f32[16,8,512]{2,1,0:T(8,128)S(1)}, f32[16,8,512]{2,1,0:T(8,128)S(1)}, u32[]{:S(2)}, u32[]{:S(2)}) collective-permute-start(f32[16,8,512]{2,1,0:T(8,128)S(1)} %multiply_add_fusion.5), channel_id=1, source_target_pairs={{0,8},{4,12},{8,16},{12,20},{16,24},{20,28},{1,9},{5,13},{9,17},{1... | collective-permute-start | bytes 786440 | tf_op jit(solution)/shard_map/ppermute | solution.py:359
  40.0 3.8 collective-permute-done.2
  43.9 5.4 %collective-permute-start.3 = (f32[16,8,512]{2,1,0:T(8,128)S(1)}, f32[16,8,512]{2,1,0:T(8,128)S(1)}, u32[]{:S(2)}, u32[]{:S(2)}) collective-permute-start(f32[16,8,512]{2,1,0:T(8,128)S(1)} %multiply_add_fusion.4), channel_id=1, source_target_pairs={{0,16},{4,20},{8,24},{12,28},{1,17},{5,21},{9,25},{13,29},{2,18},{... | collective-permute-start | bytes 786440 | tf_op jit(solution)/shard_map/ppermute | solution.py:359
  50.1 3.0 collective-permute-done.3
  53.2 12.4 %average.1 = (f32[8,256,512]{2,1,0:T(8,128)S(1)}, f32[16,8,512]{2,1,0:T(8,128)S(1)}) custom-call(f32[256,8,512]{2,1,0:T(8,128)} %get-tuple-element.25.turned_ref, f32[16,512]{1,0:T(8,128)S(1)} %get-tuple-element.132.retain_ref, f32[16,512]{1,0:T(8,128)S(1)} %get-tuple-element.131.mix_ref, f32[16,8,512]{2,1,0:T(8,128)S(1)} %multiply_add_fusion.3.start_ref), custom_call_target="tpu_custom_call" | custom-call | tf_op jit(solution)/shard_map/average/pallas_call | solution.py:147
  65.7 3.4 bitcast_add_fusion.1
  69.2 8.7 %fusion.108 = f32[2048,2176]{1,0:T(8,128)} fusion(bf16[2048,512]{1,0:T(8,128)(2,1)S(1)} %get-tuple-element.54, bf16[512,2176]{1,0:T(8,128)(2,1)S(1)} %copy-done), kind=kOutput, calls=%fused_computation.350 | convolution fusion | flops 4563402752 | bytes 22151168 | tf_op jit(solution)/shard_map/dot_general | solution.py:454
  81.0 5.3 %multiply_convert_fusion.2 = (bf16[2048,1024]{1,0:T(8,128)(2,1)S(1)}, f32[2048,1024]{1,0:T(8,128)}) fusion(bf16[2048,512]{1,0:T(8,128)(2,1)S(1)} %get-tuple-element.61, bf16[512,1024]{1,0:T(8,128)(2,1)S(1)} %copy-done.75), kind=kOutput, calls=%fused_computation.24 | convolution fusion | flops 2157969408 | bytes 15728640 | tf_op jit(solution)/shard_map/dot_general | solution.py:454
  87.7 8.3 %fusion.10 = bf16[2048,1024]{1,0:T(8,128)(2,1)S(1)} fusion(f32[16,128,1024]{2,1,0:T(8,128)S(1)} %fusion.60, f32[2048,2176]{1,0:T(8,128)} %fusion.108), kind=kLoop, calls=%fused_computation.18 | loop fusion | flops 12582912 | bytes 20971520 | tf_op jit(solution)/shard_map/convert_element_type | solution.py:559
  96.0 8.6 %fusion.96 = (f32[2048]{0:T(1024)S(1)}, f32[2048,512]{1,0:T(8,128)}, f32[2048,512]{1,0:T(8,128)}) fusion(f32[2048,2176]{1,0:T(8,128)} %fusion.108, bf16[8,256,512]{2,1,0:T(8,128)(2,1)S(1)} %copy-done.2, bf16[2048,1024]{1,0:T(8,128)(2,1)S(1)} %fusion.10, bf16[1024,512]{1,0:T(8,128)(2,1)S(1)} %copy-done.73), kind=kOutput, calls=%fused_computation.342 | convolution fusion | flops 2161113088 | bytes 24125440 | tf_op jit(solution)/shard_map/dot_general | solution.py:454
  104.6 3.0 multiply_reduce_fusion.2
  108.1 6.1 %multiply_convert_fusion.1 = (bf16[2048,1024]{1,0:T(8,128)(2,1)S(1)}, f32[2048,1024]{1,0:T(8,128)}) fusion(bf16[512,1024]{1,0:T(8,128)(2,1)S(1)} %copy-done.71, f32[2048,512]{1,0:T(8,128)S(1)} %copy-done.12, f32[512]{0:T(512)S(1)} %convert_element_type.95, f32[2048]{0:T(1024)S(1)} %fusion.83, f32[2048]{0:T(1024)S(1)} %broadcast_multiply_fusion.1), kind=kOutput, calls=%fused_computation.20 | convolution fusion | flops 2162163712 | bytes 17844224 | tf_op jit(solution)/shard_map/dot_general | solution.py:454
  114.2 8.3 %fusion.3 = bf16[2048,1024]{1,0:T(8,128)(2,1)} fusion(f32[2048,1024]{1,0:T(8,128)} %get-tuple-element.153, bf16[2048,512]{1,0:T(8,128)(2,1)S(1)} %bitcast.227, bf16[1024,512]{1,0:T(8,128)(2,1)S(1)} %copy-done.72), kind=kOutput, calls=%fused_computation.7 | convolution fusion | flops 2168455168 | bytes 15728640 | tf_op jit(solution)/shard_map/dot_general | solution.py:464
  122.5 6.0 %fusion.93 = f32[512,1024]{1,0:T(8,128)} fusion(bf16[2048,1024]{1,0:T(8,128)(2,1)} %fusion.3, f32[2048,512]{1,0:T(8,128)S(1)} %copy-done.12, f32[512]{0:T(512)S(1)} %convert_element_type.95, f32[2048]{0:T(1024)S(1)} %fusion.83, f32[2048]{0:T(1024)S(1)} %broadcast_multiply_fusion.1), kind=kOutput, calls=%fused_computation.339 | convolution fusion | flops 2151677952 | bytes 10504192 | tf_op jit(solution)/shard_map/dot_general | solution.py:458
  128.5 4.9 %multiply_reduce_fusion = (f32[512]{0:T(512)S(1)}, f32[2048]{0:T(1024)S(1)}, f32[2048,512]{1,0:T(8,128)S(1)}) fusion(f32[2048,512]{1,0:T(8,128)S(1)} %copy-done.12, f32[2048]{0:T(1024)S(1)} %fusion.83, f32[2048]{0:T(1024)S(1)} %broadcast_multiply_fusion.1, f32[512]{0:T(512)S(1)} %convert_element_type.95, bf16[2048,1024]{1,0:T(8,128)(2,1)} %fusion.3, ...), kind=kOutput, calls=%fused_computation.65 | convolution fusion | flops 2154821120 | bytes 13660160 | tf_op jit(solution)/shard_map/dot_general | solution.py:464
  133.4 3.7 add_convert_fusion.1
  137.1 3.7 fusion.112
  142.6 8.7 %fusion.16 = (bf16[2048,512]{1,0:T(8,128)(2,1)}, bf16[2048,512]{1,0:T(8,128)(2,1)S(1)}) fusion(bf16[8,256,512]{2,1,0:T(8,128)(2,1)S(1)} %copy-done.2, f32[2048,512]{1,0:T(8,128)} %get-tuple-element.151, f32[2048,512]{1,0:T(8,128)S(1)} %get-tuple-element.43, f32[2048]{0:T(1024)S(1)} %negate_multiply_fusion.1, bf16[8,256,512]{2,1,0:T(8,128)(2,1)S(1)} %copy-done.9, ...), kind=kLoop, calls=%fused_computation.36 | loop fusion | flops 26214400 | bytes 20979712 | tf_op jit(solution)/shard_map/convert.3
  151.2 3.7 fusion.111
  155.0 10.4 %multiply_convert_fusion = (bf16[2048,1024]{1,0:T(8,128)(2,1)S(1)}, bf16[2048,1024]{1,0:T(8,128)(2,1)}) fusion(f32[2048,2176]{1,0:T(8,128)} %fusion.108, f32[16,128,1024]{2,1,0:T(8,128)} %copy-done.8, bf16[2048,512]{1,0:T(8,128)(2,1)S(1)} %get-tuple-element.47, bf16[1024,512]{1,0:T(8,128)(2,1)S(1)} %copy-done.74), kind=kOutput, calls=%fused_computation.19 | convolution fusion | flops 2176843776 | bytes 28311552 | tf_op jit(solution)/shard_map/dot_general | solution.py:464
  167.4 2.2 fusion.109
  169.6 4.2 fusion.105
  173.8 4.3 fusion.102
  178.2 4.0 fusion.58
  184.2 10.5 %fusion.36 = f32[512,2176]{1,0:T(8,128)} fusion(bf16[2048,512]{1,0:T(8,128)(2,1)S(1)} %copy-done.35, bf16[2048,512]{1,0:T(8,128)(2,1)S(1)} %copy-done.20, bf16[2048,512]{1,0:T(8,128)(2,1)S(1)} %copy-done.36, bf16[2048,1024]{1,0:T(8,128)(2,1)} %get-tuple-element.49, bf16[2048,128]{1,0:T(8,128)(2,1)S(1)} %get-tuple-element.50), kind=kOutput, calls=%fused_computation.81 | convolution fusion | flops 4599054336 | bytes 15466496 | tf_op jit(solution)/shard_map/dot_general | solution.py:458
  194.7 10.1 %fusion.18 = f32[2048,512]{1,0:T(8,128)} fusion(f32[2048,512]{1,0:T(8,128)} %get-tuple-element.53, bf16[512,2176]{1,0:T(8,128)(2,1)S(1)} %copy-done, bf16[2048,512]{1,0:T(8,128)(2,1)S(1)} %copy-done.20, bf16[2048,512]{1,0:T(8,128)(2,1)} %get-tuple-element.46, bf16[2048,1024]{1,0:T(8,128)(2,1)} %get-tuple-element.49, bf16[2048,128]{1,0:T(8,128)(2,1)S(1)} %get-tuple-element.50), kind=kOutput, calls=%fused_computation.38 | convolution fusion | flops 4608491520 | bytes 19529728 | tf_op jit(solution)/shard_map/dot_general | solution.py:464
  204.8 4.1 fusion.97
  215.2 8.3 %back_enter.1 = (f32[256,8,512]{2,1,0:T(8,128)S(1)}, f32[16,8,512]{2,1,0:T(8,128)S(1)}) custom-call(f32[8,256,512]{2,1,0:T(8,128)} %bitcast.233, f32[16,512]{1,0:T(8,128)S(1)} %get-tuple-element.132.retain_ref), custom_call_target="tpu_custom_call" | custom-call | tf_op jit(solution)/shard_map/back_enter/pallas_call | solution.py:205
  224.9 6.1 %fusion.9 = bf16[2048,1024]{1,0:T(8,128)(2,1)S(1)} fusion(f32[16,128,1024]{2,1,0:T(8,128)S(1)} %fusion.58, f32[2048,1024]{1,0:T(8,128)} %get-tuple-element.148), kind=kLoop, calls=%fused_computation.13 | loop fusion | flops 20971520 | bytes 20971520 | tf_op jit(solution)/shard_map/convert_element_type | solution.py:639
  235.0 2.3 fusion.110
  238.4 8.6 %collective-permute-done.5 = f32[16,8,512]{2,1,0:T(8,128)S(1)} collective-permute-done((f32[16,8,512]{2,1,0:T(8,128)S(1)}, f32[16,8,512]{2,1,0:T(8,128)S(1)}, u32[]{:S(2)}, u32[]{:S(2)}) %collective-permute-start.5) | collective-permute-done | bytes 262176 | tf_op jit(solution)/shard_map/ppermute | solution.py:359
  248.5 7.6 %collective-permute-done.6 = f32[16,8,512]{2,1,0:T(8,128)S(1)} collective-permute-done((f32[16,8,512]{2,1,0:T(8,128)S(1)}, f32[16,8,512]{2,1,0:T(8,128)S(1)}, u32[]{:S(2)}, u32[]{:S(2)}) %collective-permute-start.6) | collective-permute-done | bytes 262176 | tf_op jit(solution)/shard_map/ppermute | solution.py:359
  262.0 2.7 collective-permute-start.56
  268.0 8.0 %collective-permute-done.7 = f32[16,8,512]{2,1,0:T(8,128)S(1)} collective-permute-done((f32[16,8,512]{2,1,0:T(8,128)S(1)}, f32[16,8,512]{2,1,0:T(8,128)S(1)}, u32[]{:S(2)}, u32[]{:S(2)}) %collective-permute-start.7) | collective-permute-done | bytes 262176 | tf_op jit(solution)/shard_map/ppermute | solution.py:359
  277.6 27.1 %adjoint.1 = (f32[8,256,512]{2,1,0:T(8,128)S(1)}, f32[16,8,512]{2,1,0:T(8,128)S(1)}, f32[16,8,512]{2,1,0:T(8,128)S(1)}, f32[8,8,512]{2,1,0:T(8,128)S(1)}) custom-call(f32[256,8,512]{2,1,0:T(8,128)} %copy-done.4, f32[256,8,512]{2,1,0:T(8,128)} %get-tuple-element.25.turned_ref, f32[16,512]{1,0:T(8,128)S(1)} %get-tuple-element.132.retain_ref, ...), custom_call_target="tpu_custom_call" | custom-call | tf_op jit(solution)/shard_map/adjoint/pallas_call | solution.py:323
  307.8 4.9 %fusion.33 = (f32[2048]{0:T(1024)S(1)}, f32[2048,512]{1,0:T(8,128)S(1)}) fusion(bf16[8,256,512]{2,1,0:T(8,128)(2,1)S(1)} %copy-done.3, f32[512]{0:T(512)S(1)} %copy-done.6, f32[2048]{0:T(1024)S(1)} %bitcast.240, bf16[2048,1024]{1,0:T(8,128)(2,1)} %copy-done.25, bf16[512,1024]{1,0:T(8,128)(2,1)S(1)} %copy-done.76, ...), kind=kOutput, calls=%fused_computation.62 | convolution fusion | flops 2155870208 | bytes 19943424 | tf_op jit(solution)/shard_map/dot_general | solution.py:464
  312.8 2.4 fusion.32
  315.6 9.1 %add_convert_fusion = bf16[2048,512]{1,0:T(8,128)(2,1)} fusion(f32[2048]{0:T(1024)S(1)} %negate_multiply_fusion, f32[2048,512]{1,0:T(8,128)} %copy-done.7, f32[2048]{0:T(1024)S(1)} %negate_multiply_fusion.1, bf16[8,256,512]{2,1,0:T(8,128)(2,1)} %param.31, f32[2048]{0:T(1024)S(1)} %multiply_multiply_fusion.4, f32[2048]{0:T(1024)S(1)} %bitcast.242, ...), kind=kLoop, calls=%fused_computation.66 | loop fusion | flops 19922944 | bytes 18917376 | tf_op jit(solution)/shard_map/convert_element_type | solution.py:648
  329.5 2.6 collective-permute-start.11
  338.3 4.3 collective-permute-start.12
  342.6 2.8 collective-permute-done.14
  349.3 2.2 collective-permute-start.26
  355.3 5.0 %collective-permute-done.46 = f32[256,512]{1,0:T(8,128)S(1)} collective-permute-done((f32[256,512]{1,0:T(8,128)S(1)}, f32[256,512]{1,0:T(8,128)S(1)}, u32[]{:S(2)}, u32[]{:S(2)}) %collective-permute-start.46) | collective-permute-done | bytes 524320 | tf_op jit(solution)/shard_map/ppermute | solution.py:382
  364.6 4.2 collective-permute-done.26
  373.0 2.5 collective-permute-done.17
  375.6 8.7 %collective-permute-done.37 = f32[32,2176]{1,0:T(8,128)S(1)} collective-permute-done((f32[32,2176]{1,0:T(8,128)S(1)}, f32[32,2176]{1,0:T(8,128)S(1)}, u32[]{:S(2)}, u32[]{:S(2)}) %collective-permute-start.37) | collective-permute-done | bytes 278560 | tf_op jit(solution)/shard_map/ppermute | solution.py:382
  404.7 4.2 collective-permute-start.71
  415.7 2.7 collective-permute-start.72
  420.0 2.5 collective-permute-start.31
  422.6 3.2 collective-permute-done.41
  425.7 2.7 collective-permute-start.22
  429.2 2.6 collective-permute-start.42
  431.9 3.7 collective-permute-start.32
  437.9 3.9 collective-permute-start.53
  442.1 3.4 collective-permute-start.43
  445.6 6.8 %collective-permute-done.63 = f32[128,1024]{1,0:T(8,128)S(1)} collective-permute-done((f32[128,1024]{1,0:T(8,128)S(1)}, f32[128,1024]{1,0:T(8,128)S(1)}, u32[]{:S(2)}, u32[]{:S(2)}) %collective-permute-start.63) | collective-permute-done | bytes 524320 | tf_op jit(solution)/shard_map/ppermute | solution.py:382
  452.8 6.6 %collective-permute-done.53 = f32[256,512]{1,0:T(8,128)S(1)} collective-permute-done((f32[256,512]{1,0:T(8,128)S(1)}, f32[256,512]{1,0:T(8,128)S(1)}, u32[]{:S(2)}, u32[]{:S(2)}) %collective-permute-start.53) | collective-permute-done | bytes 524320 | tf_op jit(solution)/shard_map/ppermute | solution.py:382
  460.7 4.7 collective-permute-done.33
  473.5 2.4 pad_maximum_fusion.1
  (448 shorter events, 115.4 us)
Async XLA Ops:
  14.1 10.4 %collective-permute-start = (f32[16,8,512]{2,1,0:T(8,128)S(1)}, f32[16,8,512]{2,1,0:T(8,128)S(1)}, u32[]{:S(2)}, u32[]{:S(2)}) collective-permute-start(f32[16,8,512]{2,1,0:T(8,128)S(1)} %get-tuple-element.26), channel_id=1, source_target_pairs={{0,4},{4,8},{8,12},{12,16},{16,20},{20,24},{24,28},{1,5},{5,9},{9,... | collective-permute-start | bytes 786440 | tf_op jit(solution)/shard_map/ppermute | solution.py:359
  24.6 9.1 %collective-permute-start.1 = (f32[16,8,512]{2,1,0:T(8,128)S(1)}, f32[16,8,512]{2,1,0:T(8,128)S(1)}, u32[]{:S(2)}, u32[]{:S(2)}) collective-permute-start(f32[16,8,512]{2,1,0:T(8,128)S(1)} %collective-permute-done), channel_id=1, source_target_pairs={{0,4},{4,8},{8,12},{12,16},{16,20},{20,24},{24,28},{1,5},{5,9},{9,... | collective-permute-start | bytes 786440 | tf_op jit(solution)/shard_map/ppermute | solution.py:359
  33.7 10.1 %collective-permute-start.2 = (f32[16,8,512]{2,1,0:T(8,128)S(1)}, f32[16,8,512]{2,1,0:T(8,128)S(1)}, u32[]{:S(2)}, u32[]{:S(2)}) collective-permute-start(f32[16,8,512]{2,1,0:T(8,128)S(1)} %multiply_add_fusion.5), channel_id=1, source_target_pairs={{0,8},{4,12},{8,16},{12,20},{16,24},{20,28},{1,9},{5,13},{9,17},{1... | collective-permute-start | bytes 786440 | tf_op jit(solution)/shard_map/ppermute | solution.py:359
  43.9 9.3 %collective-permute-start.3 = (f32[16,8,512]{2,1,0:T(8,128)S(1)}, f32[16,8,512]{2,1,0:T(8,128)S(1)}, u32[]{:S(2)}, u32[]{:S(2)}) collective-permute-start(f32[16,8,512]{2,1,0:T(8,128)S(1)} %multiply_add_fusion.4), channel_id=1, source_target_pairs={{0,16},{4,20},{8,24},{12,28},{1,17},{5,21},{9,25},{13,29},{2,18},{... | collective-permute-start | bytes 786440 | tf_op jit(solution)/shard_map/ppermute | solution.py:359
  213.1 43.1 %collective-permute-start.55 = (f32[256,1024]{1,0:T(8,128)}, f32[256,1024]{1,0:T(8,128)}, u32[]{:S(2)}, u32[]{:S(2)}) collective-permute-start(f32[256,1024]{1,0:T(8,128)} %constant_dynamic-slice_fusion.9), channel_id=1, source_target_pairs={{0,1},{1,0},{2,3},{3,2},{4,5},{5,4},{6,7},{7,6},{8,9},{9,8},{10,11... | collective-permute-start | bytes 3145736 | tf_op jit(solution)/shard_map/ppermute | solution.py:382
  213.1 46.0 %collective-permute-start.65 = (f32[512,512]{1,0:T(8,128)}, f32[512,512]{1,0:T(8,128)}, u32[]{:S(2)}, u32[]{:S(2)}) collective-permute-start(f32[512,512]{1,0:T(8,128)} %constant_dynamic-slice_fusion.4), channel_id=1, source_target_pairs={{0,1},{1,0},{2,3},{3,2},{4,5},{5,4},{6,7},{7,6},{8,9},{9,8},{10,11... | collective-permute-start | bytes 3145736 | tf_op jit(solution)/shard_map/ppermute | solution.py:382
  213.6 48.4 %collective-permute-start.45 = (f32[512,512]{1,0:T(8,128)}, f32[512,512]{1,0:T(8,128)}, u32[]{:S(2)}, u32[]{:S(2)}) collective-permute-start(f32[512,512]{1,0:T(8,128)} %constant_dynamic-slice_fusion.14), channel_id=1, source_target_pairs={{0,1},{1,0},{2,3},{3,2},{4,5},{5,4},{6,7},{7,6},{8,9},{9,8},{10,11... | collective-permute-start | bytes 3145736 | tf_op jit(solution)/shard_map/ppermute | solution.py:382
  214.7 111.7 %collective-permute-start.35 = (f32[128,2176]{1,0:T(8,128)}, f32[128,2176]{1,0:T(8,128)}, u32[]{:S(2)}, u32[]{:S(2)}) collective-permute-start(f32[128,2176]{1,0:T(8,128)} %constant_dynamic-slice_fusion.19), channel_id=1, source_target_pairs={{0,1},{1,0},{2,3},{3,2},{4,5},{5,4},{6,7},{7,6},{8,9},{9,8},{10,11... | collective-permute-start | bytes 3342344 | tf_op jit(solution)/shard_map/ppermute | solution.py:382
  223.6 10.1 %collective-permute-start.4 = (f32[16,8,512]{2,1,0:T(8,128)S(1)}, f32[16,8,512]{2,1,0:T(8,128)S(1)}, u32[]{:S(2)}, u32[]{:S(2)}) collective-permute-start(f32[16,8,512]{2,1,0:T(8,128)S(1)} %get-tuple-element.29), channel_id=1, source_target_pairs={{4,0},{8,4},{12,8},{16,12},{20,16},{24,20},{28,24},{5,1},{9,5},{13... | collective-permute-start | bytes 786440 | tf_op jit(solution)/shard_map/ppermute | solution.py:359
  233.7 13.3 %collective-permute-start.5 = (f32[16,8,512]{2,1,0:T(8,128)S(1)}, f32[16,8,512]{2,1,0:T(8,128)S(1)}, u32[]{:S(2)}, u32[]{:S(2)}) collective-permute-start(f32[16,8,512]{2,1,0:T(8,128)S(1)} %collective-permute-done.4), channel_id=1, source_target_pairs={{4,0},{8,4},{12,8},{16,12},{20,16},{24,20},{28,24},{5,1},{9,5},{13... | collective-permute-start | bytes 786440 | tf_op jit(solution)/shard_map/ppermute | solution.py:359
  247.1 9.1 %collective-permute-start.6 = (f32[16,8,512]{2,1,0:T(8,128)S(1)}, f32[16,8,512]{2,1,0:T(8,128)S(1)}, u32[]{:S(2)}, u32[]{:S(2)}) collective-permute-start(f32[16,8,512]{2,1,0:T(8,128)S(1)} %multiply_add_fusion.2), channel_id=1, source_target_pairs={{8,0},{12,4},{16,8},{20,12},{24,16},{28,20},{9,1},{13,5},{17,9},{2... | collective-permute-start | bytes 786440 | tf_op jit(solution)/shard_map/ppermute | solution.py:359
  256.2 71.7 %collective-permute-start.25 = (f32[128,2176]{1,0:T(8,128)}, f32[128,2176]{1,0:T(8,128)}, u32[]{:S(2)}, u32[]{:S(2)}) collective-permute-start(f32[128,2176]{1,0:T(8,128)} %constant_dynamic-slice_fusion.24), channel_id=1, source_target_pairs={{0,1},{1,0},{2,3},{3,2},{4,5},{5,4},{6,7},{7,6},{8,9},{9,8},{10,11... | collective-permute-start | bytes 3342344 | tf_op jit(solution)/shard_map/ppermute | solution.py:382
  256.2 68.5 %collective-permute-start.15 = (f32[256,1024]{1,0:T(8,128)}, f32[256,1024]{1,0:T(8,128)}, u32[]{:S(2)}, u32[]{:S(2)}) collective-permute-start(f32[256,1024]{1,0:T(8,128)} %constant_dynamic-slice_fusion.29), channel_id=1, source_target_pairs={{0,1},{1,0},{2,3},{3,2},{4,5},{5,4},{6,7},{7,6},{8,9},{9,8},{10,11... | collective-permute-start | bytes 3145736 | tf_op jit(solution)/shard_map/ppermute | solution.py:382
  259.1 16.9 %collective-permute-start.7 = (f32[16,8,512]{2,1,0:T(8,128)S(1)}, f32[16,8,512]{2,1,0:T(8,128)S(1)}, u32[]{:S(2)}, u32[]{:S(2)}) collective-permute-start(f32[16,8,512]{2,1,0:T(8,128)S(1)} %multiply_add_fusion.1), channel_id=1, source_target_pairs={{16,0},{20,4},{24,8},{28,12},{17,1},{21,5},{25,9},{29,13},{18,2},{... | collective-permute-start | bytes 786440 | tf_op jit(solution)/shard_map/ppermute | solution.py:359
  262.0 87.2 %collective-permute-start.56 = (f32[128,1024]{1,0:T(8,128)}, f32[128,1024]{1,0:T(8,128)}, u32[]{:S(2)}, u32[]{:S(2)}) collective-permute-start(f32[128,1024]{1,0:T(8,128)} %constant_dynamic-slice_fusion.8), channel_id=1, source_target_pairs={{0,4},{1,5},{2,6},{3,7},{4,0},{5,1},{6,2},{7,3},{8,12},{9,13},{10,... | collective-permute-start | bytes 1572872 | tf_op jit(solution)/shard_map/ppermute | solution.py:382
  276.0 76.6 %collective-permute-start.66 = (f32[256,512]{1,0:T(8,128)}, f32[256,512]{1,0:T(8,128)}, u32[]{:S(2)}, u32[]{:S(2)}) collective-permute-start(f32[256,512]{1,0:T(8,128)} %constant_dynamic-slice_fusion.3), channel_id=1, source_target_pairs={{0,2},{1,3},{2,0},{3,1},{4,6},{5,7},{6,4},{7,5},{8,10},{9,11},{10,... | collective-permute-start | bytes 1572872 | tf_op jit(solution)/shard_map/ppermute | solution.py:382
  338.1 7.3 %collective-permute-start.14 = (f32[40,512]{1,0:T(8,128)S(1)}, f32[40,512]{1,0:T(8,128)S(1)}, u32[]{:S(2)}, u32[]{:S(2)}) collective-permute-start(f32[40,512]{1,0:T(8,128)S(1)} %add_add_fusion.4), channel_id=1, source_target_pairs={{0,24},{1,25},{2,26},{3,27},{4,28},{5,29},{6,30},{7,31},{8,16},{9,... | collective-permute-start | bytes 245768 | tf_op jit(solution)/shard_map/ppermute | solution.py:382
  338.2 8.5 %collective-permute-start.13 = (f32[40,512]{1,0:T(8,128)S(1)}, f32[40,512]{1,0:T(8,128)S(1)}, u32[]{:S(2)}, u32[]{:S(2)}) collective-permute-start(f32[40,512]{1,0:T(8,128)S(1)} %add_add_fusion.4), channel_id=1, source_target_pairs={{0,16},{1,17},{2,18},{3,19},{4,20},{5,21},{6,22},{7,23},{8,24},{9,... | collective-permute-start | bytes 245768 | tf_op jit(solution)/shard_map/ppermute | solution.py:382
  338.3 8.9 %collective-permute-start.12 = (f32[40,512]{1,0:T(8,128)S(1)}, f32[40,512]{1,0:T(8,128)S(1)}, u32[]{:S(2)}, u32[]{:S(2)}) collective-permute-start(f32[40,512]{1,0:T(8,128)S(1)} %add_add_fusion.4), channel_id=1, source_target_pairs={{0,8},{1,9},{2,10},{3,11},{4,12},{5,13},{6,14},{7,15},{8,0},{9,1},... | collective-permute-start | bytes 245768 | tf_op jit(solution)/shard_map/ppermute | solution.py:382
  345.4 14.9 %collective-permute-start.46 = (f32[256,512]{1,0:T(8,128)S(1)}, f32[256,512]{1,0:T(8,128)S(1)}, u32[]{:S(2)}, u32[]{:S(2)}) collective-permute-start(f32[256,512]{1,0:T(8,128)S(1)} %copy-done.46), channel_id=1, source_target_pairs={{0,2},{1,3},{2,0},{3,1},{4,6},{5,7},{6,4},{7,5},{8,10},{9,11},{10,... | collective-permute-start | bytes 1572872 | tf_op jit(solution)/shard_map/ppermute | solution.py:382
  346.7 14.4 %collective-permute-start.16 = (f32[128,1024]{1,0:T(8,128)S(1)}, f32[128,1024]{1,0:T(8,128)S(1)}, u32[]{:S(2)}, u32[]{:S(2)}) collective-permute-start(f32[128,1024]{1,0:T(8,128)S(1)} %constant_dynamic-slice_fusion.28), channel_id=1, source_target_pairs={{0,8},{1,9},{2,10},{3,11},{4,12},{5,13},{6,14},{7,15},{8,0},{9,1},... | collective-permute-start | bytes 1572872 | tf_op jit(solution)/shard_map/ppermute | solution.py:382
  347.1 15.5 %collective-permute-start.36 = (f32[64,2176]{1,0:T(8,128)S(1)}, f32[64,2176]{1,0:T(8,128)S(1)}, u32[]{:S(2)}, u32[]{:S(2)}) collective-permute-start(f32[64,2176]{1,0:T(8,128)S(1)} %constant_dynamic-slice_fusion.18), channel_id=1, source_target_pairs={{0,4},{1,5},{2,6},{3,7},{4,0},{5,1},{6,2},{7,3},{8,12},{9,13},{10,... | collective-permute-start | bytes 1671176 | tf_op jit(solution)/shard_map/ppermute | solution.py:382
  349.3 19.5 %collective-permute-start.26 = (f32[64,2176]{1,0:T(8,128)S(1)}, f32[64,2176]{1,0:T(8,128)S(1)}, u32[]{:S(2)}, u32[]{:S(2)}) collective-permute-start(f32[64,2176]{1,0:T(8,128)S(1)} %constant_dynamic-slice_fusion.23), channel_id=1, source_target_pairs={{0,2},{1,3},{2,0},{3,1},{4,6},{5,7},{6,4},{7,5},{8,10},{9,11},{10,... | collective-permute-start | bytes 1671176 | tf_op jit(solution)/shard_map/ppermute | solution.py:382
  352.6 16.2 %collective-permute-start.57 = (f32[64,1024]{1,0:T(8,128)S(1)}, f32[64,1024]{1,0:T(8,128)S(1)}, u32[]{:S(2)}, u32[]{:S(2)}) collective-permute-start(f32[64,1024]{1,0:T(8,128)S(1)} %constant_dynamic-slice_fusion.7), channel_id=1, source_target_pairs={{0,8},{1,9},{2,10},{3,11},{4,12},{5,13},{6,14},{7,15},{8,0},{9,1},... | collective-permute-start | bytes 786440 | tf_op jit(solution)/shard_map/ppermute | solution.py:382
  360.3 9.4 %collective-permute-start.67 = (f32[128,512]{1,0:T(8,128)S(1)}, f32[128,512]{1,0:T(8,128)S(1)}, u32[]{:S(2)}, u32[]{:S(2)}) collective-permute-start(f32[128,512]{1,0:T(8,128)S(1)} %constant_dynamic-slice_fusion.2), channel_id=1, source_target_pairs={{0,4},{1,5},{2,6},{3,7},{4,0},{5,1},{6,2},{7,3},{8,12},{9,13},{10,... | collective-permute-start | bytes 786440 | tf_op jit(solution)/shard_map/ppermute | solution.py:382
  361.1 11.8 %collective-permute-start.47 = (f32[128,512]{1,0:T(8,128)S(1)}, f32[128,512]{1,0:T(8,128)S(1)}, u32[]{:S(2)}, u32[]{:S(2)}) collective-permute-start(f32[128,512]{1,0:T(8,128)S(1)} %constant_dynamic-slice_fusion.12), channel_id=1, source_target_pairs={{0,4},{1,5},{2,6},{3,7},{4,0},{5,1},{6,2},{7,3},{8,12},{9,13},{10,... | collective-permute-start | bytes 786440 | tf_op jit(solution)/shard_map/ppermute | solution.py:382
  362.7 12.8 %collective-permute-start.17 = (f32[64,1024]{1,0:T(8,128)S(1)}, f32[64,1024]{1,0:T(8,128)S(1)}, u32[]{:S(2)}, u32[]{:S(2)}) collective-permute-start(f32[64,1024]{1,0:T(8,128)S(1)} %constant_dynamic-slice_fusion.27), channel_id=1, source_target_pairs={{0,16},{1,17},{2,18},{3,19},{4,20},{5,21},{6,22},{7,23},{8,24},{9,... | collective-permute-start | bytes 786440 | tf_op jit(solution)/shard_map/ppermute | solution.py:382
  368.7 15.5 %collective-permute-start.37 = (f32[32,2176]{1,0:T(8,128)S(1)}, f32[32,2176]{1,0:T(8,128)S(1)}, u32[]{:S(2)}, u32[]{:S(2)}) collective-permute-start(f32[32,2176]{1,0:T(8,128)S(1)} %constant_dynamic-slice_fusion.17), channel_id=1, source_target_pairs={{0,8},{1,9},{2,10},{3,11},{4,12},{5,13},{6,14},{7,15},{8,0},{9,1},... | collective-permute-start | bytes 835592 | tf_op jit(solution)/shard_map/ppermute | solution.py:382
  368.9 15.5 %collective-permute-start.27 = (f32[32,2176]{1,0:T(8,128)S(1)}, f32[32,2176]{1,0:T(8,128)S(1)}, u32[]{:S(2)}, u32[]{:S(2)}) collective-permute-start(f32[32,2176]{1,0:T(8,128)S(1)} %constant_dynamic-slice_fusion.22), channel_id=1, source_target_pairs={{0,4},{1,5},{2,6},{3,7},{4,0},{5,1},{6,2},{7,3},{8,12},{9,13},{10,... | collective-permute-start | bytes 835592 | tf_op jit(solution)/shard_map/ppermute | solution.py:382
  369.7 14.8 %collective-permute-start.58 = (f32[32,1024]{1,0:T(8,128)S(1)}, f32[32,1024]{1,0:T(8,128)S(1)}, u32[]{:S(2)}, u32[]{:S(2)}) collective-permute-start(f32[32,1024]{1,0:T(8,128)S(1)} %constant_dynamic-slice_fusion.6), channel_id=1, source_target_pairs={{0,16},{1,17},{2,18},{3,19},{4,20},{5,21},{6,22},{7,23},{8,24},{9,... | collective-permute-start | bytes 393224 | tf_op jit(solution)/shard_map/ppermute | solution.py:382
  372.9 13.8 %collective-permute-start.68 = (f32[64,512]{1,0:T(8,128)S(1)}, f32[64,512]{1,0:T(8,128)S(1)}, u32[]{:S(2)}, u32[]{:S(2)}) collective-permute-start(f32[64,512]{1,0:T(8,128)S(1)} %constant_dynamic-slice_fusion.1), channel_id=1, source_target_pairs={{0,8},{1,9},{2,10},{3,11},{4,12},{5,13},{6,14},{7,15},{8,0},{9,1},... | collective-permute-start | bytes 393224 | tf_op jit(solution)/shard_map/ppermute | solution.py:382
  375.5 13.4 %collective-permute-start.48 = (f32[64,512]{1,0:T(8,128)S(1)}, f32[64,512]{1,0:T(8,128)S(1)}, u32[]{:S(2)}, u32[]{:S(2)}) collective-permute-start(f32[64,512]{1,0:T(8,128)S(1)} %constant_dynamic-slice_fusion.11), channel_id=1, source_target_pairs={{0,8},{1,9},{2,10},{3,11},{4,12},{5,13},{6,14},{7,15},{8,0},{9,1},... | collective-permute-start | bytes 393224 | tf_op jit(solution)/shard_map/ppermute | solution.py:382
  384.4 14.9 %collective-permute-start.38 = (f32[16,2176]{1,0:T(8,128)S(1)}, f32[16,2176]{1,0:T(8,128)S(1)}, u32[]{:S(2)}, u32[]{:S(2)}) collective-permute-start(f32[16,2176]{1,0:T(8,128)S(1)} %constant_dynamic-slice_fusion.16), channel_id=1, source_target_pairs={{0,16},{1,17},{2,18},{3,19},{4,20},{5,21},{6,22},{7,23},{8,24},{9,... | collective-permute-start | bytes 417800 | tf_op jit(solution)/shard_map/ppermute | solution.py:382
  384.5 16.3 %collective-permute-start.28 = (f32[16,2176]{1,0:T(8,128)S(1)}, f32[16,2176]{1,0:T(8,128)S(1)}, u32[]{:S(2)}, u32[]{:S(2)}) collective-permute-start(f32[16,2176]{1,0:T(8,128)S(1)} %constant_dynamic-slice_fusion.21), channel_id=1, source_target_pairs={{0,8},{1,9},{2,10},{3,11},{4,12},{5,13},{6,14},{7,15},{8,0},{9,1},... | collective-permute-start | bytes 417800 | tf_op jit(solution)/shard_map/ppermute | solution.py:382
  394.8 6.8 %collective-permute-start.60 = (f32[16,1024]{1,0:T(8,128)S(1)}, f32[16,1024]{1,0:T(8,128)S(1)}, u32[]{:S(2)}, u32[]{:S(2)}) collective-permute-start(f32[16,1024]{1,0:T(8,128)S(1)} %dynamic-slice_add_fusion.27), channel_id=1, source_target_pairs={{0,2},{1,3},{2,0},{3,1},{4,6},{5,7},{6,4},{7,5},{8,10},{9,11},{10,... | collective-permute-start | bytes 196616 | tf_op jit(solution)/shard_map/ppermute | solution.py:382
  396.2 7.1 %collective-permute-start.70 = (f32[32,512]{1,0:T(8,128)S(1)}, f32[32,512]{1,0:T(8,128)S(1)}, u32[]{:S(2)}, u32[]{:S(2)}) collective-permute-start(f32[32,512]{1,0:T(8,128)S(1)} %dynamic-slice_add_fusion.26), channel_id=1, source_target_pairs={{0,16},{1,17},{2,18},{3,19},{4,20},{5,21},{6,22},{7,23},{8,24},{9,... | collective-permute-start | bytes 196616 | tf_op jit(solution)/shard_map/ppermute | solution.py:382
  397.9 6.9 %collective-permute-start.50 = (f32[32,512]{1,0:T(8,128)S(1)}, f32[32,512]{1,0:T(8,128)S(1)}, u32[]{:S(2)}, u32[]{:S(2)}) collective-permute-start(f32[32,512]{1,0:T(8,128)S(1)} %dynamic-slice_add_fusion.28), channel_id=1, source_target_pairs={{0,16},{1,17},{2,18},{3,19},{4,20},{5,21},{6,22},{7,23},{8,24},{9,... | collective-permute-start | bytes 196616 | tf_op jit(solution)/shard_map/ppermute | solution.py:382
  399.3 9.7 %collective-permute-start.20 = (f32[16,1024]{1,0:T(8,128)S(1)}, f32[16,1024]{1,0:T(8,128)S(1)}, u32[]{:S(2)}, u32[]{:S(2)}) collective-permute-start(f32[16,1024]{1,0:T(8,128)S(1)} %dynamic-slice_add_fusion.29), channel_id=1, source_target_pairs={{0,4},{1,5},{2,6},{3,7},{4,0},{5,1},{6,2},{7,3},{8,12},{9,13},{10,... | collective-permute-start | bytes 196616 | tf_op jit(solution)/shard_map/ppermute | solution.py:382
  400.9 8.2 %collective-permute-start.39 = (f32[8,2176]{1,0:T(8,128)S(1)}, f32[8,2176]{1,0:T(8,128)S(1)}, u32[]{:S(2)}, u32[]{:S(2)}) collective-permute-start(f32[8,2176]{1,0:T(8,128)S(1)} %constant_dynamic-slice_fusion.15), channel_id=1, source_target_pairs={{0,2},{1,3},{2,0},{3,1},{4,6},{5,7},{6,4},{7,5},{8,10},{9,11},{10,... | collective-permute-start | bytes 208904 | tf_op jit(solution)/shard_map/ppermute | solution.py:382
  401.6 8.1 %collective-permute-start.29 = (f32[8,2176]{1,0:T(8,128)S(1)}, f32[8,2176]{1,0:T(8,128)S(1)}, u32[]{:S(2)}, u32[]{:S(2)}) collective-permute-start(f32[8,2176]{1,0:T(8,128)S(1)} %constant_dynamic-slice_fusion.20), channel_id=1, source_target_pairs={{0,16},{1,17},{2,18},{3,19},{4,20},{5,21},{6,22},{7,23},{8,24},{9,... | collective-permute-start | bytes 208904 | tf_op jit(solution)/shard_map/ppermute | solution.py:382
  403.3 8.9 %collective-permute-start.61 = (f32[32,1024]{1,0:T(8,128)S(1)}, f32[32,1024]{1,0:T(8,128)S(1)}, u32[]{:S(2)}, u32[]{:S(2)}) collective-permute-start(f32[32,1024]{1,0:T(8,128)S(1)} %pad_maximum_fusion.32), channel_id=1, source_target_pairs={{0,16},{1,17},{2,18},{3,19},{4,20},{5,21},{6,22},{7,23},{8,24},{9,... | collective-permute-start | bytes 393224 | tf_op jit(solution)/shard_map/ppermute | solution.py:382
  404.7 8.8 %collective-permute-start.71 = (f32[64,512]{1,0:T(8,128)S(1)}, f32[64,512]{1,0:T(8,128)S(1)}, u32[]{:S(2)}, u32[]{:S(2)}) collective-permute-start(f32[64,512]{1,0:T(8,128)S(1)} %pad_maximum_fusion.33), channel_id=1, source_target_pairs={{0,8},{1,9},{2,10},{3,11},{4,12},{5,13},{6,14},{7,15},{8,0},{9,1},... | collective-permute-start | bytes 393224 | tf_op jit(solution)/shard_map/ppermute | solution.py:382
  409.1 10.9 %collective-permute-start.21 = (f32[32,1024]{1,0:T(8,128)S(1)}, f32[32,1024]{1,0:T(8,128)S(1)}, u32[]{:S(2)}, u32[]{:S(2)}) collective-permute-start(f32[32,1024]{1,0:T(8,128)S(1)} %pad_maximum_fusion.30), channel_id=1, source_target_pairs={{0,2},{1,3},{2,0},{3,1},{4,6},{5,7},{6,4},{7,5},{8,10},{9,11},{10,... | collective-permute-start | bytes 393224 | tf_op jit(solution)/shard_map/ppermute | solution.py:382
  409.7 8.7 %collective-permute-start.40 = (f32[8,2176]{1,0:T(8,128)S(1)}, f32[8,2176]{1,0:T(8,128)S(1)}, u32[]{:S(2)}, u32[]{:S(2)}) collective-permute-start(f32[8,2176]{1,0:T(8,128)S(1)} %dynamic-slice_add_fusion.24), channel_id=1, source_target_pairs={{0,2},{1,3},{2,0},{3,1},{4,6},{5,7},{6,4},{7,5},{8,10},{9,11},{10,... | collective-permute-start | bytes 208904 | tf_op jit(solution)/shard_map/ppermute | solution.py:382
  413.6 18.3 %collective-permute-start.62 = (f32[64,1024]{1,0:T(8,128)S(1)}, f32[64,1024]{1,0:T(8,128)S(1)}, u32[]{:S(2)}, u32[]{:S(2)}) collective-permute-start(f32[64,1024]{1,0:T(8,128)S(1)} %pad_maximum_fusion.26), channel_id=1, source_target_pairs={{0,8},{1,9},{2,10},{3,11},{4,12},{5,13},{6,14},{7,15},{8,0},{9,1},... | collective-permute-start | bytes 786440 | tf_op jit(solution)/shard_map/ppermute | solution.py:382
  415.7 20.0 %collective-permute-start.72 = (f32[128,512]{1,0:T(8,128)S(1)}, f32[128,512]{1,0:T(8,128)S(1)}, u32[]{:S(2)}, u32[]{:S(2)}) collective-permute-start(f32[128,512]{1,0:T(8,128)S(1)} %pad_maximum_fusion.27), channel_id=1, source_target_pairs={{0,4},{1,5},{2,6},{3,7},{4,0},{5,1},{6,2},{7,3},{8,12},{9,13},{10,... | collective-permute-start | bytes 786440 | tf_op jit(solution)/shard_map/ppermute | solution.py:382
  418.4 17.5 %collective-permute-start.52 = (f32[128,512]{1,0:T(8,128)S(1)}, f32[128,512]{1,0:T(8,128)S(1)}, u32[]{:S(2)}, u32[]{:S(2)}) collective-permute-start(f32[128,512]{1,0:T(8,128)S(1)} %pad_maximum_fusion.25), channel_id=1, source_target_pairs={{0,4},{1,5},{2,6},{3,7},{4,0},{5,1},{6,2},{7,3},{8,12},{9,13},{10,... | collective-permute-start | bytes 786440 | tf_op jit(solution)/shard_map/ppermute | solution.py:382
  418.6 7.2 %collective-permute-start.41 = (f32[16,2176]{1,0:T(8,128)S(1)}, f32[16,2176]{1,0:T(8,128)S(1)}, u32[]{:S(2)}, u32[]{:S(2)}) collective-permute-start(f32[16,2176]{1,0:T(8,128)S(1)} %pad_maximum_fusion.29), channel_id=1, source_target_pairs={{0,16},{1,17},{2,18},{3,19},{4,20},{5,21},{6,22},{7,23},{8,24},{9,... | collective-permute-start | bytes 417800 | tf_op jit(solution)/shard_map/ppermute | solution.py:382
  420.0 9.2 %collective-permute-start.31 = (f32[16,2176]{1,0:T(8,128)S(1)}, f32[16,2176]{1,0:T(8,128)S(1)}, u32[]{:S(2)}, u32[]{:S(2)}) collective-permute-start(f32[16,2176]{1,0:T(8,128)S(1)} %pad_maximum_fusion.28), channel_id=1, source_target_pairs={{0,8},{1,9},{2,10},{3,11},{4,12},{5,13},{6,14},{7,15},{8,0},{9,1},... | collective-permute-start | bytes 417800 | tf_op jit(solution)/shard_map/ppermute | solution.py:382
  425.7 12.1 %collective-permute-start.22 = (f32[64,1024]{1,0:T(8,128)S(1)}, f32[64,1024]{1,0:T(8,128)S(1)}, u32[]{:S(2)}, u32[]{:S(2)}) collective-permute-start(f32[64,1024]{1,0:T(8,128)S(1)} %pad_maximum_fusion.24), channel_id=1, source_target_pairs={{0,16},{1,17},{2,18},{3,19},{4,20},{5,21},{6,22},{7,23},{8,24},{9,... | collective-permute-start | bytes 786440 | tf_op jit(solution)/shard_map/ppermute | solution.py:382
  429.2 12.7 %collective-permute-start.42 = (f32[32,2176]{1,0:T(8,128)S(1)}, f32[32,2176]{1,0:T(8,128)S(1)}, u32[]{:S(2)}, u32[]{:S(2)}) collective-permute-start(f32[32,2176]{1,0:T(8,128)S(1)} %pad_maximum_fusion.23), channel_id=1, source_target_pairs={{0,8},{1,9},{2,10},{3,11},{4,12},{5,13},{6,14},{7,15},{8,0},{9,1},... | collective-permute-start | bytes 835592 | tf_op jit(solution)/shard_map/ppermute | solution.py:382
  431.9 10.2 %collective-permute-start.32 = (f32[32,2176]{1,0:T(8,128)S(1)}, f32[32,2176]{1,0:T(8,128)S(1)}, u32[]{:S(2)}, u32[]{:S(2)}) collective-permute-start(f32[32,2176]{1,0:T(8,128)S(1)} %pad_maximum_fusion.22), channel_id=1, source_target_pairs={{0,4},{1,5},{2,6},{3,7},{4,0},{5,1},{6,2},{7,3},{8,12},{9,13},{10,... | collective-permute-start | bytes 835592 | tf_op jit(solution)/shard_map/ppermute | solution.py:382
  435.7 16.6 %collective-permute-start.63 = (f32[128,1024]{1,0:T(8,128)S(1)}, f32[128,1024]{1,0:T(8,128)S(1)}, u32[]{:S(2)}, u32[]{:S(2)}) collective-permute-start(f32[128,1024]{1,0:T(8,128)S(1)} %pad_maximum_fusion.20), channel_id=1, source_target_pairs={{0,4},{1,5},{2,6},{3,7},{4,0},{5,1},{6,2},{7,3},{8,12},{9,13},{10,... | collective-permute-start | bytes 1572872 | tf_op jit(solution)/shard_map/ppermute | solution.py:382
  435.9 16.6 %collective-permute-start.73 = (f32[256,512]{1,0:T(8,128)S(1)}, f32[256,512]{1,0:T(8,128)S(1)}, u32[]{:S(2)}, u32[]{:S(2)}) collective-permute-start(f32[256,512]{1,0:T(8,128)S(1)} %pad_maximum_fusion.21), channel_id=1, source_target_pairs={{0,2},{1,3},{2,0},{3,1},{4,6},{5,7},{6,4},{7,5},{8,10},{9,11},{10,... | collective-permute-start | bytes 1572872 | tf_op jit(solution)/shard_map/ppermute | solution.py:382
  437.9 21.6 %collective-permute-start.53 = (f32[256,512]{1,0:T(8,128)S(1)}, f32[256,512]{1,0:T(8,128)S(1)}, u32[]{:S(2)}, u32[]{:S(2)}) collective-permute-start(f32[256,512]{1,0:T(8,128)S(1)} %pad_maximum_fusion.19), channel_id=1, source_target_pairs={{0,2},{1,3},{2,0},{3,1},{4,6},{5,7},{6,4},{7,5},{8,10},{9,11},{10,... | collective-permute-start | bytes 1572872 | tf_op jit(solution)/shard_map/ppermute | solution.py:382
  441.9 17.8 %collective-permute-start.23 = (f32[128,1024]{1,0:T(8,128)S(1)}, f32[128,1024]{1,0:T(8,128)S(1)}, u32[]{:S(2)}, u32[]{:S(2)}) collective-permute-start(f32[128,1024]{1,0:T(8,128)S(1)} %pad_maximum_fusion.18), channel_id=1, source_target_pairs={{0,8},{1,9},{2,10},{3,11},{4,12},{5,13},{6,14},{7,15},{8,0},{9,1},... | collective-permute-start | bytes 1572872 | tf_op jit(solution)/shard_map/ppermute | solution.py:382
  442.1 18.4 %collective-permute-start.43 = (f32[64,2176]{1,0:T(8,128)S(1)}, f32[64,2176]{1,0:T(8,128)S(1)}, u32[]{:S(2)}, u32[]{:S(2)}) collective-permute-start(f32[64,2176]{1,0:T(8,128)S(1)} %pad_maximum_fusion.17), channel_id=1, source_target_pairs={{0,4},{1,5},{2,6},{3,7},{4,0},{5,1},{6,2},{7,3},{8,12},{9,13},{10,... | collective-permute-start | bytes 1671176 | tf_op jit(solution)/shard_map/ppermute | solution.py:382
  452.4 13.0 %collective-permute-start.33 = (f32[64,2176]{1,0:T(8,128)S(1)}, f32[64,2176]{1,0:T(8,128)S(1)}, u32[]{:S(2)}, u32[]{:S(2)}) collective-permute-start(f32[64,2176]{1,0:T(8,128)S(1)} %pad_maximum_fusion.16), channel_id=1, source_target_pairs={{0,2},{1,3},{2,0},{3,1},{4,6},{5,7},{6,4},{7,5},{8,10},{9,11},{10,... | collective-permute-start | bytes 1671176 | tf_op jit(solution)/shard_map/ppermute | solution.py:382
  452.6 13.0 %collective-permute-start.64 = (f32[256,1024]{1,0:T(8,128)S(1)}, f32[256,1024]{1,0:T(8,128)S(1)}, u32[]{:S(2)}, u32[]{:S(2)}) collective-permute-start(f32[256,1024]{1,0:T(8,128)S(1)} %pad_maximum_fusion.12), channel_id=1, source_target_pairs={{0,1},{1,0},{2,3},{3,2},{4,5},{5,4},{6,7},{7,6},{8,9},{9,8},{10,11... | collective-permute-start | bytes 3145736 | tf_op jit(solution)/shard_map/ppermute | solution.py:382
  459.4 7.0 %collective-permute-start.74 = (f32[512,512]{1,0:T(8,128)S(1)}, f32[512,512]{1,0:T(8,128)S(1)}, u32[]{:S(2)}, u32[]{:S(2)}) collective-permute-start(f32[512,512]{1,0:T(8,128)S(1)} %pad_maximum_fusion.13), channel_id=1, source_target_pairs={{0,1},{1,0},{2,3},{3,2},{4,5},{5,4},{6,7},{7,6},{8,9},{9,8},{10,11... | collective-permute-start | bytes 3145736 | tf_op jit(solution)/shard_map/ppermute | solution.py:382
  459.7 10.0 %collective-permute-start.54 = (f32[512,512]{1,0:T(8,128)S(1)}, f32[512,512]{1,0:T(8,128)S(1)}, u32[]{:S(2)}, u32[]{:S(2)}) collective-permute-start(f32[512,512]{1,0:T(8,128)S(1)} %pad_maximum_fusion.11), channel_id=1, source_target_pairs={{0,1},{1,0},{2,3},{3,2},{4,5},{5,4},{6,7},{7,6},{8,9},{9,8},{10,11... | collective-permute-start | bytes 3145736 | tf_op jit(solution)/shard_map/ppermute | solution.py:382
  460.4 9.5 %collective-permute-start.24 = (f32[256,1024]{1,0:T(8,128)S(1)}, f32[256,1024]{1,0:T(8,128)S(1)}, u32[]{:S(2)}, u32[]{:S(2)}) collective-permute-start(f32[256,1024]{1,0:T(8,128)S(1)} %pad_maximum_fusion.10), channel_id=1, source_target_pairs={{0,1},{1,0},{2,3},{3,2},{4,5},{5,4},{6,7},{7,6},{8,9},{9,8},{10,11... | collective-permute-start | bytes 3145736 | tf_op jit(solution)/shard_map/ppermute | solution.py:382
  465.4 7.8 %collective-permute-start.44 = (f32[128,2176]{1,0:T(8,128)S(1)}, f32[128,2176]{1,0:T(8,128)S(1)}, u32[]{:S(2)}, u32[]{:S(2)}) collective-permute-start(f32[128,2176]{1,0:T(8,128)S(1)} %pad_maximum_fusion.9), channel_id=1, source_target_pairs={{0,1},{1,0},{2,3},{3,2},{4,5},{5,4},{6,7},{7,6},{8,9},{9,8},{10,11... | collective-permute-start | bytes 3342344 | tf_op jit(solution)/shard_map/ppermute | solution.py:382
  465.6 7.8 %collective-permute-start.34 = (f32[128,2176]{1,0:T(8,128)S(1)}, f32[128,2176]{1,0:T(8,128)S(1)}, u32[]{:S(2)}, u32[]{:S(2)}) collective-permute-start(f32[128,2176]{1,0:T(8,128)S(1)} %pad_maximum_fusion.8), channel_id=1, source_target_pairs={{0,1},{1,0},{2,3},{3,2},{4,5},{5,4},{6,7},{7,6},{8,9},{9,8},{10,11... | collective-permute-start | bytes 3342344 | tf_op jit(solution)/shard_map/ppermute | solution.py:382
  (88 other events, 1233.0 us)

commit v2 on v1

v2 whole, which is shorter than its diff:
```python
import functools

import jax
import jax.numpy as jnp
from jax import lax
from jax.experimental import pallas as pl
from jax.experimental.pallas import tpu as pltpu
from jax.sharding import PartitionSpec as P

GROUP = 128
STEPS = 32
LAG = 8
LANES = 128

epsilon = 1e-05
very_low = -1e30
scan_params = pltpu.CompilerParams(vmem_limit_bytes=48 * 2**20)
dense_params = pltpu.CompilerParams(vmem_limit_bytes=56 * 2**20)


def work_cost(flops, seconds):
    return pl.CostEstimate(flops=int(flops), bytes_accessed=int(seconds * 3.0e12), transcendentals=0)


def sigmoid(value):
    return 0.5 * jnp.tanh(0.5 * value) + 0.5


def unit_norm(values):
    centered = values - jnp.mean(values, axis=-1, keepdims=True)
    spread = jnp.mean(centered * centered, axis=-1, keepdims=True)
    scale = lax.rsqrt(spread + epsilon)
    return centered * scale, scale


def norm_backward(grad, unit_values, scale):
    along = jnp.mean(grad * unit_values, axis=-1, keepdims=True)
    return scale * (grad - jnp.mean(grad, axis=-1, keepdims=True) - unit_values * along)


def whole_spec(shape):
    return pl.BlockSpec(shape, lambda step: (0,) * len(shape))


def lane_slices(width):
    return [slice(low, low + LANES) for low in range(0, width, LANES)]


def spread_rows(ref, index, lanes, rows):
    return jnp.broadcast_to(ref[index : index + 1, lanes], (rows, LANES))


def add_all(parts):
    while len(parts) > 1:
        parts = [
            parts[at] + parts[at + 1] if at + 1 < len(parts) else parts[at]
            for at in range(0, len(parts), 2)
        ]
    return parts[0]


def enter_body(count_ref, tokens_ref, gain_ref, retain_ref, low_ref, turned_ref, end_ref, state):
    step = pl.program_id(0)
    rows, steps, width = tokens_ref.shape
    states = retain_ref.shape[0]

    @pl.when(step == 0)
    def _():
        state[...] = jnp.zeros_like(state)

    values = tokens_ref[...].astype(jnp.float32)
    centered = values - jnp.mean(values, axis=-1, keepdims=True)
    spread = jnp.mean(centered * centered, axis=-1, keepdims=True)
    normed = centered * lax.rsqrt(spread + epsilon) * gain_ref[...]
    low_ref[...] = normed.astype(jnp.bfloat16)
    places = step * steps + lax.broadcasted_iota(jnp.int32, (steps, 1), 0)
    kept = jnp.stack([jnp.where(places < count_ref[row], normed[row], 0.0) for row in range(rows)])
    for lanes in lane_slices(width):
        for unit in range(steps // LAG):
            part = slice(unit * LAG, (unit + 1) * LAG)
            turned_ref[part, :, lanes] = jnp.swapaxes(kept[:, part, lanes], 0, 1)
    for lanes in lane_slices(width):
        retain = [spread_rows(retain_ref, j, lanes, rows) for j in range(states)]

        def unit_step(unit, hidden):
            for within in range(LAG):
                entry = turned_ref[unit * LAG + within, :, lanes]
                hidden = [retain[j] * hidden[j] + entry for j in range(states)]
            return hidden

        hidden = lax.fori_loop(
            0, steps // LAG, unit_step, [state[j, :, lanes] for j in range(states)]
        )
        for j in range(states):
            state[j, :, lanes] = hidden[j]

    @pl.when(step == pl.num_programs(0) - 1)
    def _():
        end_ref[...] = state[...]


def enter_call(counts, tokens, gain, retain):
    rows, length, width = tokens.shape
    states = retain.shape[0]
    natural = pl.BlockSpec((rows, STEPS, width), lambda step: (0, step, 0))
    return pl.pallas_call(
        enter_body,
        grid=(length // STEPS,),
        in_specs=[
            pl.BlockSpec(memory_space=pltpu.SMEM),
            natural,
            whole_spec((1, width)),
            whole_spec((states, width)),
        ],
        out_specs=(
            natural,
            pl.BlockSpec((STEPS, rows, width), lambda step: (step, 0, 0)),
            whole_spec((states, rows, width)),
        ),
        out_shape=(
            jax.ShapeDtypeStruct(tokens.shape, jnp.bfloat16),
            jax.ShapeDtypeStruct((length, rows, width), jnp.float32),
            jax.ShapeDtypeStruct((states, rows, width), jnp.float32),
        ),
        scratch_shapes=[pltpu.VMEM((states, rows, width), jnp.float32)],
        compiler_params=scan_params,
        cost_estimate=work_cost(0.0, 9e-6),
        name="enter",
    )(counts, tokens, gain, retain)


def average_body(turned_ref, retain_ref, mix_ref, start_ref, out_ref, end_ref, state):
    step = pl.program_id(0)
    steps, rows, width = turned_ref.shape
    states = retain_ref.shape[0]

    @pl.when(step == 0)
    def _():
        state[...] = start_ref[...]

    for lanes in lane_slices(width):
        retain = [spread_rows(retain_ref, j, lanes, rows) for j in range(states)]
        mix = [spread_rows(mix_ref, j, lanes, rows) for j in range(states)]

        def unit_step(unit, hidden):
            sums = []
            for within in range(LAG):
                entry = turned_ref[unit * LAG + within, :, lanes]
                hidden = [retain[j] * hidden[j] + entry for j in range(states)]
                sums.append(add_all([mix[j] * hidden[j] for j in range(states)]))
            out_ref[:, pl.ds(unit * LAG, LAG), lanes] = jnp.swapaxes(jnp.stack(sums), 0, 1)
            return hidden

        hidden = lax.fori_loop(
            0, steps // LAG, unit_step, [state[j, :, lanes] for j in range(states)]
        )
        for j in range(states):
            state[j, :, lanes] = hidden[j]

    @pl.when(step == pl.num_programs(0) - 1)
    def _():
        end_ref[...] = state[...]


def average_call(turned, retain, mix, start):
    length, rows, width = turned.shape
    states = retain.shape[0]
    held = (states, rows, width)
    return pl.pallas_call(
        average_body,
        grid=(length // STEPS,),
        in_specs=[
            pl.BlockSpec((STEPS, rows, width), lambda step: (step, 0, 0)),
            whole_spec((states, width)),
            whole_spec((states, width)),
            whole_spec(held),
        ],
        out_specs=(
            pl.BlockSpec((rows, STEPS, width), lambda step: (0, step, 0)),
            whole_spec(held),
        ),
        out_shape=(
            jax.ShapeDtypeStruct((rows, length, width), jnp.float32),
            jax.ShapeDtypeStruct(held, jnp.float32),
        ),
        scratch_shapes=[pltpu.VMEM(held, jnp.float32)],
        compiler_params=scan_params,
        cost_estimate=work_cost(0.0, 12e-6),
        name="average",
    )(turned, retain, mix, start)


def return_body(grad_ref, retain_ref, turned_ref, end_ref, state):
    step = pl.program_id(0)
    rows, steps, width = grad_ref.shape
    states = retain_ref.shape[0]

    @pl.when(step == 0)
    def _():
        state[...] = jnp.zeros_like(state)

    for lanes in lane_slices(width):
        retain = [spread_rows(retain_ref, j, lanes, rows) for j in range(states)]

        def unit_step(unit, hidden):
            part = pl.ds((steps // LAG - 1 - unit) * LAG, LAG)
            turned = jnp.swapaxes(grad_ref[:, part, lanes], 0, 1)
            turned_ref[part, :, lanes] = turned
            for within in reversed(range(LAG)):
                hidden = [retain[j] * hidden[j] + turned[within] for j in range(states)]
            return hidden

        hidden = lax.fori_loop(
            0, steps // LAG, unit_step, [state[j, :, lanes] for j in range(states)]
        )
        for j in range(states):
            state[j, :, lanes] = hidden[j]

    @pl.when(step == pl.num_programs(0) - 1)
    def _():
        end_ref[...] = state[...]


def return_call(grad, retain):
    rows, length, width = grad.shape
    states = retain.shape[0]
    last = length // STEPS - 1
    return pl.pallas_call(
        return_body,
        grid=(length // STEPS,),
        in_specs=[
            pl.BlockSpec((rows, STEPS, width), lambda step: (0, last - step, 0)),
            whole_spec((states, width)),
        ],
        out_specs=(
            pl.BlockSpec((STEPS, rows, width), lambda step: (last - step, 0, 0)),
            whole_spec((states, rows, width)),
        ),
        out_shape=(
            jax.ShapeDtypeStruct((length, rows, width), jnp.float32),
            jax.ShapeDtypeStruct((states, rows, width), jnp.float32),
        ),
        scratch_shapes=[pltpu.VMEM((states, rows, width), jnp.float32)],
        compiler_params=scan_params,
        cost_estimate=work_cost(0.0, 8e-6),
        name="back_enter",
    )(grad, retain)


def sums_body(
    grad_ref,
    turned_ref,
    retain_ref,
    inverse_ref,
    unit_ref,
    held_ref,
    lag_in_ref,
    carry_ref,
    lag_ref,
):
    step = pl.program_id(0)
    steps, rows, width = grad_ref.shape
    states = retain_ref.shape[0]
    half = states // 2
    units = steps // LAG

    @pl.when(step == 0)
    def _():
        carry_ref[...] = held_ref[...]
        lag_ref[...] = lag_in_ref[...]

    for lanes in lane_slices(width):
        for first in range(0, states, half):
            chosen = range(first, first + half)
            retain = [spread_rows(retain_ref, j, lanes, rows) for j in chosen]
            inverse = [spread_rows(inverse_ref, j, lanes, rows) for j in chosen]

            def unit_step(unit, carried):
                after, hidden, cross = carried
                unit = units - 1 - unit
                later = after
                for within in reversed(range(LAG)):
                    place = unit * LAG + within
                    entry = turned_ref[place, :, lanes]
                    grad = grad_ref[place, :, lanes]
                    after = [retain[m] * after[m] + grad for m in range(half)]
                    hidden = [(hidden[m] - entry) * inverse[m] for m in range(half)]
                    cross = [cross[m] + after[m] * hidden[m] for m in range(half)]
                for m, j in enumerate(chosen):
                    unit_decay = spread_rows(unit_ref, j, lanes, rows)
                    carry_ref[3, j, :, lanes] += hidden[m] * (after[m] - unit_decay * later[m])
                return after, hidden, cross

            results = lax.fori_loop(
                0,
                units,
                unit_step,
                tuple([carry_ref[kind, j, :, lanes] for j in chosen] for kind in range(3)),
            )
            for kind in range(3):
                for m, j in enumerate(chosen):
                    carry_ref[kind, j, :, lanes] = results[kind][m]

        def lag_step(unit, lags):
            entries = [turned_ref[unit * LAG + at, :, lanes] for at in range(LAG)]
            grads = [grad_ref[unit * LAG + at, :, lanes] for at in range(LAG)]
            return [
                lags[lag] + add_all([grads[at] * entries[at - lag] for at in range(lag, LAG)])
                for lag in range(LAG)
            ]

        lags = lax.fori_loop(0, units, lag_step, [lag_ref[at, :, lanes] for at in range(LAG)])
        for at in range(LAG):
            lag_ref[at, :, lanes] = lags[at]


def sums_call(low_end, high_end, grad, turned, params, carried):
    rows, width = grad.shape[1:]
    states = params[0].shape[0]
    last = high_end // STEPS - 1
    turned_spec = pl.BlockSpec((STEPS, rows, width), lambda step: (last - step, 0, 0))
    carried_specs = [whole_spec(value.shape) for value in carried]
    return pl.pallas_call(
        sums_body,
        grid=((high_end - low_end) // STEPS,),
        in_specs=[turned_spec] * 2 + [whole_spec((states, width))] * 3 + carried_specs,
        out_specs=carried_specs,
        out_shape=[jax.ShapeDtypeStruct(value.shape, jnp.float32) for value in carried],
        compiler_params=scan_params,
        cost_estimate=work_cost(0.0, 8e-6),
        name="adjoint_sums",
    )(grad, turned, *params, *carried)


def leave_body(
    count_ref,
    tokens_ref,
    gain_ref,
    part_ref,
    residual_ref,
    grad_ref,
    retain_ref,
    mix_ref,
    held_ref,
    _,
    carry_ref,
    out_ref,
    path,
    *,
    places_before,
):
    step = pl.program_id(0)
    steps, rows, width = grad_ref.shape
    states = retain_ref.shape[0]
    units = steps // LAG

    @pl.when(step == 0)
    def _():
        carry_ref[...] = held_ref[...]

    for lanes in lane_slices(width):
        retain = [spread_rows(retain_ref, j, lanes, rows) for j in range(states)]
        mix = [spread_rows(mix_ref, j, lanes, rows) for j in range(states)]

        def unit_step(unit, after):
            unit = units - 1 - unit
            sums = []
            for within in reversed(range(LAG)):
                grad = grad_ref[unit * LAG + within, :, lanes]
                after = [retain[j] * after[j] + grad for j in range(states)]
                sums.append(add_all([mix[j] * after[j] for j in range(states)]))
            path[:, pl.ds(unit * LAG, LAG), lanes] = jnp.swapaxes(jnp.stack(sums[::-1]), 0, 1)
            return after

        after = lax.fori_loop(
            0, units, unit_step, [carry_ref[j, :, lanes] for j in range(states)]
        )
        for j in range(states):
            carry_ref[j, :, lanes] = after[j]

    first_place = places_before + (pl.num_programs(0) - 1 - step) * steps
    places = first_place + lax.broadcasted_iota(jnp.int32, (steps, 1), 0)
    gain = gain_ref[...]
    for row in range(rows):
        unit_values, scale = unit_norm(tokens_ref[row].astype(jnp.float32))
        grad = part_ref[row].astype(jnp.float32)
        grad = grad + jnp.where(places < count_ref[row], path[row], 0.0)
        out = norm_backward(grad * gain, unit_values, scale)
        out_ref[row] = (out + residual_ref[row].astype(jnp.float32)).astype(jnp.bfloat16)


def leave_call(
    low_end, high_end, counts, tokens, gain, part, grad, retain, mix, carried
):
    rows, length, width = tokens.shape
    held = carried[0].shape
    last = high_end // STEPS - 1
    natural = pl.BlockSpec((rows, STEPS, width), lambda step: (0, last - step, 0))
    return pl.pallas_call(
        functools.partial(leave_body, places_before=low_end),
        grid=((high_end - low_end) // STEPS,),
        in_specs=[
            pl.BlockSpec(memory_space=pltpu.SMEM),
            natural,
            whole_spec((1, width)),
            natural,
            natural,
            pl.BlockSpec((STEPS, rows, width), lambda step: (last - step, 0, 0)),
            whole_spec(retain.shape),
            whole_spec(mix.shape),
            whole_spec(held),
            pl.BlockSpec(memory_space=pl.ANY),
        ],
        out_specs=[whole_spec(held), natural],
        out_shape=[
            jax.ShapeDtypeStruct(held, jnp.float32),
            jax.ShapeDtypeStruct((rows, length, width), jnp.bfloat16),
        ],
        input_output_aliases={9: 1},
        scratch_shapes=[pltpu.VMEM((rows, STEPS, width), jnp.float32)],
        compiler_params=scan_params,
        cost_estimate=work_cost(0.0, 8e-6),
        name="leave",
    )(counts, tokens, gain, part, carried[1], grad, retain, mix, *carried)


class Exchange:
    def __init__(self, local, decay, axis, backward):
        self.axis, self.backward = axis, backward
        self.count = lax.axis_size(axis)
        place = lax.axis_index(axis)
        self.place = self.count - 1 - place if backward else place
        self.low = self.place % 2
        self.half = local.shape[-1] // 2
        self.local = local
        self.decay = self.part(decay, self.low)

    def part(self, value, which):
        return lax.dynamic_slice_in_dim(value, which * self.half, self.half, value.ndim - 1)

    def moved(self, value, pairs):
        last = self.count - 1
        if self.backward:
            pairs = [(last - source, last - target) for source, target in pairs]
        return lax.ppermute(value, self.axis, pairs)

    def swapped(self, value):
        return self.moved(value, [(at, at ^ 1) for at in range(self.count)])

    def later(self, value, hop):
        return self.moved(value, [(at, at + 2 * hop) for at in range(self.count - 2 * hop)])

    def share(self):
        own = self.part(self.local, self.low)
        other = self.swapped(self.part(self.local, 1 - self.low))
        self.first = jnp.where(self.low == 0, own, other)
        self.pair = self.decay * self.first + jnp.where(self.low == 0, other, own)

    def cross(self):
        pairs = self.count // 2
        decay = self.decay * self.decay
        if pairs <= 4:
            arrived = [self.later(self.pair, hop) for hop in range(1, pairs)]
            total = arrived[-1]
            for value in arrived[-2::-1]:
                total = decay * total + value
        else:
            total, hop = self.later(self.pair, 1), 1
            while hop < pairs - 1:
                total = total + decay * self.later(total, hop)
                decay = decay * decay
                hop *= 2
        self.start = total

    def give(self):
        second = self.decay * self.start + self.first
        kept = jnp.where(self.low == 0, self.start, second)
        got = self.swapped(jnp.where(self.low == 0, second, self.start))
        return jnp.concatenate(
            [jnp.where(self.low == 0, kept, got), jnp.where(self.low == 0, got, kept)], axis=-1
        )


mesh_axes = ("seq", "row")


def device_total():
    return lax.axis_size("seq") * lax.axis_size("row")


def device_place():
    return lax.axis_index("seq") * lax.axis_size("row") + lax.axis_index("row")


def swapped(value, bit):
    return lax.ppermute(value, mesh_axes, [(at, at ^ bit) for at in range(device_total())])


def half_summed(value, bit):
    half = value.shape[0] // 2
    mine = (device_place() // bit) % 2
    sent = lax.dynamic_slice_in_dim(value, (1 - mine) * half, half, 0)
    kept = lax.dynamic_slice_in_dim(value, mine * half, half, 0)
    return kept + swapped(sent, bit)


def both_halves(value, bit):
    mine = (device_place() // bit) % 2 == 1
    other = swapped(value, bit)
    return jnp.concatenate([jnp.where(mine, other, value), jnp.where(mine, value, other)], axis=0)


def link_orders():
    total = device_total()
    bits = [1 << at for at in range(total.bit_length() - 1)]
    if (lax.axis_size("seq"), lax.axis_size("row")) == (8, 4):
        core, x, y, z_low, z_high = bits
        return (
            (core, x, y, z_low, z_high),
            (core, y, z_low, z_high, x),
            (core, z_low, z_high, x, y),
        )
    third = len(bits) // 3
    return tuple(bits[turn * third :] + bits[: turn * third] for turn in range(3))


def summed_everywhere(values):
    orders = link_orders()
    for at in range(len(orders[0])):
        values = [half_summed(v, orders[n % 3][at]) for n, v in enumerate(values)]
    for at in reversed(range(len(orders[0]))):
        values = [both_halves(v, orders[n % 3][at]) for n, v in enumerate(values)]
    return values


def paired_sum(value, group):
    partners = [group[0]] if len(group) == 1 else [group[0], group[1], group[0] + group[1]]
    arrived = [swapped(value, partner) for partner in partners]
    if len(arrived) == 1:
        return value + arrived[0]
    return (value + arrived[0]) + (arrived[1] + arrived[2])


def small_sum(value):
    bits = [1 << at for at in range(device_total().bit_length() - 1)]
    for at in range(0, len(bits), 2):
        value = paired_sum(value, bits[at : at + 2])
    return value


def power_of(value, exponent):
    result = None
    while exponent:
        if exponent & 1:
            result = value if result is None else result * value
        value = value * value
        exponent >>= 1
    return result


def dot(first_op, second_op):
    return jnp.dot(first_op, second_op, preferred_element_type=jnp.float32)


def dot_back(first_op, second_op):
    return lax.dot_general(
        first_op, second_op, (((1,), (1,)), ((), ())), preferred_element_type=jnp.float32
    )


def dot_outer(first_op, second_op):
    return lax.dot_general(
        first_op, second_op, (((0,), (0,)), ((), ())), preferred_element_type=jnp.float32
    )


def low(value):
    return value.astype(jnp.bfloat16)


def chunks(low_end, high_end, size):
    return [slice(at, min(at + size, high_end)) for at in range(low_end, high_end, size)]


def forward_body(
    count_ref,
    tokens_ref,
    cotangent_ref,
    average_ref,
    normed_ref,
    omega_ref,
    value_weight_ref,
    base_weight_ref,
    gains_ref,
    biases_ref,
    output_weight_ref,
    ffn_gain_ref,
    ffn_in_ref,
    ffn_out_ref,
    out_ref,
    mixed_ref,
    mixed_slope_ref,
    value_ref,
    value_slope_ref,
    probs_ref,
    query_ref,
    key_ref,
    shared_ref,
    shared_slope_ref,
    product_ref,
    ffn_low_ref,
    act_ref,
    grad_inner_ref,
    grad_proj_ref,
    grad_attended_ref,
    grad_main_ref,
    residual_ref,
    ffn_gain_grad_ref,
    reset_ref,
    reset_slope_ref,
):
    row = pl.program_id(0)
    length, width = tokens_ref.shape
    zdim = query_ref.shape[1]
    vdim = value_ref.shape[1]
    inner = act_ref.shape[1]

    @pl.when(row == 0)
    def _():
        ffn_gain_grad_ref[...] = jnp.zeros_like(ffn_gain_grad_ref)

    normed = normed_ref[...]
    sums = average_ref[...] + omega_ref[...] * normed.astype(jnp.float32)
    gate = sigmoid(sums)
    mixed = sums * gate
    mixed_ref[...] = low(mixed)
    mixed_slope_ref[...] = low(gate + mixed * (1.0 - gate))
    mixed_low = mixed_ref[...]

    shared = dot(mixed_low, base_weight_ref[:, :zdim])
    gate = sigmoid(shared)
    shared_act = shared * gate
    shared_ref[...] = shared_act
    shared_slope_ref[...] = gate + shared_act * (1.0 - gate)
    query_ref[...] = low(shared_act * gains_ref[0:1] + biases_ref[0:1])
    key_ref[...] = low(shared_act * gains_ref[1:2] + biases_ref[1:2])

    for part in chunks(0, vdim, 256):
        value_pre = dot(normed, value_weight_ref[:, part])
        gate = sigmoid(value_pre)
        value = value_pre * gate
        value_ref[:, part] = low(value)
        value_slope_ref[:, part] = low(gate + value * (1.0 - gate))

    to_place = lax.broadcasted_iota(jnp.int32, (GROUP, GROUP), 0)
    from_place = lax.broadcasted_iota(jnp.int32, (GROUP, GROUP), 1)
    for block in chunks(0, length, GROUP):
        allowed = (from_place <= to_place) & (
            (from_place < count_ref[row] - block.start) | (from_place == to_place)
        )
        scores = dot_back(query_ref[block], key_ref[block]) * zdim**-0.5
        scores = jnp.where(allowed, scores, very_low)
        weights = jnp.exp(scores - jnp.max(scores, axis=-1, keepdims=True))
        weights = jnp.where(allowed, weights, 0.0)
        probs_ref[block] = weights / jnp.sum(weights, axis=-1, keepdims=True)

    for part in chunks(0, vdim, 256):
        base_part = slice(zdim + part.start, zdim + part.stop)
        reset = dot(mixed_low, base_weight_ref[:, base_part])
        gate = sigmoid(reset)
        reset_act = reset * gate
        reset_slope = gate + reset_act * (1.0 - gate)
        reset_ref[:, part] = low(reset_act)
        for block in chunks(0, length, GROUP):
            attended = dot(low(probs_ref[block]), value_ref[block, part])
            product_ref[block, part] = low(attended * reset_act[block])
            reset_slope_ref[block, part] = low(attended * reset_slope[block])

    update_gate = sigmoid(dot(mixed_low, base_weight_ref[:, zdim + vdim : zdim + vdim + width]))
    candidate = dot(mixed_low, base_weight_ref[:, zdim + vdim + width :])
    candidate = candidate + dot(product_ref[...], output_weight_ref[...])
    candidate_gate = sigmoid(candidate)
    candidate_act = candidate * candidate_gate
    candidate_slope = candidate_gate + candidate_act * (1.0 - candidate_gate)
    tokens = tokens_ref[...].astype(jnp.float32)
    change = candidate_act - tokens
    after = tokens + update_gate * change
    unit_values, scale = unit_norm(after)
    ffn_low_ref[...] = low(unit_values * ffn_gain_ref[...])
    ffn_low = ffn_low_ref[...]
    cotangent = cotangent_ref[...]

    out = after
    grad_normed = jnp.zeros_like(after)
    for part in chunks(0, inner, 256):
        inner_pre = dot(ffn_low, ffn_in_ref[:, part])
        gate = sigmoid(inner_pre)
        act = inner_pre * gate
        slope = gate + act * (1.0 - gate)
        act_ref[:, part] = low(act)
        grad_act = dot_back(cotangent, ffn_out_ref[part])
        grad_inner_ref[:, part] = low(grad_act * slope)
    out = after + dot(act_ref[...], ffn_out_ref[...])
    out_ref[...] = low(out)
    grad_normed = dot_back(grad_inner_ref[...], ffn_in_ref[...])
    ffn_gain_grad_ref[...] += jnp.sum(grad_normed * unit_values, axis=0, keepdims=True)
    grad_after = cotangent.astype(jnp.float32) + norm_backward(
        grad_normed * ffn_gain_ref[...], unit_values, scale
    )
    grad_change = grad_after * update_gate
    grad_proj = low(grad_change * candidate_slope)
    grad_proj_ref[...] = grad_proj
    grad_main_ref[:, vdim : vdim + width] = low(grad_change * change * (1.0 - update_gate))
    grad_main_ref[:, vdim + width :] = grad_proj
    for part in chunks(0, vdim, 256):
        grad_product = dot_back(grad_proj, output_weight_ref[part])
        grad_attended_ref[:, part] = low(grad_product * reset_ref[:, part].astype(jnp.float32))
        grad_main_ref[:, part] = low(grad_product * reset_slope_ref[:, part].astype(jnp.float32))
    residual_ref[...] = low(grad_after - grad_change)


def row_spec(length, width):
    return pl.BlockSpec((None, length, width), lambda row: (row, 0, 0))


def once_spec(shape):
    return pl.BlockSpec(shape, lambda row: (0,) * len(shape), pipeline_mode=pl.Buffered(1))


def forward_call(
    counts,
    tokens,
    cotangent,
    average,
    normed,
    omega,
    value_weight,
    base_weight,
    gains,
    biases,
    output_weight,
    ffn_gain,
    ffn_in,
    ffn_out,
):
    rows, length, width = tokens.shape
    zdim, vdim, inner = gains.shape[1], value_weight.shape[1], ffn_in.shape[1]
    half, full = jnp.bfloat16, jnp.float32
    outs = [
        (width, half),
        (width, half),
        (width, half),
        (vdim, half),
        (vdim, half),
        (GROUP, full),
        (zdim, half),
        (zdim, half),
        (zdim, full),
        (zdim, full),
        (vdim, half),
        (width, half),
        (inner, half),
        (inner, half),
        (width, half),
        (vdim, half),
        (vdim + 2 * width, half),
        (width, half),
    ]
    tied = [
        omega,
        value_weight,
        base_weight,
        gains,
        biases,
        output_weight,
        ffn_gain,
        ffn_in,
        ffn_out,
    ]
    return pl.pallas_call(
        forward_body,
        grid=(rows,),
        in_specs=[pl.BlockSpec(memory_space=pltpu.SMEM)]
        + [row_spec(length, width)] * 4
        + [once_spec(value.shape) for value in tied],
        out_specs=[row_spec(length, size) for size, _ in outs] + [whole_spec((1, width))],
        out_shape=[jax.ShapeDtypeStruct((rows, length, size), kind) for size, kind in outs]
        + [jax.ShapeDtypeStruct((1, width), full)],
        scratch_shapes=[pltpu.VMEM((length, vdim), half)] * 2,
        compiler_params=dense_params,
        cost_estimate=work_cost(18e9, 40e-6),
        name="dense_forward",
    )(counts, tokens, cotangent, average, normed, *tied)


def backward_body(
    grad_attended_ref,
    grad_main_ref,
    normed_ref,
    mixed_slope_ref,
    value_ref,
    value_slope_ref,
    probs_ref,
    query_ref,
    key_ref,
    shared_ref,
    shared_slope_ref,
    omega_ref,
    gains_ref,
    value_weight_ref,
    base_weight_ref,
    grad_shared_ref,
    grad_vpre_ref,
    grad_average_ref,
    part_ref,
    grad_gains_ref,
    grad_omega_ref,
    grad_gain_ref,
):
    row = pl.program_id(0)
    length = grad_attended_ref.shape[0]
    zdim = query_ref.shape[1]
    vdim = value_ref.shape[1]

    @pl.when(row == 0)
    def _():
        grad_gains_ref[...] = jnp.zeros_like(grad_gains_ref)
        grad_omega_ref[...] = jnp.zeros_like(grad_omega_ref)
        grad_gain_ref[...] = jnp.zeros_like(grad_gain_ref)

    grad_gains = jnp.zeros(grad_gains_ref.shape, jnp.float32)
    for block in chunks(0, length, GROUP):
        probs = probs_ref[block]
        probs_low = low(probs)
        grad_probs = dot_back(grad_attended_ref[block], value_ref[block])
        for part in chunks(0, vdim, 512):
            grad_value = dot_outer(probs_low, grad_attended_ref[block, part])
            grad_vpre_ref[block, part] = low(
                grad_value * value_slope_ref[block, part].astype(jnp.float32)
            )
        total = jnp.sum(grad_probs * probs, axis=-1, keepdims=True)
        grad_raw = low(probs * (grad_probs - total) * zdim**-0.5)
        grad_query = dot(grad_raw, key_ref[block])
        grad_key = dot_outer(grad_raw, query_ref[block])
        shared = shared_ref[block]
        grad_gains = grad_gains + jnp.concatenate(
            [
                jnp.sum(value, axis=0, keepdims=True)
                for value in (grad_query * shared, grad_key * shared, grad_query, grad_key)
            ],
            axis=0,
        )
        grad_shared = grad_query * gains_ref[0:1] + grad_key * gains_ref[1:2]
        grad_shared_ref[block] = low(grad_shared * shared_slope_ref[block])
    grad_gains_ref[...] += grad_gains
    grad_average = dot_back(grad_main_ref[...], base_weight_ref[:, zdim:])
    grad_average = grad_average + dot_back(grad_shared_ref[...], base_weight_ref[:, :zdim])
    grad_average = grad_average * mixed_slope_ref[...].astype(jnp.float32)
    grad_average_ref[...] = grad_average
    part = dot_back(grad_vpre_ref[...], value_weight_ref[...]) + grad_average * omega_ref[...]
    part_ref[...] = part
    normed = normed_ref[...].astype(jnp.float32)
    grad_omega_ref[...] += jnp.sum(grad_average * normed, axis=0, keepdims=True)
    grad_gain_ref[...] += jnp.sum(part * normed, axis=0, keepdims=True)


def backward_call(inputs, tied_inputs):
    rows, length, vdim = inputs[0].shape
    omega, gains, _, _ = tied_inputs
    width, zdim = omega.shape[1], gains.shape[1]
    outs = [
        (zdim, jnp.bfloat16),
        (vdim, jnp.bfloat16),
        (width, jnp.float32),
        (width, jnp.float32),
    ]
    return pl.pallas_call(
        backward_body,
        grid=(rows,),
        in_specs=[row_spec(length, value.shape[2]) for value in inputs]
        + [once_spec(value.shape) for value in tied_inputs],
        out_specs=[row_spec(length, size) for size, _ in outs]
        + [whole_spec((4, zdim))]
        + [whole_spec((1, width))] * 2,
        out_shape=[jax.ShapeDtypeStruct((rows, length, size), kind) for size, kind in outs]
        + [
            jax.ShapeDtypeStruct((4, zdim), jnp.float32),
            jax.ShapeDtypeStruct((1, width), jnp.float32),
            jax.ShapeDtypeStruct((1, width), jnp.float32),
        ],
        compiler_params=dense_params,
        cost_estimate=work_cost(10e9, 25e-6),
        name="dense_backward",
    )(*inputs, *tied_inputs)


def joined_body(*refs, widths, split):
    refs = refs[1:] if split else refs
    outs_per_chain = 2 if split else 1
    outs = refs[len(refs) - outs_per_chain * len(widths) :]
    at = 0
    for chain, parts in enumerate(widths):
        for side in range(outs_per_chain):
            column = 0
            for width in parts:
                total = refs[at][...] + refs[at + 1][...]
                outs[chain * outs_per_chain + side][:, column : column + width] = total
                column += width
                at += 2


def joined(chains):
    split = chains[0][2] is not None
    sides = 2 if split else 1
    widths = [[value.shape[1] for value in kept] for kept, _, _ in chains]
    sizes = [kept[0].shape[0] // sides for kept, _, _ in chains]
    steps = 4
    while any(size % (8 * steps) for size in sizes):
        steps //= 2
    operands, in_specs, out_specs, out_shape = [], [], [], []
    for chain, (kept, arrived, _) in enumerate(chains):
        block = sizes[chain] // steps
        for side in range(sides):

            def place(step, *held, chain=chain, side=side):
                if not held:
                    return step, 0
                mine = held[0][chain]
                return (1 - mine if side else mine) * steps + step, 0

            for pair in zip(kept, arrived):
                for value in pair:
                    operands.append(value)
                    in_specs.append(pl.BlockSpec((block, value.shape[1]), place))
            total = sum(widths[chain])
            out_specs.append(pl.BlockSpec((block, total), lambda step, *held: (step, 0)))
            out_shape.append(jax.ShapeDtypeStruct((sizes[chain], total), jnp.float32))
    if split:
        mine = [(device_place() // bit) % 2 for _, _, bit in chains]
        operands.insert(0, jnp.stack(mine).astype(jnp.int32))
    outs = pl.pallas_call(
        functools.partial(joined_body, widths=widths, split=split),
        grid_spec=pltpu.PrefetchScalarGridSpec(
            num_scalar_prefetch=1 if split else 0,
            grid=(steps,),
            in_specs=in_specs,
            out_specs=out_specs,
        ),
        out_shape=out_shape,
        compiler_params=scan_params,
        cost_estimate=work_cost(0.0, 2e-6),
        name="joined",
    )(*operands)
    return [tuple(outs[at : at + sides]) for at in range(0, len(outs), sides)]


def placed_body(*refs, copies, sources):
    mine, refs = refs[0], refs[1:]
    half = pl.program_id(0)
    for own, arrived, which, taken, result, column in copies:
        there = slice(column, column + taken.stop - taken.start)

        @pl.when(half == mine[which])
        def _(own=own, taken=taken, result=result, there=there):
            refs[sources + result][:, there] = refs[own][:, taken]

        @pl.when(half != mine[which])
        def _(arrived=arrived, taken=taken, result=result, there=there):
            refs[sources + result][:, there] = refs[arrived][:, taken]


def placed(values, bits, copies, shapes):
    steps = 4
    while any(value.shape[0] % (8 * steps) for value in values):
        steps //= 2
    in_specs = []
    for at, value in enumerate(values):

        def place(half, step, mine, which=at // 2, other=at % 2):
            wanted = (half == mine[which]) != bool(other)
            return jnp.where(wanted, step, jnp.where(half == 0, 0, steps - 1)), 0

        in_specs.append(pl.BlockSpec((value.shape[0] // steps, value.shape[1]), place))
    mine = jnp.stack([(device_place() // bit) % 2 for bit in bits]).astype(jnp.int32)
    return pl.pallas_call(
        functools.partial(placed_body, copies=copies, sources=len(values)),
        grid_spec=pltpu.PrefetchScalarGridSpec(
            num_scalar_prefetch=1,
            grid=(2, steps),
            in_specs=in_specs,
            out_specs=[
                pl.BlockSpec(
                    (shape[0] // (2 * steps), shape[1]),
                    lambda half, step, mine: (half * steps + step, 0),
                )
                for shape in shapes
            ],
        ),
        out_shape=[jax.ShapeDtypeStruct(shape, jnp.float32) for shape in shapes],
        compiler_params=scan_params,
        cost_estimate=work_cost(0.0, 2e-6),
        name="placed",
    )(mine, *values)


def gathered_body(*refs, copies):
    where, refs = refs[0], refs[1:]
    results = refs[len(refs) - 1 - max(result for _, _, result, _ in copies) :]
    turn = pl.program_id(0)
    for chain, taken, result, column in copies:
        there = slice(column, column + taken.stop - taken.start)
        for piece in range(2):

            @pl.when(turn == where[2 * chain + piece])
            def _(source=2 * chain + piece, taken=taken, result=result, there=there):
                results[result][:, there] = refs[source][:, taken]


def gathered(chains, copies, shapes, before=None):
    values, where = [], []
    for one in chains:
        low = (device_place() // one.order[1]) % 2
        values += one.held if before is None else one.arrived
        where += [low, 1 - low]
    core = (device_place() // chains[0].order[0]) % 2
    where.append(core if before is None else 1 - core)
    steps = 2
    in_specs = []
    for at, value in enumerate(values):

        def place(turn, step, where, at=at):
            early = jnp.where(turn < where[at], 0, steps - 1)
            return jnp.where(turn == where[at], step, early), 0

        in_specs.append(pl.BlockSpec((value.shape[0] // steps, value.shape[1]), place))
    aliases = {}
    if before is not None:
        aliases = {1 + len(values) + at: at for at in range(len(shapes))}
        in_specs += [pl.BlockSpec(memory_space=pl.ANY)] * len(shapes)
    side = len(where) - 1
    return pl.pallas_call(
        functools.partial(gathered_body, copies=copies),
        grid_spec=pltpu.PrefetchScalarGridSpec(
            num_scalar_prefetch=1,
            grid=(2, steps),
            in_specs=in_specs,
            out_specs=[
                pl.BlockSpec(
                    (shape[0] // (4 * steps), shape[1]),
                    lambda turn, step, where: ((2 * where[side] + turn) * steps + step, 0),
                )
                for shape in shapes
            ],
        ),
        out_shape=[jax.ShapeDtypeStruct(shape, jnp.float32) for shape in shapes],
        input_output_aliases=aliases,
        compiler_params=scan_params,
        cost_estimate=work_cost(0.0, 4e-6),
        name="gathered",
    )(jnp.stack(where).astype(jnp.int32), *values, *(before or ()))


class Chain:
    def __init__(self, order, sent, kept):
        self.order, self.at = order, 0
        self.sent, self.kept, self.arrived = list(sent), list(kept), []

    def state(self):
        return self.sent, self.kept, self.arrived

    def set_state(self, state):
        self.sent, self.kept, self.arrived = state

    def send(self):
        total = len(self.order)
        bit = self.order[self.at if self.at < total else 2 * total - 1 - self.at]
        self.arrived = [swapped(value, bit) for value in self.sent]

    def give(self):
        self.held = self.sent + self.arrived
        self.arrived = [swapped(value, self.order[0]) for value in self.held]

    def pieces(self):
        return self.held + self.arrived


def join(*chains):
    total = len(chains[0].order)
    if chains[0].at < total:
        last = chains[0].at == total - 1
        results = joined(
            [
                (one.kept, one.arrived, None if last else one.order[one.at + 1])
                for one in chains
            ]
        )
        for one, result in zip(chains, results):
            if last:
                one.sent, one.kept = [result[0]], []
            else:
                one.sent, one.kept = [result[1]], [result[0]]
    else:
        values, copies, shapes = [], [], []
        for at, one in enumerate(chains):
            rows, columns = one.sent[0].shape
            values += [one.sent[0], one.arrived[0]]
            copies.append((2 * at, 2 * at + 1, at, slice(0, columns), at, 0))
            shapes.append((2 * rows, columns))
        bits = [one.order[2 * total - 1 - one.at] for one in chains]
        for one, result in zip(chains, placed(values, bits, copies, shapes)):
            one.sent = [result]
    for one in chains:
        one.arrived = []
        one.at += 1


def tied(value, *chains):
    value, states = lax.optimization_barrier((value, [one.state() for one in chains]))
    for one, state in zip(chains, states):
        one.set_state(state)
    return value


def weight_halves(first_op, second_op, bit):
    first_op = first_op.reshape(-1, first_op.shape[-1])
    second_op = second_op.reshape(-1, second_op.shape[-1])
    half = first_op.shape[1] // 2
    mine = (device_place() // bit) % 2
    return [
        dot_outer(lax.dynamic_slice_in_dim(first_op, which * half, half, 1), second_op)
        for which in (1 - mine, mine)
    ]


def weight_grad(first_op, second_op):
    return dot_outer(
        first_op.reshape(-1, first_op.shape[-1]), second_op.reshape(-1, second_op.shape[-1])
    )


def per_device(
    tokens,
    valid_count,
    norm_gain,
    value_weight,
    ema_forget,
    ema_beta,
    ema_eta,
    ema_omega,
    base_weight,
    qk_gain,
    qk_bias,
    output_weight,
    ffn_gain,
    ffn_in,
    ffn_out,
    cotangent,
):
    length, width = tokens.shape[1:]
    counts = valid_count - lax.axis_index("seq") * length
    norm_gain = norm_gain.astype(jnp.float32)[None]
    ffn_gain = ffn_gain.astype(jnp.float32)[None]
    omega = ema_omega[None]
    gains, biases = qk_gain.astype(jnp.float32), qk_bias.astype(jnp.float32)
    forget, beta, eta = ema_forget.T, ema_beta.T, ema_eta.T
    retain = 1.0 - forget
    gate = jnp.sqrt(forget * (2.0 - forget))
    inflow = beta * gate
    mix = eta * inflow
    span_decay = power_of(retain, length)[:, None, :]

    normed, turned, device_end = enter_call(counts, tokens, norm_gain, retain)
    ahead = Exchange(device_end, span_decay, "seq", False)
    ahead.share()
    ahead.cross()
    incoming = ahead.give()
    average, state_end = average_call(turned, retain, mix, incoming)
    (
        block_out,
        mixed,
        mixed_slope,
        value,
        value_slope,
        probs,
        query,
        key,
        shared,
        shared_slope,
        product,
        ffn_low,
        act,
        grad_inner,
        grad_proj,
        grad_attended,
        grad_main,
        residual,
        grad_ffn_gain,
    ) = forward_call(
        counts,
        tokens,
        cotangent,
        average,
        normed,
        omega,
        value_weight,
        base_weight,
        gains,
        biases,
        output_weight,
        ffn_gain,
        ffn_in,
        ffn_out,
    )
    back_inputs = [
        grad_attended,
        grad_main,
        normed,
        mixed_slope,
        value,
        value_slope,
        probs,
        query,
        key,
        shared,
        shared_slope,
    ]
    orders = link_orders()
    chained = device_total() == 32
    early, late, chains = [], None, []
    if chained:
        core = orders[0][0]
        sums = [
            weight_halves(act, cotangent, core),
            weight_halves(product, grad_proj, core),
            weight_halves(mixed, grad_main, core),
            weight_halves(ffn_low, grad_inner, core),
        ]
        outs = Chain(orders[0], [sums[0][0], sums[1][0]], [sums[0][1], sums[1][1]])
        main = Chain(orders[1], [sums[2][0]], [sums[2][1]])
        inner = Chain(orders[2], [sums[3][0]], [sums[3][1]])
        early = [outs, main, inner]
        for one in early:
            one.send()
        join(*early)
        back_inputs = tied(back_inputs, *early)
        for one in early:
            one.send()
    back_outputs = backward_call(back_inputs, [omega, gains, value_weight, base_weight])
    if chained:
        back_outputs = tied(back_outputs, *early)
        join(*early)
        back_outputs = tied(back_outputs, *early)
        for one in early:
            one.send()
    grad_shared, grad_vpre, grad_average, part, grad_query_key, grad_omega, grad_gain = (
        back_outputs
    )
    if chained:
        sums = [weight_halves(normed, grad_vpre, core), weight_halves(mixed, grad_shared, core)]
        late = Chain(orders[0], [sums[0][0], sums[1][0]], [sums[0][1], sums[1][1]])
        chains = [late, *early]
        grad_average = tied(grad_average, late)
        late.send()

    def halve(value, *moving):
        if chained:
            value = tied(value, *chains)
            if early[0] in moving:
                join(*early)
            join(late)
            value = tied(value, *chains)
            for one in moving:
                one.send()
        return value

    grad_turned, device_start = return_call(grad_average, retain)
    behind = Exchange(device_start, span_decay, "seq", True)
    behind.local = halve(behind.local, late, *early)
    behind.share()
    behind.pair = halve(behind.pair, late)
    behind.cross()
    behind.start = halve(behind.start, late, *early)
    later = behind.give()
    states = retain.shape[0]
    carried = [
        jnp.stack([later, state_end, jnp.zeros_like(later), jnp.zeros_like(later)]),
        jnp.zeros((LAG,) + later.shape[1:], jnp.float32),
    ]
    parts = length // STEPS
    inverse, unit_decay = 1.0 / retain, power_of(retain, LAG)
    ends = [at * STEPS for at in (parts, 5 * parts // 8, 2 * parts // 8, 0)]
    for high_end, low_end in zip(ends, ends[1:]):
        carried = halve(carried, late, *early)
        carried = sums_call(
            low_end, high_end, grad_turned, turned, [retain, inverse, unit_decay], carried
        )
    (_, _, cross, border), lags = carried
    left = [later, residual]
    if chained:
        left = halve([left, cross], late, *early)
        left, cross = left
    cross = jnp.sum(cross, axis=1)
    lags = jnp.sum(lags, axis=1)
    paired = retain * jnp.sum(border, axis=1)
    decay = jnp.ones_like(retain)
    for lag in range(LAG):
        paired = paired + decay * lags[lag]
        decay = decay * retain
    small = jnp.concatenate(
        [
            paired,
            cross,
            grad_gain,
            grad_omega,
            grad_ffn_gain,
            grad_query_key.reshape(-1, width),
        ],
        axis=0,
    )
    used = small.shape[0]
    small = jnp.pad(small, ((0, -used % 8), (0, 0)))
    ends = [at * STEPS for at in (parts, 5 * parts // 8, 3 * parts // 8, 0)]
    if chained:
        core, _, _, z_low, z_high = orders[0]
        first_bits = [core, z_high, z_low]
    for turn, (high_end, low_end) in enumerate(zip(ends, ends[1:])):
        if chained:
            left, small = lax.optimization_barrier((left, small))
            small = small + swapped(small, first_bits[turn])
        left = leave_call(
            low_end, high_end, counts, tokens, norm_gain, part, grad_turned, retain, mix, left
        )
    if chained:
        left, small = tied((left, small), *chains)
        for one in early:
            one.give()
        join(late)
        late.send()
        small = paired_sum(small, orders[0][1:3])
    else:
        small = small_sum(small)
    grad_tokens = left[1]
    paired, cross = small[:states], small[states : 2 * states]
    grad_gain, grad_omega, grad_ffn_gain = (small[2 * states + at] for at in range(3))
    grad_norm_gain = (grad_gain + jnp.sum(mix * paired, axis=0)) / norm_gain[0]
    grad_query_key = small[2 * states + 3 : used].reshape(grad_query_key.shape)
    grad_eta = (inflow * paired).T
    grad_beta = (eta * paired * gate).T
    grad_forget = (eta * paired * beta * (1.0 - forget) / gate - mix * cross).T
    vdim = value_weight.shape[1]
    if chained:
        outs, main, inner = early
        zdim = gains.shape[1]
        groups = [
            (
                [outs, inner],
                [
                    (0, slice(0, width), 0, 0),
                    (0, slice(width, 2 * width), 1, 0),
                    (1, slice(0, ffn_in.shape[1]), 2, 0),
                ],
                [ffn_out.shape, output_weight.shape, ffn_in.shape],
            ),
            (
                [main, late],
                [
                    (0, slice(0, grad_main.shape[-1]), 0, zdim),
                    (1, slice(0, vdim), 1, 0),
                    (1, slice(vdim, vdim + zdim), 0, 0),
                ],
                [base_weight.shape, value_weight.shape],
            ),
        ]
        first = gathered(*groups[0])
        late.give()
        second = gathered(*groups[1])
        grad_ffn_out, grad_output_weight, grad_ffn_in = gathered(*groups[0], first)
        grad_base_weight, grad_value_weight = gathered(*groups[1], second)
    else:
        grad_base = jnp.concatenate([grad_shared, grad_main], axis=-1)
        (
            grad_ffn_out,
            grad_output_weight,
            grad_base_weight,
            grad_ffn_in,
            grad_value_weight,
        ) = summed_everywhere(
            [
                weight_grad(act, cotangent),
                weight_grad(product, grad_proj),
                weight_grad(mixed, grad_base),
                weight_grad(ffn_low, grad_inner),
                weight_grad(normed, grad_vpre),
            ]
        )
    return (
        block_out,
        grad_tokens,
        grad_norm_gain,
        grad_value_weight,
        grad_forget,
        grad_beta,
        grad_eta,
        grad_omega,
        grad_base_weight,
        grad_query_key[:2],
        grad_query_key[2:],
        grad_output_weight,
        grad_ffn_gain,
        grad_ffn_in,
        grad_ffn_out,
    )


def solution(mesh):
    return jax.shard_map(
        per_device,
        mesh=mesh,
        in_specs=(
            P("row", "seq", None),
            P("row"),
            P(),
            P(),
            P(),
            P(),
            P(),
            P(),
            P(),
            P(),
            P(),
            P(),
            P(),
            P(),
            P(),
            P("row", "seq", None),
        ),
        out_specs=(
            P("row", "seq", None),
            P("row", "seq", None),
            P(),
            P(),
            P(),
            P(),
            P(),
            P(),
            P(),
            P(),
            P(),
            P(),
            P(),
            P(),
            P(),
        ),
        check_vma=False,
    )
```

time: 480 us -> 364 us (0.76)
  Pallas kernels: 57.4 us -> 171 us
  matrix products: 114 us -> 28.8 us
  other arithmetic: 78 us -> 7.52 us
  waiting for transfers between devices: 96.2 us -> 52.4 us
  starting transfers between devices: 103 us -> 78.4 us
    pallas_call x1 -> x28, Pallas kernels: 27.1 us -> 141 us  [the longest x1 39.7 us: forward_call(): pl.pallas_call(forward_body, grid=(rows,), in_specs=[pl.BlockSpec(memory_...]
    dot_general x21 -> x12, matrix products: 114 us -> 28.8 us  [dot_outer(): lax.dot_general(first_op, second_op, (((0,), (0,)), ((), ())), preferred_...]
    convert_element_type x9 -> x3, other arithmetic: 28.7 us -> 1.81 us  [the longest x2 1.13 us: per_device(): gains, biases = (qk_gain.astype(jnp.float32), qk_bias.astype(jnp.float32))]
    ppermute x8 -> x10, waiting for transfers between devices: 38.7 us -> 15.3 us  [moved(): return lax.ppermute(value, self.axis, pairs)]
    ppermute x67 -> x52, waiting for transfers between devices: 57.5 us -> 37.1 us  [swapped(): lax.ppermute(value, mesh_axes, [(at, at ^ bit) for at in range(device_tot...]
    ppermute x67 -> x52, starting transfers between devices: 77.1 us -> 58 us  [swapped(): lax.ppermute(value, mesh_axes, [(at, at ^ bit) for at in range(device_tot...]
    add x43 -> x7, other arithmetic: 15.5 us -> 0.88 us  [the longest x2 0.77 us: share(): self.pair = self.decay * self.first + jnp.where(self.low == 0, other, own)]
    unnamed x156 -> x91, local copies, waits for them, and re-layouts: 8.05 us -> 21 us
  transfers between devices with their start and end apart: 75 -> 62, of which waited for: 28 -> 16; matrix products, arithmetic and copies ran while one was open for 12% -> 8% of each run, Pallas kernels for 7% -> 24%
where the time goes in v2:
time: 364 us; the launch traced here: 363 us
  Pallas kernels  171 us (47%)
  starting transfers between devices  78.4 us (22%)
  waiting for transfers between devices  52.4 us (14%)
  matrix products  28.8 us (8%)
  local copies, waits for them, and re-layouts  23.3 us (6%)
  other arithmetic  7.52 us (2%)
    ppermute x52, starting transfers between devices, swapped(): lax.ppermute(value, mesh_axes, [(at, at ^ bit) for at in range(device_tot...  58 us
    pallas_call x1, Pallas kernels, forward_call(): pl.pallas_call(forward_body, grid=(rows,), in_specs=[pl.BlockSpec(memory_...  39.7 us
    ppermute x52, waiting for transfers between devices, swapped(): lax.ppermute(value, mesh_axes, [(at, at ^ bit) for at in range(device_tot...  37.1 us
    dot_general x12, matrix products, dot_outer(): lax.dot_general(first_op, second_op, (((0,), (0,)), ((), ())), preferred_...  28.8 us
    pallas_call x3, Pallas kernels, sums_call(): pl.pallas_call(sums_body, grid=((high_end - low_end) // STEPS,), in_specs...  24.4 us
    pallas_call x1, Pallas kernels, backward_call(): pl.pallas_call(backward_body, grid=(rows,), in_specs=[row_spec(length, va...  21.2 us
    unnamed x91, local copies, waits for them, and re-layouts  21 us
    ppermute x10, starting transfers between devices, moved(): return lax.ppermute(value, self.axis, pairs)  20.4 us
  transfers between devices with their start and end apart: 62, of which 16 were waited for; matrix products, arithmetic and copies ran while one was open for 8% of the time, Pallas kernels for 24%

profile of v2, /device:TPU:0, one launch (start us, length us, event | category | flops | bytes accessed | tf_op | source)
XLA Modules:
  0.0 362.7 jit_solution(6608492152557088552)
XLA Ops:
  2.9 1.6 copy-done.1
  4.5 9.5 %enter.1 = (bf16[8,256,512]{2,1,0:T(8,128)(2,1)S(1)}, f32[256,8,512]{2,1,0:T(8,128)}, f32[16,8,512]{2,1,0:T(8,128)S(1)}) custom-call(s32[8]{0:T(128)S(1)} %broadcast_subtract_fusion.count_ref, bf16[8,256,512]{2,1,0:T(8,128)(2,1)S(1)} %copy-done.1, f32[1,512]{1,0:T(1,128)S(1)} %bitcast.104, f32[16,512]{1,0:T(8,128)S(1)} %get-tuple-element.618.retain_ref), custom_call_target="tpu_custom_call" | custom-call | bytes 27000000 | tf_op jit(solution)/shard_map/enter/pallas_call | solution.py:106
  15.3 3.0 collective-permute-start
  19.0 2.9 collective-permute-done
  21.9 5.7 %collective-permute-start.1 = (f32[16,8,256]{2,1,0:T(8,128)S(1)}, f32[16,8,256]{2,1,0:T(8,128)S(1)}, u32[]{:S(2)}, u32[]{:S(2)}) collective-permute-start(f32[16,8,256]{2,1,0:T(8,128)S(1)} %select_add_fusion.1), channel_id=1, source_target_pairs={{0,24},{4,28},{1,25},{5,29},{2,26},{6,30},{3,27},{7,31}} | collective-permute-start | bytes 393224 | tf_op jit(solution)/shard_map/ppermute | solution.py:445
  28.9 2.5 collective-permute-start.3
  31.6 2.2 collective-permute-done.2
  35.2 1.6 collective-permute-start.4
  38.6 1.6 collective-permute-done.4
  40.3 12.0 %average.1 = (f32[8,256,512]{2,1,0:T(8,128)S(1)}, f32[16,8,512]{2,1,0:T(8,128)S(1)}) custom-call(f32[256,8,512]{2,1,0:T(8,128)} %get-tuple-element.303.turned_ref, f32[16,512]{1,0:T(8,128)S(1)} %get-tuple-element.618.retain_ref, f32[16,512]{1,0:T(8,128)S(1)} %get-tuple-element.617.mix_ref, f32[16,8,512]{2,1,0:T(8,128)S(1)} %pad_maximum_fusion.start_ref), custom_call_target="tpu_custom_call" | custom-call | bytes 36000000 | tf_op jit(solution)/shard_map/average/pallas_call | solution.py:169
  52.4 2.0 copy-done.11
  54.4 39.7 %dense_forward.1 = (bf16[8,256,512]{2,1,0:T(8,128)(2,1)}, bf16[8,256,512]{2,1,0:T(8,128)(2,1)}, bf16[8,256,512]{2,1,0:T(8,128)(2,1)}, bf16[8,256,1024]{2,1,0:T(8...) custom-call(s32[8]{0:T(128)} %copy-done.9, ...), custom_call_target="tpu_custom_call" | custom-call | flops 17999998976 | bytes 120000000 | tf_op jit(solution)/shard_map/dense_forward/pallas_call | solution.py:780
  94.2 3.9 %fusion.12 = f32[256,1024]{1,0:T(8,128)S(1)} fusion(bf16[2048,1024]{1,0:T(8,128)(2,1)} %bitcast.143, bf16[2048,512]{1,0:T(8,128)(2,1)} %bitcast.147, s32[]{:T(128)S(6)} %select_n.276), kind=kOutput, calls=%fused_computation.13 | convolution fusion | flops 1073741824 | bytes 6291460 | tf_op jit(solution)/shard_map/dot_general | solution.py:572
  98.2 5.9 %fusion.18 = f32[256,2048]{1,0:T(8,128)S(1)} fusion(bf16[2048,2048]{1,0:T(8,128)(2,1)} %bitcast.110, bf16[2048,512]{1,0:T(8,128)(2,1)S(1)} %bitcast.114, s32[]{:T(128)S(6)} %select_n.276), kind=kOutput, calls=%fused_computation.19 | convolution fusion | flops 2147483648 | bytes 11534340 | tf_op jit(solution)/shard_map/dot_general | solution.py:572
  108.9 2.3 fusion.2.refs_3_.refs_7_
  112.0 2.2 fusion.14.refs_13_.refs_15_
  114.3 2.3 fusion.6.refs_1_.refs_5_
  116.6 3.7 %fusion.22.refs_9_.refs_11_ = f32[256,2048]{1,0:T(8,128)} fusion(bf16[2048,2048]{1,0:T(8,128)(2,1)S(1)} %bitcast.113, bf16[2048,512]{1,0:T(8,128)(2,1)S(1)} %bitcast.115, s32[]{:T(128)S(6)} %select_n.275), kind=kOutput, calls=%fused_computation.23 | convolution fusion | flops 2147483648 | bytes 11534340 | tf_op jit(solution)/shard_map/dot_general | solution.py:572
  123.2 5.6 %joined.10 = (f32[256,1024]{1,0:T(8,128)S(1)}, f32[256,1024]{1,0:T(8,128)S(1)}, f32[128,2048]{1,0:T(8,128)S(1)}, f32[128,2048]{1,0:T(8,128)S(1)}, f32[128,1024]{1,0:T(8,128)S(1)}, /*index=5*/f32[128,1024]{1,0:T(8,128)S(1)}) custom-call(s32[3]{0:T(128)S(1)} %pad_add_fusion.refs_0_, f32[512,512]{1,0:T(8,128)} %fusion.6.refs_1_.refs_5_, f32[512,512]{1,0:T(8,128)} %copy-done.19, ...), custom_call_target="tpu_custom_call" | custom-call | bytes 6000000 | tf_op jit(solution)/shard_map/joined/pallas_call | solution.py:941
  132.9 4.7 %collective-permute-start.11 = (f32[128,1024]{1,0:T(8,128)S(1)}, f32[128,1024]{1,0:T(8,128)S(1)}, u32[]{:S(2)}, u32[]{:S(2)}) collective-permute-start(f32[128,1024]{1,0:T(8,128)S(1)} %get-tuple-element.352), channel_id=1, source_target_pairs={{0,8},{1,9},{2,10},{3,11},{4,12},{5,13},{6,14},{7,15},{8,0},{9,1},... | collective-permute-start | bytes 1572872 | tf_op jit(solution)/shard_map/ppermute | solution.py:496
  137.7 21.2 %dense_backward.1 = (bf16[8,256,128]{2,1,0:T(8,128)(2,1)}, bf16[8,256,1024]{2,1,0:T(8,128)(2,1)}, f32[8,256,512]{2,1,0:T(8,128)}, f32[8,256,512]{2,1,0:T(8,128)}...) custom-call(bf16[8,256,1024]{2,1,0:T(8,128)(2,1)} %get-tuple-element.330.grad_attended_ref, ...), custom_call_target="tpu_custom_call" | custom-call | flops 10000000000 | bytes 75000000 | tf_op jit(solution)/shard_map/dense_backward/pallas_call | solution.py:877
  159.8 3.6 joined.11
  165.0 3.6 fusion.8.refs_1_.refs_5_
  170.6 1.7 collective-permute-start.15
  172.3 2.3 collective-permute-start.16
  174.5 8.3 %back_enter.1 = (f32[256,8,512]{2,1,0:T(8,128)S(1)}, f32[16,8,512]{2,1,0:T(8,128)S(1)}) custom-call(f32[8,256,512]{2,1,0:T(8,128)} %get-tuple-element.377.grad_ref, f32[16,512]{1,0:T(8,128)S(1)} %get-tuple-element.618.retain_ref), custom_call_target="tpu_custom_call" | custom-call | bytes 24000000 | tf_op jit(solution)/shard_map/back_enter/pallas_call | solution.py:228
  182.9 2.0 copy-done
  184.9 4.5 %collective-permute-done.16.refs_10_.refs_12_ = f32[64,1024]{1,0:T(8,128)S(1)} collective-permute-done((f32[64,1024]{1,0:T(8,128)S(1)}, f32[64,1024]{1,0:T(8,128)S(1)}, u32[]{:S(2)}, u32[]{:S(2)}) %collective-permute-start.16) | collective-permute-done | bytes 262176 | tf_op jit(solution)/shard_map/ppermute | solution.py:496
  191.6 2.0 joined.13
  196.5 3.7 %collective-permute-start.19 = (f32[64,1024]{1,0:T(8,128)}, f32[64,1024]{1,0:T(8,128)S(1)}, u32[]{:S(2)}, u32[]{:S(2)}) collective-permute-start(f32[64,1024]{1,0:T(8,128)} %get-tuple-element.411), channel_id=1, source_target_pairs={{0,8},{1,9},{2,10},{3,11},{4,12},{5,13},{6,14},{7,15},{8,0},{9,1},... | collective-permute-start | bytes 786440 | tf_op jit(solution)/shard_map/ppermute | solution.py:496
  202.5 8.7 %collective-permute-done.21.refs_10_.refs_12_ = f32[32,1024]{1,0:T(8,128)S(1)} collective-permute-done((f32[32,1024]{1,0:T(8,128)S(1)}, f32[32,1024]{1,0:T(8,128)S(1)}, u32[]{:S(2)}, u32[]{:S(2)}) %collective-permute-start.21) | collective-permute-done | bytes 131104 | tf_op jit(solution)/shard_map/ppermute | solution.py:496
  211.2 2.3 collective-permute-done.20.refs_6_.refs_8_
  218.9 4.4 %collective-permute-done.22 = f32[16,8,256]{2,1,0:T(8,128)S(1)} collective-permute-done((f32[16,8,256]{2,1,0:T(8,128)S(1)}, f32[16,8,256]{2,1,0:T(8,128)S(1)}, u32[]{:S(2)}, u32[]{:S(2)}) %collective-permute-start.22) | collective-permute-done | bytes 131104 | tf_op jit(solution)/shard_map/ppermute | solution.py:445
  223.3 2.6 collective-permute-done.23
  226.9 1.6 collective-permute-start.26
  228.5 2.0 collective-permute-start.27
  230.5 3.6 collective-permute-start.28
  235.1 3.3 collective-permute-done.30.refs_5_
  238.4 2.5 collective-permute-done.28.refs_1_
  241.8 2.8 collective-permute-start.31
  244.7 9.0 %adjoint_sums.3 = (f32[4,16,8,512]{3,2,1,0:T(8,128)S(1)}, f32[8,8,512]{2,1,0:T(8,128)S(1)}) custom-call(f32[256,8,512]{2,1,0:T(8,128)} %copy-done, f32[256,8,512]{2,1,0:T(8,128)} %get-tuple-element.303.turned_ref, f32[16,512]{1,0:T(8,128)S(1)} %get-tuple-element.618.retain_ref, f32[16,512]{1,0:T(8,128)S(1)} %get-tuple-element.616.inverse_ref, ...), custom_call_target="tpu_custom_call" | custom-call | bytes 24000000 | tf_op jit(solution)/shard_map/adjoint_sums/pallas_call | solution.py:323
  254.7 2.0 collective-permute-start.37
  256.7 2.0 collective-permute-start.38
  259.1 9.0 %adjoint_sums.4 = (f32[4,16,8,512]{3,2,1,0:T(8,128)S(1)}, f32[8,8,512]{2,1,0:T(8,128)S(1)}) custom-call(f32[256,8,512]{2,1,0:T(8,128)} %copy-done, f32[256,8,512]{2,1,0:T(8,128)} %get-tuple-element.303.turned_ref, f32[16,512]{1,0:T(8,128)S(1)} %get-tuple-element.618.retain_ref, f32[16,512]{1,0:T(8,128)S(1)} %get-tuple-element.616.inverse_ref, ...), custom_call_target="tpu_custom_call" | custom-call | bytes 24000000 | tf_op jit(solution)/shard_map/adjoint_sums/pallas_call | solution.py:323
  269.4 2.1 collective-permute-start.40
  271.5 1.9 collective-permute-start.41
  274.2 1.9 collective-permute-start.39
  276.1 6.4 %adjoint_sums.5 = (f32[4,16,8,512]{3,2,1,0:T(8,128)S(1)}, f32[8,8,512]{2,1,0:T(8,128)S(1)}) custom-call(f32[256,8,512]{2,1,0:T(8,128)} %copy-done, f32[256,8,512]{2,1,0:T(8,128)} %get-tuple-element.303.turned_ref, f32[16,512]{1,0:T(8,128)S(1)} %get-tuple-element.618.retain_ref, f32[16,512]{1,0:T(8,128)S(1)} %get-tuple-element.616.inverse_ref, ...), custom_call_target="tpu_custom_call" | custom-call | bytes 24000000 | tf_op jit(solution)/shard_map/adjoint_sums/pallas_call | solution.py:323
  282.7 5.4 %collective-permute-done.39.refs_2_ = f32[32,1152]{1,0:T(8,128)S(1)} collective-permute-done((f32[32,1152]{1,0:T(8,128)S(1)}, f32[32,1152]{1,0:T(8,128)S(1)}, u32[]{:S(2)}, u32[]{:S(2)}) %collective-permute-start.39) | collective-permute-done | bytes 147488 | tf_op jit(solution)/shard_map/ppermute | solution.py:496
  288.4 3.5 placed.10
  292.2 1.6 collective-permute-start.48
  295.8 1.7 copy.39._
  297.9 6.6 %leave.3 = (f32[16,8,512]{2,1,0:T(8,128)S(1)}, bf16[8,256,512]{2,1,0:T(8,128)(2,1)S(1)}) custom-call(s32[8]{0:T(128)S(1)} %copy-done.10, bf16[8,256,512]{2,1,0:T(8,128)(2,1)S(1)} %copy-done.2, f32[1,512]{1,0:T(1,128)S(1)} %bitcast.105, f32[8,256,512]{2,1,0:T(8,128)} %get-tuple-element.373.part_ref, ...), custom_call_target="tpu_custom_call", output_to_operand_aliasing={{1}: (9, {})} | custom-call | bytes 24000000 | tf_op jit(solution)/shard_map/leave/pallas_call | solution.py:399
  304.6 3.4 collective-permute-start.44
  308.2 4.9 %leave.4 = (f32[16,8,512]{2,1,0:T(8,128)S(1)}, bf16[8,256,512]{2,1,0:T(8,128)(2,1)S(1)}) custom-call(s32[8]{0:T(128)S(1)} %copy-done.10, bf16[8,256,512]{2,1,0:T(8,128)(2,1)S(1)} %copy-done.2, f32[1,512]{1,0:T(1,128)S(1)} %bitcast.106, f32[8,256,512]{2,1,0:T(8,128)} %get-tuple-element.373.part_ref, ...), custom_call_target="tpu_custom_call", output_to_operand_aliasing={{1}: (9, {})} | custom-call | bytes 24000000 | tf_op jit(solution)/shard_map/leave/pallas_call | solution.py:399
  314.7 7.2 %leave.5 = (f32[16,8,512]{2,1,0:T(8,128)}, bf16[8,256,512]{2,1,0:T(8,128)(2,1)}) custom-call(s32[8]{0:T(128)S(1)} %copy-done.10, bf16[8,256,512]{2,1,0:T(8,128)(2,1)S(1)} %copy-done.2, f32[1,512]{1,0:T(1,128)S(1)} %bitcast.107, f32[8,256,512]{2,1,0:T(8,128)} %get-tuple-element.373.part_ref, ...), custom_call_target="tpu_custom_call", output_to_operand_aliasing={{1}: (9, {})} | custom-call | bytes 24000000 | tf_op jit(solution)/shard_map/leave/pallas_call | solution.py:399
  324.1 2.0 collective-permute-start.50
  326.2 1.7 collective-permute-start.51
  329.3 1.7 collective-permute-start.56
  332.8 5.2 %gathered.6 = (f32[1024,512]{1,0:T(8,128)}, f32[1024,512]{1,0:T(8,128)}, f32[512,1024]{1,0:T(8,128)}) custom-call(s32[5]{0:T(128)S(1)} %stack.62.refs_0_, f32[256,1024]{1,0:T(8,128)} %get-tuple-element.581.refs_1_, f32[256,1024]{1,0:T(8,128)} %collective-permute-done.47.refs_2_, f32[128,1024]{1,0:T(8,128)} %get-tuple-element.583.refs_3_, ...), custom_call_target="tpu_custom_call" | custom-call | bytes 12000000 | tf_op jit(solution)/shard_map/gathered/pallas_call | solution.py:1041
  338.0 9.3 %collective-permute-done.52 = f32[40,512]{1,0:T(8,128)S(1)} collective-permute-done((f32[40,512]{1,0:T(8,128)S(1)}, f32[40,512]{1,0:T(8,128)S(1)}, u32[]{:S(2)}, u32[]{:S(2)}) %collective-permute-start.52) | collective-permute-done | bytes 81952 | tf_op jit(solution)/shard_map/ppermute | solution.py:496
  350.9 4.4 %gathered.4 = (f32[512,2176]{1,0:T(8,128)}, f32[512,1024]{1,0:T(8,128)}) custom-call(s32[5]{0:T(128)S(1)} %stack.59.refs_0_, f32[128,2048]{1,0:T(8,128)S(1)} %get-tuple-element.573.refs_1_, f32[128,2048]{1,0:T(8,128)S(1)} %copy-done.6, f32[128,1152]{1,0:T(8,128)S(1)} %placed.11.refs_3_, f32[128,1152]{1,0:T(8,128)} %collective-permute-done.56.refs_4_), custom_call_target="tpu_custom_call" | custom-call | bytes 12000000 | tf_op jit(solution)/shard_map/gathered/pallas_call | solution.py:1041
  355.3 4.5 %gathered.7 = (f32[1024,512]{1,0:T(8,128)}, f32[1024,512]{1,0:T(8,128)}, f32[512,1024]{1,0:T(8,128)}) custom-call(s32[5]{0:T(128)S(1)} %stack.61.refs_0_, f32[256,1024]{1,0:T(8,128)S(1)} %collective-permute-done.58.refs_1_, f32[256,1024]{1,0:T(8,128)S(1)} %collective-permute-done.59.refs_2_, ...), custom_call_target="tpu_custom_call", output_to_operand_aliasing={{0}: (5, {}), {1}: (6, {}), {2}: (7, {})} | custom-call | bytes 12000000 | tf_op jit(solution)/shard_map/gathered/pallas_call | solution.py:1041
  359.8 2.8 gathered.5
  (241 shorter events, 59.0 us)
Async XLA Ops:
  2.0 34.8 %copy-start.9 = (s32[8]{0:T(128)}, s32[8]{0:T(128)S(1)}, u32[]{:S(2)}) copy-start(s32[8]{0:T(128)S(1)} %broadcast_subtract_fusion.count_ref) | copy-start | bytes 100
  2.9 35.1 %copy-start.35 = (bf16[2,128]{1,0:T(2,128)(2,1)S(1)}, bf16[2,128]{1,0:T(2,128)(2,1)}, u32[]{:S(2)}) copy-start(bf16[2,128]{1,0:T(2,128)(2,1)} %param.26) | copy-start | bytes 1540
  15.3 6.5 %collective-permute-start = (f32[16,8,256]{2,1,0:T(8,128)S(1)}, f32[16,8,256]{2,1,0:T(8,128)S(1)}, u32[]{:S(2)}, u32[]{:S(2)}) collective-permute-start(f32[16,8,256]{2,1,0:T(8,128)S(1)} %constant_dynamic-slice_fusion.2), channel_id=1, source_target_pairs={{0,4},{4,0},{8,12},{12,8},{16,20},{20,16},{24,28},{28,24},{1,5},{5... | collective-permute-start | bytes 393224 | tf_op jit(solution)/shard_map/ppermute | solution.py:445
  21.9 9.7 %collective-permute-start.1 = (f32[16,8,256]{2,1,0:T(8,128)S(1)}, f32[16,8,256]{2,1,0:T(8,128)S(1)}, u32[]{:S(2)}, u32[]{:S(2)}) collective-permute-start(f32[16,8,256]{2,1,0:T(8,128)S(1)} %select_add_fusion.1), channel_id=1, source_target_pairs={{0,24},{4,28},{1,25},{5,29},{2,26},{6,30},{3,27},{7,31}} | collective-permute-start | bytes 393224 | tf_op jit(solution)/shard_map/ppermute | solution.py:445
  27.6 6.1 %collective-permute-start.2 = (f32[16,8,256]{2,1,0:T(8,128)S(1)}, f32[16,8,256]{2,1,0:T(8,128)S(1)}, u32[]{:S(2)}, u32[]{:S(2)}) collective-permute-start(f32[16,8,256]{2,1,0:T(8,128)S(1)} %select_add_fusion.1), channel_id=1, source_target_pairs={{0,16},{4,20},{8,24},{12,28},{1,17},{5,21},{9,25},{13,29},{2,18},{... | collective-permute-start | bytes 393224 | tf_op jit(solution)/shard_map/ppermute | solution.py:445
  28.9 6.2 %collective-permute-start.3 = (f32[16,8,256]{2,1,0:T(8,128)S(1)}, f32[16,8,256]{2,1,0:T(8,128)S(1)}, u32[]{:S(2)}, u32[]{:S(2)}) collective-permute-start(f32[16,8,256]{2,1,0:T(8,128)S(1)} %select_add_fusion.1), channel_id=1, source_target_pairs={{0,8},{4,12},{8,16},{12,20},{16,24},{20,28},{1,9},{5,13},{9,17},{1... | collective-permute-start | bytes 393224 | tf_op jit(solution)/shard_map/ppermute | solution.py:445
  35.2 5.0 %collective-permute-start.4 = (f32[16,8,256]{2,1,0:T(8,128)S(1)}, f32[16,8,256]{2,1,0:T(8,128)S(1)}, u32[]{:S(2)}, u32[]{:S(2)}) collective-permute-start(f32[16,8,256]{2,1,0:T(8,128)S(1)} %get-tuple-element.597), channel_id=1, source_target_pairs={{0,4},{4,0},{8,12},{12,8},{16,20},{20,16},{24,28},{28,24},{1,5},{5... | collective-permute-start | bytes 393224 | tf_op jit(solution)/shard_map/ppermute | solution.py:445
  98.1 22.1 %collective-permute-start.8 = (f32[256,1024]{1,0:T(8,128)S(1)}, f32[256,1024]{1,0:T(8,128)S(1)}, u32[]{:S(2)}, u32[]{:S(2)}) collective-permute-start(f32[256,1024]{1,0:T(8,128)S(1)} %fusion.12), channel_id=1, source_target_pairs={{0,1},{1,0},{2,3},{3,2},{4,5},{5,4},{6,7},{7,6},{8,9},{9,8},{10,11... | collective-permute-start | bytes 3145736 | tf_op jit(solution)/shard_map/ppermute | solution.py:496
  104.1 16.2 %collective-permute-start.7 = (f32[256,2048]{1,0:T(8,128)S(1)}, f32[256,2048]{1,0:T(8,128)S(1)}, u32[]{:S(2)}, u32[]{:S(2)}) collective-permute-start(f32[256,2048]{1,0:T(8,128)S(1)} %fusion.18), channel_id=1, source_target_pairs={{0,1},{1,0},{2,3},{3,2},{4,5},{5,4},{6,7},{7,6},{8,9},{9,8},{10,11... | collective-permute-start | bytes 6291464 | tf_op jit(solution)/shard_map/ppermute | solution.py:496
  105.9 14.3 %collective-permute-start.6 = (f32[512,512]{1,0:T(8,128)S(1)}, f32[512,512]{1,0:T(8,128)S(1)}, u32[]{:S(2)}, u32[]{:S(2)}) collective-permute-start(f32[512,512]{1,0:T(8,128)S(1)} %fusion), channel_id=1, source_target_pairs={{0,1},{1,0},{2,3},{3,2},{4,5},{5,4},{6,7},{7,6},{8,9},{9,8},{10,11... | collective-permute-start | bytes 3145736 | tf_op jit(solution)/shard_map/ppermute | solution.py:496
  108.8 11.5 %collective-permute-start.5 = (f32[512,512]{1,0:T(8,128)S(1)}, f32[512,512]{1,0:T(8,128)S(1)}, u32[]{:S(2)}, u32[]{:S(2)}) collective-permute-start(f32[512,512]{1,0:T(8,128)S(1)} %fusion.4), channel_id=1, source_target_pairs={{0,1},{1,0},{2,3},{3,2},{4,5},{5,4},{6,7},{7,6},{8,9},{9,8},{10,11... | collective-permute-start | bytes 3145736 | tf_op jit(solution)/shard_map/ppermute | solution.py:496
  129.8 29.0 %collective-permute-start.10 = (f32[128,2048]{1,0:T(8,128)S(1)}, f32[128,2048]{1,0:T(8,128)S(1)}, u32[]{:S(2)}, u32[]{:S(2)}) collective-permute-start(f32[128,2048]{1,0:T(8,128)S(1)} %get-tuple-element.350), channel_id=1, source_target_pairs={{0,4},{1,5},{2,6},{3,7},{4,0},{5,1},{6,2},{7,3},{8,12},{9,13},{10,... | collective-permute-start | bytes 3145736 | tf_op jit(solution)/shard_map/ppermute | solution.py:496
  131.4 27.5 %collective-permute-start.9 = (f32[256,1024]{1,0:T(8,128)S(1)}, f32[256,1024]{1,0:T(8,128)S(1)}, u32[]{:S(2)}, u32[]{:S(2)}) collective-permute-start(f32[256,1024]{1,0:T(8,128)S(1)} %get-tuple-element.348), channel_id=1, source_target_pairs={{0,2},{1,3},{2,0},{3,1},{4,6},{5,7},{6,4},{7,5},{8,10},{9,11},{10,... | collective-permute-start | bytes 3145736 | tf_op jit(solution)/shard_map/ppermute | solution.py:496
  132.9 25.9 %collective-permute-start.11 = (f32[128,1024]{1,0:T(8,128)S(1)}, f32[128,1024]{1,0:T(8,128)S(1)}, u32[]{:S(2)}, u32[]{:S(2)}) collective-permute-start(f32[128,1024]{1,0:T(8,128)S(1)} %get-tuple-element.352), channel_id=1, source_target_pairs={{0,8},{1,9},{2,10},{3,11},{4,12},{5,13},{6,14},{7,15},{8,0},{9,1},... | collective-permute-start | bytes 1572872 | tf_op jit(solution)/shard_map/ppermute | solution.py:496
  170.0 20.2 %collective-permute-start.12 = (f32[256,1024]{1,0:T(8,128)S(1)}, f32[256,1024]{1,0:T(8,128)S(1)}, u32[]{:S(2)}, u32[]{:S(2)}) collective-permute-start(f32[256,1024]{1,0:T(8,128)S(1)} %fusion.10), channel_id=1, source_target_pairs={{0,1},{1,0},{2,3},{3,2},{4,5},{5,4},{6,7},{7,6},{8,9},{9,8},{10,11... | collective-permute-start | bytes 3145736 | tf_op jit(solution)/shard_map/ppermute | solution.py:496
  170.0 19.3 %collective-permute-start.14 = (f32[128,1024]{1,0:T(8,128)S(1)}, f32[128,1024]{1,0:T(8,128)S(1)}, u32[]{:S(2)}, u32[]{:S(2)}) collective-permute-start(f32[128,1024]{1,0:T(8,128)S(1)} %get-tuple-element.383), channel_id=1, source_target_pairs={{0,4},{1,5},{2,6},{3,7},{4,0},{5,1},{6,2},{7,3},{8,12},{9,13},{10,... | collective-permute-start | bytes 1572872 | tf_op jit(solution)/shard_map/ppermute | solution.py:496
  170.6 19.6 %collective-permute-start.15 = (f32[64,2048]{1,0:T(8,128)S(1)}, f32[64,2048]{1,0:T(8,128)S(1)}, u32[]{:S(2)}, u32[]{:S(2)}) collective-permute-start(f32[64,2048]{1,0:T(8,128)S(1)} %get-tuple-element.385), channel_id=1, source_target_pairs={{0,8},{1,9},{2,10},{3,11},{4,12},{5,13},{6,14},{7,15},{8,0},{9,1},... | collective-permute-start | bytes 1572872 | tf_op jit(solution)/shard_map/ppermute | solution.py:496
  172.3 17.1 %collective-permute-start.16 = (f32[64,1024]{1,0:T(8,128)S(1)}, f32[64,1024]{1,0:T(8,128)S(1)}, u32[]{:S(2)}, u32[]{:S(2)}) collective-permute-start(f32[64,1024]{1,0:T(8,128)S(1)} %get-tuple-element.387), channel_id=1, source_target_pairs={{0,16},{1,17},{2,18},{3,19},{4,20},{5,21},{6,22},{7,23},{8,24},{9,... | collective-permute-start | bytes 786440 | tf_op jit(solution)/shard_map/ppermute | solution.py:496
  174.5 10.4 %collective-permute-start.13 = (f32[256,128]{1,0:T(8,128)S(1)}, f32[256,128]{1,0:T(8,128)S(1)}, u32[]{:S(2)}, u32[]{:S(2)}) collective-permute-start(f32[256,128]{1,0:T(8,128)S(1)} %fusion.16), channel_id=1, source_target_pairs={{0,1},{1,0},{2,3},{3,2},{4,5},{5,4},{6,7},{7,6},{8,9},{9,8},{10,11... | collective-permute-start | bytes 393224 | tf_op jit(solution)/shard_map/ppermute | solution.py:496
  193.6 19.9 %collective-permute-start.18 = (f32[128,1152]{1,0:T(8,128)}, f32[128,1152]{1,0:T(8,128)S(1)}, u32[]{:S(2)}, u32[]{:S(2)}) collective-permute-start(f32[128,1152]{1,0:T(8,128)} %get-tuple-element.409), channel_id=1, source_target_pairs={{0,2},{1,3},{2,0},{3,1},{4,6},{5,7},{6,4},{7,5},{8,10},{9,11},{10,... | collective-permute-start | bytes 1769480 | tf_op jit(solution)/shard_map/ppermute | solution.py:496
  195.7 6.1 %collective-permute-start.17 = (f32[16,8,256]{2,1,0:T(8,128)}, f32[16,8,256]{2,1,0:T(8,128)S(1)}, u32[]{:S(2)}, u32[]{:S(2)}) collective-permute-start(f32[16,8,256]{2,1,0:T(8,128)} %constant_dynamic-slice_fusion), channel_id=1, source_target_pairs={{28,24},{24,28},{20,16},{16,20},{12,8},{8,12},{4,0},{0,4},{29,25},... | collective-permute-start | bytes 393224 | tf_op jit(solution)/shard_map/ppermute | solution.py:445
  196.5 14.7 %collective-permute-start.19 = (f32[64,1024]{1,0:T(8,128)}, f32[64,1024]{1,0:T(8,128)S(1)}, u32[]{:S(2)}, u32[]{:S(2)}) collective-permute-start(f32[64,1024]{1,0:T(8,128)} %get-tuple-element.411), channel_id=1, source_target_pairs={{0,8},{1,9},{2,10},{3,11},{4,12},{5,13},{6,14},{7,15},{8,0},{9,1},... | collective-permute-start | bytes 786440 | tf_op jit(solution)/shard_map/ppermute | solution.py:496
  200.2 13.3 %collective-permute-start.20 = (f32[32,2048]{1,0:T(8,128)S(1)}, f32[32,2048]{1,0:T(8,128)S(1)}, u32[]{:S(2)}, u32[]{:S(2)}) collective-permute-start(f32[32,2048]{1,0:T(8,128)S(1)} %get-tuple-element.413), channel_id=1, source_target_pairs={{0,16},{1,17},{2,18},{3,19},{4,20},{5,21},{6,22},{7,23},{8,24},{9,... | collective-permute-start | bytes 786440 | tf_op jit(solution)/shard_map/ppermute | solution.py:496
  200.4 10.8 %collective-permute-start.21 = (f32[32,1024]{1,0:T(8,128)S(1)}, f32[32,1024]{1,0:T(8,128)S(1)}, u32[]{:S(2)}, u32[]{:S(2)}) collective-permute-start(f32[32,1024]{1,0:T(8,128)S(1)} %get-tuple-element.415), channel_id=1, source_target_pairs={{0,2},{1,3},{2,0},{3,1},{4,6},{5,7},{6,4},{7,5},{8,10},{9,11},{10,... | collective-permute-start | bytes 393224 | tf_op jit(solution)/shard_map/ppermute | solution.py:496
  213.6 9.7 %collective-permute-start.22 = (f32[16,8,256]{2,1,0:T(8,128)S(1)}, f32[16,8,256]{2,1,0:T(8,128)S(1)}, u32[]{:S(2)}, u32[]{:S(2)}) collective-permute-start(f32[16,8,256]{2,1,0:T(8,128)S(1)} %select_add_fusion), channel_id=1, source_target_pairs={{28,4},{24,0},{29,5},{25,1},{30,6},{26,2},{31,7},{27,3}} | collective-permute-start | bytes 393224 | tf_op jit(solution)/shard_map/ppermute | solution.py:445
  214.9 11.0 %collective-permute-start.23 = (f32[16,8,256]{2,1,0:T(8,128)S(1)}, f32[16,8,256]{2,1,0:T(8,128)S(1)}, u32[]{:S(2)}, u32[]{:S(2)}) collective-permute-start(f32[16,8,256]{2,1,0:T(8,128)S(1)} %select_add_fusion), channel_id=1, source_target_pairs={{28,12},{24,8},{20,4},{16,0},{29,13},{25,9},{21,5},{17,1},{30,14},... | collective-permute-start | bytes 393224 | tf_op jit(solution)/shard_map/ppermute | solution.py:445
  216.2 9.7 %collective-permute-start.24 = (f32[16,8,256]{2,1,0:T(8,128)S(1)}, f32[16,8,256]{2,1,0:T(8,128)S(1)}, u32[]{:S(2)}, u32[]{:S(2)}) collective-permute-start(f32[16,8,256]{2,1,0:T(8,128)S(1)} %select_add_fusion), channel_id=1, source_target_pairs={{28,20},{24,16},{20,12},{16,8},{12,4},{8,0},{29,21},{25,17},{21,13... | collective-permute-start | bytes 393224 | tf_op jit(solution)/shard_map/ppermute | solution.py:445
  217.5 8.5 %collective-permute-start.25 = (f32[64,1152]{1,0:T(8,128)S(1)}, f32[64,1152]{1,0:T(8,128)S(1)}, u32[]{:S(2)}, u32[]{:S(2)}) collective-permute-start(f32[64,1152]{1,0:T(8,128)S(1)} %get-tuple-element.429), channel_id=1, source_target_pairs={{0,4},{1,5},{2,6},{3,7},{4,0},{5,1},{6,2},{7,3},{8,12},{9,13},{10,... | collective-permute-start | bytes 884744 | tf_op jit(solution)/shard_map/ppermute | solution.py:496
  226.9 7.9 %collective-permute-start.26 = (f32[16,8,256]{2,1,0:T(8,128)S(1)}, f32[16,8,256]{2,1,0:T(8,128)S(1)}, u32[]{:S(2)}, u32[]{:S(2)}) collective-permute-start(f32[16,8,256]{2,1,0:T(8,128)S(1)} %fusion.24), channel_id=1, source_target_pairs={{28,24},{24,28},{20,16},{16,20},{12,8},{8,12},{4,0},{0,4},{29,25},... | collective-permute-start | bytes 393224 | tf_op jit(solution)/shard_map/ppermute | solution.py:445
  228.5 12.3 %collective-permute-start.27 = (f32[32,1152]{1,0:T(8,128)S(1)}, f32[32,1152]{1,0:T(8,128)S(1)}, u32[]{:S(2)}, u32[]{:S(2)}) collective-permute-start(f32[32,1152]{1,0:T(8,128)S(1)} %get-tuple-element.458), channel_id=1, source_target_pairs={{0,8},{1,9},{2,10},{3,11},{4,12},{5,13},{6,14},{7,15},{8,0},{9,1},... | collective-permute-start | bytes 442376 | tf_op jit(solution)/shard_map/ppermute | solution.py:496
  230.5 10.4 %collective-permute-start.28 = (f32[32,1024]{1,0:T(8,128)S(1)}, f32[32,1024]{1,0:T(8,128)S(1)}, u32[]{:S(2)}, u32[]{:S(2)}) collective-permute-start(f32[32,1024]{1,0:T(8,128)S(1)} %get-tuple-element.460), channel_id=1, source_target_pairs={{0,16},{1,17},{2,18},{3,19},{4,20},{5,21},{6,22},{7,23},{8,24},{9,... | collective-permute-start | bytes 393224 | tf_op jit(solution)/shard_map/ppermute | solution.py:496
  234.1 6.8 %collective-permute-start.29 = (f32[16,2048]{1,0:T(8,128)S(1)}, f32[16,2048]{1,0:T(8,128)S(1)}, u32[]{:S(2)}, u32[]{:S(2)}) collective-permute-start(f32[16,2048]{1,0:T(8,128)S(1)} %get-tuple-element.462), channel_id=1, source_target_pairs={{0,2},{1,3},{2,0},{3,1},{4,6},{5,7},{6,4},{7,5},{8,10},{9,11},{10,... | collective-permute-start | bytes 393224 | tf_op jit(solution)/shard_map/ppermute | solution.py:496
  234.1 4.3 %collective-permute-start.30 = (f32[16,1024]{1,0:T(8,128)S(1)}, f32[16,1024]{1,0:T(8,128)S(1)}, u32[]{:S(2)}, u32[]{:S(2)}) collective-permute-start(f32[16,1024]{1,0:T(8,128)S(1)} %get-tuple-element.464), channel_id=1, source_target_pairs={{0,4},{1,5},{2,6},{3,7},{4,0},{5,1},{6,2},{7,3},{8,12},{9,13},{10,... | collective-permute-start | bytes 196616 | tf_op jit(solution)/shard_map/ppermute | solution.py:496
  241.0 12.7 %collective-permute-start.32 = (f32[32,1024]{1,0:T(8,128)S(1)}, f32[32,1024]{1,0:T(8,128)S(1)}, u32[]{:S(2)}, u32[]{:S(2)}) collective-permute-start(f32[32,1024]{1,0:T(8,128)S(1)} %get-tuple-element.494.refs_1_), channel_id=1, source_target_pairs={{0,16},{1,17},{2,18},{3,19},{4,20},{5,21},{6,22},{7,23},{8,24},{9,... | collective-permute-start | bytes 393224 | tf_op jit(solution)/shard_map/ppermute | solution.py:496
  241.2 12.5 %collective-permute-start.33 = (f32[16,2048]{1,0:T(8,128)S(1)}, f32[16,2048]{1,0:T(8,128)S(1)}, u32[]{:S(2)}, u32[]{:S(2)}) collective-permute-start(f32[16,2048]{1,0:T(8,128)S(1)} %get-tuple-element.496.refs_3_), channel_id=1, source_target_pairs={{0,2},{1,3},{2,0},{3,1},{4,6},{5,7},{6,4},{7,5},{8,10},{9,11},{10,... | collective-permute-start | bytes 393224 | tf_op jit(solution)/shard_map/ppermute | solution.py:496
  241.8 11.9 %collective-permute-start.31 = (f32[16,1152]{1,0:T(8,128)S(1)}, f32[16,1152]{1,0:T(8,128)S(1)}, u32[]{:S(2)}, u32[]{:S(2)}) collective-permute-start(f32[16,1152]{1,0:T(8,128)S(1)} %get-tuple-element.485), channel_id=1, source_target_pairs={{0,16},{1,17},{2,18},{3,19},{4,20},{5,21},{6,22},{7,23},{8,24},{9,... | collective-permute-start | bytes 221192 | tf_op jit(solution)/shard_map/ppermute | solution.py:496
  244.7 9.0 %collective-permute-start.34 = (f32[16,1024]{1,0:T(8,128)S(1)}, f32[16,1024]{1,0:T(8,128)S(1)}, u32[]{:S(2)}, u32[]{:S(2)}) collective-permute-start(f32[16,1024]{1,0:T(8,128)S(1)} %get-tuple-element.498.refs_5_), channel_id=1, source_target_pairs={{0,4},{1,5},{2,6},{3,7},{4,0},{5,1},{6,2},{7,3},{8,12},{9,13},{10,... | collective-permute-start | bytes 196616 | tf_op jit(solution)/shard_map/ppermute | solution.py:496
  254.7 13.5 %collective-permute-start.36 = (f32[64,1024]{1,0:T(8,128)S(1)}, f32[64,1024]{1,0:T(8,128)S(1)}, u32[]{:S(2)}, u32[]{:S(2)}) collective-permute-start(f32[64,1024]{1,0:T(8,128)S(1)} %get-tuple-element.515.refs_1_), channel_id=1, source_target_pairs={{0,8},{1,9},{2,10},{3,11},{4,12},{5,13},{6,14},{7,15},{8,0},{9,1},... | collective-permute-start | bytes 786440 | tf_op jit(solution)/shard_map/ppermute | solution.py:496
  254.7 13.4 %collective-permute-start.37 = (f32[32,2048]{1,0:T(8,128)S(1)}, f32[32,2048]{1,0:T(8,128)S(1)}, u32[]{:S(2)}, u32[]{:S(2)}) collective-permute-start(f32[32,2048]{1,0:T(8,128)S(1)} %get-tuple-element.517.refs_3_), channel_id=1, source_target_pairs={{0,16},{1,17},{2,18},{3,19},{4,20},{5,21},{6,22},{7,23},{8,24},{9,... | collective-permute-start | bytes 786440 | tf_op jit(solution)/shard_map/ppermute | solution.py:496
  256.7 11.4 %collective-permute-start.38 = (f32[32,1024]{1,0:T(8,128)S(1)}, f32[32,1024]{1,0:T(8,128)S(1)}, u32[]{:S(2)}, u32[]{:S(2)}) collective-permute-start(f32[32,1024]{1,0:T(8,128)S(1)} %get-tuple-element.519.refs_5_), channel_id=1, source_target_pairs={{0,2},{1,3},{2,0},{3,1},{4,6},{5,7},{6,4},{7,5},{8,10},{9,11},{10,... | collective-permute-start | bytes 393224 | tf_op jit(solution)/shard_map/ppermute | solution.py:496
  258.7 9.4 %collective-permute-start.35 = (f32[16,1152]{1,0:T(8,128)S(1)}, f32[16,1152]{1,0:T(8,128)S(1)}, u32[]{:S(2)}, u32[]{:S(2)}) collective-permute-start(f32[16,1152]{1,0:T(8,128)S(1)} %joined.19.refs_1_), channel_id=1, source_target_pairs={{0,16},{1,17},{2,18},{3,19},{4,20},{5,21},{6,22},{7,23},{8,24},{9,... | collective-permute-start | bytes 221192 | tf_op jit(solution)/shard_map/ppermute | solution.py:496
  269.4 18.6 %collective-permute-start.40 = (f32[128,1024]{1,0:T(8,128)S(1)}, f32[128,1024]{1,0:T(8,128)S(1)}, u32[]{:S(2)}, u32[]{:S(2)}) collective-permute-start(f32[128,1024]{1,0:T(8,128)S(1)} %get-tuple-element.536.refs_1_), channel_id=1, source_target_pairs={{0,4},{1,5},{2,6},{3,7},{4,0},{5,1},{6,2},{7,3},{8,12},{9,13},{10,... | collective-permute-start | bytes 1572872 | tf_op jit(solution)/shard_map/ppermute | solution.py:496
  271.5 16.6 %collective-permute-start.41 = (f32[64,2048]{1,0:T(8,128)S(1)}, f32[64,2048]{1,0:T(8,128)S(1)}, u32[]{:S(2)}, u32[]{:S(2)}) collective-permute-start(f32[64,2048]{1,0:T(8,128)S(1)} %get-tuple-element.538.refs_3_), channel_id=1, source_target_pairs={{0,8},{1,9},{2,10},{3,11},{4,12},{5,13},{6,14},{7,15},{8,0},{9,1},... | collective-permute-start | bytes 1572872 | tf_op jit(solution)/shard_map/ppermute | solution.py:496
  273.5 14.6 %collective-permute-start.42 = (f32[64,1024]{1,0:T(8,128)S(1)}, f32[64,1024]{1,0:T(8,128)S(1)}, u32[]{:S(2)}, u32[]{:S(2)}) collective-permute-start(f32[64,1024]{1,0:T(8,128)S(1)} %get-tuple-element.540.refs_5_), channel_id=1, source_target_pairs={{0,16},{1,17},{2,18},{3,19},{4,20},{5,21},{6,22},{7,23},{8,24},{9,... | collective-permute-start | bytes 786440 | tf_op jit(solution)/shard_map/ppermute | solution.py:496
  274.2 13.9 %collective-permute-start.39 = (f32[32,1152]{1,0:T(8,128)S(1)}, f32[32,1152]{1,0:T(8,128)S(1)}, u32[]{:S(2)}, u32[]{:S(2)}) collective-permute-start(f32[32,1152]{1,0:T(8,128)S(1)} %placed.7.refs_1_), channel_id=1, source_target_pairs={{0,8},{1,9},{2,10},{3,11},{4,12},{5,13},{6,14},{7,15},{8,0},{9,1},... | collective-permute-start | bytes 442376 | tf_op jit(solution)/shard_map/ppermute | solution.py:496
  291.9 30.8 %collective-permute-start.47 = (f32[256,1024]{1,0:T(8,128)}, f32[256,1024]{1,0:T(8,128)}, u32[]{:S(2)}, u32[]{:S(2)}) collective-permute-start(f32[256,1024]{1,0:T(8,128)} %get-tuple-element.581.refs_1_), channel_id=1, source_target_pairs={{0,2},{1,3},{2,0},{3,1},{4,6},{5,7},{6,4},{7,5},{8,10},{9,11},{10,... | collective-permute-start | bytes 3145736 | tf_op jit(solution)/shard_map/ppermute | solution.py:496
  292.2 30.5 %collective-permute-start.48 = (f32[128,2048]{1,0:T(8,128)S(1)}, f32[128,2048]{1,0:T(8,128)S(1)}, u32[]{:S(2)}, u32[]{:S(2)}) collective-permute-start(f32[128,2048]{1,0:T(8,128)S(1)} %get-tuple-element.573.refs_1_), channel_id=1, source_target_pairs={{0,4},{1,5},{2,6},{3,7},{4,0},{5,1},{6,2},{7,3},{8,12},{9,13},{10,... | collective-permute-start | bytes 3145736 | tf_op jit(solution)/shard_map/ppermute | solution.py:496
  293.8 28.9 %collective-permute-start.49 = (f32[128,1024]{1,0:T(8,128)}, f32[128,1024]{1,0:T(8,128)}, u32[]{:S(2)}, u32[]{:S(2)}) collective-permute-start(f32[128,1024]{1,0:T(8,128)} %get-tuple-element.583.refs_3_), channel_id=1, source_target_pairs={{0,8},{1,9},{2,10},{3,11},{4,12},{5,13},{6,14},{7,15},{8,0},{9,1},... | collective-permute-start | bytes 1572872 | tf_op jit(solution)/shard_map/ppermute | solution.py:496
  295.1 26.9 %collective-permute-start.46 = (f32[64,1152]{1,0:T(8,128)S(1)}, f32[64,1152]{1,0:T(8,128)S(1)}, u32[]{:S(2)}, u32[]{:S(2)}) collective-permute-start(f32[64,1152]{1,0:T(8,128)S(1)} %placed.9.refs_1_), channel_id=1, source_target_pairs={{0,4},{1,5},{2,6},{3,7},{4,0},{5,1},{6,2},{7,3},{8,12},{9,13},{10,... | collective-permute-start | bytes 884744 | tf_op jit(solution)/shard_map/ppermute | solution.py:496
  295.7 8.8 %collective-permute-start.43 = (f32[40,512]{1,0:T(8,128)S(1)}, f32[40,512]{1,0:T(8,128)S(1)}, u32[]{:S(2)}, u32[]{:S(2)}) collective-permute-start(f32[40,512]{1,0:T(8,128)S(1)} %pad.4), channel_id=1, source_target_pairs={{0,1},{1,0},{2,3},{3,2},{4,5},{5,4},{6,7},{7,6},{8,9},{9,8},{10,11... | collective-permute-start | bytes 245768 | tf_op jit(solution)/shard_map/ppermute | solution.py:496
  304.6 8.4 %collective-permute-start.44 = (f32[40,512]{1,0:T(8,128)S(1)}, f32[40,512]{1,0:T(8,128)S(1)}, u32[]{:S(2)}, u32[]{:S(2)}) collective-permute-start(f32[40,512]{1,0:T(8,128)S(1)} %add.253), channel_id=1, source_target_pairs={{0,16},{1,17},{2,18},{3,19},{4,20},{5,21},{6,22},{7,23},{8,24},{9,... | collective-permute-start | bytes 245768 | tf_op jit(solution)/shard_map/ppermute | solution.py:496
  313.0 8.9 %collective-permute-start.45 = (f32[40,512]{1,0:T(8,128)S(1)}, f32[40,512]{1,0:T(8,128)S(1)}, u32[]{:S(2)}, u32[]{:S(2)}) collective-permute-start(f32[40,512]{1,0:T(8,128)S(1)} %add.254), channel_id=1, source_target_pairs={{0,8},{1,9},{2,10},{3,11},{4,12},{5,13},{6,14},{7,15},{8,0},{9,1},... | collective-permute-start | bytes 245768 | tf_op jit(solution)/shard_map/ppermute | solution.py:496
  323.6 25.4 %collective-permute-start.58 = (f32[256,1024]{1,0:T(8,128)}, f32[256,1024]{1,0:T(8,128)S(1)}, u32[]{:S(2)}, u32[]{:S(2)}) collective-permute-start(f32[256,1024]{1,0:T(8,128)} %get-tuple-element.581.refs_1_), channel_id=1, source_target_pairs={{0,1},{1,0},{2,3},{3,2},{4,5},{5,4},{6,7},{7,6},{8,9},{9,8},{10,11... | collective-permute-start | bytes 3145736 | tf_op jit(solution)/shard_map/ppermute | solution.py:496
  323.6 23.7 %collective-permute-start.60 = (f32[128,1024]{1,0:T(8,128)}, f32[128,1024]{1,0:T(8,128)}, u32[]{:S(2)}, u32[]{:S(2)}) collective-permute-start(f32[128,1024]{1,0:T(8,128)} %get-tuple-element.583.refs_3_), channel_id=1, source_target_pairs={{0,1},{1,0},{2,3},{3,2},{4,5},{5,4},{6,7},{7,6},{8,9},{9,8},{10,11... | collective-permute-start | bytes 1572872 | tf_op jit(solution)/shard_map/ppermute | solution.py:496
  324.1 23.7 %collective-permute-start.61 = (f32[128,1024]{1,0:T(8,128)}, f32[128,1024]{1,0:T(8,128)}, u32[]{:S(2)}, u32[]{:S(2)}) collective-permute-start(f32[128,1024]{1,0:T(8,128)} %collective-permute-done.49.refs_4_), channel_id=1, source_target_pairs={{0,1},{1,0},{2,3},{3,2},{4,5},{5,4},{6,7},{7,6},{8,9},{9,8},{10,11... | collective-permute-start | bytes 1572872 | tf_op jit(solution)/shard_map/ppermute | solution.py:496
  324.1 5.1 %collective-permute-start.50 = (f32[40,512]{1,0:T(8,128)S(1)}, f32[40,512]{1,0:T(8,128)S(1)}, u32[]{:S(2)}, u32[]{:S(2)}) collective-permute-start(f32[40,512]{1,0:T(8,128)S(1)} %add.255), channel_id=1, source_target_pairs={{0,2},{1,3},{2,0},{3,1},{4,6},{5,7},{6,4},{7,5},{8,10},{9,11},{10,... | collective-permute-start | bytes 245768 | tf_op jit(solution)/shard_map/ppermute | solution.py:496
  326.2 4.9 %collective-permute-start.51 = (f32[40,512]{1,0:T(8,128)S(1)}, f32[40,512]{1,0:T(8,128)S(1)}, u32[]{:S(2)}, u32[]{:S(2)}) collective-permute-start(f32[40,512]{1,0:T(8,128)S(1)} %add.255), channel_id=1, source_target_pairs={{0,4},{1,5},{2,6},{3,7},{4,0},{5,1},{6,2},{7,3},{8,12},{9,13},{10,... | collective-permute-start | bytes 245768 | tf_op jit(solution)/shard_map/ppermute | solution.py:496
  329.3 19.3 %collective-permute-start.56 = (f32[128,1152]{1,0:T(8,128)S(1)}, f32[128,1152]{1,0:T(8,128)}, u32[]{:S(2)}, u32[]{:S(2)}) collective-permute-start(f32[128,1152]{1,0:T(8,128)S(1)} %placed.11.refs_3_), channel_id=1, source_target_pairs={{0,2},{1,3},{2,0},{3,1},{4,6},{5,7},{6,4},{7,5},{8,10},{9,11},{10,... | collective-permute-start | bytes 1769480 | tf_op jit(solution)/shard_map/ppermute | solution.py:496
  331.0 16.3 %collective-permute-start.52 = (f32[40,512]{1,0:T(8,128)S(1)}, f32[40,512]{1,0:T(8,128)S(1)}, u32[]{:S(2)}, u32[]{:S(2)}) collective-permute-start(f32[40,512]{1,0:T(8,128)S(1)} %add.255), channel_id=1, source_target_pairs={{0,6},{1,7},{2,4},{3,5},{4,2},{5,3},{6,0},{7,1},{8,14},{9,15},{10,... | collective-permute-start | bytes 245768 | tf_op jit(solution)/shard_map/ppermute | solution.py:496
  347.3 8.0 %collective-permute-start.59 = (f32[256,1024]{1,0:T(8,128)}, f32[256,1024]{1,0:T(8,128)S(1)}, u32[]{:S(2)}, u32[]{:S(2)}) collective-permute-start(f32[256,1024]{1,0:T(8,128)} %collective-permute-done.47.refs_2_), channel_id=1, source_target_pairs={{0,1},{1,0},{2,3},{3,2},{4,5},{5,4},{6,7},{7,6},{8,9},{9,8},{10,11... | collective-permute-start | bytes 3145736 | tf_op jit(solution)/shard_map/ppermute | solution.py:496
  347.3 12.5 %collective-permute-start.53 = (f32[128,2048]{1,0:T(8,128)S(1)}, f32[128,2048]{1,0:T(8,128)S(1)}, u32[]{:S(2)}, u32[]{:S(2)}) collective-permute-start(f32[128,2048]{1,0:T(8,128)S(1)} %get-tuple-element.573.refs_1_), channel_id=1, source_target_pairs={{0,1},{1,0},{2,3},{3,2},{4,5},{5,4},{6,7},{7,6},{8,9},{9,8},{10,11... | collective-permute-start | bytes 3145736 | tf_op jit(solution)/shard_map/ppermute | solution.py:496
  347.8 12.0 %collective-permute-start.54 = (f32[128,2048]{1,0:T(8,128)S(1)}, f32[128,2048]{1,0:T(8,128)S(1)}, u32[]{:S(2)}, u32[]{:S(2)}) collective-permute-start(f32[128,2048]{1,0:T(8,128)S(1)} %copy-done.6), channel_id=1, source_target_pairs={{0,1},{1,0},{2,3},{3,2},{4,5},{5,4},{6,7},{7,6},{8,9},{9,8},{10,11... | collective-permute-start | bytes 3145736 | tf_op jit(solution)/shard_map/ppermute | solution.py:496
  348.6 11.2 %collective-permute-start.55 = (f32[128,1152]{1,0:T(8,128)S(1)}, f32[128,1152]{1,0:T(8,128)S(1)}, u32[]{:S(2)}, u32[]{:S(2)}) collective-permute-start(f32[128,1152]{1,0:T(8,128)S(1)} %placed.11.refs_3_), channel_id=1, source_target_pairs={{0,1},{1,0},{2,3},{3,2},{4,5},{5,4},{6,7},{7,6},{8,9},{9,8},{10,11... | collective-permute-start | bytes 1769480 | tf_op jit(solution)/shard_map/ppermute | solution.py:496
  349.1 10.8 %collective-permute-start.57 = (f32[128,1152]{1,0:T(8,128)}, f32[128,1152]{1,0:T(8,128)S(1)}, u32[]{:S(2)}, u32[]{:S(2)}) collective-permute-start(f32[128,1152]{1,0:T(8,128)} %collective-permute-done.56.refs_4_), channel_id=1, source_target_pairs={{0,1},{1,0},{2,3},{3,2},{4,5},{5,4},{6,7},{7,6},{8,9},{9,8},{10,11... | collective-permute-start | bytes 1769480 | tf_op jit(solution)/shard_map/ppermute | solution.py:496
  (42 other events, 310.4 us)

commit v3 on v2

--- a/solution.py
+++ b/solution.py
@@ -14,8 +14,9 @@
 
 epsilon = 1e-05
 very_low = -1e30
-scan_params = pltpu.CompilerParams(vmem_limit_bytes=48 * 2**20)
-dense_params = pltpu.CompilerParams(vmem_limit_bytes=56 * 2**20)
+scan_params = pltpu.CompilerParams(vmem_limit_bytes=20 * 2**20)
+front_params = pltpu.CompilerParams(vmem_limit_bytes=52 * 2**20)
+dense_params = pltpu.CompilerParams(vmem_limit_bytes=36 * 2**20)
 
 
 def work_cost(flops, seconds):
@@ -123,20 +124,20 @@
             jax.ShapeDtypeStruct((states, rows, width), jnp.float32),
         ),
         scratch_shapes=[pltpu.VMEM((states, rows, width), jnp.float32)],
-        compiler_params=scan_params,
+        compiler_params=front_params,
         cost_estimate=work_cost(0.0, 9e-6),
         name="enter",
     )(counts, tokens, gain, retain)
 
 
-def average_body(turned_ref, retain_ref, mix_ref, start_ref, out_ref, end_ref, state):
+def average_body(turned_ref, retain_ref, mix_ref, held_ref, state, out_ref):
     step = pl.program_id(0)
     steps, rows, width = turned_ref.shape
     states = retain_ref.shape[0]
 
     @pl.when(step == 0)
     def _():
-        state[...] = start_ref[...]
+        state[...] = held_ref[...]
 
     for lanes in lane_slices(width):
         retain = [spread_rows(retain_ref, j, lanes, rows) for j in range(states)]
@@ -156,10 +157,6 @@
         )
         for j in range(states):
             state[j, :, lanes] = hidden[j]
-
-    @pl.when(step == pl.num_programs(0) - 1)
-    def _():
-        end_ref[...] = state[...]
 
 
 def average_call(turned, retain, mix, start):
@@ -176,15 +173,14 @@
             whole_spec(held),
         ],
         out_specs=(
+            whole_spec(held),
             pl.BlockSpec((rows, STEPS, width), lambda step: (0, step, 0)),
-            whole_spec(held),
         ),
         out_shape=(
+            jax.ShapeDtypeStruct(held, jnp.float32),
             jax.ShapeDtypeStruct((rows, length, width), jnp.float32),
-            jax.ShapeDtypeStruct(held, jnp.float32),
         ),
-        scratch_shapes=[pltpu.VMEM(held, jnp.float32)],
-        compiler_params=scan_params,
+        compiler_params=front_params,
         cost_estimate=work_cost(0.0, 12e-6),
         name="average",
     )(turned, retain, mix, start)
@@ -342,13 +338,10 @@
     retain_ref,
     mix_ref,
     held_ref,
-    _,
-    carry_ref,
-    out_ref,
-    path,
-    *,
+    *others,
     places_before,
 ):
+    carry_ref, out_ref, path = others[-3:]
     step = pl.program_id(0)
     steps, rows, width = grad_ref.shape
     states = retain_ref.shape[0]
@@ -390,11 +383,12 @@
 
 
 def leave_call(
-    low_end, high_end, counts, tokens, gain, part, grad, retain, mix, carried
+    low_end, high_end, counts, tokens, gain, part, residual, grad, retain, mix, carried
 ):
     rows, length, width = tokens.shape
     held = carried[0].shape
     last = high_end // STEPS - 1
+    going_on = len(carried) > 1
     natural = pl.BlockSpec((rows, STEPS, width), lambda step: (0, last - step, 0))
     return pl.pallas_call(
         functools.partial(leave_body, places_before=low_end),
@@ -409,19 +403,19 @@
             whole_spec(retain.shape),
             whole_spec(mix.shape),
             whole_spec(held),
-            pl.BlockSpec(memory_space=pl.ANY),
-        ],
+        ]
+        + [pl.BlockSpec(memory_space=pl.ANY)] * going_on,
         out_specs=[whole_spec(held), natural],
         out_shape=[
             jax.ShapeDtypeStruct(held, jnp.float32),
             jax.ShapeDtypeStruct((rows, length, width), jnp.bfloat16),
         ],
-        input_output_aliases={9: 1},
+        input_output_aliases={9: 1} if going_on else {},
         scratch_shapes=[pltpu.VMEM((rows, STEPS, width), jnp.float32)],
         compiler_params=scan_params,
         cost_estimate=work_cost(0.0, 8e-6),
         name="leave",
-    )(counts, tokens, gain, part, carried[1], grad, retain, mix, *carried)
+    )(counts, tokens, gain, part, residual, grad, retain, mix, *carried)
 
 
 class Exchange:
@@ -517,8 +511,8 @@
         core, x, y, z_low, z_high = bits
         return (
             (core, x, y, z_low, z_high),
-            (core, y, z_low, z_high, x),
-            (core, z_low, z_high, x, y),
+            (core, y, z_low, x, z_high),
+            (core, z_low, x, y, z_high),
         )
     third = len(bits) // 3
     return tuple(bits[turn * third :] + bits[: turn * third] for turn in range(3))
@@ -582,14 +576,45 @@
     return [slice(at, min(at + size, high_end)) for at in range(low_end, high_end, size)]
 
 
+def gated(value):
+    half = 0.5 * value
+    turn = jnp.tanh(half)
+    gate = 0.5 * turn + 0.5
+    act = half * turn + half
+    return act, gate + act * (1.0 - gate)
+
+
+def value_body(normed_ref, value_weight_ref, value_ref, value_slope_ref):
+    for part in chunks(0, value_ref.shape[1], 256):
+        value, slope = gated(low(dot(normed_ref[...], value_weight_ref[:, part])))
+        value_ref[:, part] = low(value)
+        value_slope_ref[:, part] = low(slope)
+
+
+def value_call(normed, value_weight):
+    rows, length, width = normed.shape
+    vdim = value_weight.shape[1]
+    return pl.pallas_call(
+        value_body,
+        grid=(rows,),
+        in_specs=[row_spec(length, width), once_spec(value_weight.shape)],
+        out_specs=[row_spec(length, vdim)] * 2,
+        out_shape=[jax.ShapeDtypeStruct((rows, length, vdim), jnp.bfloat16)] * 2,
+        compiler_params=front_params,
+        cost_estimate=work_cost(2e9, 5e-6),
+        name="value",
+    )(normed, value_weight)
+
+
 def forward_body(
     count_ref,
     tokens_ref,
     cotangent_ref,
     average_ref,
     normed_ref,
+    value_ref,
+    value_slope_ref,
     omega_ref,
-    value_weight_ref,
     base_weight_ref,
     gains_ref,
     biases_ref,
@@ -600,24 +625,25 @@
     out_ref,
     mixed_ref,
     mixed_slope_ref,
-    value_ref,
-    value_slope_ref,
+    product_ref,
+    ffn_low_ref,
+    act_ref,
+    grad_inner_ref,
+    grad_proj_ref,
+    grad_main_ref,
+    grad_shared_ref,
+    grad_vpre_ref,
+    residual_ref,
+    ffn_gain_grad_ref,
+    grad_gains_ref,
+    reset_ref,
+    reset_slope_ref,
+    grad_attended_ref,
     probs_ref,
     query_ref,
     key_ref,
     shared_ref,
     shared_slope_ref,
-    product_ref,
-    ffn_low_ref,
-    act_ref,
-    grad_inner_ref,
-    grad_proj_ref,
-    grad_attended_ref,
-    grad_main_ref,
-    residual_ref,
-    ffn_gain_grad_ref,
-    reset_ref,
-    reset_slope_ref,
 ):
     row = pl.program_id(0)
     length, width = tokens_ref.shape
@@ -628,6 +654,7 @@
     @pl.when(row == 0)
     def _():
         ffn_gain_grad_ref[...] = jnp.zeros_like(ffn_gain_grad_ref)
+        grad_gains_ref[...] = jnp.zeros_like(grad_gains_ref)
 
     normed = normed_ref[...]
     sums = average_ref[...] + omega_ref[...] * normed.astype(jnp.float32)
@@ -644,13 +671,6 @@
     shared_slope_ref[...] = gate + shared_act * (1.0 - gate)
     query_ref[...] = low(shared_act * gains_ref[0:1] + biases_ref[0:1])
     key_ref[...] = low(shared_act * gains_ref[1:2] + biases_ref[1:2])
-
-    for part in chunks(0, vdim, 256):
-        value_pre = dot(normed, value_weight_ref[:, part])
-        gate = sigmoid(value_pre)
-        value = value_pre * gate
-        value_ref[:, part] = low(value)
-        value_slope_ref[:, part] = low(gate + value * (1.0 - gate))
 
     to_place = lax.broadcasted_iota(jnp.int32, (GROUP, GROUP), 0)
     from_place = lax.broadcasted_iota(jnp.int32, (GROUP, GROUP), 1)
@@ -666,13 +686,10 @@
 
     for part in chunks(0, vdim, 256):
         base_part = slice(zdim + part.start, zdim + part.stop)
-        reset = dot(mixed_low, base_weight_ref[:, base_part])
-        gate = sigmoid(reset)
-        reset_act = reset * gate
-        reset_slope = gate + reset_act * (1.0 - gate)
+        reset_act, reset_slope = gated(low(dot(mixed_low, base_weight_ref[:, base_part])))
         reset_ref[:, part] = low(reset_act)
         for block in chunks(0, length, GROUP):
-            attended = dot(low(probs_ref[block]), value_ref[block, part])
+            attended = low(dot(low(probs_ref[block]), value_ref[block, part]))
             product_ref[block, part] = low(attended * reset_act[block])
             reset_slope_ref[block, part] = low(attended * reset_slope[block])
 
@@ -693,12 +710,9 @@
     out = after
     grad_normed = jnp.zeros_like(after)
     for part in chunks(0, inner, 256):
-        inner_pre = dot(ffn_low, ffn_in_ref[:, part])
-        gate = sigmoid(inner_pre)
-        act = inner_pre * gate
-        slope = gate + act * (1.0 - gate)
+        act, slope = gated(low(dot(ffn_low, ffn_in_ref[:, part])))
         act_ref[:, part] = low(act)
-        grad_act = dot_back(cotangent, ffn_out_ref[part])
+        grad_act = low(dot_back(cotangent, ffn_out_ref[part]))
         grad_inner_ref[:, part] = low(grad_act * slope)
     out = after + dot(act_ref[...], ffn_out_ref[...])
     out_ref[...] = low(out)
@@ -713,120 +727,9 @@
     grad_main_ref[:, vdim : vdim + width] = low(grad_change * change * (1.0 - update_gate))
     grad_main_ref[:, vdim + width :] = grad_proj
     for part in chunks(0, vdim, 256):
-        grad_product = dot_back(grad_proj, output_weight_ref[part])
-        grad_attended_ref[:, part] = low(grad_product * reset_ref[:, part].astype(jnp.float32))
-        grad_main_ref[:, part] = low(grad_product * reset_slope_ref[:, part].astype(jnp.float32))
-    residual_ref[...] = low(grad_after - grad_change)
-
-
-def row_spec(length, width):
-    return pl.BlockSpec((None, length, width), lambda row: (row, 0, 0))
-
-
-def once_spec(shape):
-    return pl.BlockSpec(shape, lambda row: (0,) * len(shape), pipeline_mode=pl.Buffered(1))
-
-
-def forward_call(
-    counts,
-    tokens,
-    cotangent,
-    average,
-    normed,
-    omega,
-    value_weight,
-    base_weight,
-    gains,
-    biases,
-    output_weight,
-    ffn_gain,
-    ffn_in,
-    ffn_out,
-):
-    rows, length, width = tokens.shape
-    zdim, vdim, inner = gains.shape[1], value_weight.shape[1], ffn_in.shape[1]
-    half, full = jnp.bfloat16, jnp.float32
-    outs = [
-        (width, half),
-        (width, half),
-        (width, half),
-        (vdim, half),
-        (vdim, half),
-        (GROUP, full),
-        (zdim, half),
-        (zdim, half),
-        (zdim, full),
-        (zdim, full),
-        (vdim, half),
-        (width, half),
-        (inner, half),
-        (inner, half),
-        (width, half),
-        (vdim, half),
-        (vdim + 2 * width, half),
-        (width, half),
-    ]
-    tied = [
-        omega,
-        value_weight,
-        base_weight,
-        gains,
-        biases,
-        output_weight,
-        ffn_gain,
-        ffn_in,
-        ffn_out,
-    ]
-    return pl.pallas_call(
-        forward_body,
-        grid=(rows,),
-        in_specs=[pl.BlockSpec(memory_space=pltpu.SMEM)]
-        + [row_spec(length, width)] * 4
-        + [once_spec(value.shape) for value in tied],
-        out_specs=[row_spec(length, size) for size, _ in outs] + [whole_spec((1, width))],
-        out_shape=[jax.ShapeDtypeStruct((rows, length, size), kind) for size, kind in outs]
-        + [jax.ShapeDtypeStruct((1, width), full)],
-        scratch_shapes=[pltpu.VMEM((length, vdim), half)] * 2,
-        compiler_params=dense_params,
-        cost_estimate=work_cost(18e9, 40e-6),
-        name="dense_forward",
-    )(counts, tokens, cotangent, average, normed, *tied)
-
-
-def backward_body(
-    grad_attended_ref,
-    grad_main_ref,
-    normed_ref,
-    mixed_slope_ref,
-    value_ref,
-    value_slope_ref,
-    probs_ref,
-    query_ref,
-    key_ref,
-    shared_ref,
-    shared_slope_ref,
-    omega_ref,
-    gains_ref,
-    value_weight_ref,
-    base_weight_ref,
-    grad_shared_ref,
-    grad_vpre_ref,
-    grad_average_ref,
-    part_ref,
-    grad_gains_ref,
-    grad_omega_ref,
-    grad_gain_ref,
-):
-    row = pl.program_id(0)
-    length = grad_attended_ref.shape[0]
-    zdim = query_ref.shape[1]
-    vdim = value_ref.shape[1]
-
-    @pl.when(row == 0)
-    def _():
-        grad_gains_ref[...] = jnp.zeros_like(grad_gains_ref)
-        grad_omega_ref[...] = jnp.zeros_like(grad_omega_ref)
-        grad_gain_ref[...] = jnp.zeros_like(grad_gain_ref)
+        grad_product = low(dot_back(grad_proj, output_weight_ref[part]))
+        grad_attended_ref[:, part] = low(grad_product * reset_ref[:, part])
+        grad_main_ref[:, part] = low(grad_product * reset_slope_ref[:, part])
 
     grad_gains = jnp.zeros(grad_gains_ref.shape, jnp.float32)
     for block in chunks(0, length, GROUP):
@@ -835,9 +738,7 @@
         grad_probs = dot_back(grad_attended_ref[block], value_ref[block])
         for part in chunks(0, vdim, 512):
             grad_value = dot_outer(probs_low, grad_attended_ref[block, part])
-            grad_vpre_ref[block, part] = low(
-                grad_value * value_slope_ref[block, part].astype(jnp.float32)
-            )
+            grad_vpre_ref[block, part] = low(low(grad_value) * value_slope_ref[block, part])
         total = jnp.sum(grad_probs * probs, axis=-1, keepdims=True)
         grad_raw = low(probs * (grad_probs - total) * zdim**-0.5)
         grad_query = dot(grad_raw, key_ref[block])
@@ -853,6 +754,103 @@
         grad_shared = grad_query * gains_ref[0:1] + grad_key * gains_ref[1:2]
         grad_shared_ref[block] = low(grad_shared * shared_slope_ref[block])
     grad_gains_ref[...] += grad_gains
+    residual_ref[...] = low(grad_after - grad_change)
+
+
+def row_spec(length, width):
+    return pl.BlockSpec((None, length, width), lambda row: (row, 0, 0))
+
+
+def once_spec(shape):
+    return pl.BlockSpec(shape, lambda row: (0,) * len(shape), pipeline_mode=pl.Buffered(1))
+
+
+def forward_call(
+    counts,
+    tokens,
+    cotangent,
+    average,
+    normed,
+    value,
+    value_slope,
+    omega,
+    base_weight,
+    gains,
+    biases,
+    output_weight,
+    ffn_gain,
+    ffn_in,
+    ffn_out,
+):
+    rows, length, width = tokens.shape
+    zdim, vdim, inner = gains.shape[1], value.shape[2], ffn_in.shape[1]
+    half, full = jnp.bfloat16, jnp.float32
+    outs = [
+        (width, half),
+        (width, half),
+        (width, half),
+        (vdim, half),
+        (width, half),
+        (inner, half),
+        (inner, half),
+        (width, half),
+        (vdim + 2 * width, half),
+        (zdim, half),
+        (vdim, half),
+        (width, half),
+    ]
+    tied = [
+        omega,
+        base_weight,
+        gains,
+        biases,
+        output_weight,
+        ffn_gain,
+        ffn_in,
+        ffn_out,
+    ]
+    return pl.pallas_call(
+        forward_body,
+        grid=(rows,),
+        in_specs=[pl.BlockSpec(memory_space=pltpu.SMEM)]
+        + [row_spec(length, width)] * 4
+        + [row_spec(length, vdim)] * 2
+        + [once_spec(weight.shape) for weight in tied],
+        out_specs=[row_spec(length, size) for size, _ in outs]
+        + [whole_spec((1, width)), whole_spec((4, zdim))],
+        out_shape=[jax.ShapeDtypeStruct((rows, length, size), kind) for size, kind in outs]
+        + [jax.ShapeDtypeStruct((1, width), full), jax.ShapeDtypeStruct((4, zdim), full)],
+        scratch_shapes=[pltpu.VMEM((length, vdim), half)] * 3
+        + [pltpu.VMEM((length, GROUP), full)]
+        + [pltpu.VMEM((length, zdim), half)] * 2
+        + [pltpu.VMEM((length, zdim), full)] * 2,
+        compiler_params=dense_params,
+        cost_estimate=work_cost(18e9, 40e-6),
+        name="dense_forward",
+    )(counts, tokens, cotangent, average, normed, value, value_slope, *tied)
+
+
+def backward_body(
+    grad_main_ref,
+    grad_shared_ref,
+    grad_vpre_ref,
+    normed_ref,
+    mixed_slope_ref,
+    omega_ref,
+    value_weight_ref,
+    base_weight_ref,
+    grad_average_ref,
+    part_ref,
+    grad_omega_ref,
+    grad_gain_ref,
+):
+    zdim = grad_shared_ref.shape[1]
+
+    @pl.when(pl.program_id(0) == 0)
+    def _():
+        grad_omega_ref[...] = jnp.zeros_like(grad_omega_ref)
+        grad_gain_ref[...] = jnp.zeros_like(grad_gain_ref)
+
     grad_average = dot_back(grad_main_ref[...], base_weight_ref[:, zdim:])
     grad_average = grad_average + dot_back(grad_shared_ref[...], base_weight_ref[:, :zdim])
     grad_average = grad_average * mixed_slope_ref[...].astype(jnp.float32)
@@ -865,31 +863,18 @@
 
 
 def backward_call(inputs, tied_inputs):
-    rows, length, vdim = inputs[0].shape
-    omega, gains, _, _ = tied_inputs
-    width, zdim = omega.shape[1], gains.shape[1]
-    outs = [
-        (zdim, jnp.bfloat16),
-        (vdim, jnp.bfloat16),
-        (width, jnp.float32),
-        (width, jnp.float32),
-    ]
+    rows, length, _ = inputs[0].shape
+    width = tied_inputs[0].shape[1]
     return pl.pallas_call(
         backward_body,
         grid=(rows,),
         in_specs=[row_spec(length, value.shape[2]) for value in inputs]
         + [once_spec(value.shape) for value in tied_inputs],
-        out_specs=[row_spec(length, size) for size, _ in outs]
-        + [whole_spec((4, zdim))]
-        + [whole_spec((1, width))] * 2,
-        out_shape=[jax.ShapeDtypeStruct((rows, length, size), kind) for size, kind in outs]
-        + [
-            jax.ShapeDtypeStruct((4, zdim), jnp.float32),
-            jax.ShapeDtypeStruct((1, width), jnp.float32),
-            jax.ShapeDtypeStruct((1, width), jnp.float32),
-        ],
+        out_specs=[row_spec(length, width)] * 2 + [whole_spec((1, width))] * 2,
+        out_shape=[jax.ShapeDtypeStruct((rows, length, width), jnp.float32)] * 2
+        + [jax.ShapeDtypeStruct((1, width), jnp.float32)] * 2,
         compiler_params=dense_params,
-        cost_estimate=work_cost(10e9, 25e-6),
+        cost_estimate=work_cost(7e9, 12e-6),
         name="dense_backward",
     )(*inputs, *tied_inputs)
 
@@ -1024,7 +1009,7 @@
         where += [low, 1 - low]
     core = (device_place() // chains[0].order[0]) % 2
     where.append(core if before is None else 1 - core)
-    steps = 2
+    steps = 4
     in_specs = []
     for at, value in enumerate(values):
 
@@ -1173,36 +1158,35 @@
     ahead = Exchange(device_end, span_decay, "seq", False)
     ahead.share()
     ahead.cross()
+    value, value_slope = value_call(normed, value_weight)
+    ahead.start, value, value_slope = lax.optimization_barrier((ahead.start, value, value_slope))
     incoming = ahead.give()
-    average, state_end = average_call(turned, retain, mix, incoming)
+    state_end, average = average_call(turned, retain, mix, incoming)
+    unit_decay = power_of(retain, LAG)
     (
         block_out,
         mixed,
         mixed_slope,
-        value,
-        value_slope,
-        probs,
-        query,
-        key,
-        shared,
-        shared_slope,
         product,
         ffn_low,
         act,
         grad_inner,
         grad_proj,
-        grad_attended,
         grad_main,
+        grad_shared,
+        grad_vpre,
         residual,
         grad_ffn_gain,
+        grad_query_key,
     ) = forward_call(
         counts,
         tokens,
         cotangent,
         average,
         normed,
+        value,
+        value_slope,
         omega,
-        value_weight,
         base_weight,
         gains,
         biases,
@@ -1211,75 +1195,44 @@
         ffn_in,
         ffn_out,
     )
-    back_inputs = [
-        grad_attended,
-        grad_main,
-        normed,
-        mixed_slope,
-        value,
-        value_slope,
-        probs,
-        query,
-        key,
-        shared,
-        shared_slope,
-    ]
     orders = link_orders()
+    core = orders[0][0]
     chained = device_total() == 32
-    early, late, chains = [], None, []
+    chains = []
+    back_inputs = [grad_main, grad_shared, grad_vpre, normed, mixed_slope]
     if chained:
-        core = orders[0][0]
-        sums = [
-            weight_halves(act, cotangent, core),
-            weight_halves(product, grad_proj, core),
-            weight_halves(mixed, grad_main, core),
-            weight_halves(ffn_low, grad_inner, core),
+        products = [
+            [(act, cotangent), (product, grad_proj)],
+            [(mixed, grad_main)],
+            [(ffn_low, grad_inner), (normed, grad_vpre), (mixed, grad_shared)],
         ]
-        outs = Chain(orders[0], [sums[0][0], sums[1][0]], [sums[0][1], sums[1][1]])
-        main = Chain(orders[1], [sums[2][0]], [sums[2][1]])
-        inner = Chain(orders[2], [sums[3][0]], [sums[3][1]])
-        early = [outs, main, inner]
-        for one in early:
+        halves = [[weight_halves(*pair, core) for pair in pairs] for pairs in products]
+        for order, pairs in zip(orders, halves):
+            chains.append(Chain(order, [pair[0] for pair in pairs], [pair[1] for pair in pairs]))
+            chains[-1].send()
+        join(*chains)
+        back_inputs = tied(back_inputs, *chains)
+        for one in chains:
             one.send()
-        join(*early)
-        back_inputs = tied(back_inputs, *early)
-        for one in early:
-            one.send()
-    back_outputs = backward_call(back_inputs, [omega, gains, value_weight, base_weight])
-    if chained:
-        back_outputs = tied(back_outputs, *early)
-        join(*early)
-        back_outputs = tied(back_outputs, *early)
-        for one in early:
-            one.send()
-    grad_shared, grad_vpre, grad_average, part, grad_query_key, grad_omega, grad_gain = (
-        back_outputs
+    grad_average, part, grad_omega, grad_gain = backward_call(
+        back_inputs, [omega, value_weight, base_weight]
     )
-    if chained:
-        sums = [weight_halves(normed, grad_vpre, core), weight_halves(mixed, grad_shared, core)]
-        late = Chain(orders[0], [sums[0][0], sums[1][0]], [sums[0][1], sums[1][1]])
-        chains = [late, *early]
-        grad_average = tied(grad_average, late)
-        late.send()
-
-    def halve(value, *moving):
+
+    def halve(value):
         if chained:
             value = tied(value, *chains)
-            if early[0] in moving:
-                join(*early)
-            join(late)
+            join(*chains)
             value = tied(value, *chains)
-            for one in moving:
+            for one in chains:
                 one.send()
         return value
 
     grad_turned, device_start = return_call(grad_average, retain)
     behind = Exchange(device_start, span_decay, "seq", True)
-    behind.local = halve(behind.local, late, *early)
     behind.share()
-    behind.pair = halve(behind.pair, late)
+    behind.pair = halve(behind.pair)
     behind.cross()
-    behind.start = halve(behind.start, late, *early)
+    behind.start = halve(behind.start)
     later = behind.give()
     states = retain.shape[0]
     carried = [
@@ -1287,21 +1240,36 @@
         jnp.zeros((LAG,) + later.shape[1:], jnp.float32),
     ]
     parts = length // STEPS
-    inverse, unit_decay = 1.0 / retain, power_of(retain, LAG)
-    ends = [at * STEPS for at in (parts, 5 * parts // 8, 2 * parts // 8, 0)]
+    inverse = 1.0 / retain
+    ends = [at * STEPS // 8 for at in (8 * parts, 5 * parts, 2 * parts, 0)]
+    ends = [at // STEPS * STEPS for at in ends]
     for high_end, low_end in zip(ends, ends[1:]):
-        carried = halve(carried, late, *early)
+        carried = halve(carried)
         carried = sums_call(
             low_end, high_end, grad_turned, turned, [retain, inverse, unit_decay], carried
         )
-    (_, _, cross, border), lags = carried
-    left = [later, residual]
-    if chained:
-        left = halve([left, cross], late, *early)
-        left, cross = left
-    cross = jnp.sum(cross, axis=1)
+    carry, lags = carried
+    ends = [at * STEPS for at in (parts, 5 * parts // 8, 0)]
+    left = [later]
+    for high_end, low_end in zip(ends, ends[1:]):
+        left, carry, lags = halve((left, carry, lags))
+        left = leave_call(
+            low_end,
+            high_end,
+            counts,
+            tokens,
+            norm_gain,
+            part,
+            residual,
+            grad_turned,
+            retain,
+            mix,
+            left,
+        )
+    left, carry, lags = lax.optimization_barrier((left, carry, lags))
+    cross, border = jnp.sum(carry[2:], axis=2)
     lags = jnp.sum(lags, axis=1)
-    paired = retain * jnp.sum(border, axis=1)
+    paired = retain * border
     decay = jnp.ones_like(retain)
     for lag in range(LAG):
         paired = paired + decay * lags[lag]
@@ -1319,27 +1287,16 @@
     )
     used = small.shape[0]
     small = jnp.pad(small, ((0, -used % 8), (0, 0)))
-    ends = [at * STEPS for at in (parts, 5 * parts // 8, 3 * parts // 8, 0)]
+    grad_tokens = left[1]
     if chained:
-        core, _, _, z_low, z_high = orders[0]
-        first_bits = [core, z_high, z_low]
-    for turn, (high_end, low_end) in enumerate(zip(ends, ends[1:])):
-        if chained:
-            left, small = lax.optimization_barrier((left, small))
-            small = small + swapped(small, first_bits[turn])
-        left = leave_call(
-            low_end, high_end, counts, tokens, norm_gain, part, grad_turned, retain, mix, left
-        )
-    if chained:
-        left, small = tied((left, small), *chains)
-        for one in early:
+        small = tied(small, *chains)
+        small = small + swapped(small, core)
+        for one in chains:
             one.give()
-        join(late)
-        late.send()
         small = paired_sum(small, orders[0][1:3])
+        small = paired_sum(small, orders[0][3:5])
     else:
         small = small_sum(small)
-    grad_tokens = left[1]
     paired, cross = small[:states], small[states : 2 * states]
     grad_gain, grad_omega, grad_ffn_gain = (small[2 * states + at] for at in range(3))
     grad_norm_gain = (grad_gain + jnp.sum(mix * paired, axis=0)) / norm_gain[0]
@@ -1349,33 +1306,29 @@
     grad_forget = (eta * paired * beta * (1.0 - forget) / gate - mix * cross).T
     vdim = value_weight.shape[1]
     if chained:
-        outs, main, inner = early
-        zdim = gains.shape[1]
-        groups = [
-            (
-                [outs, inner],
-                [
-                    (0, slice(0, width), 0, 0),
-                    (0, slice(width, 2 * width), 1, 0),
-                    (1, slice(0, ffn_in.shape[1]), 2, 0),
-                ],
-                [ffn_out.shape, output_weight.shape, ffn_in.shape],
-            ),
-            (
-                [main, late],
-                [
-                    (0, slice(0, grad_main.shape[-1]), 0, zdim),
-                    (1, slice(0, vdim), 1, 0),
-                    (1, slice(vdim, vdim + zdim), 0, 0),
-                ],
-                [base_weight.shape, value_weight.shape],
-            ),
+        zdim, main_end, inner_dim = gains.shape[1], grad_main.shape[-1], ffn_in.shape[1]
+        copies = [
+            (0, slice(0, width), 0, 0),
+            (0, slice(width, 2 * width), 1, 0),
+            (1, slice(0, main_end), 2, zdim),
+            (2, slice(inner_dim + vdim, inner_dim + vdim + zdim), 2, 0),
+            (2, slice(0, inner_dim), 3, 0),
+            (2, slice(inner_dim, inner_dim + vdim), 4, 0),
         ]
-        first = gathered(*groups[0])
-        late.give()
-        second = gathered(*groups[1])
-        grad_ffn_out, grad_output_weight, grad_ffn_in = gathered(*groups[0], first)
-        grad_base_weight, grad_value_weight = gathered(*groups[1], second)
+        shapes = [
+            ffn_out.shape,
+            output_weight.shape,
+            base_weight.shape,
+            ffn_in.shape,
+            value_weight.shape,
+        ]
+        (
+            grad_ffn_out,
+            grad_output_weight,
+            grad_base_weight,
+            grad_ffn_in,
+            grad_value_weight,
+        ) = gathered(chains, copies, shapes, gathered(chains, copies, shapes))
     else:
         grad_base = jnp.concatenate([grad_shared, grad_main], axis=-1)
         (

time: 364 us -> 329 us (0.904)
  starting transfers between devices: 78.4 us -> 52.6 us
  Pallas kernels: 171 us -> 155 us
  waiting for transfers between devices: 52.4 us -> 66.4 us
  matrix products: 28.8 us -> 21.7 us
  local copies, waits for them, and re-layouts: 23.3 us -> 18.7 us
  other arithmetic: 7.52 us -> 11.3 us
    ppermute x52 -> x43, starting transfers between devices: 58 us -> 33.9 us  [swapped(): lax.ppermute(value, mesh_axes, [(at, at ^ bit) for at in range(device_tot...]
    ppermute x10, waiting for transfers between devices: 15.3 us -> 32.9 us  [moved(): return lax.ppermute(value, self.axis, pairs)]
    pallas_call x1, Pallas kernels: 21.2 us -> 11.2 us  [backward_call(): pl.pallas_call(backward_body, grid=(rows,), in_specs=[row_spec(length, va...]
    pallas_call x0 -> x1, Pallas kernels: none -> 8.45 us  [value_call(): pl.pallas_call(value_body, grid=(rows,), in_specs=[row_spec(length, width...]
    dot_general x12, matrix products: 28.8 us -> 21.7 us  [dot_outer(): lax.dot_general(first_op, second_op, (((0,), (0,)), ((), ())), preferred_...]
    pallas_call x10 -> x5, Pallas kernels: 13.7 us -> 7.84 us  [joined(): pl.pallas_call(functools.partial(joined_body, widths=widths, split=split)...]
    unnamed x91 -> x112, local copies, waits for them, and re-layouts: 21 us -> 16.5 us
    pallas_call x3, Pallas kernels: 24.4 us -> 20.7 us  [sums_call(): pl.pallas_call(sums_body, grid=((high_end - low_end) // STEPS,), in_specs...]
  transfers between devices with their start and end apart: 62 -> 53, of which waited for: 16 -> 23; matrix products, arithmetic and copies ran while one was open for 8% -> 9% of each run, Pallas kernels for 24% -> 22%
where the time goes in v3:
time: 329 us; the launch traced here: 328 us
  Pallas kernels  155 us (47%)
  waiting for transfers between devices  66.4 us (20%)
  starting transfers between devices  52.6 us (16%)
  matrix products  21.7 us (7%)
  local copies, waits for them, and re-layouts  18.7 us (6%)
  other arithmetic  11.3 us (3%)
    pallas_call x1, Pallas kernels, forward_call(): pl.pallas_call(forward_body, grid=(rows,), in_specs=[pl.BlockSpec(memory_...  41.3 us
    ppermute x43, starting transfers between devices, swapped(): lax.ppermute(value, mesh_axes, [(at, at ^ bit) for at in range(device_tot...  33.9 us
    ppermute x43, waiting for transfers between devices, swapped(): lax.ppermute(value, mesh_axes, [(at, at ^ bit) for at in range(device_tot...  33.4 us
    ppermute x10, waiting for transfers between devices, moved(): return lax.ppermute(value, self.axis, pairs)  32.9 us
    dot_general x12, matrix products, dot_outer(): lax.dot_general(first_op, second_op, (((0,), (0,)), ((), ())), preferred_...  21.7 us
    pallas_call x3, Pallas kernels, sums_call(): pl.pallas_call(sums_body, grid=((high_end - low_end) // STEPS,), in_specs...  20.7 us
    ppermute x10, starting transfers between devices, moved(): return lax.ppermute(value, self.axis, pairs)  18.7 us
    pallas_call x2, Pallas kernels, leave_call(): pl.pallas_call(functools.partial(leave_body, places_before=low_end), grid...  16.8 us
  transfers between devices with their start and end apart: 53, of which 23 were waited for; matrix products, arithmetic and copies ran while one was open for 9% of the time, Pallas kernels for 22%

profile of v3, /device:TPU:0, one launch (start us, length us, event | category | flops | bytes accessed | tf_op | source)
XLA Modules:
  0.0 327.8 jit_solution(5094426156808768641)
XLA Ops:
  2.1 1.4 fusion.42
  3.5 10.3 %enter.1 = (bf16[8,256,512]{2,1,0:T(8,128)(2,1)}, f32[256,8,512]{2,1,0:T(8,128)}, f32[16,8,512]{2,1,0:T(8,128)S(1)}) custom-call(s32[8]{0:T(128)S(1)} %broadcast_subtract_fusion.count_ref, bf16[8,256,512]{2,1,0:T(8,128)(2,1)} %tokens_ref.7, f32[1,512]{1,0:T(1,128)S(1)} %bitcast.119, f32[16,512]{1,0:T(8,128)S(1)} %get-tuple-element.454.retain_ref), custom_call_target="tpu_custom_call" | custom-call | bytes 27000000 | tf_op jit(solution)/shard_map/enter/pallas_call | solution.py:107
  13.9 3.0 collective-permute-start
  17.5 2.9 collective-permute-done
  20.5 5.7 %collective-permute-start.1 = (f32[16,8,256]{2,1,0:T(8,128)S(1)}, f32[16,8,256]{2,1,0:T(8,128)S(1)}, u32[]{:S(2)}, u32[]{:S(2)}) collective-permute-start(f32[16,8,256]{2,1,0:T(8,128)S(1)} %select_add_fusion.1), channel_id=1, source_target_pairs={{0,24},{4,28},{1,25},{5,29},{2,26},{6,30},{3,27},{7,31}} | collective-permute-start | bytes 393224 | tf_op jit(solution)/shard_map/ppermute | solution.py:439
  26.2 1.3 collective-permute-start.2
  27.5 2.5 collective-permute-start.3
  30.0 8.4 %value.1 = (bf16[8,256,1024]{2,1,0:T(8,128)(2,1)}, bf16[8,256,1024]{2,1,0:T(8,128)(2,1)}) custom-call(bf16[8,256,512]{2,1,0:T(8,128)(2,1)} %get-tuple-element.252.normed_ref, bf16[512,1024]{1,0:T(8,128)(2,1)S(1)} %copy-done.32), custom_call_target="tpu_custom_call" | custom-call | flops 2000000000 | bytes 15000000 | tf_op jit(solution)/shard_map/value/pallas_call | solution.py:597
  38.6 1.6 collective-permute-start.4
  40.4 3.3 collective-permute-done.4
  43.8 12.7 %average.1 = (f32[16,8,512]{2,1,0:T(8,128)S(1)}, f32[8,256,512]{2,1,0:T(8,128)}) custom-call(f32[256,8,512]{2,1,0:T(8,128)} %get-tuple-element.223.turned_ref, f32[16,512]{1,0:T(8,128)S(1)} %get-tuple-element.454.retain_ref, f32[16,512]{1,0:T(8,128)S(1)} %get-tuple-element.453.mix_ref, f32[16,8,512]{2,1,0:T(8,128)S(1)} %pad_maximum_fusion.held_ref), custom_call_target="tpu_custom_call" | custom-call | bytes 36000000 | tf_op jit(solution)/shard_map/average/pallas_call | solution.py:166
  56.5 1.3 copy-done.30
  59.0 41.3 %dense_forward.1 = (bf16[8,256,512]{2,1,0:T(8,128)(2,1)}, bf16[8,256,512]{2,1,0:T(8,128)(2,1)S(1)}, bf16[8,256,512]{2,1,0:T(8,128)(2,1)S(1)}, bf16[8,256,1024]{2...) custom-call(s32[8]{0:T(128)S(1)} %broadcast_subtract_fusion.count_re, ...), custom_call_target="tpu_custom_call" | custom-call | flops 17999998976 | bytes 120000000 | tf_op jit(solution)/shard_map/dense_forward/pallas_call | solution.py:812
  100.9 4.5 %fusion.12 = f32[256,1024]{1,0:T(8,128)S(1)} fusion(bf16[2048,1024]{1,0:T(8,128)(2,1)} %bitcast.155, bf16[2048,512]{1,0:T(8,128)(2,1)S(1)} %bitcast.130, s32[]{:T(128)S(6)} %select_n.243), kind=kOutput, calls=%fused_computation.13 | convolution fusion | flops 1073741824 | bytes 6291460 | tf_op jit(solution)/shard_map/dot_general | solution.py:566
  105.8 2.4 fusion.18
  110.8 1.3 fusion
  113.0 1.3 fusion.2.refs_3_.refs_7_
  115.8 3.6 %fusion.14.refs_13_.refs_19_ = f32[256,1024]{1,0:T(8,128)S(1)} fusion(bf16[2048,1024]{1,0:T(8,128)(2,1)} %bitcast.156, bf16[2048,512]{1,0:T(8,128)(2,1)S(1)} %bitcast.131, s32[]{:T(128)S(6)} %select_n.242), kind=kOutput, calls=%fused_computation.15 | convolution fusion | flops 1073741824 | bytes 6291460 | tf_op jit(solution)/shard_map/dot_general | solution.py:566
  123.1 2.5 fusion.22.refs_9_.refs_11_
  125.7 2.8 joined.5
  130.6 1.5 collective-permute-start.12
  132.1 1.5 collective-permute-start.13
  133.6 11.2 %dense_backward.1 = (f32[8,256,512]{2,1,0:T(8,128)S(1)}, f32[8,256,512]{2,1,0:T(8,128)S(1)}, f32[1,512]{1,0:T(1,128)S(1)}, f32[1,512]{1,0:T(1,128)S(1)}) custom-call(bf16[8,256,2048]{2,1,0:T(8,128)(2,1)} %get-tuple-element.249.grad_main_ref, bf16[8,256,128]{2,1,0:T(8,128)(2,1)S(1)} %get-tuple-element.250.grad_shared_ref, ...), custom_call_target="tpu_custom_call" | custom-call | flops 7000000000 | bytes 36000000 | tf_op jit(solution)/shard_map/dense_backward/pallas_call | solution.py:868
  146.0 6.8 %back_enter.1 = (f32[256,8,512]{2,1,0:T(8,128)S(1)}, f32[16,8,512]{2,1,0:T(8,128)S(1)}) custom-call(f32[8,256,512]{2,1,0:T(8,128)S(1)} %get-tuple-element.256.grad_ref, f32[16,512]{1,0:T(8,128)S(1)} %get-tuple-element.454.retain_ref), custom_call_target="tpu_custom_call" | custom-call | bytes 24000000 | tf_op jit(solution)/shard_map/back_enter/pallas_call | solution.py:224
  152.8 2.0 copy-done
  156.0 4.9 %collective-permute-done.11 = f32[16,8,256]{2,1,0:T(8,128)} collective-permute-done((f32[16,8,256]{2,1,0:T(8,128)}, f32[16,8,256]{2,1,0:T(8,128)}, u32[]{:S(2)}, u32[]{:S(2)}) %collective-permute-start.11) | collective-permute-done | bytes 131104 | tf_op jit(solution)/shard_map/ppermute | solution.py:439
  164.4 3.4 %joined.6 = (f32[128,1024]{1,0:T(8,128)S(1)}, f32[128,1024]{1,0:T(8,128)S(1)}, f32[64,2048]{1,0:T(8,128)S(1)}, f32[64,2048]{1,0:T(8,128)S(1)}, f32[64,2176]{1,0:T(8,128)S(1)}, /*index=5*/f32[64,2176]{1,0:T(8,128)S(1)}) custom-call(s32[3]{0:T(128)S(1)} %get-tuple-element.465.refs_0_, f32[256,1024]{1,0:T(8,128)S(1)} %copy-done.10, ...), custom_call_target="tpu_custom_call" | custom-call | bytes 6000000 | tf_op jit(solution)/shard_map/joined/pallas_call | solution.py:926
  169.3 1.7 collective-permute-start.19
  172.3 1.3 collective-permute-start.16
  173.6 14.6 %collective-permute-done.15 = f32[16,8,256]{2,1,0:T(8,128)S(1)} collective-permute-done((f32[16,8,256]{2,1,0:T(8,128)S(1)}, f32[16,8,256]{2,1,0:T(8,128)S(1)}, u32[]{:S(2)}, u32[]{:S(2)}) %collective-permute-start.15) | collective-permute-done | bytes 131104 | tf_op jit(solution)/shard_map/ppermute | solution.py:439
  189.6 5.6 %collective-permute-done.17 = f32[16,8,256]{2,1,0:T(8,128)S(1)} collective-permute-done((f32[16,8,256]{2,1,0:T(8,128)S(1)}, f32[16,8,256]{2,1,0:T(8,128)S(1)}, u32[]{:S(2)}, u32[]{:S(2)}) %collective-permute-start.17) | collective-permute-done | bytes 131104 | tf_op jit(solution)/shard_map/ppermute | solution.py:439
  198.2 1.6 fusion.24
  200.1 1.8 collective-permute-start.24
  201.9 1.5 collective-permute-start.23
  203.4 1.7 collective-permute-done.21
  206.5 2.8 collective-permute-done.22.refs_2_.refs_4_
  210.1 2.9 collective-permute-start.25
  213.2 2.2 copy-done.2
  215.4 7.7 %adjoint_sums.3 = (f32[4,16,8,512]{3,2,1,0:T(8,128)S(1)}, f32[8,8,512]{2,1,0:T(8,128)S(1)}) custom-call(f32[256,8,512]{2,1,0:T(8,128)S(1)} %copy-done.1, f32[256,8,512]{2,1,0:T(8,128)S(1)} %copy-done.2, f32[16,512]{1,0:T(8,128)S(1)} %get-tuple-element.454.retain_ref, f32[16,512]{1,0:T(8,128)S(1)} %copy-done.14, f32[16,512]{1,0:T(8,128)S(1)} %copy-done.13, ...), custom_call_target="tpu_custom_call" | custom-call | bytes 24000000 | tf_op jit(solution)/shard_map/adjoint_sums/pallas_call | solution.py:319
  223.1 4.3 %collective-permute-done.25.refs_1_ = f32[32,1024]{1,0:T(8,128)S(1)} collective-permute-done((f32[32,1024]{1,0:T(8,128)S(1)}, f32[32,1024]{1,0:T(8,128)S(1)}, u32[]{:S(2)}, u32[]{:S(2)}) %collective-permute-start.25) | collective-permute-done | bytes 131104 | tf_op jit(solution)/shard_map/ppermute | solution.py:490
  227.4 2.8 collective-permute-done.26.refs_3_
  230.4 2.9 collective-permute-start.28
  233.4 7.7 %adjoint_sums.4 = (f32[4,16,8,512]{3,2,1,0:T(8,128)S(1)}, f32[8,8,512]{2,1,0:T(8,128)S(1)}) custom-call(f32[256,8,512]{2,1,0:T(8,128)S(1)} %copy-done.1, f32[256,8,512]{2,1,0:T(8,128)S(1)} %copy-done.3, f32[16,512]{1,0:T(8,128)S(1)} %get-tuple-element.454.retain_ref, f32[16,512]{1,0:T(8,128)S(1)} %copy-done.14, f32[16,512]{1,0:T(8,128)S(1)} %copy-done.13, ...), custom_call_target="tpu_custom_call" | custom-call | bytes 24000000 | tf_op jit(solution)/shard_map/adjoint_sums/pallas_call | solution.py:319
  243.9 1.5 collective-permute-start.32
  245.4 5.2 %adjoint_sums.5 = (f32[4,16,8,512]{3,2,1,0:T(8,128)S(1)}, f32[8,8,512]{2,1,0:T(8,128)S(1)}) custom-call(f32[256,8,512]{2,1,0:T(8,128)S(1)} %copy-done.1, f32[256,8,512]{2,1,0:T(8,128)S(1)} %copy-done.3, f32[16,512]{1,0:T(8,128)S(1)} %get-tuple-element.454.retain_ref, f32[16,512]{1,0:T(8,128)S(1)} %copy-done.14, f32[16,512]{1,0:T(8,128)S(1)} %copy-done.13, ...), custom_call_target="tpu_custom_call" | custom-call | bytes 24000000 | tf_op jit(solution)/shard_map/adjoint_sums/pallas_call | solution.py:319
  250.6 1.8 collective-permute-done.31.refs_2_
  254.1 1.6 collective-permute-start.36
  255.6 2.0 collective-permute-start.34
  257.8 6.6 %leave.2 = (f32[16,8,512]{2,1,0:T(8,128)S(1)}, bf16[8,256,512]{2,1,0:T(8,128)(2,1)}) custom-call(s32[8]{0:T(128)S(1)} %broadcast_subtract_fusion.count_ref, bf16[8,256,512]{2,1,0:T(8,128)(2,1)S(1)} %copy-done.4, f32[1,512]{1,0:T(1,128)S(1)} %bitcast.120, f32[8,256,512]{2,1,0:T(8,128)S(1)} %copy-done.6, bf16[8,256,512]{2,1,0:T(8,128)(2,1)S(1)} %copy-done.8, ...), custom_call_target="tpu_custom_call" | custom-call | bytes 24000000 | tf_op jit(solution)/shard_map/leave/pallas_call | solution.py:393
  264.4 3.5 %collective-permute-done.34.refs_2_ = f32[128,1024]{1,0:T(8,128)S(1)} collective-permute-done((f32[128,1024]{1,0:T(8,128)S(1)}, f32[128,1024]{1,0:T(8,128)S(1)}, u32[]{:S(2)}, u32[]{:S(2)}) %collective-permute-start.34) | collective-permute-done | bytes 524320 | tf_op jit(solution)/shard_map/ppermute | solution.py:490
  267.9 3.9 %collective-permute-done.35.refs_4_ = f32[64,2048]{1,0:T(8,128)S(1)} collective-permute-done((f32[64,2048]{1,0:T(8,128)S(1)}, f32[64,2048]{1,0:T(8,128)S(1)}, u32[]{:S(2)}, u32[]{:S(2)}) %collective-permute-start.35) | collective-permute-done | bytes 524320 | tf_op jit(solution)/shard_map/ppermute | solution.py:490
  271.9 3.8 %placed.5 = (f32[256,1024]{1,0:T(8,128)}, f32[128,2048]{1,0:T(8,128)}, f32[128,2176]{1,0:T(8,128)S(1)}) custom-call(s32[3]{0:T(128)S(1)} %get-tuple-element.465.refs_0_, f32[128,1024]{1,0:T(8,128)S(1)} %get-tuple-element.390.refs_1_, f32[128,1024]{1,0:T(8,128)S(1)} %collective-permute-done.34.refs_2_, f32[64,2048]{1,0:T(8,128)S(1)} %get-tuple-element.392.refs_3_, ...), custom_call_target="tpu_custom_call" | custom-call | bytes 6000000 | tf_op jit(solution)/shard_map/placed/pallas_call | solution.py:970
  276.1 10.2 %leave.3 = (f32[16,8,512]{2,1,0:T(8,128)}, bf16[8,256,512]{2,1,0:T(8,128)(2,1)}) custom-call(s32[8]{0:T(128)S(1)} %broadcast_subtract_fusion.count_ref, bf16[8,256,512]{2,1,0:T(8,128)(2,1)S(1)} %copy-done.4, f32[1,512]{1,0:T(1,128)S(1)} %bitcast.121, f32[8,256,512]{2,1,0:T(8,128)S(1)} %copy-done.6, ...), custom_call_target="tpu_custom_call", output_to_operand_aliasing={{1}: (9, {})} | custom-call | bytes 24000000 | tf_op jit(solution)/shard_map/leave/pallas_call | solution.py:393
  287.7 3.2 collective-permute-done.37.refs_2_
  291.8 1.9 collective-permute-done.40
  293.7 1.7 collective-permute-start.41
  295.4 1.9 collective-permute-start.43
  298.5 3.1 collective-permute-done.42
  301.7 2.0 collective-permute-start.44
  303.7 1.4 collective-permute-start.45
  306.6 8.7 %gathered.2 = (f32[1024,512]{1,0:T(8,128)}, f32[1024,512]{1,0:T(8,128)}, f32[512,2176]{1,0:T(8,128)}, f32[512,1024]{1,0:T(8,128)}, f32[512,1024]{1,0:T(8,128)}) custom-call(s32[7]{0:T(128)S(1)} %stack.101.refs_0_, f32[256,1024]{1,0:T(8,128)} %get-tuple-element.415.refs_1_, f32[256,1024]{1,0:T(8,128)} %collective-permute-done.37.refs_2_, ...), custom_call_target="tpu_custom_call" | custom-call | bytes 12000000 | tf_op jit(solution)/shard_map/gathered/pallas_call | solution.py:1026
  319.9 1.5 collective-permute-done.49.refs_3_
  321.4 1.5 collective-permute-done.50.refs_4_
  322.9 4.8 %gathered.3 = (f32[1024,512]{1,0:T(8,128)}, f32[1024,512]{1,0:T(8,128)}, f32[512,2176]{1,0:T(8,128)}, f32[512,1024]{1,0:T(8,128)}, f32[512,1024]{1,0:T(8,128)}) custom-call(s32[7]{0:T(128)S(1)} %stack.99.refs_0_, f32[256,1024]{1,0:T(8,128)S(1)} %collective-permute-done.47.refs_1_, ...), custom_call_target="tpu_custom_call", output_to_operand_aliasing={{0}: (7, {}), {1}: (8, {}), {2}: (9, {}), {3}: (10, {}), {4... | custom-call | bytes 12000000 | tf_op jit(solution)/shard_map/gathered/pallas_call | solution.py:1026
  (232 shorter events, 45.5 us)
Async XLA Ops:
  0.6 29.3 %copy-start.32 = (bf16[512,1024]{1,0:T(8,128)(2,1)S(1)}, bf16[512,1024]{1,0:T(8,128)(2,1)}, u32[]{:S(2)}) copy-start(bf16[512,1024]{1,0:T(8,128)(2,1)} %value_weight_ref.3) | copy-start | bytes 3145732
  13.9 6.5 %collective-permute-start = (f32[16,8,256]{2,1,0:T(8,128)S(1)}, f32[16,8,256]{2,1,0:T(8,128)S(1)}, u32[]{:S(2)}, u32[]{:S(2)}) collective-permute-start(f32[16,8,256]{2,1,0:T(8,128)S(1)} %constant_dynamic-slice_fusion.2), channel_id=1, source_target_pairs={{0,4},{4,0},{8,12},{12,8},{16,20},{20,16},{24,28},{28,24},{1,5},{5... | collective-permute-start | bytes 393224 | tf_op jit(solution)/shard_map/ppermute | solution.py:439
  20.5 18.0 %collective-permute-start.1 = (f32[16,8,256]{2,1,0:T(8,128)S(1)}, f32[16,8,256]{2,1,0:T(8,128)S(1)}, u32[]{:S(2)}, u32[]{:S(2)}) collective-permute-start(f32[16,8,256]{2,1,0:T(8,128)S(1)} %select_add_fusion.1), channel_id=1, source_target_pairs={{0,24},{4,28},{1,25},{5,29},{2,26},{6,30},{3,27},{7,31}} | collective-permute-start | bytes 393224 | tf_op jit(solution)/shard_map/ppermute | solution.py:439
  26.2 12.3 %collective-permute-start.2 = (f32[16,8,256]{2,1,0:T(8,128)S(1)}, f32[16,8,256]{2,1,0:T(8,128)S(1)}, u32[]{:S(2)}, u32[]{:S(2)}) collective-permute-start(f32[16,8,256]{2,1,0:T(8,128)S(1)} %select_add_fusion.1), channel_id=1, source_target_pairs={{0,16},{4,20},{8,24},{12,28},{1,17},{5,21},{9,25},{13,29},{2,18},{... | collective-permute-start | bytes 393224 | tf_op jit(solution)/shard_map/ppermute | solution.py:439
  27.5 11.0 %collective-permute-start.3 = (f32[16,8,256]{2,1,0:T(8,128)S(1)}, f32[16,8,256]{2,1,0:T(8,128)S(1)}, u32[]{:S(2)}, u32[]{:S(2)}) collective-permute-start(f32[16,8,256]{2,1,0:T(8,128)S(1)} %select_add_fusion.1), channel_id=1, source_target_pairs={{0,8},{4,12},{8,16},{12,20},{16,24},{20,28},{1,9},{5,13},{9,17},{1... | collective-permute-start | bytes 393224 | tf_op jit(solution)/shard_map/ppermute | solution.py:439
  38.6 5.0 %collective-permute-start.4 = (f32[16,8,256]{2,1,0:T(8,128)S(1)}, f32[16,8,256]{2,1,0:T(8,128)S(1)}, u32[]{:S(2)}, u32[]{:S(2)}) collective-permute-start(f32[16,8,256]{2,1,0:T(8,128)S(1)} %fusion.26), channel_id=1, source_target_pairs={{0,4},{4,0},{8,12},{12,8},{16,20},{20,16},{24,28},{28,24},{1,5},{5... | collective-permute-start | bytes 393224 | tf_op jit(solution)/shard_map/ppermute | solution.py:439
  43.7 12.8 %copy-start.29 = (bf16[1024,512]{1,0:T(8,128)(2,1)S(1)}, bf16[1024,512]{1,0:T(8,128)(2,1)}, u32[]{:S(2)}) copy-start(bf16[1024,512]{1,0:T(8,128)(2,1)} %output_weight_ref.1) | copy-start | bytes 3145732
  43.7 12.7 %copy-start.4 = (bf16[8,256,512]{2,1,0:T(8,128)(2,1)S(1)}, bf16[8,256,512]{2,1,0:T(8,128)(2,1)}, u32[]{:S(2)}) copy-start(bf16[8,256,512]{2,1,0:T(8,128)(2,1)} %tokens_ref.7) | copy-start | bytes 6291460
  43.7 12.7 %copy-start.27 = (bf16[8,256,512]{2,1,0:T(8,128)(2,1)S(1)}, bf16[8,256,512]{2,1,0:T(8,128)(2,1)}, u32[]{:S(2)}) copy-start(bf16[8,256,512]{2,1,0:T(8,128)(2,1)} %cotangent_ref.1) | copy-start | bytes 6291460
  43.8 12.7 %copy-start.37 = (f32[512]{0:T(512)S(1)}, f32[512]{0:T(512)}, u32[]{:S(2)}) copy-start(f32[512]{0:T(512)} %param.23) | copy-start | bytes 6148
  56.4 43.9 %copy-start.16 = (f32[16,8,512]{2,1,0:T(8,128)}, f32[16,8,512]{2,1,0:T(8,128)S(1)}, u32[]{:S(2)}) copy-start(f32[16,8,512]{2,1,0:T(8,128)S(1)} %get-tuple-element.299) | copy-start | bytes 786436
  100.9 20.3 %collective-permute-start.10 = (f32[256,128]{1,0:T(8,128)S(1)}, f32[256,128]{1,0:T(8,128)S(1)}, u32[]{:S(2)}, u32[]{:S(2)}) collective-permute-start(f32[256,128]{1,0:T(8,128)S(1)} %fusion.16), channel_id=1, source_target_pairs={{0,1},{1,0},{2,3},{3,2},{4,5},{5,4},{6,7},{7,6},{8,9},{9,8},{10,11... | collective-permute-start | bytes 393224 | tf_op jit(solution)/shard_map/ppermute | solution.py:490
  105.4 20.2 %collective-permute-start.8 = (f32[256,1024]{1,0:T(8,128)S(1)}, f32[256,1024]{1,0:T(8,128)S(1)}, u32[]{:S(2)}, u32[]{:S(2)}) collective-permute-start(f32[256,1024]{1,0:T(8,128)S(1)} %fusion.12), channel_id=1, source_target_pairs={{0,1},{1,0},{2,3},{3,2},{4,5},{5,4},{6,7},{7,6},{8,9},{9,8},{10,11... | collective-permute-start | bytes 3145736 | tf_op jit(solution)/shard_map/ppermute | solution.py:490
  108.1 17.6 %collective-permute-start.7 = (f32[256,2048]{1,0:T(8,128)S(1)}, f32[256,2048]{1,0:T(8,128)S(1)}, u32[]{:S(2)}, u32[]{:S(2)}) collective-permute-start(f32[256,2048]{1,0:T(8,128)S(1)} %fusion.18), channel_id=1, source_target_pairs={{0,1},{1,0},{2,3},{3,2},{4,5},{5,4},{6,7},{7,6},{8,9},{9,8},{10,11... | collective-permute-start | bytes 6291464 | tf_op jit(solution)/shard_map/ppermute | solution.py:490
  109.9 15.8 %collective-permute-start.9 = (f32[256,1024]{1,0:T(8,128)S(1)}, f32[256,1024]{1,0:T(8,128)S(1)}, u32[]{:S(2)}, u32[]{:S(2)}) collective-permute-start(f32[256,1024]{1,0:T(8,128)S(1)} %fusion.8), channel_id=1, source_target_pairs={{0,1},{1,0},{2,3},{3,2},{4,5},{5,4},{6,7},{7,6},{8,9},{9,8},{10,11... | collective-permute-start | bytes 3145736 | tf_op jit(solution)/shard_map/ppermute | solution.py:490
  112.1 13.6 %collective-permute-start.6 = (f32[512,512]{1,0:T(8,128)S(1)}, f32[512,512]{1,0:T(8,128)S(1)}, u32[]{:S(2)}, u32[]{:S(2)}) collective-permute-start(f32[512,512]{1,0:T(8,128)S(1)} %fusion), channel_id=1, source_target_pairs={{0,1},{1,0},{2,3},{3,2},{4,5},{5,4},{6,7},{7,6},{8,9},{9,8},{10,11... | collective-permute-start | bytes 3145736 | tf_op jit(solution)/shard_map/ppermute | solution.py:490
  121.2 4.5 %collective-permute-start.5 = (f32[512,512]{1,0:T(8,128)S(1)}, f32[512,512]{1,0:T(8,128)S(1)}, u32[]{:S(2)}, u32[]{:S(2)}) collective-permute-start(f32[512,512]{1,0:T(8,128)S(1)} %fusion.4), channel_id=1, source_target_pairs={{0,1},{1,0},{2,3},{3,2},{4,5},{5,4},{6,7},{7,6},{8,9},{9,8},{10,11... | collective-permute-start | bytes 3145736 | tf_op jit(solution)/shard_map/ppermute | solution.py:490
  130.5 31.4 %collective-permute-start.14 = (f32[128,2176]{1,0:T(8,128)}, f32[128,2176]{1,0:T(8,128)}, u32[]{:S(2)}, u32[]{:S(2)}) collective-permute-start(f32[128,2176]{1,0:T(8,128)} %get-tuple-element.263), channel_id=1, source_target_pairs={{0,8},{1,9},{2,10},{3,11},{4,12},{5,13},{6,14},{7,15},{8,0},{9,1},... | collective-permute-start | bytes 3342344 | tf_op jit(solution)/shard_map/ppermute | solution.py:490
  130.6 31.4 %collective-permute-start.12 = (f32[256,1024]{1,0:T(8,128)}, f32[256,1024]{1,0:T(8,128)}, u32[]{:S(2)}, u32[]{:S(2)}) collective-permute-start(f32[256,1024]{1,0:T(8,128)} %get-tuple-element.259), channel_id=1, source_target_pairs={{0,2},{1,3},{2,0},{3,1},{4,6},{5,7},{6,4},{7,5},{8,10},{9,11},{10,... | collective-permute-start | bytes 3145736 | tf_op jit(solution)/shard_map/ppermute | solution.py:490
  132.1 29.9 %collective-permute-start.13 = (f32[128,2048]{1,0:T(8,128)}, f32[128,2048]{1,0:T(8,128)}, u32[]{:S(2)}, u32[]{:S(2)}) collective-permute-start(f32[128,2048]{1,0:T(8,128)} %get-tuple-element.261), channel_id=1, source_target_pairs={{0,4},{1,5},{2,6},{3,7},{4,0},{5,1},{6,2},{7,3},{8,12},{9,13},{10,... | collective-permute-start | bytes 3145736 | tf_op jit(solution)/shard_map/ppermute | solution.py:490
  155.5 5.5 %collective-permute-start.11 = (f32[16,8,256]{2,1,0:T(8,128)}, f32[16,8,256]{2,1,0:T(8,128)}, u32[]{:S(2)}, u32[]{:S(2)}) collective-permute-start(f32[16,8,256]{2,1,0:T(8,128)} %constant_dynamic-slice_fusion), channel_id=1, source_target_pairs={{28,24},{24,28},{20,16},{16,20},{12,8},{8,12},{4,0},{0,4},{29,25},... | collective-permute-start | bytes 393224 | tf_op jit(solution)/shard_map/ppermute | solution.py:439
  164.4 30.7 %copy-start.44 = (f32[16,256]{1,0:T(8,128)S(1)}, f32[16,256]{1,0:T(8,128)}, u32[]{:S(2)}) copy-start(f32[16,256]{1,0:T(8,128)} %get-tuple-element.433) | copy-start | bytes 49156
  167.9 27.3 %collective-permute-start.20 = (f32[64,2176]{1,0:T(8,128)S(1)}, f32[64,2176]{1,0:T(8,128)S(1)}, u32[]{:S(2)}, u32[]{:S(2)}) collective-permute-start(f32[64,2176]{1,0:T(8,128)S(1)} %get-tuple-element.283), channel_id=1, source_target_pairs={{0,2},{1,3},{2,0},{3,1},{4,6},{5,7},{6,4},{7,5},{8,10},{9,11},{10,... | collective-permute-start | bytes 1671176 | tf_op jit(solution)/shard_map/ppermute | solution.py:490
  168.4 26.7 %collective-permute-start.18 = (f32[128,1024]{1,0:T(8,128)S(1)}, f32[128,1024]{1,0:T(8,128)S(1)}, u32[]{:S(2)}, u32[]{:S(2)}) collective-permute-start(f32[128,1024]{1,0:T(8,128)S(1)} %get-tuple-element.279), channel_id=1, source_target_pairs={{0,4},{1,5},{2,6},{3,7},{4,0},{5,1},{6,2},{7,3},{8,12},{9,13},{10,... | collective-permute-start | bytes 1572872 | tf_op jit(solution)/shard_map/ppermute | solution.py:490
  169.3 25.9 %collective-permute-start.19 = (f32[64,2048]{1,0:T(8,128)S(1)}, f32[64,2048]{1,0:T(8,128)S(1)}, u32[]{:S(2)}, u32[]{:S(2)}) collective-permute-start(f32[64,2048]{1,0:T(8,128)S(1)} %get-tuple-element.281), channel_id=1, source_target_pairs={{0,8},{1,9},{2,10},{3,11},{4,12},{5,13},{6,14},{7,15},{8,0},{9,1},... | collective-permute-start | bytes 1572872 | tf_op jit(solution)/shard_map/ppermute | solution.py:490
  171.0 17.2 %collective-permute-start.15 = (f32[16,8,256]{2,1,0:T(8,128)S(1)}, f32[16,8,256]{2,1,0:T(8,128)S(1)}, u32[]{:S(2)}, u32[]{:S(2)}) collective-permute-start(f32[16,8,256]{2,1,0:T(8,128)S(1)} %select_add_fusion), channel_id=1, source_target_pairs={{28,4},{24,0},{29,5},{25,1},{30,6},{26,2},{31,7},{27,3}} | collective-permute-start | bytes 393224 | tf_op jit(solution)/shard_map/ppermute | solution.py:439
  172.3 17.2 %collective-permute-start.16 = (f32[16,8,256]{2,1,0:T(8,128)S(1)}, f32[16,8,256]{2,1,0:T(8,128)S(1)}, u32[]{:S(2)}, u32[]{:S(2)}) collective-permute-start(f32[16,8,256]{2,1,0:T(8,128)S(1)} %select_add_fusion), channel_id=1, source_target_pairs={{28,12},{24,8},{20,4},{16,0},{29,13},{25,9},{21,5},{17,1},{30,14},... | collective-permute-start | bytes 393224 | tf_op jit(solution)/shard_map/ppermute | solution.py:439
  188.3 6.8 %collective-permute-start.17 = (f32[16,8,256]{2,1,0:T(8,128)S(1)}, f32[16,8,256]{2,1,0:T(8,128)S(1)}, u32[]{:S(2)}, u32[]{:S(2)}) collective-permute-start(f32[16,8,256]{2,1,0:T(8,128)S(1)} %select_add_fusion), channel_id=1, source_target_pairs={{28,20},{24,16},{20,12},{16,8},{12,4},{8,0},{29,21},{25,17},{21,13... | collective-permute-start | bytes 393224 | tf_op jit(solution)/shard_map/ppermute | solution.py:439
  199.8 5.3 %collective-permute-start.21 = (f32[16,8,256]{2,1,0:T(8,128)}, f32[16,8,256]{2,1,0:T(8,128)}, u32[]{:S(2)}, u32[]{:S(2)}) collective-permute-start(f32[16,8,256]{2,1,0:T(8,128)} %fusion.24), channel_id=1, source_target_pairs={{28,24},{24,28},{20,16},{16,20},{12,8},{8,12},{4,0},{0,4},{29,25},... | collective-permute-start | bytes 393224 | tf_op jit(solution)/shard_map/ppermute | solution.py:439
  200.1 9.2 %collective-permute-start.24 = (f32[32,2176]{1,0:T(8,128)}, f32[32,2176]{1,0:T(8,128)S(1)}, u32[]{:S(2)}, u32[]{:S(2)}) collective-permute-start(f32[32,2176]{1,0:T(8,128)} %copy-done.34), channel_id=1, source_target_pairs={{0,4},{1,5},{2,6},{3,7},{4,0},{5,1},{6,2},{7,3},{8,12},{9,13},{10,... | collective-permute-start | bytes 835592 | tf_op jit(solution)/shard_map/ppermute | solution.py:490
  201.9 7.4 %collective-permute-start.22 = (f32[64,1024]{1,0:T(8,128)}, f32[64,1024]{1,0:T(8,128)S(1)}, u32[]{:S(2)}, u32[]{:S(2)}) collective-permute-start(f32[64,1024]{1,0:T(8,128)} %copy-done.36), channel_id=1, source_target_pairs={{0,8},{1,9},{2,10},{3,11},{4,12},{5,13},{6,14},{7,15},{8,0},{9,1},... | collective-permute-start | bytes 786440 | tf_op jit(solution)/shard_map/ppermute | solution.py:490
  201.9 7.4 %collective-permute-start.23 = (f32[32,2048]{1,0:T(8,128)}, f32[32,2048]{1,0:T(8,128)S(1)}, u32[]{:S(2)}, u32[]{:S(2)}) collective-permute-start(f32[32,2048]{1,0:T(8,128)} %copy-done.35), channel_id=1, source_target_pairs={{0,2},{1,3},{2,0},{3,1},{4,6},{5,7},{6,4},{7,5},{8,10},{9,11},{10,... | collective-permute-start | bytes 786440 | tf_op jit(solution)/shard_map/ppermute | solution.py:490
  210.1 20.2 %collective-permute-start.27 = (f32[16,2176]{1,0:T(8,128)S(1)}, f32[16,2176]{1,0:T(8,128)S(1)}, u32[]{:S(2)}, u32[]{:S(2)}) collective-permute-start(f32[16,2176]{1,0:T(8,128)S(1)} %get-tuple-element.328), channel_id=1, source_target_pairs={{0,16},{1,17},{2,18},{3,19},{4,20},{5,21},{6,22},{7,23},{8,24},{9,... | collective-permute-start | bytes 417800 | tf_op jit(solution)/shard_map/ppermute | solution.py:490
  210.1 17.3 %collective-permute-start.25 = (f32[32,1024]{1,0:T(8,128)S(1)}, f32[32,1024]{1,0:T(8,128)S(1)}, u32[]{:S(2)}, u32[]{:S(2)}) collective-permute-start(f32[32,1024]{1,0:T(8,128)S(1)} %get-tuple-element.324), channel_id=1, source_target_pairs={{0,16},{1,17},{2,18},{3,19},{4,20},{5,21},{6,22},{7,23},{8,24},{9,... | collective-permute-start | bytes 393224 | tf_op jit(solution)/shard_map/ppermute | solution.py:490
  213.0 17.2 %collective-permute-start.26 = (f32[16,2048]{1,0:T(8,128)S(1)}, f32[16,2048]{1,0:T(8,128)S(1)}, u32[]{:S(2)}, u32[]{:S(2)}) collective-permute-start(f32[16,2048]{1,0:T(8,128)S(1)} %get-tuple-element.326), channel_id=1, source_target_pairs={{0,16},{1,17},{2,18},{3,19},{4,20},{5,21},{6,22},{7,23},{8,24},{9,... | collective-permute-start | bytes 393224 | tf_op jit(solution)/shard_map/ppermute | solution.py:490
  215.4 18.0 %copy-start.3 = (f32[256,8,512]{2,1,0:T(8,128)S(1)}, f32[256,8,512]{2,1,0:T(8,128)}, u32[]{:S(2)}) copy-start(f32[256,8,512]{2,1,0:T(8,128)} %get-tuple-element.223.turned_ref) | copy-start | bytes 12582916
  230.3 11.6 %collective-permute-start.30 = (f32[16,2176]{1,0:T(8,128)S(1)}, f32[16,2176]{1,0:T(8,128)S(1)}, u32[]{:S(2)}, u32[]{:S(2)}) collective-permute-start(f32[16,2176]{1,0:T(8,128)S(1)} %get-tuple-element.354.refs_5_), channel_id=1, source_target_pairs={{0,16},{1,17},{2,18},{3,19},{4,20},{5,21},{6,22},{7,23},{8,24},{9,... | collective-permute-start | bytes 417800 | tf_op jit(solution)/shard_map/ppermute | solution.py:490
  230.4 10.7 %collective-permute-start.28 = (f32[32,1024]{1,0:T(8,128)S(1)}, f32[32,1024]{1,0:T(8,128)S(1)}, u32[]{:S(2)}, u32[]{:S(2)}) collective-permute-start(f32[32,1024]{1,0:T(8,128)S(1)} %get-tuple-element.350.refs_1_), channel_id=1, source_target_pairs={{0,16},{1,17},{2,18},{3,19},{4,20},{5,21},{6,22},{7,23},{8,24},{9,... | collective-permute-start | bytes 393224 | tf_op jit(solution)/shard_map/ppermute | solution.py:490
  233.3 8.6 %collective-permute-start.29 = (f32[16,2048]{1,0:T(8,128)S(1)}, f32[16,2048]{1,0:T(8,128)S(1)}, u32[]{:S(2)}, u32[]{:S(2)}) collective-permute-start(f32[16,2048]{1,0:T(8,128)S(1)} %get-tuple-element.352.refs_3_), channel_id=1, source_target_pairs={{0,16},{1,17},{2,18},{3,19},{4,20},{5,21},{6,22},{7,23},{8,24},{9,... | collective-permute-start | bytes 393224 | tf_op jit(solution)/shard_map/ppermute | solution.py:490
  242.8 10.1 %collective-permute-start.33 = (f32[32,2176]{1,0:T(8,128)S(1)}, f32[32,2176]{1,0:T(8,128)S(1)}, u32[]{:S(2)}, u32[]{:S(2)}) collective-permute-start(f32[32,2176]{1,0:T(8,128)S(1)} %get-tuple-element.373.refs_5_), channel_id=1, source_target_pairs={{0,4},{1,5},{2,6},{3,7},{4,0},{5,1},{6,2},{7,3},{8,12},{9,13},{10,... | collective-permute-start | bytes 835592 | tf_op jit(solution)/shard_map/ppermute | solution.py:490
  243.6 8.9 %collective-permute-start.31 = (f32[64,1024]{1,0:T(8,128)S(1)}, f32[64,1024]{1,0:T(8,128)S(1)}, u32[]{:S(2)}, u32[]{:S(2)}) collective-permute-start(f32[64,1024]{1,0:T(8,128)S(1)} %get-tuple-element.369.refs_1_), channel_id=1, source_target_pairs={{0,8},{1,9},{2,10},{3,11},{4,12},{5,13},{6,14},{7,15},{8,0},{9,1},... | collective-permute-start | bytes 786440 | tf_op jit(solution)/shard_map/ppermute | solution.py:490
  243.9 9.0 %collective-permute-start.32 = (f32[32,2048]{1,0:T(8,128)S(1)}, f32[32,2048]{1,0:T(8,128)S(1)}, u32[]{:S(2)}, u32[]{:S(2)}) collective-permute-start(f32[32,2048]{1,0:T(8,128)S(1)} %get-tuple-element.371.refs_3_), channel_id=1, source_target_pairs={{0,2},{1,3},{2,0},{3,1},{4,6},{5,7},{6,4},{7,5},{8,10},{9,11},{10,... | collective-permute-start | bytes 786440 | tf_op jit(solution)/shard_map/ppermute | solution.py:490
  245.4 12.4 %copy-start.6 = (f32[8,256,512]{2,1,0:T(8,128)S(1)}, f32[8,256,512]{2,1,0:T(8,128)}, u32[]{:S(2)}) copy-start(f32[8,256,512]{2,1,0:T(8,128)} %copy-done.5) | copy-start | bytes 12582916
  245.4 12.4 %copy-start.8 = (bf16[8,256,512]{2,1,0:T(8,128)(2,1)S(1)}, bf16[8,256,512]{2,1,0:T(8,128)(2,1)}, u32[]{:S(2)}) copy-start(bf16[8,256,512]{2,1,0:T(8,128)(2,1)} %copy-done.7) | copy-start | bytes 6291460
  250.6 13.8 %copy-start.15 = (f32[4,16,8,512]{3,2,1,0:T(8,128)}, f32[4,16,8,512]{3,2,1,0:T(8,128)S(1)}, u32[]{:S(2)}) copy-start(f32[4,16,8,512]{3,2,1,0:T(8,128)S(1)} %get-tuple-element.405) | copy-start | bytes 3145732
  254.1 17.8 %collective-permute-start.36 = (f32[64,2176]{1,0:T(8,128)S(1)}, f32[64,2176]{1,0:T(8,128)S(1)}, u32[]{:S(2)}, u32[]{:S(2)}) collective-permute-start(f32[64,2176]{1,0:T(8,128)S(1)} %get-tuple-element.394.refs_5_), channel_id=1, source_target_pairs={{0,2},{1,3},{2,0},{3,1},{4,6},{5,7},{6,4},{7,5},{8,10},{9,11},{10,... | collective-permute-start | bytes 1671176 | tf_op jit(solution)/shard_map/ppermute | solution.py:490
  255.6 12.3 %collective-permute-start.34 = (f32[128,1024]{1,0:T(8,128)S(1)}, f32[128,1024]{1,0:T(8,128)S(1)}, u32[]{:S(2)}, u32[]{:S(2)}) collective-permute-start(f32[128,1024]{1,0:T(8,128)S(1)} %get-tuple-element.390.refs_1_), channel_id=1, source_target_pairs={{0,4},{1,5},{2,6},{3,7},{4,0},{5,1},{6,2},{7,3},{8,12},{9,13},{10,... | collective-permute-start | bytes 1572872 | tf_op jit(solution)/shard_map/ppermute | solution.py:490
  257.6 14.2 %collective-permute-start.35 = (f32[64,2048]{1,0:T(8,128)S(1)}, f32[64,2048]{1,0:T(8,128)S(1)}, u32[]{:S(2)}, u32[]{:S(2)}) collective-permute-start(f32[64,2048]{1,0:T(8,128)S(1)} %get-tuple-element.392.refs_3_), channel_id=1, source_target_pairs={{0,8},{1,9},{2,10},{3,11},{4,12},{5,13},{6,14},{7,15},{8,0},{9,1},... | collective-permute-start | bytes 1572872 | tf_op jit(solution)/shard_map/ppermute | solution.py:490
  275.6 15.7 %collective-permute-start.39 = (f32[128,2176]{1,0:T(8,128)S(1)}, f32[128,2176]{1,0:T(8,128)}, u32[]{:S(2)}, u32[]{:S(2)}) collective-permute-start(f32[128,2176]{1,0:T(8,128)S(1)} %get-tuple-element.419.refs_5_), channel_id=1, source_target_pairs={{0,8},{1,9},{2,10},{3,11},{4,12},{5,13},{6,14},{7,15},{8,0},{9,1},... | collective-permute-start | bytes 3342344 | tf_op jit(solution)/shard_map/ppermute | solution.py:490
  275.7 15.2 %collective-permute-start.37 = (f32[256,1024]{1,0:T(8,128)}, f32[256,1024]{1,0:T(8,128)}, u32[]{:S(2)}, u32[]{:S(2)}) collective-permute-start(f32[256,1024]{1,0:T(8,128)} %get-tuple-element.415.refs_1_), channel_id=1, source_target_pairs={{0,2},{1,3},{2,0},{3,1},{4,6},{5,7},{6,4},{7,5},{8,10},{9,11},{10,... | collective-permute-start | bytes 3145736 | tf_op jit(solution)/shard_map/ppermute | solution.py:490
  276.0 15.1 %collective-permute-start.38 = (f32[128,2048]{1,0:T(8,128)}, f32[128,2048]{1,0:T(8,128)}, u32[]{:S(2)}, u32[]{:S(2)}) collective-permute-start(f32[128,2048]{1,0:T(8,128)} %get-tuple-element.417.refs_3_), channel_id=1, source_target_pairs={{0,4},{1,5},{2,6},{3,7},{4,0},{5,1},{6,2},{7,3},{8,12},{9,13},{10,... | collective-permute-start | bytes 3145736 | tf_op jit(solution)/shard_map/ppermute | solution.py:490
  291.3 25.1 %collective-permute-start.47 = (f32[256,1024]{1,0:T(8,128)}, f32[256,1024]{1,0:T(8,128)S(1)}, u32[]{:S(2)}, u32[]{:S(2)}) collective-permute-start(f32[256,1024]{1,0:T(8,128)} %get-tuple-element.415.refs_1_), channel_id=1, source_target_pairs={{0,1},{1,0},{2,3},{3,2},{4,5},{5,4},{6,7},{7,6},{8,9},{9,8},{10,11... | collective-permute-start | bytes 3145736 | tf_op jit(solution)/shard_map/ppermute | solution.py:490
  291.3 2.4 collective-permute-start.40
  293.7 4.8 %collective-permute-start.41 = (f32[40,512]{1,0:T(8,128)S(1)}, f32[40,512]{1,0:T(8,128)S(1)}, u32[]{:S(2)}, u32[]{:S(2)}) collective-permute-start(f32[40,512]{1,0:T(8,128)S(1)} %add.234), channel_id=1, source_target_pairs={{0,2},{1,3},{2,0},{3,1},{4,6},{5,7},{6,4},{7,5},{8,10},{9,11},{10,... | collective-permute-start | bytes 245768 | tf_op jit(solution)/shard_map/ppermute | solution.py:490
  295.4 6.2 %collective-permute-start.42 = (f32[40,512]{1,0:T(8,128)S(1)}, f32[40,512]{1,0:T(8,128)S(1)}, u32[]{:S(2)}, u32[]{:S(2)}) collective-permute-start(f32[40,512]{1,0:T(8,128)S(1)} %add.234), channel_id=1, source_target_pairs={{0,4},{1,5},{2,6},{3,7},{4,0},{5,1},{6,2},{7,3},{8,12},{9,13},{10,... | collective-permute-start | bytes 245768 | tf_op jit(solution)/shard_map/ppermute | solution.py:490
  295.4 6.2 %collective-permute-start.43 = (f32[40,512]{1,0:T(8,128)S(1)}, f32[40,512]{1,0:T(8,128)S(1)}, u32[]{:S(2)}, u32[]{:S(2)}) collective-permute-start(f32[40,512]{1,0:T(8,128)S(1)} %add.234), channel_id=1, source_target_pairs={{0,6},{1,7},{2,4},{3,5},{4,2},{5,3},{6,0},{7,1},{8,14},{9,15},{10,... | collective-permute-start | bytes 245768 | tf_op jit(solution)/shard_map/ppermute | solution.py:490
  301.7 13.6 %collective-permute-start.44 = (f32[40,512]{1,0:T(8,128)S(1)}, f32[40,512]{1,0:T(8,128)S(1)}, u32[]{:S(2)}, u32[]{:S(2)}) collective-permute-start(f32[40,512]{1,0:T(8,128)S(1)} %add_add_fusion.1), channel_id=1, source_target_pairs={{0,8},{1,9},{2,10},{3,11},{4,12},{5,13},{6,14},{7,15},{8,0},{9,1},... | collective-permute-start | bytes 245768 | tf_op jit(solution)/shard_map/ppermute | solution.py:490
  303.7 12.2 %collective-permute-start.45 = (f32[40,512]{1,0:T(8,128)S(1)}, f32[40,512]{1,0:T(8,128)}, u32[]{:S(2)}, u32[]{:S(2)}) collective-permute-start(f32[40,512]{1,0:T(8,128)S(1)} %add_add_fusion.1), channel_id=1, source_target_pairs={{0,16},{1,17},{2,18},{3,19},{4,20},{5,21},{6,22},{7,23},{8,24},{9,... | collective-permute-start | bytes 245768 | tf_op jit(solution)/shard_map/ppermute | solution.py:490
  305.1 10.9 %collective-permute-start.46 = (f32[40,512]{1,0:T(8,128)S(1)}, f32[40,512]{1,0:T(8,128)}, u32[]{:S(2)}, u32[]{:S(2)}) collective-permute-start(f32[40,512]{1,0:T(8,128)S(1)} %add_add_fusion.1), channel_id=1, source_target_pairs={{0,24},{1,25},{2,26},{3,27},{4,28},{5,29},{6,30},{7,31},{8,16},{9,... | collective-permute-start | bytes 245768 | tf_op jit(solution)/shard_map/ppermute | solution.py:490
  306.5 16.4 %collective-permute-start.51 = (f32[128,2176]{1,0:T(8,128)S(1)}, f32[128,2176]{1,0:T(8,128)S(1)}, u32[]{:S(2)}, u32[]{:S(2)}) collective-permute-start(f32[128,2176]{1,0:T(8,128)S(1)} %get-tuple-element.419.refs_5_), channel_id=1, source_target_pairs={{0,1},{1,0},{2,3},{3,2},{4,5},{5,4},{6,7},{7,6},{8,9},{9,8},{10,11... | collective-permute-start | bytes 3342344 | tf_op jit(solution)/shard_map/ppermute | solution.py:490
  315.3 7.6 %collective-permute-start.52 = (f32[128,2176]{1,0:T(8,128)}, f32[128,2176]{1,0:T(8,128)S(1)}, u32[]{:S(2)}, u32[]{:S(2)}) collective-permute-start(f32[128,2176]{1,0:T(8,128)} %collective-permute-done.39.refs_6_), channel_id=1, source_target_pairs={{0,1},{1,0},{2,3},{3,2},{4,5},{5,4},{6,7},{7,6},{8,9},{9,8},{10,11... | collective-permute-start | bytes 3342344 | tf_op jit(solution)/shard_map/ppermute | solution.py:490
  315.9 4.1 %collective-permute-start.48 = (f32[256,1024]{1,0:T(8,128)}, f32[256,1024]{1,0:T(8,128)S(1)}, u32[]{:S(2)}, u32[]{:S(2)}) collective-permute-start(f32[256,1024]{1,0:T(8,128)} %collective-permute-done.37.refs_2_), channel_id=1, source_target_pairs={{0,1},{1,0},{2,3},{3,2},{4,5},{5,4},{6,7},{7,6},{8,9},{9,8},{10,11... | collective-permute-start | bytes 3145736 | tf_op jit(solution)/shard_map/ppermute | solution.py:490
  315.9 5.5 %collective-permute-start.49 = (f32[128,2048]{1,0:T(8,128)}, f32[128,2048]{1,0:T(8,128)S(1)}, u32[]{:S(2)}, u32[]{:S(2)}) collective-permute-start(f32[128,2048]{1,0:T(8,128)} %get-tuple-element.417.refs_3_), channel_id=1, source_target_pairs={{0,1},{1,0},{2,3},{3,2},{4,5},{5,4},{6,7},{7,6},{8,9},{9,8},{10,11... | collective-permute-start | bytes 3145736 | tf_op jit(solution)/shard_map/ppermute | solution.py:490
  316.4 6.6 %collective-permute-start.50 = (f32[128,2048]{1,0:T(8,128)}, f32[128,2048]{1,0:T(8,128)S(1)}, u32[]{:S(2)}, u32[]{:S(2)}) collective-permute-start(f32[128,2048]{1,0:T(8,128)} %collective-permute-done.38.refs_4_), channel_id=1, source_target_pairs={{0,1},{1,0},{2,3},{3,2},{4,5},{5,4},{6,7},{7,6},{8,9},{9,8},{10,11... | collective-permute-start | bytes 3145736 | tf_op jit(solution)/shard_map/ppermute | solution.py:490
  (45 other events, 240.2 us)

commit v4 on v3

--- a/solution.py
+++ b/solution.py
@@ -824,7 +824,7 @@
         + [pltpu.VMEM((length, GROUP), full)]
         + [pltpu.VMEM((length, zdim), half)] * 2
         + [pltpu.VMEM((length, zdim), full)] * 2,
-        compiler_params=dense_params,
+        compiler_params=front_params,
         cost_estimate=work_cost(18e9, 40e-6),
         name="dense_forward",
     )(counts, tokens, cotangent, average, normed, value, value_slope, *tied)
@@ -988,61 +988,71 @@
     )(mine, *values)
 
 
-def gathered_body(*refs, copies):
-    where, refs = refs[0], refs[1:]
-    results = refs[len(refs) - 1 - max(result for _, _, result, _ in copies) :]
-    turn = pl.program_id(0)
-    for chain, taken, result, column in copies:
-        there = slice(column, column + taken.stop - taken.start)
-        for piece in range(2):
-
-            @pl.when(turn == where[2 * chain + piece])
-            def _(source=2 * chain + piece, taken=taken, result=result, there=there):
-                results[result][:, there] = refs[source][:, taken]
+def gathered_body(*refs, bits, copies, results, others, per_row):
+    sources = refs[: 2 * len(bits)]
+    outs = refs[len(refs) - results - len(sources) - 2 : len(refs) - len(sources) - 2]
+    held, (in_sems, out_sems) = refs[len(refs) - len(sources) - 2 : -2], refs[-2:]
+    place = lax.axis_index("seq") * per_row + lax.axis_index("row")
+    arriving = []
+    for at, source in enumerate(sources):
+        copy = pltpu.make_async_copy(source, held[at], in_sems.at[at])
+        copy.start()
+        arriving.append(copy)
+    leaving = []
+    for at, source in enumerate(sources):
+        high_bit, low_bit = bits[at // 2]
+        high = (place // high_bit) % 2
+        low_side = (place // low_bit) % 2
+        if others:
+            high = 1 - high
+        if at % 2:
+            low_side = 1 - low_side
+        rows = source.shape[0]
+        there = pl.ds(pl.multiple_of((2 * high + low_side) * rows, 8), rows)
+        arriving[at].wait()
+        for chain, taken, result, column in copies:
+            if chain == at // 2:
+                copy = pltpu.make_async_copy(
+                    held[at].at[:, taken],
+                    outs[result].at[there, column : column + taken.stop - taken.start],
+                    out_sems.at[len(leaving)],
+                )
+                copy.start()
+                leaving.append(copy)
+    for copy in leaving:
+        copy.wait()
 
 
 def gathered(chains, copies, shapes, before=None):
-    values, where = [], []
+    values = []
     for one in chains:
-        low = (device_place() // one.order[1]) % 2
         values += one.held if before is None else one.arrived
-        where += [low, 1 - low]
-    core = (device_place() // chains[0].order[0]) % 2
-    where.append(core if before is None else 1 - core)
-    steps = 4
-    in_specs = []
-    for at, value in enumerate(values):
-
-        def place(turn, step, where, at=at):
-            early = jnp.where(turn < where[at], 0, steps - 1)
-            return jnp.where(turn == where[at], step, early), 0
-
-        in_specs.append(pl.BlockSpec((value.shape[0] // steps, value.shape[1]), place))
+    anywhere = pl.BlockSpec(memory_space=pl.ANY)
     aliases = {}
     if before is not None:
-        aliases = {1 + len(values) + at: at for at in range(len(shapes))}
-        in_specs += [pl.BlockSpec(memory_space=pl.ANY)] * len(shapes)
-    side = len(where) - 1
+        aliases = {len(values) + at: at for at in range(len(shapes))}
     return pl.pallas_call(
-        functools.partial(gathered_body, copies=copies),
-        grid_spec=pltpu.PrefetchScalarGridSpec(
-            num_scalar_prefetch=1,
-            grid=(2, steps),
-            in_specs=in_specs,
-            out_specs=[
-                pl.BlockSpec(
-                    (shape[0] // (4 * steps), shape[1]),
-                    lambda turn, step, where: ((2 * where[side] + turn) * steps + step, 0),
-                )
-                for shape in shapes
-            ],
+        functools.partial(
+            gathered_body,
+            bits=[one.order[:2] for one in chains],
+            copies=copies,
+            results=len(shapes),
+            others=before is not None,
+            per_row=lax.axis_size("row"),
         ),
+        in_specs=[anywhere] * (len(values) + len(aliases)),
+        out_specs=[anywhere] * len(shapes),
         out_shape=[jax.ShapeDtypeStruct(shape, jnp.float32) for shape in shapes],
         input_output_aliases=aliases,
+        scratch_shapes=[pltpu.VMEM(value.shape, jnp.float32) for value in values]
+        + [
+            pltpu.SemaphoreType.DMA((len(values),)),
+            pltpu.SemaphoreType.DMA((2 * len(copies),)),
+        ],
         compiler_params=scan_params,
-        cost_estimate=work_cost(0.0, 4e-6),
+        cost_estimate=work_cost(0.0, 6e-6),
         name="gathered",
-    )(jnp.stack(where).astype(jnp.int32), *values, *(before or ()))
+    )(*values, *(before or ()))
 
 
 class Chain:
@@ -1288,24 +1298,12 @@
     used = small.shape[0]
     small = jnp.pad(small, ((0, -used % 8), (0, 0)))
     grad_tokens = left[1]
+    vdim = value_weight.shape[1]
     if chained:
         small = tied(small, *chains)
         small = small + swapped(small, core)
         for one in chains:
             one.give()
-        small = paired_sum(small, orders[0][1:3])
-        small = paired_sum(small, orders[0][3:5])
-    else:
-        small = small_sum(small)
-    paired, cross = small[:states], small[states : 2 * states]
-    grad_gain, grad_omega, grad_ffn_gain = (small[2 * states + at] for at in range(3))
-    grad_norm_gain = (grad_gain + jnp.sum(mix * paired, axis=0)) / norm_gain[0]
-    grad_query_key = small[2 * states + 3 : used].reshape(grad_query_key.shape)
-    grad_eta = (inflow * paired).T
-    grad_beta = (eta * paired * gate).T
-    grad_forget = (eta * paired * beta * (1.0 - forget) / gate - mix * cross).T
-    vdim = value_weight.shape[1]
-    if chained:
         zdim, main_end, inner_dim = gains.shape[1], grad_main.shape[-1], ffn_in.shape[1]
         copies = [
             (0, slice(0, width), 0, 0),
@@ -1322,13 +1320,28 @@
             ffn_in.shape,
             value_weight.shape,
         ]
+        first = gathered(chains, copies, shapes)
+        small, first = lax.optimization_barrier((small, first))
+        small = paired_sum(small, orders[0][1:3])
+        small = paired_sum(small, orders[0][3:5])
+    else:
+        small = small_sum(small)
+    paired, cross = small[:states], small[states : 2 * states]
+    grad_gain, grad_omega, grad_ffn_gain = (small[2 * states + at] for at in range(3))
+    grad_norm_gain = (grad_gain + jnp.sum(mix * paired, axis=0)) / norm_gain[0]
+    grad_query_key = small[2 * states + 3 : used].reshape(grad_query_key.shape)
+    grad_eta = (inflow * paired).T
+    grad_beta = (eta * paired * gate).T
+    grad_forget = (eta * paired * beta * (1.0 - forget) / gate - mix * cross).T
+    vdim = value_weight.shape[1]
+    if chained:
         (
             grad_ffn_out,
             grad_output_weight,
             grad_base_weight,
             grad_ffn_in,
             grad_value_weight,
-        ) = gathered(chains, copies, shapes, gathered(chains, copies, shapes))
+        ) = gathered(chains, copies, shapes, first)
     else:
         grad_base = jnp.concatenate([grad_shared, grad_main], axis=-1)
         (

time: 329 us -> 317 us (0.964)
  Pallas kernels: 155 us -> 149 us
  other arithmetic: 11.3 us -> 7.08 us
  local copies, waits for them, and re-layouts: 18.7 us -> 14.8 us
    pallas_call x2, Pallas kernels: 13.6 us -> 7.51 us  [gathered(): pl.pallas_call(functools.partial(gathered_body, bits=[one.order[:2] for o...]
    unnamed x112 -> x98, local copies, waits for them, and re-layouts: 16.5 us -> 12.8 us
  transfers between devices with their start and end apart: 53 -> 53, of which waited for: 23 -> 23; matrix products, arithmetic and copies ran while one was open for 9% -> 8% of each run, Pallas kernels for 22% -> 22%
where the time goes in v4:
time: 317 us; the launch traced here: 316 us
  Pallas kernels  149 us (47%)
  waiting for transfers between devices  67.9 us (21%)
  starting transfers between devices  53 us (17%)
  matrix products  21.9 us (7%)
  local copies, waits for them, and re-layouts  14.8 us (5%)
  other arithmetic  7.08 us (2%)
    pallas_call x1, Pallas kernels, forward_call(): pl.pallas_call(forward_body, grid=(rows,), in_specs=[pl.BlockSpec(memory_...  41.5 us
    ppermute x43, waiting for transfers between devices, swapped(): lax.ppermute(value, mesh_axes, [(at, at ^ bit) for at in range(device_tot...  34.8 us
    ppermute x43, starting transfers between devices, swapped(): lax.ppermute(value, mesh_axes, [(at, at ^ bit) for at in range(device_tot...  33.3 us
    ppermute x10, waiting for transfers between devices, moved(): return lax.ppermute(value, self.axis, pairs)  33 us
    dot_general x12, matrix products, dot_outer(): lax.dot_general(first_op, second_op, (((0,), (0,)), ((), ())), preferred_...  21.9 us
    pallas_call x3, Pallas kernels, sums_call(): pl.pallas_call(sums_body, grid=((high_end - low_end) // STEPS,), in_specs...  20.7 us
    ppermute x10, starting transfers between devices, moved(): return lax.ppermute(value, self.axis, pairs)  19.7 us
    pallas_call x2, Pallas kernels, leave_call(): pl.pallas_call(functools.partial(leave_body, places_before=low_end), grid...  16.9 us
  transfers between devices with their start and end apart: 53, of which 23 were waited for; matrix products, arithmetic and copies ran while one was open for 8% of the time, Pallas kernels for 22%

profile of v4, /device:TPU:0, one launch (start us, length us, event | category | flops | bytes accessed | tf_op | source)
XLA Modules:
  0.0 315.6 jit_solution(11339165890354924211)
XLA Ops:
  2.9 10.4 %enter.1 = (bf16[8,256,512]{2,1,0:T(8,128)(2,1)}, f32[256,8,512]{2,1,0:T(8,128)}, f32[16,8,512]{2,1,0:T(8,128)S(1)}) custom-call(s32[8]{0:T(128)S(1)} %broadcast_subtract_fusion.count_ref, bf16[8,256,512]{2,1,0:T(8,128)(2,1)} %tokens_ref.7, f32[1,512]{1,0:T(1,128)S(1)} %bitcast.110, f32[16,512]{1,0:T(8,128)S(1)} %get-tuple-element.466.retain_ref), custom_call_target="tpu_custom_call" | custom-call | bytes 27000000 | tf_op jit(solution)/shard_map/enter/pallas_call | solution.py:107
  13.3 3.0 collective-permute-start
  17.0 2.9 collective-permute-done
  19.9 5.7 %collective-permute-start.1 = (f32[16,8,256]{2,1,0:T(8,128)S(1)}, f32[16,8,256]{2,1,0:T(8,128)S(1)}, u32[]{:S(2)}, u32[]{:S(2)}) collective-permute-start(f32[16,8,256]{2,1,0:T(8,128)S(1)} %select_add_fusion.1), channel_id=1, source_target_pairs={{0,24},{4,28},{1,25},{5,29},{2,26},{6,30},{3,27},{7,31}} | collective-permute-start | bytes 393224 | tf_op jit(solution)/shard_map/ppermute | solution.py:439
  25.6 1.3 collective-permute-start.2
  26.9 2.5 collective-permute-start.3
  29.4 8.4 %value.1 = (bf16[8,256,1024]{2,1,0:T(8,128)(2,1)}, bf16[8,256,1024]{2,1,0:T(8,128)(2,1)}) custom-call(bf16[8,256,512]{2,1,0:T(8,128)(2,1)} %get-tuple-element.258.normed_ref, bf16[512,1024]{1,0:T(8,128)(2,1)S(1)} %copy-done.26), custom_call_target="tpu_custom_call" | custom-call | flops 2000000000 | bytes 15000000 | tf_op jit(solution)/shard_map/value/pallas_call | solution.py:597
  38.0 1.6 collective-permute-start.4
  39.8 3.3 %collective-permute-done.4 = f32[16,8,256]{2,1,0:T(8,128)S(1)} collective-permute-done((f32[16,8,256]{2,1,0:T(8,128)S(1)}, f32[16,8,256]{2,1,0:T(8,128)S(1)}, u32[]{:S(2)}, u32[]{:S(2)}) %collective-permute-start.4) | collective-permute-done | bytes 131104 | tf_op jit(solution)/shard_map/ppermute | solution.py:439
  43.2 12.6 %average.1 = (f32[16,8,512]{2,1,0:T(8,128)S(1)}, f32[8,256,512]{2,1,0:T(8,128)}) custom-call(f32[256,8,512]{2,1,0:T(8,128)} %get-tuple-element.229.turned_ref, f32[16,512]{1,0:T(8,128)S(1)} %get-tuple-element.466.retain_ref, f32[16,512]{1,0:T(8,128)S(1)} %get-tuple-element.465.mix_ref, f32[16,8,512]{2,1,0:T(8,128)S(1)} %pad_maximum_fusion.held_ref), custom_call_target="tpu_custom_call" | custom-call | bytes 36000000 | tf_op jit(solution)/shard_map/average/pallas_call | solution.py:166
  56.5 41.5 %dense_forward.1 = (bf16[8,256,512]{2,1,0:T(8,128)(2,1)}, bf16[8,256,512]{2,1,0:T(8,128)(2,1)}, bf16[8,256,512]{2,1,0:T(8,128)(2,1)}, bf16[8,256,1024]{2,1,0:T(8...) custom-call(s32[8]{0:T(128)S(1)} %broadcast_subtract_fusion.count_re, ...), custom_call_target="tpu_custom_call" | custom-call | flops 17999998976 | bytes 120000000 | tf_op jit(solution)/shard_map/dense_forward/pallas_call | solution.py:812
  98.1 1.9 fusion.16
  100.0 4.2 %fusion.12 = f32[256,1024]{1,0:T(8,128)S(1)} fusion(bf16[2048,1024]{1,0:T(8,128)(2,1)} %bitcast.144, bf16[2048,512]{1,0:T(8,128)(2,1)} %bitcast.148, s32[]{:T(128)S(6)} %select_n.219), kind=kOutput, calls=%fused_computation.13 | convolution fusion | flops 1073741824 | bytes 6291460 | tf_op jit(solution)/shard_map/dot_general | solution.py:566
  104.4 3.7 %fusion.18 = f32[256,2048]{1,0:T(8,128)S(1)} fusion(bf16[2048,2048]{1,0:T(8,128)(2,1)S(1)} %bitcast.119, bf16[2048,512]{1,0:T(8,128)(2,1)} %bitcast.122, s32[]{:T(128)S(6)} %select_n.219), kind=kOutput, calls=%fused_computation.19 | convolution fusion | flops 2147483648 | bytes 11534340 | tf_op jit(solution)/shard_map/dot_general | solution.py:566
  108.7 1.3 fusion.8
  111.5 1.3 fusion
  115.6 1.3 fusion.4
  122.0 1.3 fusion.6.refs_1_.refs_5_
  123.3 2.6 fusion.22.refs_9_.refs_11_
  126.0 2.9 joined.5
  129.9 1.5 collective-permute-start.12
  131.4 1.6 collective-permute-start.13
  132.9 11.2 %dense_backward.1 = (f32[8,256,512]{2,1,0:T(8,128)S(1)}, f32[8,256,512]{2,1,0:T(8,128)S(1)}, f32[1,512]{1,0:T(1,128)S(1)}, f32[1,512]{1,0:T(1,128)S(1)}) custom-call(bf16[8,256,2048]{2,1,0:T(8,128)(2,1)} %get-tuple-element.255.grad_main_ref, bf16[8,256,128]{2,1,0:T(8,128)(2,1)S(1)} %get-tuple-element.256.grad_shared_ref, ...), custom_call_target="tpu_custom_call" | custom-call | flops 7000000000 | bytes 36000000 | tf_op jit(solution)/shard_map/dense_backward/pallas_call | solution.py:868
  144.2 6.7 %back_enter.1 = (f32[256,8,512]{2,1,0:T(8,128)S(1)}, f32[16,8,512]{2,1,0:T(8,128)S(1)}) custom-call(f32[8,256,512]{2,1,0:T(8,128)S(1)} %get-tuple-element.262.grad_ref, f32[16,512]{1,0:T(8,128)S(1)} %get-tuple-element.466.retain_ref), custom_call_target="tpu_custom_call" | custom-call | bytes 24000000 | tf_op jit(solution)/shard_map/back_enter/pallas_call | solution.py:224
  151.0 2.0 copy-done
  154.9 4.9 %collective-permute-done.11 = f32[16,8,256]{2,1,0:T(8,128)S(1)} collective-permute-done((f32[16,8,256]{2,1,0:T(8,128)}, f32[16,8,256]{2,1,0:T(8,128)S(1)}, u32[]{:S(2)}, u32[]{:S(2)}) %collective-permute-start.11) | collective-permute-done | bytes 131104 | tf_op jit(solution)/shard_map/ppermute | solution.py:439
  162.0 3.2 %joined.6 = (f32[128,1024]{1,0:T(8,128)S(1)}, f32[128,1024]{1,0:T(8,128)S(1)}, f32[64,2048]{1,0:T(8,128)S(1)}, f32[64,2048]{1,0:T(8,128)S(1)}, f32[64,2176]{1,0:T(8,128)S(1)}, /*index=5*/f32[64,2176]{1,0:T(8,128)S(1)}) custom-call(s32[3]{0:T(128)S(1)} %get-tuple-element.477.refs_0_, f32[256,1024]{1,0:T(8,128)S(1)} %get-tuple-element.272.refs_1_.refs_3_, ...), custom_call_target="tpu_custom_call" | custom-call | bytes 6000000 | tf_op jit(solution)/shard_map/joined/pallas_call | solution.py:926
  165.8 1.3 collective-permute-start.18
  167.1 1.7 collective-permute-start.19
  168.8 1.3 collective-permute-start.15
  170.1 1.3 collective-permute-start.16
  171.4 14.7 %collective-permute-done.15 = f32[16,8,256]{2,1,0:T(8,128)S(1)} collective-permute-done((f32[16,8,256]{2,1,0:T(8,128)S(1)}, f32[16,8,256]{2,1,0:T(8,128)S(1)}, u32[]{:S(2)}, u32[]{:S(2)}) %collective-permute-start.15) | collective-permute-done | bytes 131104 | tf_op jit(solution)/shard_map/ppermute | solution.py:439
  186.0 1.3 collective-permute-start.17
  187.3 6.0 %collective-permute-done.17 = f32[16,8,256]{2,1,0:T(8,128)S(1)} collective-permute-done((f32[16,8,256]{2,1,0:T(8,128)S(1)}, f32[16,8,256]{2,1,0:T(8,128)S(1)}, u32[]{:S(2)}, u32[]{:S(2)}) %collective-permute-start.17) | collective-permute-done | bytes 131104 | tf_op jit(solution)/shard_map/ppermute | solution.py:439
  196.6 1.5 collective-permute-start.23
  198.0 1.4 collective-permute-done.21
  199.8 3.7 %collective-permute-done.22.refs_2_.refs_4_ = f32[64,1024]{1,0:T(8,128)S(1)} collective-permute-done((f32[64,1024]{1,0:T(8,128)S(1)}, f32[64,1024]{1,0:T(8,128)S(1)}, u32[]{:S(2)}, u32[]{:S(2)}) %collective-permute-start.22) | collective-permute-done | bytes 262176 | tf_op jit(solution)/shard_map/ppermute | solution.py:490
  204.3 2.9 collective-permute-start.25
  207.3 2.2 copy-done.2
  209.5 7.7 %adjoint_sums.3 = (f32[4,16,8,512]{3,2,1,0:T(8,128)S(1)}, f32[8,8,512]{2,1,0:T(8,128)S(1)}) custom-call(f32[256,8,512]{2,1,0:T(8,128)S(1)} %copy-done.1, f32[256,8,512]{2,1,0:T(8,128)S(1)} %copy-done.2, f32[16,512]{1,0:T(8,128)S(1)} %get-tuple-element.466.retain_ref, f32[16,512]{1,0:T(8,128)S(1)} %get-tuple-element.464.inverse_ref, ...), custom_call_target="tpu_custom_call" | custom-call | bytes 24000000 | tf_op jit(solution)/shard_map/adjoint_sums/pallas_call | solution.py:319
  217.2 4.0 %collective-permute-done.25.refs_1_ = f32[32,1024]{1,0:T(8,128)S(1)} collective-permute-done((f32[32,1024]{1,0:T(8,128)S(1)}, f32[32,1024]{1,0:T(8,128)S(1)}, u32[]{:S(2)}, u32[]{:S(2)}) %collective-permute-start.25) | collective-permute-done | bytes 131104 | tf_op jit(solution)/shard_map/ppermute | solution.py:490
  221.2 2.8 collective-permute-done.26.refs_3_
  224.2 2.9 collective-permute-start.28
  227.2 7.7 %adjoint_sums.4 = (f32[4,16,8,512]{3,2,1,0:T(8,128)S(1)}, f32[8,8,512]{2,1,0:T(8,128)S(1)}) custom-call(f32[256,8,512]{2,1,0:T(8,128)S(1)} %copy-done.1, f32[256,8,512]{2,1,0:T(8,128)S(1)} %copy-done.3, f32[16,512]{1,0:T(8,128)S(1)} %get-tuple-element.466.retain_ref, f32[16,512]{1,0:T(8,128)S(1)} %get-tuple-element.464.inverse_ref, ...), custom_call_target="tpu_custom_call" | custom-call | bytes 24000000 | tf_op jit(solution)/shard_map/adjoint_sums/pallas_call | solution.py:319
  238.2 1.5 collective-permute-start.32
  239.7 5.2 %adjoint_sums.5 = (f32[4,16,8,512]{3,2,1,0:T(8,128)S(1)}, f32[8,8,512]{2,1,0:T(8,128)S(1)}) custom-call(f32[256,8,512]{2,1,0:T(8,128)S(1)} %copy-done.1, f32[256,8,512]{2,1,0:T(8,128)S(1)} %copy-done.3, f32[16,512]{1,0:T(8,128)S(1)} %get-tuple-element.466.retain_ref, f32[16,512]{1,0:T(8,128)S(1)} %get-tuple-element.464.inverse_ref, ...), custom_call_target="tpu_custom_call" | custom-call | bytes 24000000 | tf_op jit(solution)/shard_map/adjoint_sums/pallas_call | solution.py:319
  244.9 1.4 collective-permute-done.31.refs_2_
  248.5 1.5 collective-permute-start.36
  250.0 1.7 collective-permute-start.34
  252.0 6.6 %leave.2 = (f32[16,8,512]{2,1,0:T(8,128)S(1)}, bf16[8,256,512]{2,1,0:T(8,128)(2,1)}) custom-call(s32[8]{0:T(128)S(1)} %broadcast_subtract_fusion.count_ref, bf16[8,256,512]{2,1,0:T(8,128)(2,1)S(1)} %copy-done.4, f32[1,512]{1,0:T(1,128)S(1)} %bitcast.111, f32[8,256,512]{2,1,0:T(8,128)S(1)} %copy-done.6, bf16[8,256,512]{2,1,0:T(8,128)(2,1)S(1)} %copy-done.7, ...), custom_call_target="tpu_custom_call" | custom-call | bytes 24000000 | tf_op jit(solution)/shard_map/leave/pallas_call | solution.py:393
  258.6 4.0 %collective-permute-done.34.refs_2_ = f32[128,1024]{1,0:T(8,128)S(1)} collective-permute-done((f32[128,1024]{1,0:T(8,128)S(1)}, f32[128,1024]{1,0:T(8,128)S(1)}, u32[]{:S(2)}, u32[]{:S(2)}) %collective-permute-start.34) | collective-permute-done | bytes 524320 | tf_op jit(solution)/shard_map/ppermute | solution.py:490
  262.6 3.7 %collective-permute-done.35.refs_4_ = f32[64,2048]{1,0:T(8,128)S(1)} collective-permute-done((f32[64,2048]{1,0:T(8,128)S(1)}, f32[64,2048]{1,0:T(8,128)S(1)}, u32[]{:S(2)}, u32[]{:S(2)}) %collective-permute-start.35) | collective-permute-done | bytes 524320 | tf_op jit(solution)/shard_map/ppermute | solution.py:490
  266.3 3.5 %placed.5 = (f32[256,1024]{1,0:T(8,128)}, f32[128,2048]{1,0:T(8,128)S(1)}, f32[128,2176]{1,0:T(8,128)S(1)}) custom-call(s32[3]{0:T(128)S(1)} %get-tuple-element.477.refs_0_, f32[128,1024]{1,0:T(8,128)S(1)} %get-tuple-element.396.refs_1_, f32[128,1024]{1,0:T(8,128)S(1)} %collective-permute-done.34.refs_2_, f32[64,2048]{1,0:T(8,128)S(1)} %get-tuple-element.398.refs_3_, ...), custom_call_target="tpu_custom_call" | custom-call | bytes 6000000 | tf_op jit(solution)/shard_map/placed/pallas_call | solution.py:970
  271.0 10.2 %leave.3 = (f32[16,8,512]{2,1,0:T(8,128)}, bf16[8,256,512]{2,1,0:T(8,128)(2,1)}) custom-call(s32[8]{0:T(128)S(1)} %broadcast_subtract_fusion.count_ref, bf16[8,256,512]{2,1,0:T(8,128)(2,1)S(1)} %copy-done.4, f32[1,512]{1,0:T(1,128)S(1)} %bitcast.112, f32[8,256,512]{2,1,0:T(8,128)S(1)} %copy-done.6, ...), custom_call_target="tpu_custom_call", output_to_operand_aliasing={{1}: (9, {})} | custom-call | bytes 24000000 | tf_op jit(solution)/shard_map/leave/pallas_call | solution.py:393
  282.7 2.4 collective-permute-done.37.refs_1_
  286.0 4.1 %gathered.2 = (f32[1024,512]{1,0:T(8,128)}, f32[1024,512]{1,0:T(8,128)}, f32[512,2176]{1,0:T(8,128)}, f32[512,1024]{1,0:T(8,128)}, f32[512,1024]{1,0:T(8,128)}) custom-call(f32[256,1024]{1,0:T(8,128)} %get-tuple-element.421.refs_0_, f32[256,1024]{1,0:T(8,128)} %collective-permute-done.37.refs_1_, f32[128,2048]{1,0:T(8,128)S(1)} %get-tuple-element.423.refs_2_, ...), custom_call_target="tpu_custom_call" | custom-call | bytes 18000000 | tf_op jit(solution)/shard_map/gathered/pallas_call | solution.py:1034
  290.1 1.6 collective-permute-start.41
  291.7 1.9 collective-permute-start.43
  294.6 2.9 collective-permute-done.42
  297.5 2.0 collective-permute-start.44
  299.5 1.4 collective-permute-start.45
  302.7 3.4 %collective-permute-done.45 = f32[40,512]{1,0:T(8,128)S(1)} collective-permute-done((f32[40,512]{1,0:T(8,128)S(1)}, f32[40,512]{1,0:T(8,128)S(1)}, u32[]{:S(2)}, u32[]{:S(2)}) %collective-permute-start.45) | collective-permute-done | bytes 81952 | tf_op jit(solution)/shard_map/ppermute | solution.py:490
  310.2 1.5 collective-permute-done.49.refs_2_
  312.0 3.4 %gathered.3 = (f32[1024,512]{1,0:T(8,128)}, f32[1024,512]{1,0:T(8,128)}, f32[512,2176]{1,0:T(8,128)}, f32[512,1024]{1,0:T(8,128)}, f32[512,1024]{1,0:T(8,128)}) custom-call(f32[256,1024]{1,0:T(8,128)S(1)} %collective-permute-done.47.refs_0_, ...), custom_call_target="tpu_custom_call", output_to_operand_aliasing={{0}: (6, {}), {1}: (7, {}), {2}: (8, {}), {3}: (9, {}), {4}... | custom-call | bytes 18000000 | tf_op jit(solution)/shard_map/gathered/pallas_call | solution.py:1034
  (215 shorter events, 40.5 us)
Async XLA Ops:
  0.6 28.8 %copy-start.26 = (bf16[512,1024]{1,0:T(8,128)(2,1)S(1)}, bf16[512,1024]{1,0:T(8,128)(2,1)}, u32[]{:S(2)}) copy-start(bf16[512,1024]{1,0:T(8,128)(2,1)} %value_weight_ref.3) | copy-start | bytes 3145732
  13.3 6.5 %collective-permute-start = (f32[16,8,256]{2,1,0:T(8,128)S(1)}, f32[16,8,256]{2,1,0:T(8,128)S(1)}, u32[]{:S(2)}, u32[]{:S(2)}) collective-permute-start(f32[16,8,256]{2,1,0:T(8,128)S(1)} %constant_dynamic-slice_fusion.2), channel_id=1, source_target_pairs={{0,4},{4,0},{8,12},{12,8},{16,20},{20,16},{24,28},{28,24},{1,5},{5... | collective-permute-start | bytes 393224 | tf_op jit(solution)/shard_map/ppermute | solution.py:439
  19.9 18.0 %collective-permute-start.1 = (f32[16,8,256]{2,1,0:T(8,128)S(1)}, f32[16,8,256]{2,1,0:T(8,128)S(1)}, u32[]{:S(2)}, u32[]{:S(2)}) collective-permute-start(f32[16,8,256]{2,1,0:T(8,128)S(1)} %select_add_fusion.1), channel_id=1, source_target_pairs={{0,24},{4,28},{1,25},{5,29},{2,26},{6,30},{3,27},{7,31}} | collective-permute-start | bytes 393224 | tf_op jit(solution)/shard_map/ppermute | solution.py:439
  25.6 12.3 %collective-permute-start.2 = (f32[16,8,256]{2,1,0:T(8,128)S(1)}, f32[16,8,256]{2,1,0:T(8,128)S(1)}, u32[]{:S(2)}, u32[]{:S(2)}) collective-permute-start(f32[16,8,256]{2,1,0:T(8,128)S(1)} %select_add_fusion.1), channel_id=1, source_target_pairs={{0,16},{4,20},{8,24},{12,28},{1,17},{5,21},{9,25},{13,29},{2,18},{... | collective-permute-start | bytes 393224 | tf_op jit(solution)/shard_map/ppermute | solution.py:439
  26.9 11.0 %collective-permute-start.3 = (f32[16,8,256]{2,1,0:T(8,128)S(1)}, f32[16,8,256]{2,1,0:T(8,128)S(1)}, u32[]{:S(2)}, u32[]{:S(2)}) collective-permute-start(f32[16,8,256]{2,1,0:T(8,128)S(1)} %select_add_fusion.1), channel_id=1, source_target_pairs={{0,8},{4,12},{8,16},{12,20},{16,24},{20,28},{1,9},{5,13},{9,17},{1... | collective-permute-start | bytes 393224 | tf_op jit(solution)/shard_map/ppermute | solution.py:439
  38.0 5.0 %collective-permute-start.4 = (f32[16,8,256]{2,1,0:T(8,128)S(1)}, f32[16,8,256]{2,1,0:T(8,128)S(1)}, u32[]{:S(2)}, u32[]{:S(2)}) collective-permute-start(f32[16,8,256]{2,1,0:T(8,128)S(1)} %fusion.26), channel_id=1, source_target_pairs={{0,4},{4,0},{8,12},{12,8},{16,20},{20,16},{24,28},{28,24},{1,5},{5... | collective-permute-start | bytes 393224 | tf_op jit(solution)/shard_map/ppermute | solution.py:439
  43.1 13.4 %copy-start.25 = (bf16[1024,512]{1,0:T(8,128)(2,1)S(1)}, bf16[1024,512]{1,0:T(8,128)(2,1)}, u32[]{:S(2)}) copy-start(bf16[1024,512]{1,0:T(8,128)(2,1)} %output_weight_ref.1) | copy-start | bytes 3145732
  43.1 13.4 %copy-start.28 = (f32[512]{0:T(512)S(1)}, f32[512]{0:T(512)}, u32[]{:S(2)}) copy-start(f32[512]{0:T(512)} %param.23) | copy-start | bytes 6148
  99.9 21.9 %collective-permute-start.10 = (f32[256,128]{1,0:T(8,128)S(1)}, f32[256,128]{1,0:T(8,128)S(1)}, u32[]{:S(2)}, u32[]{:S(2)}) collective-permute-start(f32[256,128]{1,0:T(8,128)S(1)} %fusion.16), channel_id=1, source_target_pairs={{0,1},{1,0},{2,3},{3,2},{4,5},{5,4},{6,7},{7,6},{8,9},{9,8},{10,11... | collective-permute-start | bytes 393224 | tf_op jit(solution)/shard_map/ppermute | solution.py:490
  104.3 21.7 %collective-permute-start.8 = (f32[256,1024]{1,0:T(8,128)S(1)}, f32[256,1024]{1,0:T(8,128)S(1)}, u32[]{:S(2)}, u32[]{:S(2)}) collective-permute-start(f32[256,1024]{1,0:T(8,128)S(1)} %fusion.12), channel_id=1, source_target_pairs={{0,1},{1,0},{2,3},{3,2},{4,5},{5,4},{6,7},{7,6},{8,9},{9,8},{10,11... | collective-permute-start | bytes 3145736 | tf_op jit(solution)/shard_map/ppermute | solution.py:490
  108.1 17.9 %collective-permute-start.7 = (f32[256,2048]{1,0:T(8,128)S(1)}, f32[256,2048]{1,0:T(8,128)S(1)}, u32[]{:S(2)}, u32[]{:S(2)}) collective-permute-start(f32[256,2048]{1,0:T(8,128)S(1)} %fusion.18), channel_id=1, source_target_pairs={{0,1},{1,0},{2,3},{3,2},{4,5},{5,4},{6,7},{7,6},{8,9},{9,8},{10,11... | collective-permute-start | bytes 6291464 | tf_op jit(solution)/shard_map/ppermute | solution.py:490
  110.0 16.0 %collective-permute-start.9 = (f32[256,1024]{1,0:T(8,128)S(1)}, f32[256,1024]{1,0:T(8,128)S(1)}, u32[]{:S(2)}, u32[]{:S(2)}) collective-permute-start(f32[256,1024]{1,0:T(8,128)S(1)} %fusion.8), channel_id=1, source_target_pairs={{0,1},{1,0},{2,3},{3,2},{4,5},{5,4},{6,7},{7,6},{8,9},{9,8},{10,11... | collective-permute-start | bytes 3145736 | tf_op jit(solution)/shard_map/ppermute | solution.py:490
  112.8 13.1 %collective-permute-start.6 = (f32[512,512]{1,0:T(8,128)S(1)}, f32[512,512]{1,0:T(8,128)S(1)}, u32[]{:S(2)}, u32[]{:S(2)}) collective-permute-start(f32[512,512]{1,0:T(8,128)S(1)} %fusion), channel_id=1, source_target_pairs={{0,1},{1,0},{2,3},{3,2},{4,5},{5,4},{6,7},{7,6},{8,9},{9,8},{10,11... | collective-permute-start | bytes 3145736 | tf_op jit(solution)/shard_map/ppermute | solution.py:490
  121.9 4.1 %collective-permute-start.5 = (f32[512,512]{1,0:T(8,128)S(1)}, f32[512,512]{1,0:T(8,128)S(1)}, u32[]{:S(2)}, u32[]{:S(2)}) collective-permute-start(f32[512,512]{1,0:T(8,128)S(1)} %fusion.4), channel_id=1, source_target_pairs={{0,1},{1,0},{2,3},{3,2},{4,5},{5,4},{6,7},{7,6},{8,9},{9,8},{10,11... | collective-permute-start | bytes 3145736 | tf_op jit(solution)/shard_map/ppermute | solution.py:490
  129.8 30.9 %collective-permute-start.14 = (f32[128,2176]{1,0:T(8,128)}, f32[128,2176]{1,0:T(8,128)S(1)}, u32[]{:S(2)}, u32[]{:S(2)}) collective-permute-start(f32[128,2176]{1,0:T(8,128)} %get-tuple-element.269), channel_id=1, source_target_pairs={{0,8},{1,9},{2,10},{3,11},{4,12},{5,13},{6,14},{7,15},{8,0},{9,1},... | collective-permute-start | bytes 3342344 | tf_op jit(solution)/shard_map/ppermute | solution.py:490
  129.9 30.8 %collective-permute-start.12 = (f32[256,1024]{1,0:T(8,128)}, f32[256,1024]{1,0:T(8,128)}, u32[]{:S(2)}, u32[]{:S(2)}) collective-permute-start(f32[256,1024]{1,0:T(8,128)} %get-tuple-element.265), channel_id=1, source_target_pairs={{0,2},{1,3},{2,0},{3,1},{4,6},{5,7},{6,4},{7,5},{8,10},{9,11},{10,... | collective-permute-start | bytes 3145736 | tf_op jit(solution)/shard_map/ppermute | solution.py:490
  131.4 29.4 %collective-permute-start.13 = (f32[128,2048]{1,0:T(8,128)}, f32[128,2048]{1,0:T(8,128)}, u32[]{:S(2)}, u32[]{:S(2)}) collective-permute-start(f32[128,2048]{1,0:T(8,128)} %get-tuple-element.267), channel_id=1, source_target_pairs={{0,4},{1,5},{2,6},{3,7},{4,0},{5,1},{6,2},{7,3},{8,12},{9,13},{10,... | collective-permute-start | bytes 3145736 | tf_op jit(solution)/shard_map/ppermute | solution.py:490
  154.4 5.4 %collective-permute-start.11 = (f32[16,8,256]{2,1,0:T(8,128)}, f32[16,8,256]{2,1,0:T(8,128)S(1)}, u32[]{:S(2)}, u32[]{:S(2)}) collective-permute-start(f32[16,8,256]{2,1,0:T(8,128)} %constant_dynamic-slice_fusion), channel_id=1, source_target_pairs={{28,24},{24,28},{20,16},{16,20},{12,8},{8,12},{4,0},{0,4},{29,25},... | collective-permute-start | bytes 393224 | tf_op jit(solution)/shard_map/ppermute | solution.py:439
  162.0 31.3 %copy-start.37 = (f32[16,256]{1,0:T(8,128)S(1)}, f32[16,256]{1,0:T(8,128)}, u32[]{:S(2)}) copy-start(f32[16,256]{1,0:T(8,128)} %get-tuple-element.445) | copy-start | bytes 49156
  165.2 28.2 %collective-permute-start.20 = (f32[64,2176]{1,0:T(8,128)S(1)}, f32[64,2176]{1,0:T(8,128)S(1)}, u32[]{:S(2)}, u32[]{:S(2)}) collective-permute-start(f32[64,2176]{1,0:T(8,128)S(1)} %get-tuple-element.289), channel_id=1, source_target_pairs={{0,2},{1,3},{2,0},{3,1},{4,6},{5,7},{6,4},{7,5},{8,10},{9,11},{10,... | collective-permute-start | bytes 1671176 | tf_op jit(solution)/shard_map/ppermute | solution.py:490
  165.8 27.6 %collective-permute-start.18 = (f32[128,1024]{1,0:T(8,128)S(1)}, f32[128,1024]{1,0:T(8,128)S(1)}, u32[]{:S(2)}, u32[]{:S(2)}) collective-permute-start(f32[128,1024]{1,0:T(8,128)S(1)} %get-tuple-element.285), channel_id=1, source_target_pairs={{0,4},{1,5},{2,6},{3,7},{4,0},{5,1},{6,2},{7,3},{8,12},{9,13},{10,... | collective-permute-start | bytes 1572872 | tf_op jit(solution)/shard_map/ppermute | solution.py:490
  167.1 26.3 %collective-permute-start.19 = (f32[64,2048]{1,0:T(8,128)S(1)}, f32[64,2048]{1,0:T(8,128)S(1)}, u32[]{:S(2)}, u32[]{:S(2)}) collective-permute-start(f32[64,2048]{1,0:T(8,128)S(1)} %get-tuple-element.287), channel_id=1, source_target_pairs={{0,8},{1,9},{2,10},{3,11},{4,12},{5,13},{6,14},{7,15},{8,0},{9,1},... | collective-permute-start | bytes 1572872 | tf_op jit(solution)/shard_map/ppermute | solution.py:490
  168.8 17.2 %collective-permute-start.15 = (f32[16,8,256]{2,1,0:T(8,128)S(1)}, f32[16,8,256]{2,1,0:T(8,128)S(1)}, u32[]{:S(2)}, u32[]{:S(2)}) collective-permute-start(f32[16,8,256]{2,1,0:T(8,128)S(1)} %select_add_fusion), channel_id=1, source_target_pairs={{28,4},{24,0},{29,5},{25,1},{30,6},{26,2},{31,7},{27,3}} | collective-permute-start | bytes 393224 | tf_op jit(solution)/shard_map/ppermute | solution.py:439
  170.1 17.2 %collective-permute-start.16 = (f32[16,8,256]{2,1,0:T(8,128)S(1)}, f32[16,8,256]{2,1,0:T(8,128)S(1)}, u32[]{:S(2)}, u32[]{:S(2)}) collective-permute-start(f32[16,8,256]{2,1,0:T(8,128)S(1)} %select_add_fusion), channel_id=1, source_target_pairs={{28,12},{24,8},{20,4},{16,0},{29,13},{25,9},{21,5},{17,1},{30,14},... | collective-permute-start | bytes 393224 | tf_op jit(solution)/shard_map/ppermute | solution.py:439
  186.0 7.3 %collective-permute-start.17 = (f32[16,8,256]{2,1,0:T(8,128)S(1)}, f32[16,8,256]{2,1,0:T(8,128)S(1)}, u32[]{:S(2)}, u32[]{:S(2)}) collective-permute-start(f32[16,8,256]{2,1,0:T(8,128)S(1)} %select_add_fusion), channel_id=1, source_target_pairs={{28,20},{24,16},{20,12},{16,8},{12,4},{8,0},{29,21},{25,17},{21,13... | collective-permute-start | bytes 393224 | tf_op jit(solution)/shard_map/ppermute | solution.py:439
  194.4 5.0 %collective-permute-start.21 = (f32[16,8,256]{2,1,0:T(8,128)S(1)}, f32[16,8,256]{2,1,0:T(8,128)S(1)}, u32[]{:S(2)}, u32[]{:S(2)}) collective-permute-start(f32[16,8,256]{2,1,0:T(8,128)S(1)} %fusion.24), channel_id=1, source_target_pairs={{28,24},{24,28},{20,16},{16,20},{12,8},{8,12},{4,0},{0,4},{29,25},... | collective-permute-start | bytes 393224 | tf_op jit(solution)/shard_map/ppermute | solution.py:439
  195.7 7.8 %collective-permute-start.24 = (f32[32,2176]{1,0:T(8,128)S(1)}, f32[32,2176]{1,0:T(8,128)S(1)}, u32[]{:S(2)}, u32[]{:S(2)}) collective-permute-start(f32[32,2176]{1,0:T(8,128)S(1)} %get-tuple-element.310), channel_id=1, source_target_pairs={{0,4},{1,5},{2,6},{3,7},{4,0},{5,1},{6,2},{7,3},{8,12},{9,13},{10,... | collective-permute-start | bytes 835592 | tf_op jit(solution)/shard_map/ppermute | solution.py:490
  196.6 6.9 %collective-permute-start.22 = (f32[64,1024]{1,0:T(8,128)S(1)}, f32[64,1024]{1,0:T(8,128)S(1)}, u32[]{:S(2)}, u32[]{:S(2)}) collective-permute-start(f32[64,1024]{1,0:T(8,128)S(1)} %get-tuple-element.306), channel_id=1, source_target_pairs={{0,8},{1,9},{2,10},{3,11},{4,12},{5,13},{6,14},{7,15},{8,0},{9,1},... | collective-permute-start | bytes 786440 | tf_op jit(solution)/shard_map/ppermute | solution.py:490
  196.6 6.9 %collective-permute-start.23 = (f32[32,2048]{1,0:T(8,128)S(1)}, f32[32,2048]{1,0:T(8,128)S(1)}, u32[]{:S(2)}, u32[]{:S(2)}) collective-permute-start(f32[32,2048]{1,0:T(8,128)S(1)} %get-tuple-element.308), channel_id=1, source_target_pairs={{0,2},{1,3},{2,0},{3,1},{4,6},{5,7},{6,4},{7,5},{8,10},{9,11},{10,... | collective-permute-start | bytes 786440 | tf_op jit(solution)/shard_map/ppermute | solution.py:490
  204.2 19.9 %collective-permute-start.27 = (f32[16,2176]{1,0:T(8,128)S(1)}, f32[16,2176]{1,0:T(8,128)S(1)}, u32[]{:S(2)}, u32[]{:S(2)}) collective-permute-start(f32[16,2176]{1,0:T(8,128)S(1)} %get-tuple-element.334), channel_id=1, source_target_pairs={{0,16},{1,17},{2,18},{3,19},{4,20},{5,21},{6,22},{7,23},{8,24},{9,... | collective-permute-start | bytes 417800 | tf_op jit(solution)/shard_map/ppermute | solution.py:490
  204.3 17.0 %collective-permute-start.25 = (f32[32,1024]{1,0:T(8,128)S(1)}, f32[32,1024]{1,0:T(8,128)S(1)}, u32[]{:S(2)}, u32[]{:S(2)}) collective-permute-start(f32[32,1024]{1,0:T(8,128)S(1)} %get-tuple-element.330), channel_id=1, source_target_pairs={{0,16},{1,17},{2,18},{3,19},{4,20},{5,21},{6,22},{7,23},{8,24},{9,... | collective-permute-start | bytes 393224 | tf_op jit(solution)/shard_map/ppermute | solution.py:490
  207.2 16.9 %collective-permute-start.26 = (f32[16,2048]{1,0:T(8,128)S(1)}, f32[16,2048]{1,0:T(8,128)S(1)}, u32[]{:S(2)}, u32[]{:S(2)}) collective-permute-start(f32[16,2048]{1,0:T(8,128)S(1)} %get-tuple-element.332), channel_id=1, source_target_pairs={{0,16},{1,17},{2,18},{3,19},{4,20},{5,21},{6,22},{7,23},{8,24},{9,... | collective-permute-start | bytes 393224 | tf_op jit(solution)/shard_map/ppermute | solution.py:490
  209.5 17.7 %copy-start.3 = (f32[256,8,512]{2,1,0:T(8,128)S(1)}, f32[256,8,512]{2,1,0:T(8,128)}, u32[]{:S(2)}) copy-start(f32[256,8,512]{2,1,0:T(8,128)} %get-tuple-element.229.turned_ref) | copy-start | bytes 12582916
  224.1 11.6 %collective-permute-start.30 = (f32[16,2176]{1,0:T(8,128)S(1)}, f32[16,2176]{1,0:T(8,128)S(1)}, u32[]{:S(2)}, u32[]{:S(2)}) collective-permute-start(f32[16,2176]{1,0:T(8,128)S(1)} %get-tuple-element.360.refs_5_), channel_id=1, source_target_pairs={{0,16},{1,17},{2,18},{3,19},{4,20},{5,21},{6,22},{7,23},{8,24},{9,... | collective-permute-start | bytes 417800 | tf_op jit(solution)/shard_map/ppermute | solution.py:490
  224.2 10.7 %collective-permute-start.28 = (f32[32,1024]{1,0:T(8,128)S(1)}, f32[32,1024]{1,0:T(8,128)S(1)}, u32[]{:S(2)}, u32[]{:S(2)}) collective-permute-start(f32[32,1024]{1,0:T(8,128)S(1)} %get-tuple-element.356.refs_1_), channel_id=1, source_target_pairs={{0,16},{1,17},{2,18},{3,19},{4,20},{5,21},{6,22},{7,23},{8,24},{9,... | collective-permute-start | bytes 393224 | tf_op jit(solution)/shard_map/ppermute | solution.py:490
  227.1 8.6 %collective-permute-start.29 = (f32[16,2048]{1,0:T(8,128)S(1)}, f32[16,2048]{1,0:T(8,128)S(1)}, u32[]{:S(2)}, u32[]{:S(2)}) collective-permute-start(f32[16,2048]{1,0:T(8,128)S(1)} %get-tuple-element.358.refs_3_), channel_id=1, source_target_pairs={{0,16},{1,17},{2,18},{3,19},{4,20},{5,21},{6,22},{7,23},{8,24},{9,... | collective-permute-start | bytes 393224 | tf_op jit(solution)/shard_map/ppermute | solution.py:490
  236.6 10.7 %collective-permute-start.33 = (f32[32,2176]{1,0:T(8,128)S(1)}, f32[32,2176]{1,0:T(8,128)S(1)}, u32[]{:S(2)}, u32[]{:S(2)}) collective-permute-start(f32[32,2176]{1,0:T(8,128)S(1)} %get-tuple-element.379.refs_5_), channel_id=1, source_target_pairs={{0,4},{1,5},{2,6},{3,7},{4,0},{5,1},{6,2},{7,3},{8,12},{9,13},{10,... | collective-permute-start | bytes 835592 | tf_op jit(solution)/shard_map/ppermute | solution.py:490
  237.5 8.9 %collective-permute-start.31 = (f32[64,1024]{1,0:T(8,128)S(1)}, f32[64,1024]{1,0:T(8,128)S(1)}, u32[]{:S(2)}, u32[]{:S(2)}) collective-permute-start(f32[64,1024]{1,0:T(8,128)S(1)} %get-tuple-element.375.refs_1_), channel_id=1, source_target_pairs={{0,8},{1,9},{2,10},{3,11},{4,12},{5,13},{6,14},{7,15},{8,0},{9,1},... | collective-permute-start | bytes 786440 | tf_op jit(solution)/shard_map/ppermute | solution.py:490
  238.2 9.1 %collective-permute-start.32 = (f32[32,2048]{1,0:T(8,128)S(1)}, f32[32,2048]{1,0:T(8,128)S(1)}, u32[]{:S(2)}, u32[]{:S(2)}) collective-permute-start(f32[32,2048]{1,0:T(8,128)S(1)} %get-tuple-element.377.refs_3_), channel_id=1, source_target_pairs={{0,2},{1,3},{2,0},{3,1},{4,6},{5,7},{6,4},{7,5},{8,10},{9,11},{10,... | collective-permute-start | bytes 786440 | tf_op jit(solution)/shard_map/ppermute | solution.py:490
  244.9 13.7 %copy-start.12 = (f32[4,16,8,512]{3,2,1,0:T(8,128)}, f32[4,16,8,512]{3,2,1,0:T(8,128)S(1)}, u32[]{:S(2)}) copy-start(f32[4,16,8,512]{3,2,1,0:T(8,128)S(1)} %get-tuple-element.411) | copy-start | bytes 3145732
  248.5 17.9 %collective-permute-start.36 = (f32[64,2176]{1,0:T(8,128)S(1)}, f32[64,2176]{1,0:T(8,128)S(1)}, u32[]{:S(2)}, u32[]{:S(2)}) collective-permute-start(f32[64,2176]{1,0:T(8,128)S(1)} %get-tuple-element.400.refs_5_), channel_id=1, source_target_pairs={{0,2},{1,3},{2,0},{3,1},{4,6},{5,7},{6,4},{7,5},{8,10},{9,11},{10,... | collective-permute-start | bytes 1671176 | tf_op jit(solution)/shard_map/ppermute | solution.py:490
  250.0 12.6 %collective-permute-start.34 = (f32[128,1024]{1,0:T(8,128)S(1)}, f32[128,1024]{1,0:T(8,128)S(1)}, u32[]{:S(2)}, u32[]{:S(2)}) collective-permute-start(f32[128,1024]{1,0:T(8,128)S(1)} %get-tuple-element.396.refs_1_), channel_id=1, source_target_pairs={{0,4},{1,5},{2,6},{3,7},{4,0},{5,1},{6,2},{7,3},{8,12},{9,13},{10,... | collective-permute-start | bytes 1572872 | tf_op jit(solution)/shard_map/ppermute | solution.py:490
  251.7 14.6 %collective-permute-start.35 = (f32[64,2048]{1,0:T(8,128)S(1)}, f32[64,2048]{1,0:T(8,128)S(1)}, u32[]{:S(2)}, u32[]{:S(2)}) collective-permute-start(f32[64,2048]{1,0:T(8,128)S(1)} %get-tuple-element.398.refs_3_), channel_id=1, source_target_pairs={{0,8},{1,9},{2,10},{3,11},{4,12},{5,13},{6,14},{7,15},{8,0},{9,1},... | collective-permute-start | bytes 1572872 | tf_op jit(solution)/shard_map/ppermute | solution.py:490
  269.9 12.8 %copy-start.22 = (f32[1,512]{1,0:T(1,128)S(1)}, f32[1,512]{1,0:T(1,128)}, u32[]{:S(2)}) copy-start(f32[1,512]{1,0:T(1,128)} %copy-done.21) | copy-start | bytes 6148
  269.9 15.6 %collective-permute-start.39 = (f32[128,2176]{1,0:T(8,128)S(1)}, f32[128,2176]{1,0:T(8,128)S(1)}, u32[]{:S(2)}, u32[]{:S(2)}) collective-permute-start(f32[128,2176]{1,0:T(8,128)S(1)} %get-tuple-element.425.refs_4_), channel_id=1, source_target_pairs={{0,8},{1,9},{2,10},{3,11},{4,12},{5,13},{6,14},{7,15},{8,0},{9,1},... | collective-permute-start | bytes 3342344 | tf_op jit(solution)/shard_map/ppermute | solution.py:490
  270.0 15.2 %collective-permute-start.37 = (f32[256,1024]{1,0:T(8,128)}, f32[256,1024]{1,0:T(8,128)}, u32[]{:S(2)}, u32[]{:S(2)}) collective-permute-start(f32[256,1024]{1,0:T(8,128)} %get-tuple-element.421.refs_0_), channel_id=1, source_target_pairs={{0,2},{1,3},{2,0},{3,1},{4,6},{5,7},{6,4},{7,5},{8,10},{9,11},{10,... | collective-permute-start | bytes 3145736 | tf_op jit(solution)/shard_map/ppermute | solution.py:490
  270.5 14.9 %collective-permute-start.38 = (f32[128,2048]{1,0:T(8,128)S(1)}, f32[128,2048]{1,0:T(8,128)}, u32[]{:S(2)}, u32[]{:S(2)}) collective-permute-start(f32[128,2048]{1,0:T(8,128)S(1)} %get-tuple-element.423.refs_2_), channel_id=1, source_target_pairs={{0,4},{1,5},{2,6},{3,7},{4,0},{5,1},{6,2},{7,3},{8,12},{9,13},{10,... | collective-permute-start | bytes 3145736 | tf_op jit(solution)/shard_map/ppermute | solution.py:490
  282.7 25.7 %copy-start.33 = (f32[512,16]{0,1:T(8,128)S(1)}, f32[512,16]{0,1:T(8,128)}, u32[]{:S(2)}) copy-start(f32[512,16]{0,1:T(8,128)} %param.20) | copy-start | bytes 98308
  282.7 25.7 %copy-start.35 = (f32[512,16]{0,1:T(8,128)S(1)}, f32[512,16]{0,1:T(8,128)}, u32[]{:S(2)}) copy-start(f32[512,16]{0,1:T(8,128)} %param.21) | copy-start | bytes 98308
  282.7 25.7 %copy-start.36 = (f32[512,16]{0,1:T(8,128)S(1)}, f32[512,16]{0,1:T(8,128)}, u32[]{:S(2)}) copy-start(f32[512,16]{0,1:T(8,128)} %param.22) | copy-start | bytes 98308
  282.7 26.4 %copy-start.38 = (bf16[512]{0:T(512)(128)(2,1)S(1)}, bf16[512]{0:T(512)(128)(2,1)}, u32[]{:S(2)}) copy-start(bf16[512]{0:T(512)(128)(2,1)} %param.18) | copy-start | bytes 3076
  285.4 21.8 %collective-permute-start.47 = (f32[256,1024]{1,0:T(8,128)}, f32[256,1024]{1,0:T(8,128)S(1)}, u32[]{:S(2)}, u32[]{:S(2)}) collective-permute-start(f32[256,1024]{1,0:T(8,128)} %get-tuple-element.421.refs_0_), channel_id=1, source_target_pairs={{0,1},{1,0},{2,3},{3,2},{4,5},{5,4},{6,7},{7,6},{8,9},{9,8},{10,11... | collective-permute-start | bytes 3145736 | tf_op jit(solution)/shard_map/ppermute | solution.py:490
  285.4 4.6 %collective-permute-start.40 = (f32[40,512]{1,0:T(8,128)S(1)}, f32[40,512]{1,0:T(8,128)S(1)}, u32[]{:S(2)}, u32[]{:S(2)}) collective-permute-start(f32[40,512]{1,0:T(8,128)S(1)} %pad.4), channel_id=1, source_target_pairs={{0,1},{1,0},{2,3},{3,2},{4,5},{5,4},{6,7},{7,6},{8,9},{9,8},{10,11... | collective-permute-start | bytes 245768 | tf_op jit(solution)/shard_map/ppermute | solution.py:490
  290.1 4.5 %collective-permute-start.41 = (f32[40,512]{1,0:T(8,128)S(1)}, f32[40,512]{1,0:T(8,128)S(1)}, u32[]{:S(2)}, u32[]{:S(2)}) collective-permute-start(f32[40,512]{1,0:T(8,128)S(1)} %add.218), channel_id=1, source_target_pairs={{0,2},{1,3},{2,0},{3,1},{4,6},{5,7},{6,4},{7,5},{8,10},{9,11},{10,... | collective-permute-start | bytes 245768 | tf_op jit(solution)/shard_map/ppermute | solution.py:490
  291.6 5.9 %collective-permute-start.42 = (f32[40,512]{1,0:T(8,128)S(1)}, f32[40,512]{1,0:T(8,128)S(1)}, u32[]{:S(2)}, u32[]{:S(2)}) collective-permute-start(f32[40,512]{1,0:T(8,128)S(1)} %add.218), channel_id=1, source_target_pairs={{0,4},{1,5},{2,6},{3,7},{4,0},{5,1},{6,2},{7,3},{8,12},{9,13},{10,... | collective-permute-start | bytes 245768 | tf_op jit(solution)/shard_map/ppermute | solution.py:490
  291.7 5.7 %collective-permute-start.43 = (f32[40,512]{1,0:T(8,128)S(1)}, f32[40,512]{1,0:T(8,128)S(1)}, u32[]{:S(2)}, u32[]{:S(2)}) collective-permute-start(f32[40,512]{1,0:T(8,128)S(1)} %add.218), channel_id=1, source_target_pairs={{0,6},{1,7},{2,4},{3,5},{4,2},{5,3},{6,0},{7,1},{8,14},{9,15},{10,... | collective-permute-start | bytes 245768 | tf_op jit(solution)/shard_map/ppermute | solution.py:490
  297.5 5.1 %collective-permute-start.44 = (f32[40,512]{1,0:T(8,128)S(1)}, f32[40,512]{1,0:T(8,128)S(1)}, u32[]{:S(2)}, u32[]{:S(2)}) collective-permute-start(f32[40,512]{1,0:T(8,128)S(1)} %add_add_fusion.1), channel_id=1, source_target_pairs={{0,8},{1,9},{2,10},{3,11},{4,12},{5,13},{6,14},{7,15},{8,0},{9,1},... | collective-permute-start | bytes 245768 | tf_op jit(solution)/shard_map/ppermute | solution.py:490
  299.5 6.6 %collective-permute-start.45 = (f32[40,512]{1,0:T(8,128)S(1)}, f32[40,512]{1,0:T(8,128)S(1)}, u32[]{:S(2)}, u32[]{:S(2)}) collective-permute-start(f32[40,512]{1,0:T(8,128)S(1)} %add_add_fusion.1), channel_id=1, source_target_pairs={{0,16},{1,17},{2,18},{3,19},{4,20},{5,21},{6,22},{7,23},{8,24},{9,... | collective-permute-start | bytes 245768 | tf_op jit(solution)/shard_map/ppermute | solution.py:490
  300.9 6.3 %collective-permute-start.46 = (f32[40,512]{1,0:T(8,128)S(1)}, f32[40,512]{1,0:T(8,128)S(1)}, u32[]{:S(2)}, u32[]{:S(2)}) collective-permute-start(f32[40,512]{1,0:T(8,128)S(1)} %add_add_fusion.1), channel_id=1, source_target_pairs={{0,24},{1,25},{2,26},{3,27},{4,28},{5,29},{6,30},{7,31},{8,16},{9,... | collective-permute-start | bytes 245768 | tf_op jit(solution)/shard_map/ppermute | solution.py:490
  302.2 9.8 %collective-permute-start.51 = (f32[128,2176]{1,0:T(8,128)S(1)}, f32[128,2176]{1,0:T(8,128)S(1)}, u32[]{:S(2)}, u32[]{:S(2)}) collective-permute-start(f32[128,2176]{1,0:T(8,128)S(1)} %get-tuple-element.425.refs_4_), channel_id=1, source_target_pairs={{0,1},{1,0},{2,3},{3,2},{4,5},{5,4},{6,7},{7,6},{8,9},{9,8},{10,11... | collective-permute-start | bytes 3342344 | tf_op jit(solution)/shard_map/ppermute | solution.py:490
  302.6 9.4 %collective-permute-start.52 = (f32[128,2176]{1,0:T(8,128)S(1)}, f32[128,2176]{1,0:T(8,128)S(1)}, u32[]{:S(2)}, u32[]{:S(2)}) collective-permute-start(f32[128,2176]{1,0:T(8,128)S(1)} %collective-permute-done.39.refs_5_), channel_id=1, source_target_pairs={{0,1},{1,0},{2,3},{3,2},{4,5},{5,4},{6,7},{7,6},{8,9},{9,8},{10,11... | collective-permute-start | bytes 3342344 | tf_op jit(solution)/shard_map/ppermute | solution.py:490
  306.1 4.1 %collective-permute-start.48 = (f32[256,1024]{1,0:T(8,128)}, f32[256,1024]{1,0:T(8,128)S(1)}, u32[]{:S(2)}, u32[]{:S(2)}) collective-permute-start(f32[256,1024]{1,0:T(8,128)} %collective-permute-done.37.refs_1_), channel_id=1, source_target_pairs={{0,1},{1,0},{2,3},{3,2},{4,5},{5,4},{6,7},{7,6},{8,9},{9,8},{10,11... | collective-permute-start | bytes 3145736 | tf_op jit(solution)/shard_map/ppermute | solution.py:490
  307.3 4.5 %collective-permute-start.49 = (f32[128,2048]{1,0:T(8,128)S(1)}, f32[128,2048]{1,0:T(8,128)S(1)}, u32[]{:S(2)}, u32[]{:S(2)}) collective-permute-start(f32[128,2048]{1,0:T(8,128)S(1)} %get-tuple-element.423.refs_2_), channel_id=1, source_target_pairs={{0,1},{1,0},{2,3},{3,2},{4,5},{5,4},{6,7},{7,6},{8,9},{9,8},{10,11... | collective-permute-start | bytes 3145736 | tf_op jit(solution)/shard_map/ppermute | solution.py:490
  307.3 4.7 %collective-permute-start.50 = (f32[128,2048]{1,0:T(8,128)}, f32[128,2048]{1,0:T(8,128)S(1)}, u32[]{:S(2)}, u32[]{:S(2)}) collective-permute-start(f32[128,2048]{1,0:T(8,128)} %collective-permute-done.38.refs_3_), channel_id=1, source_target_pairs={{0,1},{1,0},{2,3},{3,2},{4,5},{5,4},{6,7},{7,6},{8,9},{9,8},{10,11... | collective-permute-start | bytes 3145736 | tf_op jit(solution)/shard_map/ppermute | solution.py:490
  (38 other events, 225.9 us)

commit v5 on v4

--- a/solution.py
+++ b/solution.py
@@ -1251,7 +1251,7 @@
     ]
     parts = length // STEPS
     inverse = 1.0 / retain
-    ends = [at * STEPS // 8 for at in (8 * parts, 5 * parts, 2 * parts, 0)]
+    ends = [at * STEPS // 8 for at in (8 * parts, 4 * parts, 2 * parts, 0)]
     ends = [at // STEPS * STEPS for at in ends]
     for high_end, low_end in zip(ends, ends[1:]):
         carried = halve(carried)
@@ -1259,7 +1259,7 @@
             low_end, high_end, grad_turned, turned, [retain, inverse, unit_decay], carried
         )
     carry, lags = carried
-    ends = [at * STEPS for at in (parts, 5 * parts // 8, 0)]
+    ends = [at * STEPS for at in (parts, parts // 2, 0)]
     left = [later]
     for high_end, low_end in zip(ends, ends[1:]):
         left, carry, lags = halve((left, carry, lags))
@@ -1321,8 +1321,8 @@
             value_weight.shape,
         ]
         first = gathered(chains, copies, shapes)
-        small, first = lax.optimization_barrier((small, first))
         small = paired_sum(small, orders[0][1:3])
+        small, first = tied((small, first), *chains)
         small = paired_sum(small, orders[0][3:5])
     else:
         small = small_sum(small)

time: 317 us -> 316 us (level)
  transfers between devices with their start and end apart: 53 -> 53, of which waited for: 23 -> 20; matrix products, arithmetic and copies ran while one was open for 8% -> 8% of each run, Pallas kernels for 22% -> 23%
where the time goes in v5:
time: 316 us; the launch traced here: 314 us
  Pallas kernels  149 us (47%)
  waiting for transfers between devices  64.9 us (21%)
  starting transfers between devices  54.8 us (17%)
  matrix products  21.9 us (7%)
  local copies, waits for them, and re-layouts  14.8 us (5%)
  other arithmetic  7.09 us (2%)
    pallas_call x1, Pallas kernels, forward_call(): pl.pallas_call(forward_body, grid=(rows,), in_specs=[pl.BlockSpec(memory_...  41.5 us
    ppermute x43, starting transfers between devices, swapped(): lax.ppermute(value, mesh_axes, [(at, at ^ bit) for at in range(device_tot...  35.2 us
    ppermute x10, waiting for transfers between devices, moved(): return lax.ppermute(value, self.axis, pairs)  33 us
    ppermute x43, waiting for transfers between devices, swapped(): lax.ppermute(value, mesh_axes, [(at, at ^ bit) for at in range(device_tot...  31.9 us
    dot_general x12, matrix products, dot_outer(): lax.dot_general(first_op, second_op, (((0,), (0,)), ((), ())), preferred_...  21.9 us
    pallas_call x3, Pallas kernels, sums_call(): pl.pallas_call(sums_body, grid=((high_end - low_end) // STEPS,), in_specs...  20.7 us
    ppermute x10, starting transfers between devices, moved(): return lax.ppermute(value, self.axis, pairs)  19.7 us
    pallas_call x2, Pallas kernels, leave_call(): pl.pallas_call(functools.partial(leave_body, places_before=low_end), grid...  16.9 us
  transfers between devices with their start and end apart: 53, of which 20 were waited for; matrix products, arithmetic and copies ran while one was open for 8% of the time, Pallas kernels for 23%

profile of v5, /device:TPU:0, one launch (start us, length us, event | category | flops | bytes accessed | tf_op | source)
XLA Modules:
  0.0 314.4 jit_solution(13810849532826356677)
XLA Ops:
  2.9 10.4 %enter.1 = (bf16[8,256,512]{2,1,0:T(8,128)(2,1)}, f32[256,8,512]{2,1,0:T(8,128)}, f32[16,8,512]{2,1,0:T(8,128)S(1)}) custom-call(s32[8]{0:T(128)S(1)} %broadcast_subtract_fusion.count_ref, bf16[8,256,512]{2,1,0:T(8,128)(2,1)} %tokens_ref.7, f32[1,512]{1,0:T(1,128)S(1)} %bitcast.110, f32[16,512]{1,0:T(8,128)S(1)} %get-tuple-element.478.retain_ref), custom_call_target="tpu_custom_call" | custom-call | bytes 27000000 | tf_op jit(solution)/shard_map/enter/pallas_call | solution.py:107
  13.3 3.0 collective-permute-start
  17.0 2.9 collective-permute-done
  19.9 5.7 %collective-permute-start.1 = (f32[16,8,256]{2,1,0:T(8,128)S(1)}, f32[16,8,256]{2,1,0:T(8,128)S(1)}, u32[]{:S(2)}, u32[]{:S(2)}) collective-permute-start(f32[16,8,256]{2,1,0:T(8,128)S(1)} %select_add_fusion.1), channel_id=1, source_target_pairs={{0,24},{4,28},{1,25},{5,29},{2,26},{6,30},{3,27},{7,31}} | collective-permute-start | bytes 393224 | tf_op jit(solution)/shard_map/ppermute | solution.py:439
  25.6 1.3 collective-permute-start.2
  26.9 2.5 collective-permute-start.3
  29.4 8.4 %value.1 = (bf16[8,256,1024]{2,1,0:T(8,128)(2,1)}, bf16[8,256,1024]{2,1,0:T(8,128)(2,1)}) custom-call(bf16[8,256,512]{2,1,0:T(8,128)(2,1)} %get-tuple-element.264.normed_ref, bf16[512,1024]{1,0:T(8,128)(2,1)S(1)} %copy-done.26), custom_call_target="tpu_custom_call" | custom-call | flops 2000000000 | bytes 15000000 | tf_op jit(solution)/shard_map/value/pallas_call | solution.py:597
  38.0 1.6 collective-permute-start.4
  39.8 3.3 %collective-permute-done.4 = f32[16,8,256]{2,1,0:T(8,128)S(1)} collective-permute-done((f32[16,8,256]{2,1,0:T(8,128)S(1)}, f32[16,8,256]{2,1,0:T(8,128)S(1)}, u32[]{:S(2)}, u32[]{:S(2)}) %collective-permute-start.4) | collective-permute-done | bytes 131104 | tf_op jit(solution)/shard_map/ppermute | solution.py:439
  43.2 12.6 %average.1 = (f32[16,8,512]{2,1,0:T(8,128)S(1)}, f32[8,256,512]{2,1,0:T(8,128)}) custom-call(f32[256,8,512]{2,1,0:T(8,128)} %get-tuple-element.235.turned_ref, f32[16,512]{1,0:T(8,128)S(1)} %get-tuple-element.478.retain_ref, f32[16,512]{1,0:T(8,128)S(1)} %get-tuple-element.477.mix_ref, f32[16,8,512]{2,1,0:T(8,128)S(1)} %pad_maximum_fusion.held_ref), custom_call_target="tpu_custom_call" | custom-call | bytes 36000000 | tf_op jit(solution)/shard_map/average/pallas_call | solution.py:166
  56.5 41.5 %dense_forward.1 = (bf16[8,256,512]{2,1,0:T(8,128)(2,1)}, bf16[8,256,512]{2,1,0:T(8,128)(2,1)}, bf16[8,256,512]{2,1,0:T(8,128)(2,1)}, bf16[8,256,1024]{2,1,0:T(8...) custom-call(s32[8]{0:T(128)S(1)} %broadcast_subtract_fusion.count_re, ...), custom_call_target="tpu_custom_call" | custom-call | flops 17999998976 | bytes 120000000 | tf_op jit(solution)/shard_map/dense_forward/pallas_call | solution.py:812
  98.1 1.9 fusion.16
  100.0 4.2 %fusion.12 = f32[256,1024]{1,0:T(8,128)S(1)} fusion(bf16[2048,1024]{1,0:T(8,128)(2,1)} %bitcast.144, bf16[2048,512]{1,0:T(8,128)(2,1)} %bitcast.148, s32[]{:T(128)S(6)} %select_n.219), kind=kOutput, calls=%fused_computation.13 | convolution fusion | flops 1073741824 | bytes 6291460 | tf_op jit(solution)/shard_map/dot_general | solution.py:566
  104.4 3.7 %fusion.18 = f32[256,2048]{1,0:T(8,128)S(1)} fusion(bf16[2048,2048]{1,0:T(8,128)(2,1)S(1)} %bitcast.119, bf16[2048,512]{1,0:T(8,128)(2,1)} %bitcast.122, s32[]{:T(128)S(6)} %select_n.219), kind=kOutput, calls=%fused_computation.19 | convolution fusion | flops 2147483648 | bytes 11534340 | tf_op jit(solution)/shard_map/dot_general | solution.py:566
  108.7 1.3 fusion.8
  111.5 1.3 fusion
  115.6 1.3 fusion.4
  122.0 1.3 fusion.6.refs_1_.refs_5_
  123.3 2.6 fusion.22.refs_9_.refs_11_
  126.0 2.9 joined.5
  129.9 1.5 collective-permute-start.12
  131.4 1.6 collective-permute-start.13
  132.9 11.2 %dense_backward.1 = (f32[8,256,512]{2,1,0:T(8,128)S(1)}, f32[8,256,512]{2,1,0:T(8,128)S(1)}, f32[1,512]{1,0:T(1,128)S(1)}, f32[1,512]{1,0:T(1,128)S(1)}) custom-call(bf16[8,256,2048]{2,1,0:T(8,128)(2,1)} %get-tuple-element.261.grad_main_ref, bf16[8,256,128]{2,1,0:T(8,128)(2,1)S(1)} %get-tuple-element.262.grad_shared_ref, ...), custom_call_target="tpu_custom_call" | custom-call | flops 7000000000 | bytes 36000000 | tf_op jit(solution)/shard_map/dense_backward/pallas_call | solution.py:868
  144.2 6.7 %back_enter.1 = (f32[256,8,512]{2,1,0:T(8,128)S(1)}, f32[16,8,512]{2,1,0:T(8,128)S(1)}) custom-call(f32[8,256,512]{2,1,0:T(8,128)S(1)} %get-tuple-element.268.grad_ref, f32[16,512]{1,0:T(8,128)S(1)} %get-tuple-element.478.retain_ref), custom_call_target="tpu_custom_call" | custom-call | bytes 24000000 | tf_op jit(solution)/shard_map/back_enter/pallas_call | solution.py:224
  151.0 2.0 copy-done
  154.9 4.9 %collective-permute-done.11 = f32[16,8,256]{2,1,0:T(8,128)S(1)} collective-permute-done((f32[16,8,256]{2,1,0:T(8,128)}, f32[16,8,256]{2,1,0:T(8,128)S(1)}, u32[]{:S(2)}, u32[]{:S(2)}) %collective-permute-start.11) | collective-permute-done | bytes 131104 | tf_op jit(solution)/shard_map/ppermute | solution.py:439
  162.0 3.2 %joined.6 = (f32[128,1024]{1,0:T(8,128)S(1)}, f32[128,1024]{1,0:T(8,128)S(1)}, f32[64,2048]{1,0:T(8,128)S(1)}, f32[64,2048]{1,0:T(8,128)S(1)}, f32[64,2176]{1,0:T(8,128)S(1)}, /*index=5*/f32[64,2176]{1,0:T(8,128)S(1)}) custom-call(s32[3]{0:T(128)S(1)} %get-tuple-element.489.refs_0_, f32[256,1024]{1,0:T(8,128)S(1)} %get-tuple-element.278.refs_1_.refs_3_, ...), custom_call_target="tpu_custom_call" | custom-call | bytes 6000000 | tf_op jit(solution)/shard_map/joined/pallas_call | solution.py:926
  165.8 1.3 collective-permute-start.18
  167.1 1.7 collective-permute-start.19
  168.8 1.3 collective-permute-start.15
  170.1 1.3 collective-permute-start.16
  171.4 14.7 %collective-permute-done.15 = f32[16,8,256]{2,1,0:T(8,128)S(1)} collective-permute-done((f32[16,8,256]{2,1,0:T(8,128)S(1)}, f32[16,8,256]{2,1,0:T(8,128)S(1)}, u32[]{:S(2)}, u32[]{:S(2)}) %collective-permute-start.15) | collective-permute-done | bytes 131104 | tf_op jit(solution)/shard_map/ppermute | solution.py:439
  186.0 1.3 collective-permute-start.17
  187.3 6.0 %collective-permute-done.17 = f32[16,8,256]{2,1,0:T(8,128)S(1)} collective-permute-done((f32[16,8,256]{2,1,0:T(8,128)S(1)}, f32[16,8,256]{2,1,0:T(8,128)S(1)}, u32[]{:S(2)}, u32[]{:S(2)}) %collective-permute-start.17) | collective-permute-done | bytes 131104 | tf_op jit(solution)/shard_map/ppermute | solution.py:439
  196.6 1.5 collective-permute-start.23
  198.0 1.4 collective-permute-done.21
  199.8 3.7 %collective-permute-done.22.refs_2_.refs_4_ = f32[64,1024]{1,0:T(8,128)S(1)} collective-permute-done((f32[64,1024]{1,0:T(8,128)S(1)}, f32[64,1024]{1,0:T(8,128)S(1)}, u32[]{:S(2)}, u32[]{:S(2)}) %collective-permute-start.22) | collective-permute-done | bytes 262176 | tf_op jit(solution)/shard_map/ppermute | solution.py:490
  204.3 2.9 collective-permute-start.25
  207.3 2.2 copy-done.2
  209.5 10.3 %adjoint_sums.3 = (f32[4,16,8,512]{3,2,1,0:T(8,128)S(1)}, f32[8,8,512]{2,1,0:T(8,128)S(1)}) custom-call(f32[256,8,512]{2,1,0:T(8,128)S(1)} %copy-done.1, f32[256,8,512]{2,1,0:T(8,128)S(1)} %copy-done.2, f32[16,512]{1,0:T(8,128)S(1)} %get-tuple-element.478.retain_ref, f32[16,512]{1,0:T(8,128)S(1)} %get-tuple-element.476.inverse_ref, ...), custom_call_target="tpu_custom_call" | custom-call | bytes 24000000 | tf_op jit(solution)/shard_map/adjoint_sums/pallas_call | solution.py:319
  219.8 3.6 %collective-permute-done.26.refs_3_ = f32[16,2048]{1,0:T(8,128)S(1)} collective-permute-done((f32[16,2048]{1,0:T(8,128)S(1)}, f32[16,2048]{1,0:T(8,128)S(1)}, u32[]{:S(2)}, u32[]{:S(2)}) %collective-permute-start.26) | collective-permute-done | bytes 131104 | tf_op jit(solution)/shard_map/ppermute | solution.py:490
  223.5 2.9 collective-permute-start.28
  226.5 5.2 %adjoint_sums.4 = (f32[4,16,8,512]{3,2,1,0:T(8,128)S(1)}, f32[8,8,512]{2,1,0:T(8,128)S(1)}) custom-call(f32[256,8,512]{2,1,0:T(8,128)S(1)} %copy-done.1, f32[256,8,512]{2,1,0:T(8,128)S(1)} %copy-done.3, f32[16,512]{1,0:T(8,128)S(1)} %get-tuple-element.478.retain_ref, f32[16,512]{1,0:T(8,128)S(1)} %get-tuple-element.476.inverse_ref, ...), custom_call_target="tpu_custom_call" | custom-call | bytes 24000000 | tf_op jit(solution)/shard_map/adjoint_sums/pallas_call | solution.py:319
  232.8 2.4 collective-permute-done.29.refs_4_
  237.2 1.5 collective-permute-start.32
  238.6 5.2 %adjoint_sums.5 = (f32[4,16,8,512]{3,2,1,0:T(8,128)S(1)}, f32[8,8,512]{2,1,0:T(8,128)S(1)}) custom-call(f32[256,8,512]{2,1,0:T(8,128)S(1)} %copy-done.1, f32[256,8,512]{2,1,0:T(8,128)S(1)} %copy-done.3, f32[16,512]{1,0:T(8,128)S(1)} %get-tuple-element.478.retain_ref, f32[16,512]{1,0:T(8,128)S(1)} %get-tuple-element.476.inverse_ref, ...), custom_call_target="tpu_custom_call" | custom-call | bytes 24000000 | tf_op jit(solution)/shard_map/adjoint_sums/pallas_call | solution.py:319
  243.8 1.3 collective-permute-done.31.refs_2_
  247.6 1.5 collective-permute-start.36
  250.0 2.1 collective-permute-start.35
  252.1 8.5 %leave.2 = (f32[16,8,512]{2,1,0:T(8,128)S(1)}, bf16[8,256,512]{2,1,0:T(8,128)(2,1)}) custom-call(s32[8]{0:T(128)S(1)} %broadcast_subtract_fusion.count_ref, bf16[8,256,512]{2,1,0:T(8,128)(2,1)S(1)} %copy-done.4, f32[1,512]{1,0:T(1,128)S(1)} %bitcast.111, f32[8,256,512]{2,1,0:T(8,128)S(1)} %copy-done.6, bf16[8,256,512]{2,1,0:T(8,128)(2,1)S(1)} %copy-done.7, ...), custom_call_target="tpu_custom_call" | custom-call | bytes 24000000 | tf_op jit(solution)/shard_map/leave/pallas_call | solution.py:393
  260.6 3.8 %collective-permute-done.35.refs_4_ = f32[64,2048]{1,0:T(8,128)S(1)} collective-permute-done((f32[64,2048]{1,0:T(8,128)S(1)}, f32[64,2048]{1,0:T(8,128)S(1)}, u32[]{:S(2)}, u32[]{:S(2)}) %collective-permute-start.35) | collective-permute-done | bytes 524320 | tf_op jit(solution)/shard_map/ppermute | solution.py:490
  264.4 3.5 %placed.5 = (f32[256,1024]{1,0:T(8,128)}, f32[128,2048]{1,0:T(8,128)S(1)}, f32[128,2176]{1,0:T(8,128)S(1)}) custom-call(s32[3]{0:T(128)S(1)} %get-tuple-element.489.refs_0_, f32[128,1024]{1,0:T(8,128)S(1)} %get-tuple-element.402.refs_1_, f32[128,1024]{1,0:T(8,128)S(1)} %collective-permute-done.34.refs_2_, f32[64,2048]{1,0:T(8,128)S(1)} %get-tuple-element.404.refs_3_, ...), custom_call_target="tpu_custom_call" | custom-call | bytes 6000000 | tf_op jit(solution)/shard_map/placed/pallas_call | solution.py:970
  268.0 2.6 collective-permute-start.39
  270.6 8.4 %leave.3 = (f32[16,8,512]{2,1,0:T(8,128)}, bf16[8,256,512]{2,1,0:T(8,128)(2,1)}) custom-call(s32[8]{0:T(128)S(1)} %broadcast_subtract_fusion.count_ref, bf16[8,256,512]{2,1,0:T(8,128)(2,1)S(1)} %copy-done.4, f32[1,512]{1,0:T(1,128)S(1)} %bitcast.112, f32[8,256,512]{2,1,0:T(8,128)S(1)} %copy-done.6, ...), custom_call_target="tpu_custom_call", output_to_operand_aliasing={{1}: (9, {})} | custom-call | bytes 24000000 | tf_op jit(solution)/shard_map/leave/pallas_call | solution.py:393
  280.4 5.2 %collective-permute-done.37.refs_1_ = f32[256,1024]{1,0:T(8,128)} collective-permute-done((f32[256,1024]{1,0:T(8,128)}, f32[256,1024]{1,0:T(8,128)}, u32[]{:S(2)}, u32[]{:S(2)}) %collective-permute-start.37) | collective-permute-done | bytes 1048608 | tf_op jit(solution)/shard_map/ppermute | solution.py:490
  286.1 1.9 collective-permute-done.40
  288.1 1.9 collective-permute-start.41
  290.1 1.6 collective-permute-start.43
  291.6 1.3 collective-permute-done.41
  292.9 3.2 %collective-permute-done.42 = f32[40,512]{1,0:T(8,128)S(1)} collective-permute-done((f32[40,512]{1,0:T(8,128)S(1)}, f32[40,512]{1,0:T(8,128)S(1)}, u32[]{:S(2)}, u32[]{:S(2)}) %collective-permute-start.42) | collective-permute-done | bytes 81952 | tf_op jit(solution)/shard_map/ppermute | solution.py:490
  296.7 4.1 %gathered.2 = (f32[1024,512]{1,0:T(8,128)}, f32[1024,512]{1,0:T(8,128)}, f32[512,2176]{1,0:T(8,128)}, f32[512,1024]{1,0:T(8,128)}, f32[512,1024]{1,0:T(8,128)}) custom-call(f32[256,1024]{1,0:T(8,128)} %get-tuple-element.427.refs_0_, f32[256,1024]{1,0:T(8,128)} %collective-permute-done.37.refs_1_, f32[128,2048]{1,0:T(8,128)S(1)} %get-tuple-element.429.refs_2_, ...), custom_call_target="tpu_custom_call" | custom-call | bytes 18000000 | tf_op jit(solution)/shard_map/gathered/pallas_call | solution.py:1034
  303.0 3.5 %collective-permute-start.52 = (f32[40,512]{1,0:T(8,128)S(1)}, f32[40,512]{1,0:T(8,128)S(1)}, u32[]{:S(2)}, u32[]{:S(2)}) collective-permute-start(f32[40,512]{1,0:T(8,128)S(1)} %add_add_fusion.1), channel_id=1, source_target_pairs={{0,24},{1,25},{2,26},{3,27},{4,28},{5,29},{6,30},{7,31},{8,16},{9,... | collective-permute-start | bytes 245768 | tf_op jit(solution)/shard_map/ppermute | solution.py:490
  306.5 3.4 %gathered.3 = (f32[1024,512]{1,0:T(8,128)}, f32[1024,512]{1,0:T(8,128)}, f32[512,2176]{1,0:T(8,128)}, f32[512,1024]{1,0:T(8,128)}, f32[512,1024]{1,0:T(8,128)}) custom-call(f32[256,1024]{1,0:T(8,128)S(1)} %collective-permute-done.44.refs_0_, ...), custom_call_target="tpu_custom_call", output_to_operand_aliasing={{0}: (6, {}), {1}: (7, {}), {2}: (8, {}), {3}: (9, {}), {4}... | custom-call | bytes 18000000 | tf_op jit(solution)/shard_map/gathered/pallas_call | solution.py:1034
  310.0 1.9 collective-permute-done.51
  (215 shorter events, 38.0 us)
Async XLA Ops:
  0.6 28.8 %copy-start.26 = (bf16[512,1024]{1,0:T(8,128)(2,1)S(1)}, bf16[512,1024]{1,0:T(8,128)(2,1)}, u32[]{:S(2)}) copy-start(bf16[512,1024]{1,0:T(8,128)(2,1)} %value_weight_ref.3) | copy-start | bytes 3145732
  13.3 6.5 %collective-permute-start = (f32[16,8,256]{2,1,0:T(8,128)S(1)}, f32[16,8,256]{2,1,0:T(8,128)S(1)}, u32[]{:S(2)}, u32[]{:S(2)}) collective-permute-start(f32[16,8,256]{2,1,0:T(8,128)S(1)} %constant_dynamic-slice_fusion.2), channel_id=1, source_target_pairs={{0,4},{4,0},{8,12},{12,8},{16,20},{20,16},{24,28},{28,24},{1,5},{5... | collective-permute-start | bytes 393224 | tf_op jit(solution)/shard_map/ppermute | solution.py:439
  19.9 18.0 %collective-permute-start.1 = (f32[16,8,256]{2,1,0:T(8,128)S(1)}, f32[16,8,256]{2,1,0:T(8,128)S(1)}, u32[]{:S(2)}, u32[]{:S(2)}) collective-permute-start(f32[16,8,256]{2,1,0:T(8,128)S(1)} %select_add_fusion.1), channel_id=1, source_target_pairs={{0,24},{4,28},{1,25},{5,29},{2,26},{6,30},{3,27},{7,31}} | collective-permute-start | bytes 393224 | tf_op jit(solution)/shard_map/ppermute | solution.py:439
  25.6 12.3 %collective-permute-start.2 = (f32[16,8,256]{2,1,0:T(8,128)S(1)}, f32[16,8,256]{2,1,0:T(8,128)S(1)}, u32[]{:S(2)}, u32[]{:S(2)}) collective-permute-start(f32[16,8,256]{2,1,0:T(8,128)S(1)} %select_add_fusion.1), channel_id=1, source_target_pairs={{0,16},{4,20},{8,24},{12,28},{1,17},{5,21},{9,25},{13,29},{2,18},{... | collective-permute-start | bytes 393224 | tf_op jit(solution)/shard_map/ppermute | solution.py:439
  26.9 11.0 %collective-permute-start.3 = (f32[16,8,256]{2,1,0:T(8,128)S(1)}, f32[16,8,256]{2,1,0:T(8,128)S(1)}, u32[]{:S(2)}, u32[]{:S(2)}) collective-permute-start(f32[16,8,256]{2,1,0:T(8,128)S(1)} %select_add_fusion.1), channel_id=1, source_target_pairs={{0,8},{4,12},{8,16},{12,20},{16,24},{20,28},{1,9},{5,13},{9,17},{1... | collective-permute-start | bytes 393224 | tf_op jit(solution)/shard_map/ppermute | solution.py:439
  38.0 5.0 %collective-permute-start.4 = (f32[16,8,256]{2,1,0:T(8,128)S(1)}, f32[16,8,256]{2,1,0:T(8,128)S(1)}, u32[]{:S(2)}, u32[]{:S(2)}) collective-permute-start(f32[16,8,256]{2,1,0:T(8,128)S(1)} %fusion.26), channel_id=1, source_target_pairs={{0,4},{4,0},{8,12},{12,8},{16,20},{20,16},{24,28},{28,24},{1,5},{5... | collective-permute-start | bytes 393224 | tf_op jit(solution)/shard_map/ppermute | solution.py:439
  43.1 13.4 %copy-start.25 = (bf16[1024,512]{1,0:T(8,128)(2,1)S(1)}, bf16[1024,512]{1,0:T(8,128)(2,1)}, u32[]{:S(2)}) copy-start(bf16[1024,512]{1,0:T(8,128)(2,1)} %output_weight_ref.1) | copy-start | bytes 3145732
  43.1 13.4 %copy-start.28 = (f32[512]{0:T(512)S(1)}, f32[512]{0:T(512)}, u32[]{:S(2)}) copy-start(f32[512]{0:T(512)} %param.23) | copy-start | bytes 6148
  99.9 21.9 %collective-permute-start.10 = (f32[256,128]{1,0:T(8,128)S(1)}, f32[256,128]{1,0:T(8,128)S(1)}, u32[]{:S(2)}, u32[]{:S(2)}) collective-permute-start(f32[256,128]{1,0:T(8,128)S(1)} %fusion.16), channel_id=1, source_target_pairs={{0,1},{1,0},{2,3},{3,2},{4,5},{5,4},{6,7},{7,6},{8,9},{9,8},{10,11... | collective-permute-start | bytes 393224 | tf_op jit(solution)/shard_map/ppermute | solution.py:490
  104.3 21.7 %collective-permute-start.8 = (f32[256,1024]{1,0:T(8,128)S(1)}, f32[256,1024]{1,0:T(8,128)S(1)}, u32[]{:S(2)}, u32[]{:S(2)}) collective-permute-start(f32[256,1024]{1,0:T(8,128)S(1)} %fusion.12), channel_id=1, source_target_pairs={{0,1},{1,0},{2,3},{3,2},{4,5},{5,4},{6,7},{7,6},{8,9},{9,8},{10,11... | collective-permute-start | bytes 3145736 | tf_op jit(solution)/shard_map/ppermute | solution.py:490
  108.1 17.9 %collective-permute-start.7 = (f32[256,2048]{1,0:T(8,128)S(1)}, f32[256,2048]{1,0:T(8,128)S(1)}, u32[]{:S(2)}, u32[]{:S(2)}) collective-permute-start(f32[256,2048]{1,0:T(8,128)S(1)} %fusion.18), channel_id=1, source_target_pairs={{0,1},{1,0},{2,3},{3,2},{4,5},{5,4},{6,7},{7,6},{8,9},{9,8},{10,11... | collective-permute-start | bytes 6291464 | tf_op jit(solution)/shard_map/ppermute | solution.py:490
  110.0 16.0 %collective-permute-start.9 = (f32[256,1024]{1,0:T(8,128)S(1)}, f32[256,1024]{1,0:T(8,128)S(1)}, u32[]{:S(2)}, u32[]{:S(2)}) collective-permute-start(f32[256,1024]{1,0:T(8,128)S(1)} %fusion.8), channel_id=1, source_target_pairs={{0,1},{1,0},{2,3},{3,2},{4,5},{5,4},{6,7},{7,6},{8,9},{9,8},{10,11... | collective-permute-start | bytes 3145736 | tf_op jit(solution)/shard_map/ppermute | solution.py:490
  112.8 13.1 %collective-permute-start.6 = (f32[512,512]{1,0:T(8,128)S(1)}, f32[512,512]{1,0:T(8,128)S(1)}, u32[]{:S(2)}, u32[]{:S(2)}) collective-permute-start(f32[512,512]{1,0:T(8,128)S(1)} %fusion), channel_id=1, source_target_pairs={{0,1},{1,0},{2,3},{3,2},{4,5},{5,4},{6,7},{7,6},{8,9},{9,8},{10,11... | collective-permute-start | bytes 3145736 | tf_op jit(solution)/shard_map/ppermute | solution.py:490
  121.9 4.1 %collective-permute-start.5 = (f32[512,512]{1,0:T(8,128)S(1)}, f32[512,512]{1,0:T(8,128)S(1)}, u32[]{:S(2)}, u32[]{:S(2)}) collective-permute-start(f32[512,512]{1,0:T(8,128)S(1)} %fusion.4), channel_id=1, source_target_pairs={{0,1},{1,0},{2,3},{3,2},{4,5},{5,4},{6,7},{7,6},{8,9},{9,8},{10,11... | collective-permute-start | bytes 3145736 | tf_op jit(solution)/shard_map/ppermute | solution.py:490
  129.8 30.9 %collective-permute-start.14 = (f32[128,2176]{1,0:T(8,128)}, f32[128,2176]{1,0:T(8,128)S(1)}, u32[]{:S(2)}, u32[]{:S(2)}) collective-permute-start(f32[128,2176]{1,0:T(8,128)} %get-tuple-element.275), channel_id=1, source_target_pairs={{0,8},{1,9},{2,10},{3,11},{4,12},{5,13},{6,14},{7,15},{8,0},{9,1},... | collective-permute-start | bytes 3342344 | tf_op jit(solution)/shard_map/ppermute | solution.py:490
  129.9 30.8 %collective-permute-start.12 = (f32[256,1024]{1,0:T(8,128)}, f32[256,1024]{1,0:T(8,128)}, u32[]{:S(2)}, u32[]{:S(2)}) collective-permute-start(f32[256,1024]{1,0:T(8,128)} %get-tuple-element.271), channel_id=1, source_target_pairs={{0,2},{1,3},{2,0},{3,1},{4,6},{5,7},{6,4},{7,5},{8,10},{9,11},{10,... | collective-permute-start | bytes 3145736 | tf_op jit(solution)/shard_map/ppermute | solution.py:490
  131.4 29.4 %collective-permute-start.13 = (f32[128,2048]{1,0:T(8,128)}, f32[128,2048]{1,0:T(8,128)}, u32[]{:S(2)}, u32[]{:S(2)}) collective-permute-start(f32[128,2048]{1,0:T(8,128)} %get-tuple-element.273), channel_id=1, source_target_pairs={{0,4},{1,5},{2,6},{3,7},{4,0},{5,1},{6,2},{7,3},{8,12},{9,13},{10,... | collective-permute-start | bytes 3145736 | tf_op jit(solution)/shard_map/ppermute | solution.py:490
  154.4 5.4 %collective-permute-start.11 = (f32[16,8,256]{2,1,0:T(8,128)}, f32[16,8,256]{2,1,0:T(8,128)S(1)}, u32[]{:S(2)}, u32[]{:S(2)}) collective-permute-start(f32[16,8,256]{2,1,0:T(8,128)} %constant_dynamic-slice_fusion), channel_id=1, source_target_pairs={{28,24},{24,28},{20,16},{16,20},{12,8},{8,12},{4,0},{0,4},{29,25},... | collective-permute-start | bytes 393224 | tf_op jit(solution)/shard_map/ppermute | solution.py:439
  162.0 31.3 %copy-start.37 = (f32[16,256]{1,0:T(8,128)S(1)}, f32[16,256]{1,0:T(8,128)}, u32[]{:S(2)}) copy-start(f32[16,256]{1,0:T(8,128)} %get-tuple-element.457) | copy-start | bytes 49156
  165.2 28.2 %collective-permute-start.20 = (f32[64,2176]{1,0:T(8,128)S(1)}, f32[64,2176]{1,0:T(8,128)S(1)}, u32[]{:S(2)}, u32[]{:S(2)}) collective-permute-start(f32[64,2176]{1,0:T(8,128)S(1)} %get-tuple-element.295), channel_id=1, source_target_pairs={{0,2},{1,3},{2,0},{3,1},{4,6},{5,7},{6,4},{7,5},{8,10},{9,11},{10,... | collective-permute-start | bytes 1671176 | tf_op jit(solution)/shard_map/ppermute | solution.py:490
  165.8 27.6 %collective-permute-start.18 = (f32[128,1024]{1,0:T(8,128)S(1)}, f32[128,1024]{1,0:T(8,128)S(1)}, u32[]{:S(2)}, u32[]{:S(2)}) collective-permute-start(f32[128,1024]{1,0:T(8,128)S(1)} %get-tuple-element.291), channel_id=1, source_target_pairs={{0,4},{1,5},{2,6},{3,7},{4,0},{5,1},{6,2},{7,3},{8,12},{9,13},{10,... | collective-permute-start | bytes 1572872 | tf_op jit(solution)/shard_map/ppermute | solution.py:490
  167.1 26.3 %collective-permute-start.19 = (f32[64,2048]{1,0:T(8,128)S(1)}, f32[64,2048]{1,0:T(8,128)S(1)}, u32[]{:S(2)}, u32[]{:S(2)}) collective-permute-start(f32[64,2048]{1,0:T(8,128)S(1)} %get-tuple-element.293), channel_id=1, source_target_pairs={{0,8},{1,9},{2,10},{3,11},{4,12},{5,13},{6,14},{7,15},{8,0},{9,1},... | collective-permute-start | bytes 1572872 | tf_op jit(solution)/shard_map/ppermute | solution.py:490
  168.8 17.2 %collective-permute-start.15 = (f32[16,8,256]{2,1,0:T(8,128)S(1)}, f32[16,8,256]{2,1,0:T(8,128)S(1)}, u32[]{:S(2)}, u32[]{:S(2)}) collective-permute-start(f32[16,8,256]{2,1,0:T(8,128)S(1)} %select_add_fusion), channel_id=1, source_target_pairs={{28,4},{24,0},{29,5},{25,1},{30,6},{26,2},{31,7},{27,3}} | collective-permute-start | bytes 393224 | tf_op jit(solution)/shard_map/ppermute | solution.py:439
  170.1 17.2 %collective-permute-start.16 = (f32[16,8,256]{2,1,0:T(8,128)S(1)}, f32[16,8,256]{2,1,0:T(8,128)S(1)}, u32[]{:S(2)}, u32[]{:S(2)}) collective-permute-start(f32[16,8,256]{2,1,0:T(8,128)S(1)} %select_add_fusion), channel_id=1, source_target_pairs={{28,12},{24,8},{20,4},{16,0},{29,13},{25,9},{21,5},{17,1},{30,14},... | collective-permute-start | bytes 393224 | tf_op jit(solution)/shard_map/ppermute | solution.py:439
  186.0 7.3 %collective-permute-start.17 = (f32[16,8,256]{2,1,0:T(8,128)S(1)}, f32[16,8,256]{2,1,0:T(8,128)S(1)}, u32[]{:S(2)}, u32[]{:S(2)}) collective-permute-start(f32[16,8,256]{2,1,0:T(8,128)S(1)} %select_add_fusion), channel_id=1, source_target_pairs={{28,20},{24,16},{20,12},{16,8},{12,4},{8,0},{29,21},{25,17},{21,13... | collective-permute-start | bytes 393224 | tf_op jit(solution)/shard_map/ppermute | solution.py:439
  194.4 5.0 %collective-permute-start.21 = (f32[16,8,256]{2,1,0:T(8,128)S(1)}, f32[16,8,256]{2,1,0:T(8,128)S(1)}, u32[]{:S(2)}, u32[]{:S(2)}) collective-permute-start(f32[16,8,256]{2,1,0:T(8,128)S(1)} %fusion.24), channel_id=1, source_target_pairs={{28,24},{24,28},{20,16},{16,20},{12,8},{8,12},{4,0},{0,4},{29,25},... | collective-permute-start | bytes 393224 | tf_op jit(solution)/shard_map/ppermute | solution.py:439
  195.7 7.8 %collective-permute-start.24 = (f32[32,2176]{1,0:T(8,128)S(1)}, f32[32,2176]{1,0:T(8,128)S(1)}, u32[]{:S(2)}, u32[]{:S(2)}) collective-permute-start(f32[32,2176]{1,0:T(8,128)S(1)} %get-tuple-element.316), channel_id=1, source_target_pairs={{0,4},{1,5},{2,6},{3,7},{4,0},{5,1},{6,2},{7,3},{8,12},{9,13},{10,... | collective-permute-start | bytes 835592 | tf_op jit(solution)/shard_map/ppermute | solution.py:490
  196.6 6.9 %collective-permute-start.22 = (f32[64,1024]{1,0:T(8,128)S(1)}, f32[64,1024]{1,0:T(8,128)S(1)}, u32[]{:S(2)}, u32[]{:S(2)}) collective-permute-start(f32[64,1024]{1,0:T(8,128)S(1)} %get-tuple-element.312), channel_id=1, source_target_pairs={{0,8},{1,9},{2,10},{3,11},{4,12},{5,13},{6,14},{7,15},{8,0},{9,1},... | collective-permute-start | bytes 786440 | tf_op jit(solution)/shard_map/ppermute | solution.py:490
  196.6 6.9 %collective-permute-start.23 = (f32[32,2048]{1,0:T(8,128)S(1)}, f32[32,2048]{1,0:T(8,128)S(1)}, u32[]{:S(2)}, u32[]{:S(2)}) collective-permute-start(f32[32,2048]{1,0:T(8,128)S(1)} %get-tuple-element.314), channel_id=1, source_target_pairs={{0,2},{1,3},{2,0},{3,1},{4,6},{5,7},{6,4},{7,5},{8,10},{9,11},{10,... | collective-permute-start | bytes 786440 | tf_op jit(solution)/shard_map/ppermute | solution.py:490
  204.2 19.2 %collective-permute-start.27 = (f32[16,2176]{1,0:T(8,128)S(1)}, f32[16,2176]{1,0:T(8,128)S(1)}, u32[]{:S(2)}, u32[]{:S(2)}) collective-permute-start(f32[16,2176]{1,0:T(8,128)S(1)} %get-tuple-element.340), channel_id=1, source_target_pairs={{0,16},{1,17},{2,18},{3,19},{4,20},{5,21},{6,22},{7,23},{8,24},{9,... | collective-permute-start | bytes 417800 | tf_op jit(solution)/shard_map/ppermute | solution.py:490
  204.3 15.5 %collective-permute-start.25 = (f32[32,1024]{1,0:T(8,128)S(1)}, f32[32,1024]{1,0:T(8,128)S(1)}, u32[]{:S(2)}, u32[]{:S(2)}) collective-permute-start(f32[32,1024]{1,0:T(8,128)S(1)} %get-tuple-element.336), channel_id=1, source_target_pairs={{0,16},{1,17},{2,18},{3,19},{4,20},{5,21},{6,22},{7,23},{8,24},{9,... | collective-permute-start | bytes 393224 | tf_op jit(solution)/shard_map/ppermute | solution.py:490
  207.2 16.2 %collective-permute-start.26 = (f32[16,2048]{1,0:T(8,128)S(1)}, f32[16,2048]{1,0:T(8,128)S(1)}, u32[]{:S(2)}, u32[]{:S(2)}) collective-permute-start(f32[16,2048]{1,0:T(8,128)S(1)} %get-tuple-element.338), channel_id=1, source_target_pairs={{0,16},{1,17},{2,18},{3,19},{4,20},{5,21},{6,22},{7,23},{8,24},{9,... | collective-permute-start | bytes 393224 | tf_op jit(solution)/shard_map/ppermute | solution.py:490
  209.5 17.1 %copy-start.3 = (f32[256,8,512]{2,1,0:T(8,128)S(1)}, f32[256,8,512]{2,1,0:T(8,128)}, u32[]{:S(2)}) copy-start(f32[256,8,512]{2,1,0:T(8,128)} %get-tuple-element.235.turned_ref) | copy-start | bytes 12582916
  223.5 11.7 %collective-permute-start.30 = (f32[16,2176]{1,0:T(8,128)S(1)}, f32[16,2176]{1,0:T(8,128)S(1)}, u32[]{:S(2)}, u32[]{:S(2)}) collective-permute-start(f32[16,2176]{1,0:T(8,128)S(1)} %get-tuple-element.366.refs_5_), channel_id=1, source_target_pairs={{0,16},{1,17},{2,18},{3,19},{4,20},{5,21},{6,22},{7,23},{8,24},{9,... | collective-permute-start | bytes 417800 | tf_op jit(solution)/shard_map/ppermute | solution.py:490
  223.5 9.2 %collective-permute-start.28 = (f32[32,1024]{1,0:T(8,128)S(1)}, f32[32,1024]{1,0:T(8,128)S(1)}, u32[]{:S(2)}, u32[]{:S(2)}) collective-permute-start(f32[32,1024]{1,0:T(8,128)S(1)} %get-tuple-element.362.refs_1_), channel_id=1, source_target_pairs={{0,16},{1,17},{2,18},{3,19},{4,20},{5,21},{6,22},{7,23},{8,24},{9,... | collective-permute-start | bytes 393224 | tf_op jit(solution)/shard_map/ppermute | solution.py:490
  226.4 8.7 %collective-permute-start.29 = (f32[16,2048]{1,0:T(8,128)S(1)}, f32[16,2048]{1,0:T(8,128)S(1)}, u32[]{:S(2)}, u32[]{:S(2)}) collective-permute-start(f32[16,2048]{1,0:T(8,128)S(1)} %get-tuple-element.364.refs_3_), channel_id=1, source_target_pairs={{0,16},{1,17},{2,18},{3,19},{4,20},{5,21},{6,22},{7,23},{8,24},{9,... | collective-permute-start | bytes 393224 | tf_op jit(solution)/shard_map/ppermute | solution.py:490
  236.0 10.4 %collective-permute-start.33 = (f32[32,2176]{1,0:T(8,128)S(1)}, f32[32,2176]{1,0:T(8,128)S(1)}, u32[]{:S(2)}, u32[]{:S(2)}) collective-permute-start(f32[32,2176]{1,0:T(8,128)S(1)} %get-tuple-element.385.refs_5_), channel_id=1, source_target_pairs={{0,4},{1,5},{2,6},{3,7},{4,0},{5,1},{6,2},{7,3},{8,12},{9,13},{10,... | collective-permute-start | bytes 835592 | tf_op jit(solution)/shard_map/ppermute | solution.py:490
  237.2 8.0 %collective-permute-start.31 = (f32[64,1024]{1,0:T(8,128)S(1)}, f32[64,1024]{1,0:T(8,128)S(1)}, u32[]{:S(2)}, u32[]{:S(2)}) collective-permute-start(f32[64,1024]{1,0:T(8,128)S(1)} %get-tuple-element.381.refs_1_), channel_id=1, source_target_pairs={{0,8},{1,9},{2,10},{3,11},{4,12},{5,13},{6,14},{7,15},{8,0},{9,1},... | collective-permute-start | bytes 786440 | tf_op jit(solution)/shard_map/ppermute | solution.py:490
  237.2 9.2 %collective-permute-start.32 = (f32[32,2048]{1,0:T(8,128)S(1)}, f32[32,2048]{1,0:T(8,128)S(1)}, u32[]{:S(2)}, u32[]{:S(2)}) collective-permute-start(f32[32,2048]{1,0:T(8,128)S(1)} %get-tuple-element.383.refs_3_), channel_id=1, source_target_pairs={{0,2},{1,3},{2,0},{3,1},{4,6},{5,7},{6,4},{7,5},{8,10},{9,11},{10,... | collective-permute-start | bytes 786440 | tf_op jit(solution)/shard_map/ppermute | solution.py:490
  238.6 13.5 %copy-start.4 = (bf16[8,256,512]{2,1,0:T(8,128)(2,1)S(1)}, bf16[8,256,512]{2,1,0:T(8,128)(2,1)}, u32[]{:S(2)}) copy-start(bf16[8,256,512]{2,1,0:T(8,128)(2,1)} %tokens_ref.7) | copy-start | bytes 6291460
  238.6 13.5 %copy-start.6 = (f32[8,256,512]{2,1,0:T(8,128)S(1)}, f32[8,256,512]{2,1,0:T(8,128)}, u32[]{:S(2)}) copy-start(f32[8,256,512]{2,1,0:T(8,128)} %copy-done.5) | copy-start | bytes 12582916
  238.6 13.5 %copy-start.7 = (bf16[8,256,512]{2,1,0:T(8,128)(2,1)S(1)}, bf16[8,256,512]{2,1,0:T(8,128)(2,1)}, u32[]{:S(2)}) copy-start(bf16[8,256,512]{2,1,0:T(8,128)(2,1)} %get-tuple-element.267.residual_ref) | copy-start | bytes 6291460
  243.8 16.8 %copy-start.12 = (f32[4,16,8,512]{3,2,1,0:T(8,128)}, f32[4,16,8,512]{3,2,1,0:T(8,128)S(1)}, u32[]{:S(2)}) copy-start(f32[4,16,8,512]{3,2,1,0:T(8,128)S(1)} %get-tuple-element.417) | copy-start | bytes 3145732
  247.6 16.9 %collective-permute-start.36 = (f32[64,2176]{1,0:T(8,128)S(1)}, f32[64,2176]{1,0:T(8,128)S(1)}, u32[]{:S(2)}, u32[]{:S(2)}) collective-permute-start(f32[64,2176]{1,0:T(8,128)S(1)} %get-tuple-element.406.refs_5_), channel_id=1, source_target_pairs={{0,2},{1,3},{2,0},{3,1},{4,6},{5,7},{6,4},{7,5},{8,10},{9,11},{10,... | collective-permute-start | bytes 1671176 | tf_op jit(solution)/shard_map/ppermute | solution.py:490
  249.1 11.5 %collective-permute-start.34 = (f32[128,1024]{1,0:T(8,128)S(1)}, f32[128,1024]{1,0:T(8,128)S(1)}, u32[]{:S(2)}, u32[]{:S(2)}) collective-permute-start(f32[128,1024]{1,0:T(8,128)S(1)} %get-tuple-element.402.refs_1_), channel_id=1, source_target_pairs={{0,4},{1,5},{2,6},{3,7},{4,0},{5,1},{6,2},{7,3},{8,12},{9,13},{10,... | collective-permute-start | bytes 1572872 | tf_op jit(solution)/shard_map/ppermute | solution.py:490
  250.0 14.4 %collective-permute-start.35 = (f32[64,2048]{1,0:T(8,128)S(1)}, f32[64,2048]{1,0:T(8,128)S(1)}, u32[]{:S(2)}, u32[]{:S(2)}) collective-permute-start(f32[64,2048]{1,0:T(8,128)S(1)} %get-tuple-element.404.refs_3_), channel_id=1, source_target_pairs={{0,8},{1,9},{2,10},{3,11},{4,12},{5,13},{6,14},{7,15},{8,0},{9,1},... | collective-permute-start | bytes 1572872 | tf_op jit(solution)/shard_map/ppermute | solution.py:490
  267.9 12.4 %copy-start.20 = (f32[1,512]{1,0:T(1,128)S(1)}, f32[1,512]{1,0:T(1,128)}, u32[]{:S(2)}) copy-start(f32[1,512]{1,0:T(1,128)} %copy-done.19) | copy-start | bytes 6148
  267.9 12.4 %copy-start.22 = (f32[1,512]{1,0:T(1,128)S(1)}, f32[1,512]{1,0:T(1,128)}, u32[]{:S(2)}) copy-start(f32[1,512]{1,0:T(1,128)} %copy-done.21) | copy-start | bytes 6148
  268.0 17.7 %collective-permute-start.39 = (f32[128,2176]{1,0:T(8,128)S(1)}, f32[128,2176]{1,0:T(8,128)S(1)}, u32[]{:S(2)}, u32[]{:S(2)}) collective-permute-start(f32[128,2176]{1,0:T(8,128)S(1)} %get-tuple-element.431.refs_4_), channel_id=1, source_target_pairs={{0,8},{1,9},{2,10},{3,11},{4,12},{5,13},{6,14},{7,15},{8,0},{9,1},... | collective-permute-start | bytes 3342344 | tf_op jit(solution)/shard_map/ppermute | solution.py:490
  270.5 15.1 %collective-permute-start.37 = (f32[256,1024]{1,0:T(8,128)}, f32[256,1024]{1,0:T(8,128)}, u32[]{:S(2)}, u32[]{:S(2)}) collective-permute-start(f32[256,1024]{1,0:T(8,128)} %get-tuple-element.427.refs_0_), channel_id=1, source_target_pairs={{0,2},{1,3},{2,0},{3,1},{4,6},{5,7},{6,4},{7,5},{8,10},{9,11},{10,... | collective-permute-start | bytes 3145736 | tf_op jit(solution)/shard_map/ppermute | solution.py:490
  270.5 15.1 %collective-permute-start.38 = (f32[128,2048]{1,0:T(8,128)S(1)}, f32[128,2048]{1,0:T(8,128)}, u32[]{:S(2)}, u32[]{:S(2)}) collective-permute-start(f32[128,2048]{1,0:T(8,128)S(1)} %get-tuple-element.429.refs_2_), channel_id=1, source_target_pairs={{0,4},{1,5},{2,6},{3,7},{4,0},{5,1},{6,2},{7,3},{8,12},{9,13},{10,... | collective-permute-start | bytes 3145736 | tf_op jit(solution)/shard_map/ppermute | solution.py:490
  285.6 11.0 %collective-permute-start.44 = (f32[256,1024]{1,0:T(8,128)}, f32[256,1024]{1,0:T(8,128)S(1)}, u32[]{:S(2)}, u32[]{:S(2)}) collective-permute-start(f32[256,1024]{1,0:T(8,128)} %get-tuple-element.427.refs_0_), channel_id=1, source_target_pairs={{0,1},{1,0},{2,3},{3,2},{4,5},{5,4},{6,7},{7,6},{8,9},{9,8},{10,11... | collective-permute-start | bytes 3145736 | tf_op jit(solution)/shard_map/ppermute | solution.py:490
  285.6 2.4 collective-permute-start.40
  288.1 4.9 %collective-permute-start.41 = (f32[40,512]{1,0:T(8,128)S(1)}, f32[40,512]{1,0:T(8,128)S(1)}, u32[]{:S(2)}, u32[]{:S(2)}) collective-permute-start(f32[40,512]{1,0:T(8,128)S(1)} %add.218), channel_id=1, source_target_pairs={{0,2},{1,3},{2,0},{3,1},{4,6},{5,7},{6,4},{7,5},{8,10},{9,11},{10,... | collective-permute-start | bytes 245768 | tf_op jit(solution)/shard_map/ppermute | solution.py:490
  290.0 6.2 %collective-permute-start.42 = (f32[40,512]{1,0:T(8,128)S(1)}, f32[40,512]{1,0:T(8,128)S(1)}, u32[]{:S(2)}, u32[]{:S(2)}) collective-permute-start(f32[40,512]{1,0:T(8,128)S(1)} %add.218), channel_id=1, source_target_pairs={{0,4},{1,5},{2,6},{3,7},{4,0},{5,1},{6,2},{7,3},{8,12},{9,13},{10,... | collective-permute-start | bytes 245768 | tf_op jit(solution)/shard_map/ppermute | solution.py:490
  290.1 6.1 %collective-permute-start.43 = (f32[40,512]{1,0:T(8,128)S(1)}, f32[40,512]{1,0:T(8,128)S(1)}, u32[]{:S(2)}, u32[]{:S(2)}) collective-permute-start(f32[40,512]{1,0:T(8,128)S(1)} %add.218), channel_id=1, source_target_pairs={{0,6},{1,7},{2,4},{3,5},{4,2},{5,3},{6,0},{7,1},{8,14},{9,15},{10,... | collective-permute-start | bytes 245768 | tf_op jit(solution)/shard_map/ppermute | solution.py:490
  291.6 10.4 %collective-permute-start.48 = (f32[128,2176]{1,0:T(8,128)S(1)}, f32[128,2176]{1,0:T(8,128)S(1)}, u32[]{:S(2)}, u32[]{:S(2)}) collective-permute-start(f32[128,2176]{1,0:T(8,128)S(1)} %get-tuple-element.431.refs_4_), channel_id=1, source_target_pairs={{0,1},{1,0},{2,3},{3,2},{4,5},{5,4},{6,7},{7,6},{8,9},{9,8},{10,11... | collective-permute-start | bytes 3342344 | tf_op jit(solution)/shard_map/ppermute | solution.py:490
  292.9 9.1 %collective-permute-start.49 = (f32[128,2176]{1,0:T(8,128)S(1)}, f32[128,2176]{1,0:T(8,128)S(1)}, u32[]{:S(2)}, u32[]{:S(2)}) collective-permute-start(f32[128,2176]{1,0:T(8,128)S(1)} %collective-permute-done.39.refs_5_), channel_id=1, source_target_pairs={{0,1},{1,0},{2,3},{3,2},{4,5},{5,4},{6,7},{7,6},{8,9},{9,8},{10,11... | collective-permute-start | bytes 3342344 | tf_op jit(solution)/shard_map/ppermute | solution.py:490
  296.1 4.7 %collective-permute-start.45 = (f32[256,1024]{1,0:T(8,128)}, f32[256,1024]{1,0:T(8,128)S(1)}, u32[]{:S(2)}, u32[]{:S(2)}) collective-permute-start(f32[256,1024]{1,0:T(8,128)} %collective-permute-done.37.refs_1_), channel_id=1, source_target_pairs={{0,1},{1,0},{2,3},{3,2},{4,5},{5,4},{6,7},{7,6},{8,9},{9,8},{10,11... | collective-permute-start | bytes 3145736 | tf_op jit(solution)/shard_map/ppermute | solution.py:490
  296.2 5.3 %collective-permute-start.46 = (f32[128,2048]{1,0:T(8,128)S(1)}, f32[128,2048]{1,0:T(8,128)S(1)}, u32[]{:S(2)}, u32[]{:S(2)}) collective-permute-start(f32[128,2048]{1,0:T(8,128)S(1)} %get-tuple-element.429.refs_2_), channel_id=1, source_target_pairs={{0,1},{1,0},{2,3},{3,2},{4,5},{5,4},{6,7},{7,6},{8,9},{9,8},{10,11... | collective-permute-start | bytes 3145736 | tf_op jit(solution)/shard_map/ppermute | solution.py:490
  296.7 5.4 %collective-permute-start.47 = (f32[128,2048]{1,0:T(8,128)}, f32[128,2048]{1,0:T(8,128)S(1)}, u32[]{:S(2)}, u32[]{:S(2)}) collective-permute-start(f32[128,2048]{1,0:T(8,128)} %collective-permute-done.38.refs_3_), channel_id=1, source_target_pairs={{0,1},{1,0},{2,3},{3,2},{4,5},{5,4},{6,7},{7,6},{8,9},{9,8},{10,11... | collective-permute-start | bytes 3145736 | tf_op jit(solution)/shard_map/ppermute | solution.py:490
  302.1 7.9 %collective-permute-start.50 = (f32[40,512]{1,0:T(8,128)S(1)}, f32[40,512]{1,0:T(8,128)S(1)}, u32[]{:S(2)}, u32[]{:S(2)}) collective-permute-start(f32[40,512]{1,0:T(8,128)S(1)} %add_add_fusion.1), channel_id=1, source_target_pairs={{0,8},{1,9},{2,10},{3,11},{4,12},{5,13},{6,14},{7,15},{8,0},{9,1},... | collective-permute-start | bytes 245768 | tf_op jit(solution)/shard_map/ppermute | solution.py:490
  302.2 9.7 %collective-permute-start.51 = (f32[40,512]{1,0:T(8,128)S(1)}, f32[40,512]{1,0:T(8,128)S(1)}, u32[]{:S(2)}, u32[]{:S(2)}) collective-permute-start(f32[40,512]{1,0:T(8,128)S(1)} %add_add_fusion.1), channel_id=1, source_target_pairs={{0,16},{1,17},{2,18},{3,19},{4,20},{5,21},{6,22},{7,23},{8,24},{9,... | collective-permute-start | bytes 245768 | tf_op jit(solution)/shard_map/ppermute | solution.py:490
  303.0 8.9 %collective-permute-start.52 = (f32[40,512]{1,0:T(8,128)S(1)}, f32[40,512]{1,0:T(8,128)S(1)}, u32[]{:S(2)}, u32[]{:S(2)}) collective-permute-start(f32[40,512]{1,0:T(8,128)S(1)} %add_add_fusion.1), channel_id=1, source_target_pairs={{0,24},{1,25},{2,26},{3,27},{4,28},{5,29},{6,30},{7,31},{8,16},{9,... | collective-permute-start | bytes 245768 | tf_op jit(solution)/shard_map/ppermute | solution.py:490
  (38 other events, 216.9 us)

commit v6 on v5

--- a/solution.py
+++ b/solution.py
@@ -14,9 +14,9 @@
 
 epsilon = 1e-05
 very_low = -1e30
-scan_params = pltpu.CompilerParams(vmem_limit_bytes=20 * 2**20)
+scan_params = pltpu.CompilerParams(vmem_limit_bytes=14 * 2**20)
 front_params = pltpu.CompilerParams(vmem_limit_bytes=52 * 2**20)
-dense_params = pltpu.CompilerParams(vmem_limit_bytes=36 * 2**20)
+dense_params = pltpu.CompilerParams(vmem_limit_bytes=30 * 2**20)
 
 
 def work_cost(flops, seconds):

time: 316 us -> 315 us (level)
  transfers between devices with their start and end apart: 53 -> 53, of which waited for: 20 -> 21; matrix products, arithmetic and copies ran while one was open for 8% -> 8% of each run, Pallas kernels for 23% -> 23%
where the time goes in v6:
time: 315 us; the launch traced here: 314 us
  Pallas kernels  148 us (47%)
  waiting for transfers between devices  64.9 us (21%)
  starting transfers between devices  55.2 us (18%)
  matrix products  21.9 us (7%)
  local copies, waits for them, and re-layouts  14.8 us (5%)
  other arithmetic  7.08 us (2%)
    pallas_call x1, Pallas kernels, forward_call(): pl.pallas_call(forward_body, grid=(rows,), in_specs=[pl.BlockSpec(memory_...  41.5 us
    ppermute x43, starting transfers between devices, swapped(): lax.ppermute(value, mesh_axes, [(at, at ^ bit) for at in range(device_tot...  36.2 us
    ppermute x10, waiting for transfers between devices, moved(): return lax.ppermute(value, self.axis, pairs)  33.5 us
    ppermute x43, waiting for transfers between devices, swapped(): lax.ppermute(value, mesh_axes, [(at, at ^ bit) for at in range(device_tot...  31.4 us
    dot_general x12, matrix products, dot_outer(): lax.dot_general(first_op, second_op, (((0,), (0,)), ((), ())), preferred_...  21.9 us
    pallas_call x3, Pallas kernels, sums_call(): pl.pallas_call(sums_body, grid=((high_end - low_end) // STEPS,), in_specs...  20.7 us
    ppermute x10, starting transfers between devices, moved(): return lax.ppermute(value, self.axis, pairs)  19 us
    pallas_call x2, Pallas kernels, leave_call(): pl.pallas_call(functools.partial(leave_body, places_before=low_end), grid...  16.9 us
  transfers between devices with their start and end apart: 53, of which 21 were waited for; matrix products, arithmetic and copies ran while one was open for 8% of the time, Pallas kernels for 23%

profile of v6, /device:TPU:0, one launch (start us, length us, event | category | flops | bytes accessed | tf_op | source)
XLA Modules:
  0.0 313.9 jit_solution(2698498020307228938)
XLA Ops:
  2.9 10.4 %enter.1 = (bf16[8,256,512]{2,1,0:T(8,128)(2,1)}, f32[256,8,512]{2,1,0:T(8,128)}, f32[16,8,512]{2,1,0:T(8,128)S(1)}) custom-call(s32[8]{0:T(128)S(1)} %broadcast_subtract_fusion.count_ref, bf16[8,256,512]{2,1,0:T(8,128)(2,1)} %tokens_ref.7, f32[1,512]{1,0:T(1,128)S(1)} %bitcast.110, f32[16,512]{1,0:T(8,128)S(1)} %get-tuple-element.478.retain_ref), custom_call_target="tpu_custom_call" | custom-call | bytes 27000000 | tf_op jit(solution)/shard_map/enter/pallas_call | solution.py:107
  13.3 3.0 collective-permute-start
  17.0 2.9 collective-permute-done
  19.9 5.7 %collective-permute-start.1 = (f32[16,8,256]{2,1,0:T(8,128)S(1)}, f32[16,8,256]{2,1,0:T(8,128)S(1)}, u32[]{:S(2)}, u32[]{:S(2)}) collective-permute-start(f32[16,8,256]{2,1,0:T(8,128)S(1)} %select_add_fusion.1), channel_id=1, source_target_pairs={{0,24},{4,28},{1,25},{5,29},{2,26},{6,30},{3,27},{7,31}} | collective-permute-start | bytes 393224 | tf_op jit(solution)/shard_map/ppermute | solution.py:439
  25.6 1.3 collective-permute-start.2
  26.9 2.5 collective-permute-start.3
  29.4 8.4 %value.1 = (bf16[8,256,1024]{2,1,0:T(8,128)(2,1)}, bf16[8,256,1024]{2,1,0:T(8,128)(2,1)}) custom-call(bf16[8,256,512]{2,1,0:T(8,128)(2,1)} %get-tuple-element.264.normed_ref, bf16[512,1024]{1,0:T(8,128)(2,1)S(1)} %copy-done.26), custom_call_target="tpu_custom_call" | custom-call | flops 2000000000 | bytes 15000000 | tf_op jit(solution)/shard_map/value/pallas_call | solution.py:597
  38.0 1.6 collective-permute-start.4
  39.8 3.3 %collective-permute-done.4 = f32[16,8,256]{2,1,0:T(8,128)S(1)} collective-permute-done((f32[16,8,256]{2,1,0:T(8,128)S(1)}, f32[16,8,256]{2,1,0:T(8,128)S(1)}, u32[]{:S(2)}, u32[]{:S(2)}) %collective-permute-start.4) | collective-permute-done | bytes 131104 | tf_op jit(solution)/shard_map/ppermute | solution.py:439
  43.2 12.6 %average.1 = (f32[16,8,512]{2,1,0:T(8,128)S(1)}, f32[8,256,512]{2,1,0:T(8,128)}) custom-call(f32[256,8,512]{2,1,0:T(8,128)} %get-tuple-element.235.turned_ref, f32[16,512]{1,0:T(8,128)S(1)} %get-tuple-element.478.retain_ref, f32[16,512]{1,0:T(8,128)S(1)} %get-tuple-element.477.mix_ref, f32[16,8,512]{2,1,0:T(8,128)S(1)} %pad_maximum_fusion.held_ref), custom_call_target="tpu_custom_call" | custom-call | bytes 36000000 | tf_op jit(solution)/shard_map/average/pallas_call | solution.py:166
  56.5 41.5 %dense_forward.1 = (bf16[8,256,512]{2,1,0:T(8,128)(2,1)}, bf16[8,256,512]{2,1,0:T(8,128)(2,1)}, bf16[8,256,512]{2,1,0:T(8,128)(2,1)}, bf16[8,256,1024]{2,1,0:T(8...) custom-call(s32[8]{0:T(128)S(1)} %broadcast_subtract_fusion.count_re, ...), custom_call_target="tpu_custom_call" | custom-call | flops 17999998976 | bytes 120000000 | tf_op jit(solution)/shard_map/dense_forward/pallas_call | solution.py:812
  98.0 1.9 fusion.16
  100.0 4.2 %fusion.12 = f32[256,1024]{1,0:T(8,128)S(1)} fusion(bf16[2048,1024]{1,0:T(8,128)(2,1)} %bitcast.144, bf16[2048,512]{1,0:T(8,128)(2,1)} %bitcast.148, s32[]{:T(128)S(6)} %select_n.219), kind=kOutput, calls=%fused_computation.13 | convolution fusion | flops 1073741824 | bytes 6291460 | tf_op jit(solution)/shard_map/dot_general | solution.py:566
  104.4 3.7 %fusion.18 = f32[256,2048]{1,0:T(8,128)S(1)} fusion(bf16[2048,2048]{1,0:T(8,128)(2,1)S(1)} %bitcast.121, bf16[2048,512]{1,0:T(8,128)(2,1)} %bitcast.124, s32[]{:T(128)S(6)} %select_n.219), kind=kOutput, calls=%fused_computation.19 | convolution fusion | flops 2147483648 | bytes 11534340 | tf_op jit(solution)/shard_map/dot_general | solution.py:566
  108.6 1.3 fusion.8
  115.6 1.3 fusion.4
  119.8 1.3 fusion.10.refs_15_.refs_21_
  122.0 1.3 fusion.6.refs_1_.refs_5_
  123.3 2.5 fusion.22.refs_9_.refs_11_
  125.9 2.8 joined.5
  129.7 1.5 collective-permute-start.12
  131.3 1.5 collective-permute-start.13
  132.8 10.6 %dense_backward.1 = (f32[8,256,512]{2,1,0:T(8,128)S(1)}, f32[8,256,512]{2,1,0:T(8,128)S(1)}, f32[1,512]{1,0:T(1,128)S(1)}, f32[1,512]{1,0:T(1,128)S(1)}) custom-call(bf16[8,256,2048]{2,1,0:T(8,128)(2,1)} %get-tuple-element.261.grad_main_ref, bf16[8,256,128]{2,1,0:T(8,128)(2,1)S(1)} %get-tuple-element.262.grad_shared_ref, ...), custom_call_target="tpu_custom_call" | custom-call | flops 7000000000 | bytes 36000000 | tf_op jit(solution)/shard_map/dense_backward/pallas_call | solution.py:868
  143.5 6.7 %back_enter.1 = (f32[256,8,512]{2,1,0:T(8,128)S(1)}, f32[16,8,512]{2,1,0:T(8,128)S(1)}) custom-call(f32[8,256,512]{2,1,0:T(8,128)S(1)} %get-tuple-element.268.grad_ref, f32[16,512]{1,0:T(8,128)S(1)} %get-tuple-element.478.retain_ref), custom_call_target="tpu_custom_call" | custom-call | bytes 24000000 | tf_op jit(solution)/shard_map/back_enter/pallas_call | solution.py:224
  150.2 2.0 copy-done
  154.2 5.3 %collective-permute-done.11 = f32[16,8,256]{2,1,0:T(8,128)S(1)} collective-permute-done((f32[16,8,256]{2,1,0:T(8,128)}, f32[16,8,256]{2,1,0:T(8,128)S(1)}, u32[]{:S(2)}, u32[]{:S(2)}) %collective-permute-start.11) | collective-permute-done | bytes 131104 | tf_op jit(solution)/shard_map/ppermute | solution.py:439
  161.7 3.2 %joined.6 = (f32[128,1024]{1,0:T(8,128)S(1)}, f32[128,1024]{1,0:T(8,128)S(1)}, f32[64,2048]{1,0:T(8,128)S(1)}, f32[64,2048]{1,0:T(8,128)S(1)}, f32[64,2176]{1,0:T(8,128)S(1)}, /*index=5*/f32[64,2176]{1,0:T(8,128)S(1)}) custom-call(s32[3]{0:T(128)S(1)} %get-tuple-element.489.refs_0_, f32[256,1024]{1,0:T(8,128)S(1)} %get-tuple-element.278.refs_1_.refs_3_, ...), custom_call_target="tpu_custom_call" | custom-call | bytes 6000000 | tf_op jit(solution)/shard_map/joined/pallas_call | solution.py:926
  165.5 1.5 collective-permute-start.18
  167.0 1.7 collective-permute-start.19
  170.0 1.3 collective-permute-start.16
  171.3 14.6 %collective-permute-done.15 = f32[16,8,256]{2,1,0:T(8,128)S(1)} collective-permute-done((f32[16,8,256]{2,1,0:T(8,128)S(1)}, f32[16,8,256]{2,1,0:T(8,128)S(1)}, u32[]{:S(2)}, u32[]{:S(2)}) %collective-permute-start.15) | collective-permute-done | bytes 131104 | tf_op jit(solution)/shard_map/ppermute | solution.py:439
  186.0 1.3 collective-permute-start.17
  187.3 6.0 %collective-permute-done.17 = f32[16,8,256]{2,1,0:T(8,128)S(1)} collective-permute-done((f32[16,8,256]{2,1,0:T(8,128)S(1)}, f32[16,8,256]{2,1,0:T(8,128)S(1)}, u32[]{:S(2)}, u32[]{:S(2)}) %collective-permute-start.17) | collective-permute-done | bytes 131104 | tf_op jit(solution)/shard_map/ppermute | solution.py:439
  194.9 1.6 collective-permute-start.24
  196.5 1.5 collective-permute-start.23
  198.0 1.4 collective-permute-done.21
  199.7 3.7 %collective-permute-done.22.refs_2_.refs_4_ = f32[64,1024]{1,0:T(8,128)S(1)} collective-permute-done((f32[64,1024]{1,0:T(8,128)S(1)}, f32[64,1024]{1,0:T(8,128)S(1)}, u32[]{:S(2)}, u32[]{:S(2)}) %collective-permute-start.22) | collective-permute-done | bytes 262176 | tf_op jit(solution)/shard_map/ppermute | solution.py:490
  204.2 2.9 collective-permute-start.25
  207.2 2.2 copy-done.2
  209.4 10.3 %adjoint_sums.3 = (f32[4,16,8,512]{3,2,1,0:T(8,128)S(1)}, f32[8,8,512]{2,1,0:T(8,128)S(1)}) custom-call(f32[256,8,512]{2,1,0:T(8,128)S(1)} %copy-done.1, f32[256,8,512]{2,1,0:T(8,128)S(1)} %copy-done.2, f32[16,512]{1,0:T(8,128)S(1)} %get-tuple-element.478.retain_ref, f32[16,512]{1,0:T(8,128)S(1)} %get-tuple-element.476.inverse_ref, ...), custom_call_target="tpu_custom_call" | custom-call | bytes 24000000 | tf_op jit(solution)/shard_map/adjoint_sums/pallas_call | solution.py:319
  219.7 3.7 %collective-permute-done.26.refs_3_ = f32[16,2048]{1,0:T(8,128)S(1)} collective-permute-done((f32[16,2048]{1,0:T(8,128)S(1)}, f32[16,2048]{1,0:T(8,128)S(1)}, u32[]{:S(2)}, u32[]{:S(2)}) %collective-permute-start.26) | collective-permute-done | bytes 131104 | tf_op jit(solution)/shard_map/ppermute | solution.py:490
  223.5 2.9 collective-permute-start.28
  226.5 5.2 %adjoint_sums.4 = (f32[4,16,8,512]{3,2,1,0:T(8,128)S(1)}, f32[8,8,512]{2,1,0:T(8,128)S(1)}) custom-call(f32[256,8,512]{2,1,0:T(8,128)S(1)} %copy-done.1, f32[256,8,512]{2,1,0:T(8,128)S(1)} %copy-done.3, f32[16,512]{1,0:T(8,128)S(1)} %get-tuple-element.478.retain_ref, f32[16,512]{1,0:T(8,128)S(1)} %get-tuple-element.476.inverse_ref, ...), custom_call_target="tpu_custom_call" | custom-call | bytes 24000000 | tf_op jit(solution)/shard_map/adjoint_sums/pallas_call | solution.py:319
  232.9 2.3 collective-permute-done.29.refs_4_
  236.5 1.4 collective-permute-start.32
  238.0 5.2 %adjoint_sums.5 = (f32[4,16,8,512]{3,2,1,0:T(8,128)S(1)}, f32[8,8,512]{2,1,0:T(8,128)S(1)}) custom-call(f32[256,8,512]{2,1,0:T(8,128)S(1)} %copy-done.1, f32[256,8,512]{2,1,0:T(8,128)S(1)} %copy-done.3, f32[16,512]{1,0:T(8,128)S(1)} %get-tuple-element.478.retain_ref, f32[16,512]{1,0:T(8,128)S(1)} %get-tuple-element.476.inverse_ref, ...), custom_call_target="tpu_custom_call" | custom-call | bytes 24000000 | tf_op jit(solution)/shard_map/adjoint_sums/pallas_call | solution.py:319
  243.2 1.3 collective-permute-done.31.refs_2_
  246.9 1.5 collective-permute-start.36
  248.4 1.7 collective-permute-start.34
  250.1 1.6 collective-permute-start.35
  251.6 8.5 %leave.2 = (f32[16,8,512]{2,1,0:T(8,128)S(1)}, bf16[8,256,512]{2,1,0:T(8,128)(2,1)}) custom-call(s32[8]{0:T(128)S(1)} %broadcast_subtract_fusion.count_ref, bf16[8,256,512]{2,1,0:T(8,128)(2,1)S(1)} %copy-done.4, f32[1,512]{1,0:T(1,128)S(1)} %bitcast.111, f32[8,256,512]{2,1,0:T(8,128)S(1)} %copy-done.6, bf16[8,256,512]{2,1,0:T(8,128)(2,1)S(1)} %copy-done.7, ...), custom_call_target="tpu_custom_call" | custom-call | bytes 24000000 | tf_op jit(solution)/shard_map/leave/pallas_call | solution.py:393
  260.1 3.9 %collective-permute-done.35.refs_4_ = f32[64,2048]{1,0:T(8,128)S(1)} collective-permute-done((f32[64,2048]{1,0:T(8,128)S(1)}, f32[64,2048]{1,0:T(8,128)S(1)}, u32[]{:S(2)}, u32[]{:S(2)}) %collective-permute-start.35) | collective-permute-done | bytes 524320 | tf_op jit(solution)/shard_map/ppermute | solution.py:490
  264.0 3.5 %placed.5 = (f32[256,1024]{1,0:T(8,128)}, f32[128,2048]{1,0:T(8,128)S(1)}, f32[128,2176]{1,0:T(8,128)S(1)}) custom-call(s32[3]{0:T(128)S(1)} %get-tuple-element.489.refs_0_, f32[128,1024]{1,0:T(8,128)S(1)} %get-tuple-element.402.refs_1_, f32[128,1024]{1,0:T(8,128)S(1)} %collective-permute-done.34.refs_2_, f32[64,2048]{1,0:T(8,128)S(1)} %get-tuple-element.404.refs_3_, ...), custom_call_target="tpu_custom_call" | custom-call | bytes 6000000 | tf_op jit(solution)/shard_map/placed/pallas_call | solution.py:970
  267.5 2.5 collective-permute-start.39
  270.8 8.4 %leave.3 = (f32[16,8,512]{2,1,0:T(8,128)}, bf16[8,256,512]{2,1,0:T(8,128)(2,1)}) custom-call(s32[8]{0:T(128)S(1)} %broadcast_subtract_fusion.count_ref, bf16[8,256,512]{2,1,0:T(8,128)(2,1)S(1)} %copy-done.4, f32[1,512]{1,0:T(1,128)S(1)} %bitcast.112, f32[8,256,512]{2,1,0:T(8,128)S(1)} %copy-done.6, ...), custom_call_target="tpu_custom_call", output_to_operand_aliasing={{1}: (9, {})} | custom-call | bytes 24000000 | tf_op jit(solution)/shard_map/leave/pallas_call | solution.py:393
  280.6 4.6 %collective-permute-done.37.refs_1_ = f32[256,1024]{1,0:T(8,128)} collective-permute-done((f32[256,1024]{1,0:T(8,128)}, f32[256,1024]{1,0:T(8,128)}, u32[]{:S(2)}, u32[]{:S(2)}) %collective-permute-start.37) | collective-permute-done | bytes 1048608 | tf_op jit(solution)/shard_map/ppermute | solution.py:490
  285.9 1.9 collective-permute-done.40
  287.8 1.6 collective-permute-start.41
  290.0 1.4 collective-permute-start.43
  292.6 3.1 collective-permute-done.42
  296.3 4.1 %gathered.2 = (f32[1024,512]{1,0:T(8,128)}, f32[1024,512]{1,0:T(8,128)}, f32[512,2176]{1,0:T(8,128)}, f32[512,1024]{1,0:T(8,128)}, f32[512,1024]{1,0:T(8,128)}) custom-call(f32[256,1024]{1,0:T(8,128)} %get-tuple-element.427.refs_0_, f32[256,1024]{1,0:T(8,128)} %collective-permute-done.37.refs_1_, f32[128,2048]{1,0:T(8,128)S(1)} %get-tuple-element.429.refs_2_, ...), custom_call_target="tpu_custom_call" | custom-call | bytes 18000000 | tf_op jit(solution)/shard_map/gathered/pallas_call | solution.py:1034
  302.1 4.0 %collective-permute-start.52 = (f32[40,512]{1,0:T(8,128)S(1)}, f32[40,512]{1,0:T(8,128)S(1)}, u32[]{:S(2)}, u32[]{:S(2)}) collective-permute-start(f32[40,512]{1,0:T(8,128)S(1)} %add_add_fusion.1), channel_id=1, source_target_pairs={{0,24},{1,25},{2,26},{3,27},{4,28},{5,29},{6,30},{7,31},{8,16},{9,... | collective-permute-start | bytes 245768 | tf_op jit(solution)/shard_map/ppermute | solution.py:490
  306.1 3.4 %gathered.3 = (f32[1024,512]{1,0:T(8,128)}, f32[1024,512]{1,0:T(8,128)}, f32[512,2176]{1,0:T(8,128)}, f32[512,1024]{1,0:T(8,128)}, f32[512,1024]{1,0:T(8,128)}) custom-call(f32[256,1024]{1,0:T(8,128)S(1)} %collective-permute-done.44.refs_0_, ...), custom_call_target="tpu_custom_call", output_to_operand_aliasing={{0}: (6, {}), {1}: (7, {}), {2}: (8, {}), {3}: (9, {}), {4}... | custom-call | bytes 18000000 | tf_op jit(solution)/shard_map/gathered/pallas_call | solution.py:1034
  309.5 1.9 collective-permute-done.51
  (215 shorter events, 38.1 us)
Async XLA Ops:
  0.6 28.8 %copy-start.26 = (bf16[512,1024]{1,0:T(8,128)(2,1)S(1)}, bf16[512,1024]{1,0:T(8,128)(2,1)}, u32[]{:S(2)}) copy-start(bf16[512,1024]{1,0:T(8,128)(2,1)} %value_weight_ref.3) | copy-start | bytes 3145732
  13.3 6.5 %collective-permute-start = (f32[16,8,256]{2,1,0:T(8,128)S(1)}, f32[16,8,256]{2,1,0:T(8,128)S(1)}, u32[]{:S(2)}, u32[]{:S(2)}) collective-permute-start(f32[16,8,256]{2,1,0:T(8,128)S(1)} %constant_dynamic-slice_fusion.2), channel_id=1, source_target_pairs={{0,4},{4,0},{8,12},{12,8},{16,20},{20,16},{24,28},{28,24},{1,5},{5... | collective-permute-start | bytes 393224 | tf_op jit(solution)/shard_map/ppermute | solution.py:439
  19.9 18.0 %collective-permute-start.1 = (f32[16,8,256]{2,1,0:T(8,128)S(1)}, f32[16,8,256]{2,1,0:T(8,128)S(1)}, u32[]{:S(2)}, u32[]{:S(2)}) collective-permute-start(f32[16,8,256]{2,1,0:T(8,128)S(1)} %select_add_fusion.1), channel_id=1, source_target_pairs={{0,24},{4,28},{1,25},{5,29},{2,26},{6,30},{3,27},{7,31}} | collective-permute-start | bytes 393224 | tf_op jit(solution)/shard_map/ppermute | solution.py:439
  25.6 12.3 %collective-permute-start.2 = (f32[16,8,256]{2,1,0:T(8,128)S(1)}, f32[16,8,256]{2,1,0:T(8,128)S(1)}, u32[]{:S(2)}, u32[]{:S(2)}) collective-permute-start(f32[16,8,256]{2,1,0:T(8,128)S(1)} %select_add_fusion.1), channel_id=1, source_target_pairs={{0,16},{4,20},{8,24},{12,28},{1,17},{5,21},{9,25},{13,29},{2,18},{... | collective-permute-start | bytes 393224 | tf_op jit(solution)/shard_map/ppermute | solution.py:439
  26.9 11.0 %collective-permute-start.3 = (f32[16,8,256]{2,1,0:T(8,128)S(1)}, f32[16,8,256]{2,1,0:T(8,128)S(1)}, u32[]{:S(2)}, u32[]{:S(2)}) collective-permute-start(f32[16,8,256]{2,1,0:T(8,128)S(1)} %select_add_fusion.1), channel_id=1, source_target_pairs={{0,8},{4,12},{8,16},{12,20},{16,24},{20,28},{1,9},{5,13},{9,17},{1... | collective-permute-start | bytes 393224 | tf_op jit(solution)/shard_map/ppermute | solution.py:439
  38.0 5.0 %collective-permute-start.4 = (f32[16,8,256]{2,1,0:T(8,128)S(1)}, f32[16,8,256]{2,1,0:T(8,128)S(1)}, u32[]{:S(2)}, u32[]{:S(2)}) collective-permute-start(f32[16,8,256]{2,1,0:T(8,128)S(1)} %fusion.26), channel_id=1, source_target_pairs={{0,4},{4,0},{8,12},{12,8},{16,20},{20,16},{24,28},{28,24},{1,5},{5... | collective-permute-start | bytes 393224 | tf_op jit(solution)/shard_map/ppermute | solution.py:439
  43.1 13.3 %copy-start.25 = (bf16[1024,512]{1,0:T(8,128)(2,1)S(1)}, bf16[1024,512]{1,0:T(8,128)(2,1)}, u32[]{:S(2)}) copy-start(bf16[1024,512]{1,0:T(8,128)(2,1)} %output_weight_ref.1) | copy-start | bytes 3145732
  43.1 13.3 %copy-start.28 = (f32[512]{0:T(512)S(1)}, f32[512]{0:T(512)}, u32[]{:S(2)}) copy-start(f32[512]{0:T(512)} %param.23) | copy-start | bytes 6148
  99.9 21.9 %collective-permute-start.10 = (f32[256,128]{1,0:T(8,128)S(1)}, f32[256,128]{1,0:T(8,128)S(1)}, u32[]{:S(2)}, u32[]{:S(2)}) collective-permute-start(f32[256,128]{1,0:T(8,128)S(1)} %fusion.16), channel_id=1, source_target_pairs={{0,1},{1,0},{2,3},{3,2},{4,5},{5,4},{6,7},{7,6},{8,9},{9,8},{10,11... | collective-permute-start | bytes 393224 | tf_op jit(solution)/shard_map/ppermute | solution.py:490
  104.3 21.6 %collective-permute-start.8 = (f32[256,1024]{1,0:T(8,128)S(1)}, f32[256,1024]{1,0:T(8,128)S(1)}, u32[]{:S(2)}, u32[]{:S(2)}) collective-permute-start(f32[256,1024]{1,0:T(8,128)S(1)} %fusion.12), channel_id=1, source_target_pairs={{0,1},{1,0},{2,3},{3,2},{4,5},{5,4},{6,7},{7,6},{8,9},{9,8},{10,11... | collective-permute-start | bytes 3145736 | tf_op jit(solution)/shard_map/ppermute | solution.py:490
  108.1 17.8 %collective-permute-start.7 = (f32[256,2048]{1,0:T(8,128)S(1)}, f32[256,2048]{1,0:T(8,128)S(1)}, u32[]{:S(2)}, u32[]{:S(2)}) collective-permute-start(f32[256,2048]{1,0:T(8,128)S(1)} %fusion.18), channel_id=1, source_target_pairs={{0,1},{1,0},{2,3},{3,2},{4,5},{5,4},{6,7},{7,6},{8,9},{9,8},{10,11... | collective-permute-start | bytes 6291464 | tf_op jit(solution)/shard_map/ppermute | solution.py:490
  109.9 16.0 %collective-permute-start.9 = (f32[256,1024]{1,0:T(8,128)S(1)}, f32[256,1024]{1,0:T(8,128)S(1)}, u32[]{:S(2)}, u32[]{:S(2)}) collective-permute-start(f32[256,1024]{1,0:T(8,128)S(1)} %fusion.8), channel_id=1, source_target_pairs={{0,1},{1,0},{2,3},{3,2},{4,5},{5,4},{6,7},{7,6},{8,9},{9,8},{10,11... | collective-permute-start | bytes 3145736 | tf_op jit(solution)/shard_map/ppermute | solution.py:490
  112.8 13.1 %collective-permute-start.6 = (f32[512,512]{1,0:T(8,128)S(1)}, f32[512,512]{1,0:T(8,128)S(1)}, u32[]{:S(2)}, u32[]{:S(2)}) collective-permute-start(f32[512,512]{1,0:T(8,128)S(1)} %fusion), channel_id=1, source_target_pairs={{0,1},{1,0},{2,3},{3,2},{4,5},{5,4},{6,7},{7,6},{8,9},{9,8},{10,11... | collective-permute-start | bytes 3145736 | tf_op jit(solution)/shard_map/ppermute | solution.py:490
  121.8 4.1 %collective-permute-start.5 = (f32[512,512]{1,0:T(8,128)S(1)}, f32[512,512]{1,0:T(8,128)S(1)}, u32[]{:S(2)}, u32[]{:S(2)}) collective-permute-start(f32[512,512]{1,0:T(8,128)S(1)} %fusion.4), channel_id=1, source_target_pairs={{0,1},{1,0},{2,3},{3,2},{4,5},{5,4},{6,7},{7,6},{8,9},{9,8},{10,11... | collective-permute-start | bytes 3145736 | tf_op jit(solution)/shard_map/ppermute | solution.py:490
  129.7 30.7 %collective-permute-start.14 = (f32[128,2176]{1,0:T(8,128)}, f32[128,2176]{1,0:T(8,128)S(1)}, u32[]{:S(2)}, u32[]{:S(2)}) collective-permute-start(f32[128,2176]{1,0:T(8,128)} %get-tuple-element.275), channel_id=1, source_target_pairs={{0,8},{1,9},{2,10},{3,11},{4,12},{5,13},{6,14},{7,15},{8,0},{9,1},... | collective-permute-start | bytes 3342344 | tf_op jit(solution)/shard_map/ppermute | solution.py:490
  129.7 30.7 %collective-permute-start.12 = (f32[256,1024]{1,0:T(8,128)}, f32[256,1024]{1,0:T(8,128)}, u32[]{:S(2)}, u32[]{:S(2)}) collective-permute-start(f32[256,1024]{1,0:T(8,128)} %get-tuple-element.271), channel_id=1, source_target_pairs={{0,2},{1,3},{2,0},{3,1},{4,6},{5,7},{6,4},{7,5},{8,10},{9,11},{10,... | collective-permute-start | bytes 3145736 | tf_op jit(solution)/shard_map/ppermute | solution.py:490
  131.3 29.2 %collective-permute-start.13 = (f32[128,2048]{1,0:T(8,128)}, f32[128,2048]{1,0:T(8,128)}, u32[]{:S(2)}, u32[]{:S(2)}) collective-permute-start(f32[128,2048]{1,0:T(8,128)} %get-tuple-element.273), channel_id=1, source_target_pairs={{0,4},{1,5},{2,6},{3,7},{4,0},{5,1},{6,2},{7,3},{8,12},{9,13},{10,... | collective-permute-start | bytes 3145736 | tf_op jit(solution)/shard_map/ppermute | solution.py:490
  153.6 5.9 %collective-permute-start.11 = (f32[16,8,256]{2,1,0:T(8,128)}, f32[16,8,256]{2,1,0:T(8,128)S(1)}, u32[]{:S(2)}, u32[]{:S(2)}) collective-permute-start(f32[16,8,256]{2,1,0:T(8,128)} %constant_dynamic-slice_fusion), channel_id=1, source_target_pairs={{28,24},{24,28},{20,16},{16,20},{12,8},{8,12},{4,0},{0,4},{29,25},... | collective-permute-start | bytes 393224 | tf_op jit(solution)/shard_map/ppermute | solution.py:439
  161.7 31.6 %copy-start.38 = (f32[16,256]{1,0:T(8,128)S(1)}, f32[16,256]{1,0:T(8,128)}, u32[]{:S(2)}) copy-start(f32[16,256]{1,0:T(8,128)} %get-tuple-element.457) | copy-start | bytes 49156
  164.9 28.5 %collective-permute-start.20 = (f32[64,2176]{1,0:T(8,128)S(1)}, f32[64,2176]{1,0:T(8,128)S(1)}, u32[]{:S(2)}, u32[]{:S(2)}) collective-permute-start(f32[64,2176]{1,0:T(8,128)S(1)} %get-tuple-element.295), channel_id=1, source_target_pairs={{0,2},{1,3},{2,0},{3,1},{4,6},{5,7},{6,4},{7,5},{8,10},{9,11},{10,... | collective-permute-start | bytes 1671176 | tf_op jit(solution)/shard_map/ppermute | solution.py:490
  165.5 27.9 %collective-permute-start.18 = (f32[128,1024]{1,0:T(8,128)S(1)}, f32[128,1024]{1,0:T(8,128)S(1)}, u32[]{:S(2)}, u32[]{:S(2)}) collective-permute-start(f32[128,1024]{1,0:T(8,128)S(1)} %get-tuple-element.291), channel_id=1, source_target_pairs={{0,4},{1,5},{2,6},{3,7},{4,0},{5,1},{6,2},{7,3},{8,12},{9,13},{10,... | collective-permute-start | bytes 1572872 | tf_op jit(solution)/shard_map/ppermute | solution.py:490
  167.0 26.3 %collective-permute-start.19 = (f32[64,2048]{1,0:T(8,128)S(1)}, f32[64,2048]{1,0:T(8,128)S(1)}, u32[]{:S(2)}, u32[]{:S(2)}) collective-permute-start(f32[64,2048]{1,0:T(8,128)S(1)} %get-tuple-element.293), channel_id=1, source_target_pairs={{0,8},{1,9},{2,10},{3,11},{4,12},{5,13},{6,14},{7,15},{8,0},{9,1},... | collective-permute-start | bytes 1572872 | tf_op jit(solution)/shard_map/ppermute | solution.py:490
  168.8 17.2 %collective-permute-start.15 = (f32[16,8,256]{2,1,0:T(8,128)S(1)}, f32[16,8,256]{2,1,0:T(8,128)S(1)}, u32[]{:S(2)}, u32[]{:S(2)}) collective-permute-start(f32[16,8,256]{2,1,0:T(8,128)S(1)} %select_add_fusion), channel_id=1, source_target_pairs={{28,4},{24,0},{29,5},{25,1},{30,6},{26,2},{31,7},{27,3}} | collective-permute-start | bytes 393224 | tf_op jit(solution)/shard_map/ppermute | solution.py:439
  170.0 17.2 %collective-permute-start.16 = (f32[16,8,256]{2,1,0:T(8,128)S(1)}, f32[16,8,256]{2,1,0:T(8,128)S(1)}, u32[]{:S(2)}, u32[]{:S(2)}) collective-permute-start(f32[16,8,256]{2,1,0:T(8,128)S(1)} %select_add_fusion), channel_id=1, source_target_pairs={{28,12},{24,8},{20,4},{16,0},{29,13},{25,9},{21,5},{17,1},{30,14},... | collective-permute-start | bytes 393224 | tf_op jit(solution)/shard_map/ppermute | solution.py:439
  186.0 7.3 %collective-permute-start.17 = (f32[16,8,256]{2,1,0:T(8,128)S(1)}, f32[16,8,256]{2,1,0:T(8,128)S(1)}, u32[]{:S(2)}, u32[]{:S(2)}) collective-permute-start(f32[16,8,256]{2,1,0:T(8,128)S(1)} %select_add_fusion), channel_id=1, source_target_pairs={{28,20},{24,16},{20,12},{16,8},{12,4},{8,0},{29,21},{25,17},{21,13... | collective-permute-start | bytes 393224 | tf_op jit(solution)/shard_map/ppermute | solution.py:439
  194.3 5.0 %collective-permute-start.21 = (f32[16,8,256]{2,1,0:T(8,128)S(1)}, f32[16,8,256]{2,1,0:T(8,128)S(1)}, u32[]{:S(2)}, u32[]{:S(2)}) collective-permute-start(f32[16,8,256]{2,1,0:T(8,128)S(1)} %fusion.24), channel_id=1, source_target_pairs={{28,24},{24,28},{20,16},{16,20},{12,8},{8,12},{4,0},{0,4},{29,25},... | collective-permute-start | bytes 393224 | tf_op jit(solution)/shard_map/ppermute | solution.py:439
  194.9 8.5 %collective-permute-start.24 = (f32[32,2176]{1,0:T(8,128)S(1)}, f32[32,2176]{1,0:T(8,128)S(1)}, u32[]{:S(2)}, u32[]{:S(2)}) collective-permute-start(f32[32,2176]{1,0:T(8,128)S(1)} %get-tuple-element.316), channel_id=1, source_target_pairs={{0,4},{1,5},{2,6},{3,7},{4,0},{5,1},{6,2},{7,3},{8,12},{9,13},{10,... | collective-permute-start | bytes 835592 | tf_op jit(solution)/shard_map/ppermute | solution.py:490
  196.5 6.9 %collective-permute-start.22 = (f32[64,1024]{1,0:T(8,128)S(1)}, f32[64,1024]{1,0:T(8,128)S(1)}, u32[]{:S(2)}, u32[]{:S(2)}) collective-permute-start(f32[64,1024]{1,0:T(8,128)S(1)} %get-tuple-element.312), channel_id=1, source_target_pairs={{0,8},{1,9},{2,10},{3,11},{4,12},{5,13},{6,14},{7,15},{8,0},{9,1},... | collective-permute-start | bytes 786440 | tf_op jit(solution)/shard_map/ppermute | solution.py:490
  196.5 6.9 %collective-permute-start.23 = (f32[32,2048]{1,0:T(8,128)S(1)}, f32[32,2048]{1,0:T(8,128)S(1)}, u32[]{:S(2)}, u32[]{:S(2)}) collective-permute-start(f32[32,2048]{1,0:T(8,128)S(1)} %get-tuple-element.314), channel_id=1, source_target_pairs={{0,2},{1,3},{2,0},{3,1},{4,6},{5,7},{6,4},{7,5},{8,10},{9,11},{10,... | collective-permute-start | bytes 786440 | tf_op jit(solution)/shard_map/ppermute | solution.py:490
  204.1 19.3 %collective-permute-start.27 = (f32[16,2176]{1,0:T(8,128)S(1)}, f32[16,2176]{1,0:T(8,128)S(1)}, u32[]{:S(2)}, u32[]{:S(2)}) collective-permute-start(f32[16,2176]{1,0:T(8,128)S(1)} %get-tuple-element.340), channel_id=1, source_target_pairs={{0,16},{1,17},{2,18},{3,19},{4,20},{5,21},{6,22},{7,23},{8,24},{9,... | collective-permute-start | bytes 417800 | tf_op jit(solution)/shard_map/ppermute | solution.py:490
  204.2 15.5 %collective-permute-start.25 = (f32[32,1024]{1,0:T(8,128)S(1)}, f32[32,1024]{1,0:T(8,128)S(1)}, u32[]{:S(2)}, u32[]{:S(2)}) collective-permute-start(f32[32,1024]{1,0:T(8,128)S(1)} %get-tuple-element.336), channel_id=1, source_target_pairs={{0,16},{1,17},{2,18},{3,19},{4,20},{5,21},{6,22},{7,23},{8,24},{9,... | collective-permute-start | bytes 393224 | tf_op jit(solution)/shard_map/ppermute | solution.py:490
  207.1 16.3 %collective-permute-start.26 = (f32[16,2048]{1,0:T(8,128)S(1)}, f32[16,2048]{1,0:T(8,128)S(1)}, u32[]{:S(2)}, u32[]{:S(2)}) collective-permute-start(f32[16,2048]{1,0:T(8,128)S(1)} %get-tuple-element.338), channel_id=1, source_target_pairs={{0,16},{1,17},{2,18},{3,19},{4,20},{5,21},{6,22},{7,23},{8,24},{9,... | collective-permute-start | bytes 393224 | tf_op jit(solution)/shard_map/ppermute | solution.py:490
  209.4 17.1 %copy-start.3 = (f32[256,8,512]{2,1,0:T(8,128)S(1)}, f32[256,8,512]{2,1,0:T(8,128)}, u32[]{:S(2)}) copy-start(f32[256,8,512]{2,1,0:T(8,128)} %get-tuple-element.235.turned_ref) | copy-start | bytes 12582916
  223.4 11.7 %collective-permute-start.30 = (f32[16,2176]{1,0:T(8,128)S(1)}, f32[16,2176]{1,0:T(8,128)S(1)}, u32[]{:S(2)}, u32[]{:S(2)}) collective-permute-start(f32[16,2176]{1,0:T(8,128)S(1)} %get-tuple-element.366.refs_5_), channel_id=1, source_target_pairs={{0,16},{1,17},{2,18},{3,19},{4,20},{5,21},{6,22},{7,23},{8,24},{9,... | collective-permute-start | bytes 417800 | tf_op jit(solution)/shard_map/ppermute | solution.py:490
  223.5 9.3 %collective-permute-start.28 = (f32[32,1024]{1,0:T(8,128)S(1)}, f32[32,1024]{1,0:T(8,128)S(1)}, u32[]{:S(2)}, u32[]{:S(2)}) collective-permute-start(f32[32,1024]{1,0:T(8,128)S(1)} %get-tuple-element.362.refs_1_), channel_id=1, source_target_pairs={{0,16},{1,17},{2,18},{3,19},{4,20},{5,21},{6,22},{7,23},{8,24},{9,... | collective-permute-start | bytes 393224 | tf_op jit(solution)/shard_map/ppermute | solution.py:490
  226.4 8.7 %collective-permute-start.29 = (f32[16,2048]{1,0:T(8,128)S(1)}, f32[16,2048]{1,0:T(8,128)S(1)}, u32[]{:S(2)}, u32[]{:S(2)}) collective-permute-start(f32[16,2048]{1,0:T(8,128)S(1)} %get-tuple-element.364.refs_3_), channel_id=1, source_target_pairs={{0,16},{1,17},{2,18},{3,19},{4,20},{5,21},{6,22},{7,23},{8,24},{9,... | collective-permute-start | bytes 393224 | tf_op jit(solution)/shard_map/ppermute | solution.py:490
  236.0 9.7 %collective-permute-start.33 = (f32[32,2176]{1,0:T(8,128)S(1)}, f32[32,2176]{1,0:T(8,128)S(1)}, u32[]{:S(2)}, u32[]{:S(2)}) collective-permute-start(f32[32,2176]{1,0:T(8,128)S(1)} %get-tuple-element.385.refs_5_), channel_id=1, source_target_pairs={{0,4},{1,5},{2,6},{3,7},{4,0},{5,1},{6,2},{7,3},{8,12},{9,13},{10,... | collective-permute-start | bytes 835592 | tf_op jit(solution)/shard_map/ppermute | solution.py:490
  236.5 8.0 %collective-permute-start.31 = (f32[64,1024]{1,0:T(8,128)S(1)}, f32[64,1024]{1,0:T(8,128)S(1)}, u32[]{:S(2)}, u32[]{:S(2)}) collective-permute-start(f32[64,1024]{1,0:T(8,128)S(1)} %get-tuple-element.381.refs_1_), channel_id=1, source_target_pairs={{0,8},{1,9},{2,10},{3,11},{4,12},{5,13},{6,14},{7,15},{8,0},{9,1},... | collective-permute-start | bytes 786440 | tf_op jit(solution)/shard_map/ppermute | solution.py:490
  236.5 9.2 %collective-permute-start.32 = (f32[32,2048]{1,0:T(8,128)S(1)}, f32[32,2048]{1,0:T(8,128)S(1)}, u32[]{:S(2)}, u32[]{:S(2)}) collective-permute-start(f32[32,2048]{1,0:T(8,128)S(1)} %get-tuple-element.383.refs_3_), channel_id=1, source_target_pairs={{0,2},{1,3},{2,0},{3,1},{4,6},{5,7},{6,4},{7,5},{8,10},{9,11},{10,... | collective-permute-start | bytes 786440 | tf_op jit(solution)/shard_map/ppermute | solution.py:490
  238.0 13.7 %copy-start.4 = (bf16[8,256,512]{2,1,0:T(8,128)(2,1)S(1)}, bf16[8,256,512]{2,1,0:T(8,128)(2,1)}, u32[]{:S(2)}) copy-start(bf16[8,256,512]{2,1,0:T(8,128)(2,1)} %tokens_ref.7) | copy-start | bytes 6291460
  238.0 13.7 %copy-start.6 = (f32[8,256,512]{2,1,0:T(8,128)S(1)}, f32[8,256,512]{2,1,0:T(8,128)}, u32[]{:S(2)}) copy-start(f32[8,256,512]{2,1,0:T(8,128)} %copy-done.5) | copy-start | bytes 12582916
  238.0 13.7 %copy-start.7 = (bf16[8,256,512]{2,1,0:T(8,128)(2,1)S(1)}, bf16[8,256,512]{2,1,0:T(8,128)(2,1)}, u32[]{:S(2)}) copy-start(bf16[8,256,512]{2,1,0:T(8,128)(2,1)} %get-tuple-element.267.residual_ref) | copy-start | bytes 6291460
  243.2 17.0 %copy-start.12 = (f32[4,16,8,512]{3,2,1,0:T(8,128)}, f32[4,16,8,512]{3,2,1,0:T(8,128)S(1)}, u32[]{:S(2)}) copy-start(f32[4,16,8,512]{3,2,1,0:T(8,128)S(1)} %get-tuple-element.417) | copy-start | bytes 3145732
  246.9 17.1 %collective-permute-start.36 = (f32[64,2176]{1,0:T(8,128)S(1)}, f32[64,2176]{1,0:T(8,128)S(1)}, u32[]{:S(2)}, u32[]{:S(2)}) collective-permute-start(f32[64,2176]{1,0:T(8,128)S(1)} %get-tuple-element.406.refs_5_), channel_id=1, source_target_pairs={{0,2},{1,3},{2,0},{3,1},{4,6},{5,7},{6,4},{7,5},{8,10},{9,11},{10,... | collective-permute-start | bytes 1671176 | tf_op jit(solution)/shard_map/ppermute | solution.py:490
  248.4 11.8 %collective-permute-start.34 = (f32[128,1024]{1,0:T(8,128)S(1)}, f32[128,1024]{1,0:T(8,128)S(1)}, u32[]{:S(2)}, u32[]{:S(2)}) collective-permute-start(f32[128,1024]{1,0:T(8,128)S(1)} %get-tuple-element.402.refs_1_), channel_id=1, source_target_pairs={{0,4},{1,5},{2,6},{3,7},{4,0},{5,1},{6,2},{7,3},{8,12},{9,13},{10,... | collective-permute-start | bytes 1572872 | tf_op jit(solution)/shard_map/ppermute | solution.py:490
  250.1 13.9 %collective-permute-start.35 = (f32[64,2048]{1,0:T(8,128)S(1)}, f32[64,2048]{1,0:T(8,128)S(1)}, u32[]{:S(2)}, u32[]{:S(2)}) collective-permute-start(f32[64,2048]{1,0:T(8,128)S(1)} %get-tuple-element.404.refs_3_), channel_id=1, source_target_pairs={{0,8},{1,9},{2,10},{3,11},{4,12},{5,13},{6,14},{7,15},{8,0},{9,1},... | collective-permute-start | bytes 1572872 | tf_op jit(solution)/shard_map/ppermute | solution.py:490
  267.5 13.0 %copy-start.20 = (f32[1,512]{1,0:T(1,128)S(1)}, f32[1,512]{1,0:T(1,128)}, u32[]{:S(2)}) copy-start(f32[1,512]{1,0:T(1,128)} %copy-done.19) | copy-start | bytes 6148
  267.5 13.0 %copy-start.22 = (f32[1,512]{1,0:T(1,128)S(1)}, f32[1,512]{1,0:T(1,128)}, u32[]{:S(2)}) copy-start(f32[1,512]{1,0:T(1,128)} %copy-done.21) | copy-start | bytes 6148
  267.5 17.9 %collective-permute-start.39 = (f32[128,2176]{1,0:T(8,128)S(1)}, f32[128,2176]{1,0:T(8,128)S(1)}, u32[]{:S(2)}, u32[]{:S(2)}) collective-permute-start(f32[128,2176]{1,0:T(8,128)S(1)} %get-tuple-element.431.refs_4_), channel_id=1, source_target_pairs={{0,8},{1,9},{2,10},{3,11},{4,12},{5,13},{6,14},{7,15},{8,0},{9,1},... | collective-permute-start | bytes 3342344 | tf_op jit(solution)/shard_map/ppermute | solution.py:490
  270.0 15.1 %collective-permute-start.37 = (f32[256,1024]{1,0:T(8,128)}, f32[256,1024]{1,0:T(8,128)}, u32[]{:S(2)}, u32[]{:S(2)}) collective-permute-start(f32[256,1024]{1,0:T(8,128)} %get-tuple-element.427.refs_0_), channel_id=1, source_target_pairs={{0,2},{1,3},{2,0},{3,1},{4,6},{5,7},{6,4},{7,5},{8,10},{9,11},{10,... | collective-permute-start | bytes 3145736 | tf_op jit(solution)/shard_map/ppermute | solution.py:490
  270.5 14.9 %collective-permute-start.38 = (f32[128,2048]{1,0:T(8,128)S(1)}, f32[128,2048]{1,0:T(8,128)}, u32[]{:S(2)}, u32[]{:S(2)}) collective-permute-start(f32[128,2048]{1,0:T(8,128)S(1)} %get-tuple-element.429.refs_2_), channel_id=1, source_target_pairs={{0,4},{1,5},{2,6},{3,7},{4,0},{5,1},{6,2},{7,3},{8,12},{9,13},{10,... | collective-permute-start | bytes 3145736 | tf_op jit(solution)/shard_map/ppermute | solution.py:490
  285.4 10.8 %collective-permute-start.44 = (f32[256,1024]{1,0:T(8,128)}, f32[256,1024]{1,0:T(8,128)S(1)}, u32[]{:S(2)}, u32[]{:S(2)}) collective-permute-start(f32[256,1024]{1,0:T(8,128)} %get-tuple-element.427.refs_0_), channel_id=1, source_target_pairs={{0,1},{1,0},{2,3},{3,2},{4,5},{5,4},{6,7},{7,6},{8,9},{9,8},{10,11... | collective-permute-start | bytes 3145736 | tf_op jit(solution)/shard_map/ppermute | solution.py:490
  285.4 2.4 collective-permute-start.40
  287.8 4.8 %collective-permute-start.41 = (f32[40,512]{1,0:T(8,128)S(1)}, f32[40,512]{1,0:T(8,128)S(1)}, u32[]{:S(2)}, u32[]{:S(2)}) collective-permute-start(f32[40,512]{1,0:T(8,128)S(1)} %add.218), channel_id=1, source_target_pairs={{0,2},{1,3},{2,0},{3,1},{4,6},{5,7},{6,4},{7,5},{8,10},{9,11},{10,... | collective-permute-start | bytes 245768 | tf_op jit(solution)/shard_map/ppermute | solution.py:490
  289.5 6.2 %collective-permute-start.42 = (f32[40,512]{1,0:T(8,128)S(1)}, f32[40,512]{1,0:T(8,128)S(1)}, u32[]{:S(2)}, u32[]{:S(2)}) collective-permute-start(f32[40,512]{1,0:T(8,128)S(1)} %add.218), channel_id=1, source_target_pairs={{0,4},{1,5},{2,6},{3,7},{4,0},{5,1},{6,2},{7,3},{8,12},{9,13},{10,... | collective-permute-start | bytes 245768 | tf_op jit(solution)/shard_map/ppermute | solution.py:490
  290.0 5.7 %collective-permute-start.43 = (f32[40,512]{1,0:T(8,128)S(1)}, f32[40,512]{1,0:T(8,128)S(1)}, u32[]{:S(2)}, u32[]{:S(2)}) collective-permute-start(f32[40,512]{1,0:T(8,128)S(1)} %add.218), channel_id=1, source_target_pairs={{0,6},{1,7},{2,4},{3,5},{4,2},{5,3},{6,0},{7,1},{8,14},{9,15},{10,... | collective-permute-start | bytes 245768 | tf_op jit(solution)/shard_map/ppermute | solution.py:490
  291.4 10.2 %collective-permute-start.48 = (f32[128,2176]{1,0:T(8,128)S(1)}, f32[128,2176]{1,0:T(8,128)S(1)}, u32[]{:S(2)}, u32[]{:S(2)}) collective-permute-start(f32[128,2176]{1,0:T(8,128)S(1)} %get-tuple-element.431.refs_4_), channel_id=1, source_target_pairs={{0,1},{1,0},{2,3},{3,2},{4,5},{5,4},{6,7},{7,6},{8,9},{9,8},{10,11... | collective-permute-start | bytes 3342344 | tf_op jit(solution)/shard_map/ppermute | solution.py:490
  292.6 8.9 %collective-permute-start.49 = (f32[128,2176]{1,0:T(8,128)S(1)}, f32[128,2176]{1,0:T(8,128)S(1)}, u32[]{:S(2)}, u32[]{:S(2)}) collective-permute-start(f32[128,2176]{1,0:T(8,128)S(1)} %collective-permute-done.39.refs_5_), channel_id=1, source_target_pairs={{0,1},{1,0},{2,3},{3,2},{4,5},{5,4},{6,7},{7,6},{8,9},{9,8},{10,11... | collective-permute-start | bytes 3342344 | tf_op jit(solution)/shard_map/ppermute | solution.py:490
  295.7 4.7 %collective-permute-start.45 = (f32[256,1024]{1,0:T(8,128)}, f32[256,1024]{1,0:T(8,128)S(1)}, u32[]{:S(2)}, u32[]{:S(2)}) collective-permute-start(f32[256,1024]{1,0:T(8,128)} %collective-permute-done.37.refs_1_), channel_id=1, source_target_pairs={{0,1},{1,0},{2,3},{3,2},{4,5},{5,4},{6,7},{7,6},{8,9},{9,8},{10,11... | collective-permute-start | bytes 3145736 | tf_op jit(solution)/shard_map/ppermute | solution.py:490
  295.7 5.3 %collective-permute-start.46 = (f32[128,2048]{1,0:T(8,128)S(1)}, f32[128,2048]{1,0:T(8,128)S(1)}, u32[]{:S(2)}, u32[]{:S(2)}) collective-permute-start(f32[128,2048]{1,0:T(8,128)S(1)} %get-tuple-element.429.refs_2_), channel_id=1, source_target_pairs={{0,1},{1,0},{2,3},{3,2},{4,5},{5,4},{6,7},{7,6},{8,9},{9,8},{10,11... | collective-permute-start | bytes 3145736 | tf_op jit(solution)/shard_map/ppermute | solution.py:490
  296.2 5.4 %collective-permute-start.47 = (f32[128,2048]{1,0:T(8,128)}, f32[128,2048]{1,0:T(8,128)S(1)}, u32[]{:S(2)}, u32[]{:S(2)}) collective-permute-start(f32[128,2048]{1,0:T(8,128)} %collective-permute-done.38.refs_3_), channel_id=1, source_target_pairs={{0,1},{1,0},{2,3},{3,2},{4,5},{5,4},{6,7},{7,6},{8,9},{9,8},{10,11... | collective-permute-start | bytes 3145736 | tf_op jit(solution)/shard_map/ppermute | solution.py:490
  301.6 7.9 %collective-permute-start.50 = (f32[40,512]{1,0:T(8,128)S(1)}, f32[40,512]{1,0:T(8,128)S(1)}, u32[]{:S(2)}, u32[]{:S(2)}) collective-permute-start(f32[40,512]{1,0:T(8,128)S(1)} %add_add_fusion.1), channel_id=1, source_target_pairs={{0,8},{1,9},{2,10},{3,11},{4,12},{5,13},{6,14},{7,15},{8,0},{9,1},... | collective-permute-start | bytes 245768 | tf_op jit(solution)/shard_map/ppermute | solution.py:490
  301.7 9.7 %collective-permute-start.51 = (f32[40,512]{1,0:T(8,128)S(1)}, f32[40,512]{1,0:T(8,128)S(1)}, u32[]{:S(2)}, u32[]{:S(2)}) collective-permute-start(f32[40,512]{1,0:T(8,128)S(1)} %add_add_fusion.1), channel_id=1, source_target_pairs={{0,16},{1,17},{2,18},{3,19},{4,20},{5,21},{6,22},{7,23},{8,24},{9,... | collective-permute-start | bytes 245768 | tf_op jit(solution)/shard_map/ppermute | solution.py:490
  302.1 9.4 %collective-permute-start.52 = (f32[40,512]{1,0:T(8,128)S(1)}, f32[40,512]{1,0:T(8,128)S(1)}, u32[]{:S(2)}, u32[]{:S(2)}) collective-permute-start(f32[40,512]{1,0:T(8,128)S(1)} %add_add_fusion.1), channel_id=1, source_target_pairs={{0,24},{1,25},{2,26},{3,27},{4,28},{5,29},{6,30},{7,31},{8,16},{9,... | collective-permute-start | bytes 245768 | tf_op jit(solution)/shard_map/ppermute | solution.py:490
  (38 other events, 218.2 us)
